TPU v7x, 32 devices: a whole 2x2x4 slice. The times are simulated.
32 devices in a mesh: px: 8 (over z, y), py: 4 (over x, core).
Axes of the slice: x: 2, y: 2, z: 4, core: 2. Of those that a mesh axis runs over, the one named last changes fastest.
Arguments:
- residual: float32 [32, 128, 512], P(None, 'px', 'py'), may hold values from -6 to 6
- factor_fine: bfloat16 [64, 4, 520, 256], P('px', 'py'), may hold values from -0.25 to 0.25
- factor_one: bfloat16 [32, 2, 520, 256], P('px'), may hold values from -0.25 to 0.25
- factor_two: bfloat16 [16, 1, 520, 256], P('px'), may hold values from -0.25 to 0.25
- factor_three: bfloat16 [8, 1, 264, 128], P('px'), may hold values from -0.375 to 0.375
- factor_four: bfloat16 [4, 1, 136, 64], replicated, may hold values from -0.5 to 0.5
- coarse_inverse: bfloat16 [64, 64], replicated, may hold values from -0.75 to 0.75
Outputs:
- preconditioned: float32 [32, 128, 512], P(None, 'px', 'py')
All inputs are finite; a program needn't handle non-finite values.
Results may differ from a plain program's by a relative error of at most 0.0029.
Values sent between devices are 32-bit elements; how exact they have to be, the bound alone decides.
No kernel may reach another device: no remote copies, remote signals or barrier semaphores. Data moves between devices by JAX's collectives and lax.ppermute only.
A program may use at most 128 MiB of HBM per device.

v0:
```python
import math

import jax
import jax.numpy as jnp
from jax import lax
from jax.sharding import PartitionSpec as P

tap_scale = 1.0 / math.sqrt(20.0)


def extended(block, sides, width):
    for axis, dim in sides:
        count = lax.axis_size(axis)
        forward = [(i, i + 1) for i in range(count - 1)]
        backward = [(target, source) for source, target in forward]
        low = lax.ppermute(
            lax.slice_in_dim(block, block.shape[dim] - width, None, axis=dim), axis, forward
        )
        high = lax.ppermute(lax.slice_in_dim(block, 0, width, axis=dim), axis, backward)
        block = jnp.concatenate([low, block, high], axis=dim)
    return block


def shrink(padded, dimension):
    length = padded.shape[dimension] - 2
    before = padded.shape[:dimension]
    after = padded.shape[dimension + 1 :]
    lower = lax.slice_in_dim(padded, 0, length, axis=dimension).reshape(
        before + (length // 2, 2) + after
    )
    upper = lax.slice_in_dim(padded, 2, length + 2, axis=dimension).reshape(
        before + (length // 2, 2) + after
    )
    outer_low = lax.index_in_dim(lower, 0, dimension + 1, keepdims=False)
    inner_low = lax.index_in_dim(lower, 1, dimension + 1, keepdims=False)
    inner_high = lax.index_in_dim(upper, 0, dimension + 1, keepdims=False)
    outer_high = lax.index_in_dim(upper, 1, dimension + 1, keepdims=False)
    return tap_scale * (outer_low + 3.0 * inner_low + 3.0 * inner_high + outer_high)


def prolong(padded, dimension):
    length = padded.shape[dimension] - 2
    left = lax.slice_in_dim(padded, 0, length, axis=dimension)
    centre = lax.slice_in_dim(padded, 1, length + 1, axis=dimension)
    right = lax.slice_in_dim(padded, 2, length + 2, axis=dimension)
    even_cells = tap_scale * (3.0 * centre + left)
    odd_cells = tap_scale * (3.0 * centre + right)
    stacked = jnp.stack([even_cells, odd_cells], axis=dimension + 1)
    target = list(centre.shape)
    target[dimension] = 2 * length
    return stacked.reshape(tuple(target))


def pad_both(field):
    return jnp.pad(field, ((0, 0), (1, 1), (1, 1)))


def pad_sides(field):
    return jnp.pad(field, ((0, 0), (0, 0), (1, 1)))


def restrict_both(padded):
    return shrink(shrink(padded, 1), 2)


def prolong_both(padded):
    return prolong(prolong(padded, 1), 2)


def solve_blocks(padded, factor):
    width = factor.shape[3] // 2
    systems, height, breadth = padded.shape
    inner_rows = height - 2
    inner_cols = breadth - 2
    tiles = inner_cols // width
    pairs = inner_rows // 2
    top = padded[:, :inner_rows].reshape(systems, pairs, 2, breadth)
    bottom = padded[:, 2:].reshape(systems, pairs, 2, breadth)
    strips = jnp.concatenate([top, bottom], axis=2).astype(jnp.bfloat16)
    main = strips[..., :inner_cols].reshape(systems, pairs, 4, tiles, width)
    extra = jnp.pad(strips[..., width:], ((0, 0), (0, 0), (0, 0), (0, width - 2)))
    extra = extra.reshape(systems, pairs, 4, tiles, width)[..., :2]
    windows = jnp.concatenate([main, extra], axis=4)
    shaped_factor = factor.reshape(factor.shape[0], factor.shape[1], 4, width + 2, 2, width)
    solved = jnp.einsum(
        "rbkqe,bqkejc->rbjqc", windows, shaped_factor, preferred_element_type=jnp.float32
    )
    return solved.reshape(systems, inner_rows, inner_cols)


def row_rim(field):
    return extended(field, (("px", 1),), 1)


def per_device(
    residual, factor_fine, factor_one, factor_two, factor_three, factor_four, coarse_inverse
):
    padded_fine = extended(residual, (("px", 1), ("py", 2)), 1)
    part_fine = solve_blocks(padded_fine, factor_fine)
    restricted_one = restrict_both(padded_fine)
    level_one = lax.all_gather(restricted_one, "py", axis=2, tiled=True)
    padded_one = pad_sides(row_rim(level_one))
    part_one = solve_blocks(padded_one, factor_one)
    level_two = restrict_both(padded_one)
    padded_two = pad_sides(row_rim(level_two))
    part_two = solve_blocks(padded_two, factor_two)
    level_three = restrict_both(padded_two)
    rows_three = level_three.shape[1]
    start_three = lax.axis_index("px") * rows_three
    whole_three = lax.all_gather(level_three, "px", axis=1, tiled=True)
    full_three = pad_both(whole_three)
    padded_three = lax.dynamic_slice_in_dim(full_three, start_three, rows_three + 2, 1)
    part_three = solve_blocks(padded_three, factor_three)
    whole_four = restrict_both(full_three)
    full_four = pad_both(whole_four)
    part_four = solve_blocks(full_four, factor_four)
    level_five = restrict_both(full_four)
    systems, rows_five, cols_five = level_five.shape
    flat_five = level_five.reshape(systems, rows_five * cols_five).astype(jnp.bfloat16)
    part_five = jnp.dot(flat_five, coarse_inverse, preferred_element_type=jnp.float32)
    correction_four = part_four + prolong_both(
        pad_both(part_five.reshape(systems, rows_five, cols_five))
    )
    lifted_rows = prolong(pad_both(correction_four), 1)
    own_rows = lax.dynamic_slice_in_dim(lifted_rows, start_three, rows_three, 1)
    correction_three = part_three + prolong(own_rows, 2)
    correction_two = part_two + prolong_both(pad_sides(row_rim(correction_three)))
    correction_one = part_one + prolong_both(pad_sides(row_rim(correction_two)))
    lifted_fine = prolong(pad_sides(row_rim(correction_one)), 1)
    half_cols = part_fine.shape[2] // 2
    own_cols = lax.dynamic_slice_in_dim(
        lifted_fine, lax.axis_index("py") * half_cols, half_cols + 2, 2
    )
    return part_fine + prolong(own_cols, 2)


def solution(mesh):
    placed = (
        P(None, "px", "py"),
        P("px", "py", None, None),
        P("px", None, None, None),
        P("px", None, None, None),
        P("px", None, None, None),
        P(),
        P(),
    )
    return jax.shard_map(
        per_device, mesh=mesh, in_specs=placed, out_specs=P(None, "px", "py"), check_vma=False
    )
```

profile of v0, /device:TPU:0, one launch (start us, length us, event | category | flops | bytes accessed | tf_op | source)
XLA Modules:
  0.0 131.1 jit_solution(4127775674162808595)
XLA Ops:
  0.0 1.1 fusion.146
  1.1 1.3 collective-permute-start.1
  2.4 5.5 %collective-permute-start = (f32[32,1,128]{2,1,0:T(1,128)S(1)}, f32[32,1,128]{2,1,0:T(1,128)S(1)}, u32[]{:S(2)}, u32[]{:S(2)}) collective-permute-start(f32[32,1,128]{2,1,0:T(1,128)S(1)} %get-tuple-element.47), channel_id=1, source_target_pairs={{0,4},{4,8},{8,12},{12,16},{16,20},{20,24},{24,28},{1,5},{5,9},{9,... | collective-permute-start | bytes 49160 | tf_op jit(solution)/shard_map/ppermute | solution.py:16
  8.0 1.4 %collective-permute-done = f32[32,1,128]{2,1,0:T(1,128)S(1)} collective-permute-done((f32[32,1,128]{2,1,0:T(1,128)S(1)}, f32[32,1,128]{2,1,0:T(1,128)S(1)}, u32[]{:S(2)}, u32[]{:S(2)}) %collective-permute-start) | collective-permute-done | bytes 16416 | tf_op jit(solution)/shard_map/ppermute | solution.py:16
  9.4 1.0 pad_maximum_fusion.3
  10.4 1.0 fusion.137
  11.4 1.3 collective-permute-start.3
  12.7 3.1 %collective-permute-start.2 = (f32[32,18,1]{2,1,0:T(8,128)}, f32[32,18,1]{2,1,0:T(8,128)S(1)}, u32[]{:S(2)}, u32[]{:S(2)}) collective-permute-start(f32[32,18,1]{2,1,0:T(8,128)} %get-tuple-element.23), channel_id=1, source_target_pairs={{0,1},{1,2},{2,3},{4,5},{5,6},{6,7},{8,9},{9,10},{10,11},{12,13},{... | collective-permute-start | bytes 6920 | tf_op jit(solution)/shard_map/ppermute | solution.py:16
  15.8 2.1 %reshape.298 = bf16[8,4,130,2,128]{4,3,2,1,0:T(2,128)(2,1)} reshape(bf16[8,1,520,256]{3,2,1,0:T(8,128)(2,1)S(1)} %copy-done) | data formatting | bytes 4259840 | tf_op jit(solution)/shard_map/reshape
  17.9 5.1 %reshape.306 = bf16[4,2,4,130,2,128]{5,4,3,2,1,0:T(2,128)(2,1)} reshape(bf16[4,2,520,256]{3,2,1,0:T(8,128)(2,1)} %param.9) | data formatting | bytes 4259840 | tf_op jit(solution)/shard_map/reshape | solution.py:84
  23.0 0.9 reshape.315
  24.2 0.7 copy.251
  25.0 0.5 pad_maximum_fusion
  25.6 0.3 copy.214
  26.0 0.3 copy.215
  27.1 10.4 %all-gather = f32[32,8,256,1]{0,1,3,2:T(8,128)S(1)} all-gather(f32[32,8,64,1]{0,1,3,2:T(8,128)S(1)} %fusion.42), channel_id=2, replica_groups=mesh['px'=8,'py'=4] {'py'}, dimensions={2}, use_global_device_ids=true | all-gather | bytes 327680 | tf_op jit(solution)/shard_map/all_gather | solution.py:101
  37.5 0.4 copy.220
  37.9 1.3 collective-permute-start.5
  39.2 5.7 %collective-permute-start.4 = (f32[32,1,256]{2,1,0:T(1,128)S(1)}, f32[32,1,256]{2,1,0:T(1,128)S(1)}, u32[]{:S(2)}, u32[]{:S(2)}) collective-permute-start(f32[32,1,256]{2,1,0:T(1,128)S(1)} %get-tuple-element.43), channel_id=1, source_target_pairs={{0,4},{4,8},{8,12},{12,16},{16,20},{20,24},{24,28},{1,5},{5,9},{9,... | collective-permute-start | bytes 98312 | tf_op jit(solution)/shard_map/ppermute | solution.py:16
  44.9 0.9 fusion.29
  45.8 0.7 collective-permute-done.4
  46.5 0.5 select_maximum_fusion.2
  47.4 0.3 fusion.136
  48.0 0.3 fusion.135
  49.4 0.7 fusion.39
  50.2 1.3 collective-permute-start.7
  51.5 5.7 %collective-permute-start.6 = (f32[32,1,128]{0,2,1:T(8,128)S(1)}, f32[32,1,128]{0,2,1:T(8,128)S(1)}, u32[]{:S(2)}, u32[]{:S(2)}) collective-permute-start(f32[32,1,128]{0,2,1:T(8,128)S(1)} %get-tuple-element.41), channel_id=1, source_target_pairs={{0,4},{4,8},{8,12},{12,16},{16,20},{20,24},{24,28},{1,5},{5,9},{9,... | collective-permute-start | bytes 49160 | tf_op jit(solution)/shard_map/ppermute | solution.py:16
  57.5 0.7 copy.328
  58.3 0.8 collective-permute-done.6
  60.2 35.8 %all-gather.1 = f32[32,16,64,1]{2,0,3,1:T(8,128)S(1)} all-gather(f32[32,2,64,1]{2,0,3,1:T(8,128)S(1)} %add_multiply_fusion), channel_id=3, replica_groups=mesh['px'=8,'py'=4] {'px'}, dimensions={1}, use_global_device_ids=true | all-gather | bytes 147456 | tf_op jit(solution)/shard_map/all_gather | solution.py:110
  97.7 0.3 fusion.49
  99.9 1.4 %collective-permute-start.9 = (f32[32,1,64]{2,0,1:T(8,128)S(1)}, f32[32,1,64]{2,0,1:T(8,128)S(1)}, u32[]{:S(2)}, u32[]{:S(2)}) collective-permute-start(f32[32,1,64]{2,0,1:T(8,128)S(1)} %get-tuple-element.76), channel_id=1, source_target_pairs={{4,0},{8,4},{12,8},{16,12},{20,16},{24,20},{28,24},{5,1},{9,5},{13... | collective-permute-start | bytes 24584 | tf_op jit(solution)/shard_map/ppermute | solution.py:19
  101.4 4.7 %collective-permute-start.8 = (f32[32,1,64]{2,0,1:T(8,128)S(1)}, f32[32,1,64]{2,0,1:T(8,128)S(1)}, u32[]{:S(2)}, u32[]{:S(2)}) collective-permute-start(f32[32,1,64]{2,0,1:T(8,128)S(1)} %get-tuple-element.75), channel_id=1, source_target_pairs={{0,4},{4,8},{8,12},{12,16},{16,20},{20,24},{24,28},{1,5},{5,9},{9,... | collective-permute-start | bytes 24584 | tf_op jit(solution)/shard_map/ppermute | solution.py:16
  106.6 0.8 collective-permute-done.8
  107.8 1.3 collective-permute-start.11
  109.1 4.8 %collective-permute-start.10 = (f32[32,1,128]{0,2,1:T(8,128)S(1)}, f32[32,1,128]{0,2,1:T(8,128)S(1)}, u32[]{:S(2)}, u32[]{:S(2)}) collective-permute-start(f32[32,1,128]{0,2,1:T(8,128)S(1)} %get-tuple-element.31), channel_id=1, source_target_pairs={{0,4},{4,8},{8,12},{12,16},{16,20},{20,24},{24,28},{1,5},{5,9},{9,... | collective-permute-start | bytes 49160 | tf_op jit(solution)/shard_map/ppermute | solution.py:16
  114.0 1.5 %fusion.7 = f32[32,4,2,2,128]{4,0,2,3,1:T(8,128)S(1)} fusion(bf16[4,2,4,130,2,128]{5,4,3,2,1,0:T(2,128)(2,1)S(1)} %copy-done.2, bf16[32,4,4,2,2]{4,0,2,3,1:T(8,128)(2,1)S(1)} %copy.307, bf16[32,4,4,2,128]{4,0,2,3,1:T(8,128)(2,1)} %bitcast.262), kind=kOutput, calls=%fused_computation.7 | convolution fusion | flops 68689920 | bytes 2658304 | tf_op jit(solution)/shard_map/rbkqe,bqkejc->rbjqc/dot_general | solution.py:85
  115.7 0.9 reshape.307
  117.3 0.5 copy.273
  117.8 0.4 copy.274
  118.2 1.0 add.313
  119.2 1.3 collective-permute-start.13
  120.5 5.5 %collective-permute-start.12 = (f32[32,1,256]{2,1,0:T(1,128)S(1)}, f32[32,1,256]{2,1,0:T(1,128)S(1)}, u32[]{:S(2)}, u32[]{:S(2)}) collective-permute-start(f32[32,1,256]{2,1,0:T(1,128)S(1)} %get-tuple-element.27), channel_id=1, source_target_pairs={{0,4},{4,8},{8,12},{12,16},{16,20},{20,24},{24,28},{1,5},{5,9},{9,... | collective-permute-start | bytes 98312 | tf_op jit(solution)/shard_map/ppermute | solution.py:16
  126.0 1.6 %fusion.4 = f32[32,8,2,1,128]{4,0,2,1,3:T(8,128)S(1)} fusion(bf16[8,4,130,2,128]{4,3,2,1,0:T(2,128)(2,1)S(1)} %copy-done.1, bf16[32,8,4,1,2]{4,0,2,1,3:T(8,128)(2,1)} %bitcast.266, bf16[32,8,4,1,128]{4,0,2,1,3:T(8,128)(2,1)} %get-tuple-element.15), kind=kOutput, calls=%fused_computation.6 | convolution fusion | flops 68689920 | bytes 2658304 | tf_op jit(solution)/shard_map/rbkqe,bqkejc->rbjqc/dot_general | solution.py:85
  127.8 0.5 select_maximum_fusion
  129.0 0.9 copy.278
  129.9 0.5 copy.279
  130.4 0.7 add.319
  (145 shorter events, 10.2 us)
Async XLA Ops:
  0.0 15.8 %copy-start = (bf16[8,1,520,256]{3,2,1,0:T(8,128)(2,1)S(1)}, bf16[8,1,520,256]{3,2,1,0:T(8,128)(2,1)}, u32[]{:S(2)}) copy-start(bf16[8,1,520,256]{3,2,1,0:T(8,128)(2,1)} %param.8) | copy-start | bytes 6389764
  1.1 6.8 %collective-permute-start.1 = (f32[32,1,128]{2,1,0:T(1,128)S(1)}, f32[32,1,128]{2,1,0:T(1,128)S(1)}, u32[]{:S(2)}, u32[]{:S(2)}) collective-permute-start(f32[32,1,128]{2,1,0:T(1,128)S(1)} %get-tuple-element.48), channel_id=1, source_target_pairs={{4,0},{8,4},{12,8},{16,12},{20,16},{24,20},{28,24},{5,1},{9,5},{13... | collective-permute-start | bytes 49160 | tf_op jit(solution)/shard_map/ppermute | solution.py:19
  2.4 6.9 %collective-permute-start = (f32[32,1,128]{2,1,0:T(1,128)S(1)}, f32[32,1,128]{2,1,0:T(1,128)S(1)}, u32[]{:S(2)}, u32[]{:S(2)}) collective-permute-start(f32[32,1,128]{2,1,0:T(1,128)S(1)} %get-tuple-element.47), channel_id=1, source_target_pairs={{0,4},{4,8},{8,12},{12,16},{16,20},{20,24},{24,28},{1,5},{5,9},{9,... | collective-permute-start | bytes 49160 | tf_op jit(solution)/shard_map/ppermute | solution.py:16
  11.4 13.6 %collective-permute-start.3 = (f32[32,18,1]{2,1,0:T(8,128)}, f32[32,18,1]{2,1,0:T(8,128)S(1)}, u32[]{:S(2)}, u32[]{:S(2)}) collective-permute-start(f32[32,18,1]{2,1,0:T(8,128)} %get-tuple-element.24), channel_id=1, source_target_pairs={{1,0},{2,1},{3,2},{5,4},{6,5},{7,6},{9,8},{10,9},{11,10},{13,12},{... | collective-permute-start | bytes 6920 | tf_op jit(solution)/shard_map/ppermute | solution.py:19
  12.7 12.3 %collective-permute-start.2 = (f32[32,18,1]{2,1,0:T(8,128)}, f32[32,18,1]{2,1,0:T(8,128)S(1)}, u32[]{:S(2)}, u32[]{:S(2)}) collective-permute-start(f32[32,18,1]{2,1,0:T(8,128)} %get-tuple-element.23), channel_id=1, source_target_pairs={{0,1},{1,2},{2,3},{4,5},{5,6},{6,7},{8,9},{9,10},{10,11},{12,13},{... | collective-permute-start | bytes 6920 | tf_op jit(solution)/shard_map/ppermute | solution.py:16
  17.9 5.1 %copy-start.4 = (bf16[2,1,520,256]{3,2,1,0:T(8,128)(2,1)S(1)}, bf16[2,1,520,256]{3,2,1,0:T(8,128)(2,1)}, u32[]{:S(2)}) copy-start(bf16[2,1,520,256]{3,2,1,0:T(8,128)(2,1)} %param.10) | copy-start | bytes 1597444
  17.9 6.1 %copy-start.6 = (bf16[4,1,136,64]{2,3,1,0:T(8,128)(2,1)S(1)}, bf16[4,1,136,64]{2,3,1,0:T(8,128)(2,1)}, u32[]{:S(2)}) copy-start(bf16[4,1,136,64]{2,3,1,0:T(8,128)(2,1)} %param.12) | copy-start | bytes 208900
  17.9 6.3 %copy-start.9 = (bf16[64,64]{1,0:T(8,128)(2,1)S(1)}, bf16[64,64]{1,0:T(8,128)(2,1)}, u32[]{:S(2)}) copy-start(bf16[64,64]{1,0:T(8,128)(2,1)} %param.13) | copy-start | bytes 24580
  17.9 7.0 %copy-start.7 = (bf16[1,1,264,128]{3,2,1,0:T(8,128)(2,1)S(1)}, bf16[1,1,264,128]{3,2,1,0:T(8,128)(2,1)}, u32[]{:S(2)}) copy-start(bf16[1,1,264,128]{3,2,1,0:T(8,128)(2,1)} %param.11) | copy-start | bytes 202756
  17.9 7.1 %copy-start.3 = (f32[32,16,128]{2,1,0:T(8,128)S(1)}, f32[32,16,128]{2,1,0:T(8,128)}, u32[]{:S(2)}) copy-start(f32[32,16,128]{2,1,0:T(8,128)} %param.7) | copy-start | bytes 786436
  37.9 7.9 %collective-permute-start.5 = (f32[32,1,256]{2,1,0:T(1,128)S(1)}, f32[32,1,256]{2,1,0:T(1,128)S(1)}, u32[]{:S(2)}, u32[]{:S(2)}) collective-permute-start(f32[32,1,256]{2,1,0:T(1,128)S(1)} %get-tuple-element.44), channel_id=1, source_target_pairs={{4,0},{8,4},{12,8},{16,12},{20,16},{24,20},{28,24},{5,1},{9,5},{13... | collective-permute-start | bytes 98312 | tf_op jit(solution)/shard_map/ppermute | solution.py:19
  39.2 7.2 %collective-permute-start.4 = (f32[32,1,256]{2,1,0:T(1,128)S(1)}, f32[32,1,256]{2,1,0:T(1,128)S(1)}, u32[]{:S(2)}, u32[]{:S(2)}) collective-permute-start(f32[32,1,256]{2,1,0:T(1,128)S(1)} %get-tuple-element.43), channel_id=1, source_target_pairs={{0,4},{4,8},{8,12},{12,16},{16,20},{20,24},{24,28},{1,5},{5,9},{9,... | collective-permute-start | bytes 98312 | tf_op jit(solution)/shard_map/ppermute | solution.py:16
  50.2 8.1 %collective-permute-start.7 = (f32[32,1,128]{0,2,1:T(8,128)S(1)}, f32[32,1,128]{0,2,1:T(8,128)S(1)}, u32[]{:S(2)}, u32[]{:S(2)}) collective-permute-start(f32[32,1,128]{0,2,1:T(8,128)S(1)} %get-tuple-element.42), channel_id=1, source_target_pairs={{4,0},{8,4},{12,8},{16,12},{20,16},{24,20},{28,24},{5,1},{9,5},{13... | collective-permute-start | bytes 49160 | tf_op jit(solution)/shard_map/ppermute | solution.py:19
  51.5 7.6 %collective-permute-start.6 = (f32[32,1,128]{0,2,1:T(8,128)S(1)}, f32[32,1,128]{0,2,1:T(8,128)S(1)}, u32[]{:S(2)}, u32[]{:S(2)}) collective-permute-start(f32[32,1,128]{0,2,1:T(8,128)S(1)} %get-tuple-element.41), channel_id=1, source_target_pairs={{0,4},{4,8},{8,12},{12,16},{16,20},{20,24},{24,28},{1,5},{5,9},{9,... | collective-permute-start | bytes 49160 | tf_op jit(solution)/shard_map/ppermute | solution.py:16
  97.2 1.4 %copy-start.8 = (bf16[64,64]{0,1:T(8,128)(2,1)S(1)}, bf16[64,64]{0,1:T(8,128)(2,1)}, u32[]{:S(2)}) copy-start(bf16[64,64]{0,1:T(8,128)(2,1)} %copy.251) | copy-start | bytes 24580
  98.8 7.4 %copy-start.5 = (bf16[2,4,130,2,128]{4,3,2,1,0:T(2,128)(2,1)S(1)}, bf16[2,4,130,2,128]{4,3,2,1,0:T(2,128)(2,1)}, u32[]{:S(2)}) copy-start(bf16[2,4,130,2,128]{4,3,2,1,0:T(2,128)(2,1)} %reshape.315) | copy-start | bytes 1597444
  99.9 14.1 %copy-start.2 = (bf16[4,2,4,130,2,128]{5,4,3,2,1,0:T(2,128)(2,1)S(1)}, bf16[4,2,4,130,2,128]{5,4,3,2,1,0:T(2,128)(2,1)}, u32[]{:S(2)}) copy-start(bf16[4,2,4,130,2,128]{5,4,3,2,1,0:T(2,128)(2,1)} %reshape.306) | copy-start | bytes 6389764
  99.9 6.6 %collective-permute-start.9 = (f32[32,1,64]{2,0,1:T(8,128)S(1)}, f32[32,1,64]{2,0,1:T(8,128)S(1)}, u32[]{:S(2)}, u32[]{:S(2)}) collective-permute-start(f32[32,1,64]{2,0,1:T(8,128)S(1)} %get-tuple-element.76), channel_id=1, source_target_pairs={{4,0},{8,4},{12,8},{16,12},{20,16},{24,20},{28,24},{5,1},{9,5},{13... | collective-permute-start | bytes 24584 | tf_op jit(solution)/shard_map/ppermute | solution.py:19
  101.4 6.0 %collective-permute-start.8 = (f32[32,1,64]{2,0,1:T(8,128)S(1)}, f32[32,1,64]{2,0,1:T(8,128)S(1)}, u32[]{:S(2)}, u32[]{:S(2)}) collective-permute-start(f32[32,1,64]{2,0,1:T(8,128)S(1)} %get-tuple-element.75), channel_id=1, source_target_pairs={{0,4},{4,8},{8,12},{12,16},{16,20},{20,24},{24,28},{1,5},{5,9},{9,... | collective-permute-start | bytes 24584 | tf_op jit(solution)/shard_map/ppermute | solution.py:16
  107.8 8.9 %collective-permute-start.11 = (f32[32,1,128]{0,2,1:T(8,128)S(1)}, f32[32,1,128]{0,2,1:T(8,128)S(1)}, u32[]{:S(2)}, u32[]{:S(2)}) collective-permute-start(f32[32,1,128]{0,2,1:T(8,128)S(1)} %get-tuple-element.32), channel_id=1, source_target_pairs={{4,0},{8,4},{12,8},{16,12},{20,16},{24,20},{28,24},{5,1},{9,5},{13... | collective-permute-start | bytes 49160 | tf_op jit(solution)/shard_map/ppermute | solution.py:19
  109.1 7.6 %collective-permute-start.10 = (f32[32,1,128]{0,2,1:T(8,128)S(1)}, f32[32,1,128]{0,2,1:T(8,128)S(1)}, u32[]{:S(2)}, u32[]{:S(2)}) collective-permute-start(f32[32,1,128]{0,2,1:T(8,128)S(1)} %get-tuple-element.31), channel_id=1, source_target_pairs={{0,4},{4,8},{8,12},{12,16},{16,20},{20,24},{24,28},{1,5},{5,9},{9,... | collective-permute-start | bytes 49160 | tf_op jit(solution)/shard_map/ppermute | solution.py:16
  117.2 8.7 %copy-start.1 = (bf16[8,4,130,2,128]{4,3,2,1,0:T(2,128)(2,1)S(1)}, bf16[8,4,130,2,128]{4,3,2,1,0:T(2,128)(2,1)}, u32[]{:S(2)}) copy-start(bf16[8,4,130,2,128]{4,3,2,1,0:T(2,128)(2,1)} %reshape.298) | copy-start | bytes 6389764
  119.2 8.6 %collective-permute-start.13 = (f32[32,1,256]{2,1,0:T(1,128)S(1)}, f32[32,1,256]{2,1,0:T(1,128)S(1)}, u32[]{:S(2)}, u32[]{:S(2)}) collective-permute-start(f32[32,1,256]{2,1,0:T(1,128)S(1)} %get-tuple-element.28), channel_id=1, source_target_pairs={{4,0},{8,4},{12,8},{16,12},{20,16},{24,20},{28,24},{5,1},{9,5},{13... | collective-permute-start | bytes 98312 | tf_op jit(solution)/shard_map/ppermute | solution.py:19
  120.5 7.3 %collective-permute-start.12 = (f32[32,1,256]{2,1,0:T(1,128)S(1)}, f32[32,1,256]{2,1,0:T(1,128)S(1)}, u32[]{:S(2)}, u32[]{:S(2)}) collective-permute-start(f32[32,1,256]{2,1,0:T(1,128)S(1)} %get-tuple-element.27), channel_id=1, source_target_pairs={{0,4},{4,8},{8,12},{12,16},{16,20},{20,24},{24,28},{1,5},{5,9},{9,... | collective-permute-start | bytes 98312 | tf_op jit(solution)/shard_map/ppermute | solution.py:16
where the time goes:
time: 133 us; the launch traced here: 131 us
  blocking collectives  46.3 us (35%)
  starting transfers between devices  44.1 us (33%)
  local copies, waits for them, and re-layouts  23.7 us (18%)
  other arithmetic  8.26 us (6%)
  matrix products  3.97 us (3%)
  waiting for transfers between devices  3.69 us (3%)
    all_gather x1, blocking collectives, per_device(): whole_three = lax.all_gather(level_three, 'px', axis=1, tiled=True)  35.8 us
    ppermute x7, starting transfers between devices, extended(): lax.ppermute(lax.slice_in_dim(block, block.shape[dim] - width, None, axis...  35 us
    all_gather x1, blocking collectives, per_device(): level_one = lax.all_gather(restricted_one, 'py', axis=2, tiled=True)  10.4 us
    ppermute x7, starting transfers between devices, extended(): lax.ppermute(lax.slice_in_dim(block, 0, width, axis=dim), axis, backward)  9.16 us
    reshape x1, local copies, waits for them, and re-layouts, solve_blocks(): factor.reshape(factor.shape[0], factor.shape[1], 4, width + 2, 2, width)  5.12 us
    dot_general x5, matrix products, solve_blocks(): jnp.einsum('rbkqe,bqkejc->rbjqc', windows, shaped_factor, preferred_eleme...  3.85 us
    ppermute x7, waiting for transfers between devices, extended(): lax.ppermute(lax.slice_in_dim(block, block.shape[dim] - width, None, axis...  3.67 us
    concatenate x7, other arithmetic, extended(): block = jnp.concatenate([low, block, high], axis=dim)  2.89 us
  transfers between devices with their start and end apart: 14, of which 4 were waited for; matrix products, arithmetic and copies ran while one was open for 12% of the time, Pallas kernels for 0%

commit v1 on v0

v1 whole, which is shorter than its diff:
```python
import functools

import jax
import jax.numpy as jnp
import numpy as np
from jax import lax
from jax.experimental import pallas as pl
from jax.experimental.pallas import tpu as pltpu
from jax.sharding import PartitionSpec as P

F32 = jnp.float32
BF16 = jnp.bfloat16
LANES = 128
SHRINK = 1.0 / 20.0
TAPS = (1, 3, 3, 1)
VMEM_BYTES = 24 * 1024 * 1024


def round_up(value, unit=LANES):
    return -(-value // unit) * unit


def local_shrink(fine, coarse, halo_in, first, last):
    out = np.zeros((fine + 2 * halo_in, coarse + 2))
    for i in range(-1, coarse + 1):
        if (i == -1 and first) or (i == coarse and last):
            continue
        for t, tap in enumerate(TAPS):
            j = 2 * i - 1 + t
            if -halo_in <= j < fine + halo_in:
                out[j + halo_in, i + 1] = tap
    return out


def global_prolong(coarse):
    out = np.zeros((coarse, 2 * coarse))
    for i in range(coarse):
        out[i, 2 * i] += 3
        out[i, 2 * i + 1] += 3
        if i > 0:
            out[i, 2 * i - 1] += 1
        if i + 1 < coarse:
            out[i, 2 * i + 2] += 1
    return out


def bf(array):
    return np.asarray(array, np.float32).astype(jnp.bfloat16)


class Plan:
    def __init__(self, mesh_shape, residual, factors):
        self.n, self.m = mesh_shape["px"], mesh_shape["py"]
        self.rhs, self.h0, self.w0 = residual
        self.h = [self.h0 >> l for l in range(5)]
        self.w = [self.w0 >> l for l in range(5)]
        self.ny = [self.w0 * self.m >> l for l in range(6)]
        self.nx = [self.h0 * self.n >> l for l in range(6)]
        self.tile = [f[3] // 2 for f in factors]
        self.tiles = [f[1] for f in factors]
        self.slots = self.h[1] + 2
        self.offset = [None, 0, self.w[1] + 2, self.w[1] + self.w[2] + 4]
        self.spare = self.w[1] + self.w[2] + self.w[3] + 6

    def scale(self):
        out = np.ones((1, LANES), np.float32)
        for l in (1, 2, 3):
            out[:, self.offset[l] : self.offset[l] + self.w[l] + 2] = SHRINK**l
        return out

    def shrink_columns(self):
        out = np.zeros((self.m, 3, self.w0, LANES))
        for c in range(self.m):
            ends = (c == 0, c == self.m - 1)
            now = local_shrink(self.w0, self.w[1], 0, *ends)
            for l in (1, 2, 3):
                if l > 1:
                    now = now @ local_shrink(self.w[l - 1], self.w[l], 1, *ends)
                o = self.offset[l]
                out[c, l - 1, :, o : o + self.w[l] + 2] = now
        return bf(out)

    def pick_sides(self):
        out = np.zeros((2, self.w0, LANES))
        for k in range(2):
            out[k, 0, self.spare + 2 * k] = 1
            out[k, self.w0 - 1, self.spare + 2 * k + 1] = 1
        return bf(out)

    def place(self, level, lead, width, at=0):
        out = np.zeros((self.m, LANES, width))
        for c in range(self.m):
            for k in range(self.w[level] + 2):
                column = self.w[level] * c - 1 + k
                if -lead <= column < self.ny[level]:
                    out[c, self.offset[level] + k, at + column + lead] = 1
        return out

    def halo_lanes(self):
        out = np.zeros((2, LANES, 2 * LANES))
        for k in range(2):
            for position in range(4):
                out[0, self.spare + 2 * k + 1, LANES * k + 2 * position] = 1
                out[1, self.spare + 2 * k, LANES * k + 2 * position + 1] = 1
        return bf(out)

    def lift_columns(self, level):
        out = np.eye(self.ny[level])
        for l in range(level, 0, -1):
            out = out @ global_prolong(self.ny[l])
        return out.reshape(self.ny[level], self.m, self.w0).transpose(1, 0, 2)

    def lift_rows_of(self, level):
        w, tiles = self.tile[level], self.tiles[level]
        full = self.lift_columns(level).reshape(self.m, tiles, w, self.w0)
        out = np.zeros((self.m, 2, tiles, 2 * w, self.w0))
        for j in range(2):
            out[:, j, :, j * w : (j + 1) * w] = full
        return out

    def coarse_shrink(self):
        ny3, ny4 = self.ny[3], self.ny[4]
        columns = global_prolong(ny4).T
        width = round_up(ny4 + 2)
        out = np.zeros((2, 2, ny3, width))
        for side, taps in enumerate(((1, 3), (3, 1))):
            for j in range(2):
                out[side, j, :, 1 : 1 + ny4] = taps[j] * columns
        return bf(out.reshape(2, 2 * ny3, width))

    def coarsest_shrink(self):
        nx5, ny5, ny4 = self.nx[5], self.ny[5], self.ny[4]
        columns = global_prolong(ny5).T
        width = round_up(ny4 + 2)
        out = np.zeros((nx5, width, nx5 * ny5))
        for i in range(nx5):
            out[i, 1 : 1 + ny4, i * ny5 : (i + 1) * ny5] = columns
        return bf(out.reshape(nx5 * width, nx5 * ny5))

    def coarsest_lift(self):
        rows, columns = global_prolong(self.nx[5]), global_prolong(self.ny[5])
        both = np.einsum("ia,jb->ijab", rows, columns)
        w, tiles = self.tile[4], self.tiles[4]
        both = both.reshape(self.nx[5] * self.ny[5], self.nx[4] // 2, 2, tiles, w)
        both = both.transpose(0, 1, 3, 2, 4)
        return bf(both.reshape(self.nx[5] * self.ny[5], self.nx[4] * self.ny[4]))

    def level_four_lift(self):
        pair = 2 * self.tile[4] * self.tiles[4]
        group = max(1, LANES // pair)
        width = group * pair
        rows = self.lift_rows_of(4).reshape(self.m, 2, pair, self.w0)
        out = np.zeros((self.m, group, 2, width, self.w0))
        for g in range(group):
            out[:, g, :, g * pair : (g + 1) * pair] = rows
        return bf(out), group


def split(value):
    high = value.astype(BF16)
    return high, (value - high.astype(F32)).astype(BF16)


def product(value, matrix):
    high, low = split(value)
    return jnp.dot(high, matrix, preferred_element_type=F32) + jnp.dot(
        low, matrix, preferred_element_type=F32
    )


def shrink_rows(rows, count, halo):
    out = []
    for i in range(-1, count // 2 + 1):
        total = None
        for t, tap in enumerate(TAPS):
            j = 2 * i - 1 + t
            if -halo <= j < count + halo:
                term = rows[j + halo] * float(tap) if tap > 1 else rows[j + halo]
                total = term if total is None else total + term
        out.append(total)
    return out


def lift_rows(rows, first, last):
    out = []
    for f in range(first, last):
        i = f // 2
        other = i - 1 if f % 2 == 0 else i + 1
        out.append((rows[i + 1] * 3.0 + rows[other + 1]) * SHRINK)
    return out


def lane_index(rows):
    return lax.broadcasted_iota(jnp.int32, (rows, LANES), 1)


def assemble(pieces, width):
    total = 4 * (width + 2)
    tiles = [[] for _ in range(-(-total // LANES))]
    lane = lane_index(pieces[0][0].shape[0])
    for k, piece in enumerate(pieces):
        for q, value in enumerate(piece):
            start = k * (width + 2) + LANES * q
            count = min(LANES, width + 2 - LANES * q)
            shift, at = start % LANES, start // LANES
            rolled = pltpu.roll(value, shift, 1) if shift else value
            tiles[at].append((min(LANES, shift + count), rolled))
            if shift + count > LANES:
                tiles[at + 1].append((shift + count - LANES, rolled))
    out = []
    for segments in tiles:
        segments = sorted(segments, key=lambda s: -s[0])
        end, value = segments[0]
        if end < LANES:
            value = jnp.where(lane < end, value, 0.0)
        for end, part in segments[1:]:
            value = jnp.where(lane < end, part, value)
        out.append(value)
    return jnp.concatenate(out, axis=1).astype(BF16)[:, :total]


def solve(lhs, factor):
    return jnp.dot(lhs, factor, preferred_element_type=F32)


def kernel_call(body, out_shape, scratch=()):
    return pl.pallas_call(
        body,
        out_shape=out_shape,
        scratch_shapes=list(scratch),
        compiler_params=pltpu.CompilerParams(vmem_limit_bytes=VMEM_BYTES),
    )


def shape(*dims):
    return jax.ShapeDtypeStruct(dims, F32)


def restrict_kernel(plan, x_ref, shrink_ref, sides_ref, scale_ref, own_ref, down_ref, up_ref):
    r, c = lax.axis_index("px"), lax.axis_index("py")
    rhs, slots, h = plan.rhs, plan.slots, plan.h
    above = jnp.where(r > 0, 1.0, 0.0).astype(F32)
    below = jnp.where(r < plan.n - 1, 1.0, 0.0).astype(F32)
    x = [x_ref[pl.ds(row, rhs, stride=h[0]), :] for row in range(h[0])]
    rows, total = x, None
    for level in (1, 2, 3):
        rows = shrink_rows(rows, h[level - 1], 0 if level == 1 else 1)
        rows[0] = rows[0] * above
        rows[-1] = rows[-1] * below
        part = product(jnp.concatenate(rows, axis=0), shrink_ref[c, level - 1])
        if total is None:
            total = part
        else:
            count = part.shape[0]
            total = jnp.concatenate([total[:count] + part, total[count:]], axis=0)
    sides = [jnp.zeros_like(x[0])] + x[: slots - 1]
    total = total + jnp.dot(
        jnp.concatenate(sides, axis=0).astype(BF16), sides_ref[0], preferred_element_type=F32
    )
    rest = jnp.concatenate(x[slots - 1 :], axis=0).astype(BF16)
    more = jnp.dot(rest, sides_ref[1], preferred_element_type=F32)
    count = more.shape[0]
    total = jnp.concatenate([total[:count] + more, total[count:]], axis=0)
    total = total * scale_ref[...]
    own = total.reshape(slots, rhs, LANES)
    own_ref[...] = own
    lane = lane_index(rhs)
    one, two = plan.offset[2], plan.offset[3]
    down_ref[0] = x[-1]
    up_ref[0] = x[0]
    for k in range(2):
        three_own = own[h[3] + k]
        down_ref[1 + k] = jnp.where(
            lane < one, own[h[1] + k], jnp.where(lane < two, own[h[2] + k], three_own)
        )
        up_ref[1 + k] = own[k]


def merge_kernel(plan, own_ref, down_ref, up_ref, sides_ref, out_ref):
    r = lax.axis_index("px")
    rhs, h = plan.rhs, plan.h
    above = jnp.where(r > 0, 1.0, 0.0).astype(F32)
    below = jnp.where(r < plan.n - 1, 1.0, 0.0).astype(F32)
    lane = lane_index(rhs)
    one, two, end = plan.offset[2], plan.offset[3], plan.spare
    out_ref[...] = own_ref[...]
    wrapped = jnp.logical_and(lane >= two, lane < end)
    in_band = lane < end
    for k in range(2):
        piece = down_ref[1 + k]
        piece = jnp.where(wrapped, piece, jnp.where(in_band, piece * above, 0.0))
        out_ref[k] = out_ref[k] + piece
        piece = up_ref[1 + k]
        piece = jnp.where(wrapped, piece, jnp.where(in_band, piece * below, 0.0))
        for level, low, high in ((1, 0, one), (2, one, two), (3, two, end)):
            row = h[level] + k
            chosen = jnp.logical_and(lane >= low, lane < high)
            out_ref[row] = out_ref[row] + jnp.where(chosen, piece, 0.0)
    top = (down_ref[0] * above).astype(BF16)
    out_ref[0] = out_ref[0] + jnp.dot(top, sides_ref[0], preferred_element_type=F32)
    bottom = (up_ref[0] * below).astype(BF16)
    at = h[0] + 1 - plan.slots
    out_ref[at] = out_ref[at] + jnp.dot(bottom, sides_ref[1], preferred_element_type=F32)


def gather_kernel(plan, place_ref, *refs):
    band_refs, out_ref = refs[:-1], refs[-1]
    c = lax.axis_index("py")
    rhs, width = plan.rhs, 2 * plan.ny[3]
    for half in range(2):
        total = jnp.zeros((rhs, width), F32)
        for k, band in enumerate(band_refs):
            owner = jnp.bitwise_xor(c, k)
            for j in range(2):
                total = total + product(band[2 * half + j], place_ref[owner, j])
        out_ref[half] = total


def level_rows(plan, level, band_refs, place_ref, c):
    rhs, count = plan.rhs, plan.h[level] + 2
    total = None
    for k, band in enumerate(band_refs):
        owner = jnp.bitwise_xor(c, k)
        value = band[:count].reshape(count * rhs, LANES)
        part = product(value, place_ref[owner])
        total = part if total is None else total + part
    return total


def coarse_kernel(plan, places, lifts, factors, *refs):
    bands, outs = refs[: plan.m], refs[plan.m :]
    r, c = lax.axis_index("px"), lax.axis_index("py")
    rhs = plan.rhs
    above = jnp.where(r > 0, 1.0, 0.0).astype(F32)
    below = jnp.where(r < plan.n - 1, 1.0, 0.0).astype(F32)
    down_ref, up_ref = outs[3], outs[4]
    for level in (1, 2, 3):
        w, tiles = plan.tile[level], plan.tiles[level]
        whole = level_rows(plan, level, bands, places[level - 1], c)
        count = plan.h[level] + 2
        rows = [whole[i * rhs : (i + 1) * rhs] for i in range(count)]
        if level == 3:
            rows[0] = rows[0] * above
            rows[-1] = rows[-1] * below
        lift_ref, factor_ref, out_ref = lifts[level - 1], factors[level - 1], outs[level - 1]
        solved = [[] for _ in range(tiles)]
        for b in range(plan.h[level] // 2):
            for t in range(tiles):
                pieces = []
                for k in range(4):
                    row = rows[2 * b + k]
                    lanes = range(t * w, t * w + w + 2, LANES)
                    pieces.append([row[:, lo : lo + LANES] for lo in lanes])
                solved[t].append(solve(assemble(pieces, w), factor_ref[b, t]))
        pairs = plan.h[level] // 2
        lifted = [None, None]
        for t in range(tiles):
            stacked = jnp.concatenate(solved[t], axis=0)
            for j in range(2):
                if w % LANES == 0:
                    part = product(
                        stacked[:, j * w : (j + 1) * w], lift_ref[c, t * w : (t + 1) * w]
                    )
                else:
                    part = product(stacked, lift_ref[c, j * tiles + t])
                lifted[j] = part if lifted[j] is None else lifted[j] + part
        for b in range(pairs):
            for j in range(2):
                out_ref[2 * b + j] = lifted[j][b * rhs : (b + 1) * rhs]
        down_ref[level - 1] = lifted[1][(pairs - 1) * rhs :]
        up_ref[level - 1] = lifted[0][:rhs]


def fine_kernel(plan, x_ref, down_ref, up_ref, halo_ref, factor_ref, *refs):
    bands, out_ref = refs[: plan.m], refs[plan.m]
    r, c = lax.axis_index("px"), lax.axis_index("py")
    rhs, h0, w0, slots = plan.rhs, plan.h0, plan.w0, plan.slots
    above = jnp.where(r > 0, 1.0, 0.0).astype(F32)
    below = jnp.where(r < plan.n - 1, 1.0, 0.0).astype(F32)
    halo = None
    for k, band in enumerate(bands):
        owner = jnp.bitwise_xor(c, k)
        from_left = jnp.where(owner == c - 1, 1.0, 0.0).astype(BF16)
        from_right = jnp.where(owner == c + 1, 1.0, 0.0).astype(BF16)
        matrix = halo_ref[0] * from_left + halo_ref[1] * from_right
        value = band[...].reshape(slots * rhs, LANES).astype(BF16)
        part = jnp.dot(value, matrix, preferred_element_type=F32)
        halo = part if halo is None else halo + part
    lane = lane_index(rhs)
    rows, sides = [], []
    for row in range(-1, h0 + 1):
        if row == -1:
            rows.append(down_ref[0] * above)
        elif row == h0:
            rows.append(up_ref[0] * below)
        else:
            rows.append(x_ref[pl.ds(row, rhs, stride=h0), :])
        part, slot = divmod(row + 1, slots)
        sides.append(halo[slot * rhs : (slot + 1) * rhs, part * LANES : (part + 1) * LANES])
    for b in range(h0 // 2):
        tiles, before = [], None
        for k in range(5):
            if k < 4:
                row, side = rows[2 * b + k], sides[2 * b + k]
                rolled = pltpu.roll(row, 2 * k + 1, 1)
                value = jnp.where(lane == 2 * k, side, rolled)
            else:
                value = jnp.zeros((rhs, LANES), F32)
            if before is not None:
                old, old_side = before
                value = jnp.where(lane == 2 * k - 1, old_side, value)
                value = jnp.where(lane < 2 * k - 1, old, value)
            tiles.append(value)
            before = (rolled, side)
        lhs = jnp.concatenate(tiles, axis=1).astype(BF16)[:, : 4 * (w0 + 2)]
        solved = solve(lhs, factor_ref[b, 0])
        for j in range(2):
            out_ref[2 * b + j] = solved[:, j * w0 : (j + 1) * w0]


def final_kernel(plan, group, fine_ref, one_ref, two_ref, three_ref, down_ref, up_ref, four_ref,
                 inverse_ref, shrink_ref, flat_ref, spread_ref, lift_ref, *refs):
    count = plan.n // 2
    gathered, out_ref, pair_ref, four_rows = refs[:count], refs[count], refs[-2], refs[-1]
    r, c = lax.axis_index("px"), lax.axis_index("py")
    rhs, n, ny3, ny4 = plan.rhs, plan.n, plan.ny[3], plan.ny[4]
    nx4, nx5 = plan.nx[4], plan.nx[5]
    above = jnp.where(r > 0, 1.0, 0.0).astype(F32)
    below = jnp.where(r < n - 1, 1.0, 0.0).astype(F32)
    for k, block in enumerate(gathered):
        for half in range(2):
            at = lax.rem(r + 2 * k + half, n)
            pair_ref[at] = block[half]
    lane = lax.broadcasted_iota(jnp.int32, (rhs, 2 * ny3), 1)
    ring = pair_ref[0]
    pair_ref[0] = jnp.where(lane < ny3, 0.0, ring)
    pair_ref[n] = jnp.where(lane < ny3, ring, 0.0)
    low = pair_ref[0:n].reshape(n * rhs, 2 * ny3)
    high = pair_ref[1 : n + 1].reshape(n * rhs, 2 * ny3)
    four = (product(low, shrink_ref[0]) + product(high, shrink_ref[1])) * SHRINK
    zero = jnp.zeros((rhs, four.shape[1]), F32)
    rows = [zero] + [four[i * rhs : (i + 1) * rhs] for i in range(nx4)] + [zero]
    five = shrink_rows(rows, nx4, 1)[1:-1]
    flat = product(jnp.concatenate(five, axis=1), flat_ref[...]) * SHRINK
    part_five = jnp.dot(flat.astype(BF16), inverse_ref[...], preferred_element_type=F32)
    lifted = product(part_five, spread_ref[...]) * SHRINK
    w, tiles = plan.tile[4], plan.tiles[4]
    parts = []
    for b in range(nx4 // 2):
        for t in range(tiles):
            pieces = []
            for k in range(4):
                lanes = range(t * w, t * w + w + 2, LANES)
                pieces.append([rows[2 * b + k][:, lo : lo + LANES] for lo in lanes])
            parts.append(solve(assemble(pieces, w), four_ref[b, t]))
    correction = jnp.concatenate(parts, axis=1) + lifted
    width = lift_ref.shape[3]
    bands = nx4 // 2 // group
    stacked = jnp.concatenate(
        [correction[:, i * width : (i + 1) * width] for i in range(bands)], axis=0
    )
    four_rows[0] = jnp.zeros((rhs, LANES), F32)
    four_rows[nx4 + 1] = jnp.zeros((rhs, LANES), F32)
    for g in range(group):
        for j in range(2):
            value = product(stacked, lift_ref[c, 2 * g + j])
            for i in range(bands):
                four_rows[1 + 2 * (i * group + g) + j] = value[i * rhs : (i + 1) * rhs]
    rows = [four_rows[r + k] for k in range(3)]
    for level, own_ref in ((3, three_ref), (2, two_ref), (1, one_ref)):
        height = plan.h[level]
        lifted = lift_rows(rows, -1, height + 1)
        rows = [(lifted[0] + down_ref[level - 1]) * above]
        rows += [lifted[i + 1] + own_ref[i] for i in range(height)]
        rows += [(lifted[-1] + up_ref[level - 1]) * below]
    lifted = lift_rows(rows, 0, plan.h0)
    for row in range(plan.h0):
        out_ref[pl.ds(row, rhs, stride=plan.h0), :] = lifted[row] + fine_ref[row]


def per_device(mesh_shape, residual, factor_fine, factor_one, factor_two, factor_three,
               factor_four, coarse_inverse):
    factors = [factor_fine, factor_one, factor_two, factor_three, factor_four]
    plan = Plan(mesh_shape, residual.shape, [f.shape for f in factors])
    n, m, rhs, h, h0 = plan.n, plan.m, plan.rhs, plan.h, plan.h0
    x = residual.reshape(rhs * h0, plan.w0)

    def shift(value, by):
        return lax.ppermute(value, "px", [(i, (i + by) % n) for i in range(n)])

    def swap(value, bits):
        return lax.ppermute(value, "py", [(i, i ^ bits) for i in range(m)])

    sides = jnp.asarray(plan.pick_sides())
    own, down, up = kernel_call(
        functools.partial(restrict_kernel, plan),
        (shape(plan.slots, rhs, LANES), shape(3, rhs, LANES), shape(3, rhs, LANES)),
    )(x, jnp.asarray(plan.shrink_columns()), sides, jnp.asarray(plan.scale()))
    from_above, from_below = shift(down, 1), shift(up, -1)
    band = kernel_call(functools.partial(merge_kernel, plan), shape(plan.slots, rhs, LANES))(
        own, from_above, from_below, sides
    )
    bands = {0: band}
    bit = m // 2
    while bit:
        bands.update({k ^ bit: swap(value, bit) for k, value in list(bands.items())})
        bit //= 2
    bands = [bands[k] for k in range(m)]

    width3 = 2 * plan.ny[3]
    place = np.stack([plan.place(3, 0, width3, j * plan.ny[3]) for j in range(2)], axis=1)
    pairs = kernel_call(functools.partial(gather_kernel, plan), shape(2, rhs, width3))(
        jnp.asarray(bf(place)), *bands
    )
    gathered = [pairs] + [shift(pairs, -2 * k) for k in range(1, n // 2)]

    places = [jnp.asarray(bf(plan.place(l, 1, round_up(plan.ny[l] + 2)))) for l in (1, 2, 3)]
    lifts = []
    for l in (1, 2, 3):
        if plan.tile[l] % LANES == 0:
            lifts.append(jnp.asarray(bf(plan.lift_columns(l))))
        else:
            rows = plan.lift_rows_of(l)
            lifts.append(jnp.asarray(bf(rows.reshape((m, -1) + rows.shape[3:]))))

    def coarse(*refs):
        coarse_kernel(plan, refs[0:3], refs[3:6], refs[6:9], *refs[9:])

    one, two, three, down, up = kernel_call(
        coarse,
        tuple(shape(h[l], rhs, LANES) for l in (1, 2, 3))
        + (shape(3, rhs, LANES), shape(3, rhs, LANES)),
    )(*places, *lifts, factor_one, factor_two, factor_three, *bands)
    down, up = shift(down, 1), shift(up, -1)

    fine = kernel_call(functools.partial(fine_kernel, plan), shape(h0, rhs, plan.w0))(
        x, from_above, from_below, jnp.asarray(plan.halo_lanes()), factor_fine, *bands
    )
    lift_four, group = plan.level_four_lift()
    lift_four = lift_four.reshape((m, -1) + lift_four.shape[3:])
    out = kernel_call(
        functools.partial(final_kernel, plan, group),
        shape(rhs * h0, plan.w0),
        scratch=(
            pltpu.VMEM((n + 1, rhs, width3), F32),
            pltpu.VMEM((plan.nx[4] + 2, rhs, LANES), F32),
        ),
    )(fine, one, two, three, down, up, factor_four, coarse_inverse,
      jnp.asarray(plan.coarse_shrink()), jnp.asarray(plan.coarsest_shrink()),
      jnp.asarray(plan.coarsest_lift()), jnp.asarray(lift_four), *gathered)
    return out.reshape(rhs, h0, plan.w0)


def solution(mesh):
    placed = (
        P(None, "px", "py"),
        P("px", "py", None, None),
        P("px", None, None, None),
        P("px", None, None, None),
        P("px", None, None, None),
        P(),
        P(),
    )
    return jax.shard_map(
        functools.partial(per_device, dict(mesh.shape)),
        mesh=mesh, in_specs=placed, out_specs=P(None, "px", "py"), check_vma=False,
    )
```

time: 133 us -> 47.8 us (0.36)
  blocking collectives: 46.3 us -> 0 us
  starting transfers between devices: 44.1 us -> 14.7 us
  local copies, waits for them, and re-layouts: 23.7 us -> 13.7 us
  Pallas kernels: 0 us -> 8.78 us
  other arithmetic: 8.26 us -> 0 us
  waiting for transfers between devices: 3.69 us -> 9.77 us
  matrix products: 3.97 us -> 0 us
    all_gather x2 -> x0, blocking collectives: 46.3 us -> none  [the longest x1 35.8 us: per_device(): whole_three = lax.all_gather(level_three, 'px', axis=1, tiled=True)]
    ppermute x14 -> x10, starting transfers between devices: 44.1 us -> 14.7 us  [the longest x7 13.1 us: shift(): return lax.ppermute(value, 'px', [(i, (i + by) % n) for i in range(n)])]
    unnamed x35 -> x57, local copies, waits for them, and re-layouts: 2.68 us -> 13.7 us
    reshape x14 -> x0, local copies, waits for them, and re-layouts: 10.8 us -> none  [the longest x1 5.12 us: solve_blocks(): factor.reshape(factor.shape[0], factor.shape[1], 4, width + 2, 2, width)]
    pallas_call x0 -> x6, Pallas kernels: none -> 8.78 us  [the longest x1 3.54 us: per_device(): kernel_call(coarse, tuple((shape(h[l], rhs, LANES) for l in (1, 2, 3))) +...]
    ppermute x14 -> x10, waiting for transfers between devices: 3.69 us -> 9.77 us  [the longest x3 5.09 us: swap(): return lax.ppermute(value, 'py', [(i, i ^ bits) for i in range(m)])]
    slice x33 -> x0, local copies, waits for them, and re-layouts: 5.6 us -> none  [the longest x7 2.26 us: extended(): lax.slice_in_dim(block, block.shape[dim] - width, None, axis=dim)]
    dot_general x6 -> x0, matrix products: 3.97 us -> none  [the longest x5 3.85 us: solve_blocks(): jnp.einsum('rbkqe,bqkejc->rbjqc', windows, shaped_factor, preferred_eleme...]
  transfers between devices with their start and end apart: 14 -> 10, of which waited for: 4 -> 6; matrix products, arithmetic and copies ran while one was open for 12% -> 2% of each run, Pallas kernels for 0% -> 4%
where the time goes in v1:
time: 47.8 us; the launch traced here: 47.2 us
  starting transfers between devices  14.7 us (31%)
  local copies, waits for them, and re-layouts  13.7 us (29%)
  waiting for transfers between devices  9.77 us (20%)
  Pallas kernels  8.78 us (18%)
    unnamed x57, local copies, waits for them, and re-layouts  13.7 us
    ppermute x7, starting transfers between devices, shift(): return lax.ppermute(value, 'px', [(i, (i + by) % n) for i in range(n)])  13.1 us
    ppermute x3, waiting for transfers between devices, swap(): return lax.ppermute(value, 'py', [(i, i ^ bits) for i in range(m)])  5.09 us
    ppermute x7, waiting for transfers between devices, shift(): return lax.ppermute(value, 'px', [(i, (i + by) % n) for i in range(n)])  4.68 us
    pallas_call x1, Pallas kernels, per_device(): kernel_call(coarse, tuple((shape(h[l], rhs, LANES) for l in (1, 2, 3))) +...  3.54 us
    pallas_call x1, Pallas kernels, per_device(): kernel_call(functools.partial(final_kernel, plan, group), shape(rhs * h0,...  2.73 us
    ppermute x3, starting transfers between devices, swap(): return lax.ppermute(value, 'py', [(i, i ^ bits) for i in range(m)])  1.62 us
    pallas_call x1, Pallas kernels, per_device(): kernel_call(functools.partial(fine_kernel, plan), shape(h0, rhs, plan.w0))  1.03 us
  transfers between devices with their start and end apart: 10, of which 6 were waited for; matrix products, arithmetic and copies ran while one was open for 2% of the time, Pallas kernels for 4%

profile of v1, /device:TPU:0, one launch (start us, length us, event | category | flops | bytes accessed | tf_op | source)
XLA Modules:
  0.0 47.2 jit_solution(13183789941103535532)
XLA Ops:
  0.0 0.9 %copy-done.2 = f32[32,16,128]{2,1,0:T(8,128)S(1)} copy-done((f32[32,16,128]{2,1,0:T(8,128)S(1)}, f32[32,16,128]{2,1,0:T(8,128)}, u32[]{:S(2)}) %copy-start.2) | copy-done | bytes 262168
  1.0 1.0 %copy-done.7 = bf16[4,3,128,128]{3,2,1,0:T(8,128)(2,1)S(1)} copy-done((bf16[4,3,128,128]{3,2,1,0:T(8,128)(2,1)S(1)}, bf16[4,3,128,128]{3,2,1,0:T(8,128)(2,1)}, u32[]{:S(2)}) %copy-start.7) | copy-done | bytes 393240
  1.9 0.8 %copy-done.11 = bf16[2,128,128]{2,1,0:T(8,128)(2,1)S(1)} copy-done((bf16[2,128,128]{2,1,0:T(8,128)(2,1)S(1)}, bf16[2,128,128]{2,1,0:T(8,128)(2,1)}, u32[]{:S(2)}) %copy-start.11) | copy-done | bytes 65560
  2.8 0.7 %copy-done.27 = f32[1,128]{1,0:T(1,128)S(1)} copy-done((f32[1,128]{1,0:T(1,128)S(1)}, f32[1,128]{1,0:T(1,128)}, u32[]{:S(2)}) %copy-start.27) | copy-done | bytes 536
  3.4 0.3 shard_map.208
  3.8 3.0 %collective-permute-start = (f32[3,32,128]{2,1,0:T(8,128)S(1)}, f32[3,32,128]{2,1,0:T(8,128)S(1)}, u32[]{:S(2)}, u32[]{:S(2)}) collective-permute-start(f32[3,32,128]{2,1,0:T(8,128)S(1)} %get-tuple-element.13), channel_id=1, source_target_pairs={{0,4},{4,8},{8,12},{12,16},{16,20},{20,24},{24,28},{28,0},{1,5},{5... | collective-permute-start | bytes 147464 | tf_op jit(solution)/shard_map/ppermute | solution.py:489
  6.8 3.1 %collective-permute-start.1 = (f32[3,32,128]{2,1,0:T(8,128)S(1)}, f32[3,32,128]{2,1,0:T(8,128)S(1)}, u32[]{:S(2)}, u32[]{:S(2)}) collective-permute-start(f32[3,32,128]{2,1,0:T(8,128)S(1)} %get-tuple-element.14), channel_id=1, source_target_pairs={{0,28},{4,0},{8,4},{12,8},{16,12},{20,16},{24,20},{28,24},{1,29},{... | collective-permute-start | bytes 147464 | tf_op jit(solution)/shard_map/ppermute | solution.py:489
  9.9 2.0 %collective-permute-done.down_ref = f32[3,32,128]{2,1,0:T(8,128)S(1)} collective-permute-done((f32[3,32,128]{2,1,0:T(8,128)S(1)}, f32[3,32,128]{2,1,0:T(8,128)S(1)}, u32[]{:S(2)}, u32[]{:S(2)}) %collective-permute-start) | collective-permute-done | bytes 49184 | tf_op jit(solution)/shard_map/ppermute | solution.py:489
  12.0 0.0 collective-permute-done.1.up_ref
  12.0 0.1 shard_map.209.refs_0_.refs_9_
  12.1 1.6 %collective-permute-start.3 = (f32[10,32,128]{2,1,0:T(8,128)S(1)}, f32[10,32,128]{2,1,0:T(8,128)S(1)}, u32[]{:S(2)}, u32[]{:S(2)}) collective-permute-start(f32[10,32,128]{2,1,0:T(8,128)S(1)} %shard_map.209.refs_0_.refs_9_), channel_id=1, source_target_pairs={{0,2},{1,3},{2,0},{3,1},{4,6},{5,7},{6,4},{7,5},{8,10},{9,11},{10,... | collective-permute-start | bytes 491528 | tf_op jit(solution)/shard_map/ppermute | solution.py:492
  13.7 0.0 collective-permute-start.2
  13.7 3.7 %collective-permute-done.3.refs_2_.refs_11_ = f32[10,32,128]{2,1,0:T(8,128)S(1)} collective-permute-done((f32[10,32,128]{2,1,0:T(8,128)S(1)}, f32[10,32,128]{2,1,0:T(8,128)S(1)}, u32[]{:S(2)}, u32[]{:S(2)}) %collective-permute-start.3) | collective-permute-done | bytes 163872 | tf_op jit(solution)/shard_map/ppermute | solution.py:492
  17.4 0.0 collective-permute-start.4
  17.4 0.0 collective-permute-done.2.refs_1_.refs_10_
  17.4 1.4 %collective-permute-done.4.refs_3_.refs_12_ = f32[10,32,128]{2,1,0:T(8,128)S(1)} collective-permute-done((f32[10,32,128]{2,1,0:T(8,128)S(1)}, f32[10,32,128]{2,1,0:T(8,128)S(1)}, u32[]{:S(2)}, u32[]{:S(2)}) %collective-permute-start.4) | collective-permute-done | bytes 163872 | tf_op jit(solution)/shard_map/ppermute | solution.py:492
  18.8 1.6 %copy-done = bf16[4,2,520,256]{3,2,1,0:T(8,128)(2,1)S(1)} copy-done((bf16[4,2,520,256]{3,2,1,0:T(8,128)(2,1)S(1)}, bf16[4,2,520,256]{3,2,1,0:T(8,128)(2,1)}, u32[]{:S(2)}) %copy-start) | copy-done | bytes 2129944
  20.4 1.0 %copy-done.4 = bf16[2,1,520,256]{3,2,1,0:T(8,128)(2,1)S(1)} copy-done((bf16[2,1,520,256]{3,2,1,0:T(8,128)(2,1)S(1)}, bf16[2,1,520,256]{3,2,1,0:T(8,128)(2,1)}, u32[]{:S(2)}) %copy-start.4) | copy-done | bytes 532504
  21.5 1.0 %copy-done.6 = bf16[4,128,384]{2,1,0:T(8,128)(2,1)S(1)} copy-done((bf16[4,128,384]{2,1,0:T(8,128)(2,1)S(1)}, bf16[4,128,384]{2,1,0:T(8,128)(2,1)}, u32[]{:S(2)}) %copy-start.6) | copy-done | bytes 393240
  22.5 0.9 %copy-done.8 = bf16[4,128,256]{2,1,0:T(8,128)(2,1)S(1)} copy-done((bf16[4,128,256]{2,1,0:T(8,128)(2,1)S(1)}, bf16[4,128,256]{2,1,0:T(8,128)(2,1)}, u32[]{:S(2)}) %copy-start.8) | copy-done | bytes 262168
  23.4 0.9 %copy-done.9 = bf16[4,256,128]{2,1,0:T(8,128)(2,1)S(1)} copy-done((bf16[4,256,128]{2,1,0:T(8,128)(2,1)S(1)}, bf16[4,256,128]{2,1,0:T(8,128)(2,1)}, u32[]{:S(2)}) %copy-start.9) | copy-done | bytes 262168
  24.4 0.9 %copy-done.10 = bf16[4,2,128,128]{3,2,1,0:T(8,128)(2,1)S(1)} copy-done((bf16[4,2,128,128]{3,2,1,0:T(8,128)(2,1)S(1)}, bf16[4,2,128,128]{3,2,1,0:T(8,128)(2,1)}, u32[]{:S(2)}) %copy-start.10) | copy-done | bytes 262168
  25.3 0.9 %copy-done.14 = bf16[4,128,128]{2,1,0:T(8,128)(2,1)S(1)} copy-done((bf16[4,128,128]{2,1,0:T(8,128)(2,1)S(1)}, bf16[4,128,128]{2,1,0:T(8,128)(2,1)}, u32[]{:S(2)}) %copy-start.14) | copy-done | bytes 131096
  26.2 0.9 %copy-done.15 = bf16[4,128,128]{2,1,0:T(8,128)(2,1)S(1)} copy-done((bf16[4,128,128]{2,1,0:T(8,128)(2,1)S(1)}, bf16[4,128,128]{2,1,0:T(8,128)(2,1)}, u32[]{:S(2)}) %copy-start.15) | copy-done | bytes 131096
  27.1 0.9 %copy-done.19 = bf16[1,1,264,128]{3,2,1,0:T(8,128)(2,1)S(1)} copy-done((bf16[1,1,264,128]{3,2,1,0:T(8,128)(2,1)S(1)}, bf16[1,1,264,128]{3,2,1,0:T(8,128)(2,1)}, u32[]{:S(2)}) %copy-start.19) | copy-done | bytes 67608
  28.0 3.5 %shard_map.211 = (f32[8,32,128]{2,1,0:T(8,128)S(1)}, f32[4,32,128]{2,1,0:T(8,128)S(1)}, f32[2,32,128]{2,1,0:T(8,128)S(1)}, f32[3,32,128]{2,1,0:T(8,128)}, f32[3,32,128]{2,1,0:T(8,128)}) custom-call(bf16[4,128,384]{2,1,0:T(8,128)(2,1)S(1)} %copy-done.6, bf16[4,128,256]{2,1,0:T(8,128)(2,1)S(1)} %copy-done.8, bf16[4,128,128]{2,1,0:T(8,128)(2,1)S(1)} %copy-done.14, ...), custom_call_target="tpu_custom_call" | custom-call | tf_op jit(solution)/shard_map/pallas_call | solution.py:529
  31.6 1.4 %collective-permute-start.5 = (f32[3,32,128]{2,1,0:T(8,128)}, f32[3,32,128]{2,1,0:T(8,128)}, u32[]{:S(2)}, u32[]{:S(2)}) collective-permute-start(f32[3,32,128]{2,1,0:T(8,128)} %get-tuple-element.19), channel_id=1, source_target_pairs={{0,4},{4,8},{8,12},{12,16},{16,20},{20,24},{24,28},{28,0},{1,5},{5... | collective-permute-start | bytes 147464 | tf_op jit(solution)/shard_map/ppermute | solution.py:489
  33.0 3.4 %collective-permute-start.6 = (f32[3,32,128]{2,1,0:T(8,128)}, f32[3,32,128]{2,1,0:T(8,128)}, u32[]{:S(2)}, u32[]{:S(2)}) collective-permute-start(f32[3,32,128]{2,1,0:T(8,128)} %get-tuple-element.20), channel_id=1, source_target_pairs={{0,28},{4,0},{8,4},{12,8},{16,12},{20,16},{24,20},{28,24},{1,29},{... | collective-permute-start | bytes 147464 | tf_op jit(solution)/shard_map/ppermute | solution.py:489
  36.4 1.0 %shard_map.212.refs_0_ = f32[2,32,128]{2,1,0:T(8,128)} custom-call(bf16[4,2,128,128]{3,2,1,0:T(8,128)(2,1)S(1)} %copy-done.12, f32[10,32,128]{2,1,0:T(8,128)S(1)} %shard_map.209.refs_0_.refs_9_, f32[10,32,128]{2,1,0:T(8,128)S(1)} %collective-permute-done.2.refs_1_.refs_10_, f32[10,32,128]{2,1,0:T(8,128)S(1)} %collective-permute-done.3.refs_2_.refs_11_, ...), custom_call_target="tpu_custom_call" | custom-call | tf_op jit(solution)/shard_map/pallas_call | solution.py:512
  37.4 0.7 %collective-permute-start.7 = (f32[2,32,128]{2,1,0:T(8,128)}, f32[2,32,128]{2,1,0:T(8,128)}, u32[]{:S(2)}, u32[]{:S(2)}) collective-permute-start(f32[2,32,128]{2,1,0:T(8,128)} %shard_map.212.refs_0_), channel_id=1, source_target_pairs={{0,24},{4,28},{8,0},{12,4},{16,8},{20,12},{24,16},{28,20},{1,25},{... | collective-permute-start | bytes 98312 | tf_op jit(solution)/shard_map/ppermute | solution.py:489
  38.1 0.0 collective-permute-start.8
  38.1 1.4 %collective-permute-start.9 = (f32[2,32,128]{2,1,0:T(8,128)}, f32[2,32,128]{2,1,0:T(8,128)}, u32[]{:S(2)}, u32[]{:S(2)}) collective-permute-start(f32[2,32,128]{2,1,0:T(8,128)} %shard_map.212.refs_0_), channel_id=1, source_target_pairs={{0,8},{4,12},{8,16},{12,20},{16,24},{20,28},{24,0},{28,4},{1,9},{5... | collective-permute-start | bytes 98312 | tf_op jit(solution)/shard_map/ppermute | solution.py:489
  39.5 1.1 %copy.23.four_ref = bf16[4,1,136,64]{3,2,1,0:T(8,128)(2,1)S(1)} copy(bf16[4,1,136,64]{2,3,1,0:T(8,128)(2,1)} %param.27) | data formatting | bytes 139264 | tf_op args[5]
  40.6 0.0 copy-start.5
  40.6 0.0 copy-start.18
  40.6 0.0 copy-start.20
  40.6 0.0 copy-start.23
  40.7 0.0 copy-start.26
  40.7 1.0 %shard_map.210.fine_ref = f32[16,32,128]{2,1,0:T(8,128)S(1)} custom-call(f32[512,128]{1,0:T(8,128)S(1)} %bitcast.3, f32[3,32,128]{2,1,0:T(8,128)S(1)} %collective-permute-done.down_ref, f32[3,32,128]{2,1,0:T(8,128)S(1)} %collective-permute-done.1.up_ref, bf16[2,128,256]{2,1,0:T(8,128)(2,1)S(1)} %copy-done.13, bf16[8,1,520,256]{3,2,1,0:T(8,128)(2,1)S(1)} %copy-done.1, ...), custom_call_target="tpu_custom_call" | custom-call | tf_op jit(solution)/shard_map/pallas_call | solution.py:536
  41.7 0.3 collective-permute-done.7.refs_1_
  42.0 1.3 %collective-permute-done.8.refs_2_ = f32[2,32,128]{2,1,0:T(8,128)} collective-permute-done((f32[2,32,128]{2,1,0:T(8,128)}, f32[2,32,128]{2,1,0:T(8,128)}, u32[]{:S(2)}, u32[]{:S(2)}) %collective-permute-start.8) | collective-permute-done | bytes 32800 | tf_op jit(solution)/shard_map/ppermute | solution.py:489
  43.3 1.0 %collective-permute-done.9.refs_3_ = f32[2,32,128]{2,1,0:T(8,128)} collective-permute-done((f32[2,32,128]{2,1,0:T(8,128)}, f32[2,32,128]{2,1,0:T(8,128)}, u32[]{:S(2)}, u32[]{:S(2)}) %collective-permute-start.9) | collective-permute-done | bytes 32800 | tf_op jit(solution)/shard_map/ppermute | solution.py:489
  44.3 0.0 collective-permute-done.5.down_ref
  44.4 0.0 collective-permute-done.6.up_ref
  44.4 0.0 copy-done.5
  44.4 0.0 copy-done.18
  44.4 0.0 copy-done.20
  44.4 2.7 %shard_map.213 = f32[512,128]{1,0:T(8,128)} custom-call(f32[16,32,128]{2,1,0:T(8,128)S(1)} %shard_map.210.fine_ref, f32[8,32,128]{2,1,0:T(8,128)S(1)} %copy-done.18, f32[4,32,128]{2,1,0:T(8,128)S(1)} %copy-done.22, f32[2,32,128]{2,1,0:T(8,128)S(1)} %copy-done.25, f32[3,32,128]{2,1,0:T(8,128)} %collective-permute-done.5.down_ref, ...), custom_call_target="tpu_custom_call" | custom-call | tf_op jit(solution)/shard_map/pallas_call | solution.py:541
  (35 shorter events, 0.1 us)
Async XLA Ops:
  0.0 0.9 %copy-start.2 = (f32[32,16,128]{2,1,0:T(8,128)S(1)}, f32[32,16,128]{2,1,0:T(8,128)}, u32[]{:S(2)}) copy-start(f32[32,16,128]{2,1,0:T(8,128)} %param.22) | copy-start | bytes 786436
  1.0 1.0 %copy-start.7 = (bf16[4,3,128,128]{3,2,1,0:T(8,128)(2,1)S(1)}, bf16[4,3,128,128]{3,2,1,0:T(8,128)(2,1)}, u32[]{:S(2)}) copy-start(bf16[4,3,128,128]{3,2,1,0:T(8,128)(2,1)} %constant.31.clone.shrink_ref) | copy-start | bytes 1179652
  1.9 0.8 %copy-start.11 = (bf16[2,128,128]{2,1,0:T(8,128)(2,1)S(1)}, bf16[2,128,128]{2,1,0:T(8,128)(2,1)}, u32[]{:S(2)}) copy-start(bf16[2,128,128]{2,1,0:T(8,128)(2,1)} %constant.30.clone.sides_ref) | copy-start | bytes 196612
  2.8 0.7 %copy-start.27 = (f32[1,128]{1,0:T(1,128)S(1)}, f32[1,128]{1,0:T(1,128)}, u32[]{:S(2)}) copy-start(f32[1,128]{1,0:T(1,128)} %constant.32.clone.scale_ref) | copy-start | bytes 1540
  3.8 8.2 %collective-permute-start = (f32[3,32,128]{2,1,0:T(8,128)S(1)}, f32[3,32,128]{2,1,0:T(8,128)S(1)}, u32[]{:S(2)}, u32[]{:S(2)}) collective-permute-start(f32[3,32,128]{2,1,0:T(8,128)S(1)} %get-tuple-element.13), channel_id=1, source_target_pairs={{0,4},{4,8},{8,12},{12,16},{16,20},{20,24},{24,28},{28,0},{1,5},{5... | collective-permute-start | bytes 147464 | tf_op jit(solution)/shard_map/ppermute | solution.py:489
  6.8 5.1 %collective-permute-start.1 = (f32[3,32,128]{2,1,0:T(8,128)S(1)}, f32[3,32,128]{2,1,0:T(8,128)S(1)}, u32[]{:S(2)}, u32[]{:S(2)}) collective-permute-start(f32[3,32,128]{2,1,0:T(8,128)S(1)} %get-tuple-element.14), channel_id=1, source_target_pairs={{0,28},{4,0},{8,4},{12,8},{16,12},{20,16},{24,20},{28,24},{1,29},{... | collective-permute-start | bytes 147464 | tf_op jit(solution)/shard_map/ppermute | solution.py:489
  12.0 28.6 %copy-start.3 = (f32[32,16,128]{2,1,0:T(8,128)S(1)}, f32[32,16,128]{2,1,0:T(8,128)}, u32[]{:S(2)}) copy-start(f32[32,16,128]{2,1,0:T(8,128)} %param.22) | copy-start | bytes 786436
  12.0 28.6 %copy-start.13 = (bf16[2,128,256]{2,1,0:T(8,128)(2,1)S(1)}, bf16[2,128,256]{2,1,0:T(8,128)(2,1)}, u32[]{:S(2)}) copy-start(bf16[2,128,256]{2,1,0:T(8,128)(2,1)} %constant.40.clone.halo_ref) | copy-start | bytes 393220
  12.1 5.3 %collective-permute-start.3 = (f32[10,32,128]{2,1,0:T(8,128)S(1)}, f32[10,32,128]{2,1,0:T(8,128)S(1)}, u32[]{:S(2)}, u32[]{:S(2)}) collective-permute-start(f32[10,32,128]{2,1,0:T(8,128)S(1)} %shard_map.209.refs_0_.refs_9_), channel_id=1, source_target_pairs={{0,2},{1,3},{2,0},{3,1},{4,6},{5,7},{6,4},{7,5},{8,10},{9,11},{10,... | collective-permute-start | bytes 491528 | tf_op jit(solution)/shard_map/ppermute | solution.py:492
  13.7 3.7 %collective-permute-start.2 = (f32[10,32,128]{2,1,0:T(8,128)S(1)}, f32[10,32,128]{2,1,0:T(8,128)S(1)}, u32[]{:S(2)}, u32[]{:S(2)}) collective-permute-start(f32[10,32,128]{2,1,0:T(8,128)S(1)} %shard_map.209.refs_0_.refs_9_), channel_id=1, source_target_pairs={{0,1},{1,0},{2,3},{3,2},{4,5},{5,4},{6,7},{7,6},{8,9},{9,8},{10,11... | collective-permute-start | bytes 491528 | tf_op jit(solution)/shard_map/ppermute | solution.py:492
  17.4 1.4 %collective-permute-start.4 = (f32[10,32,128]{2,1,0:T(8,128)S(1)}, f32[10,32,128]{2,1,0:T(8,128)S(1)}, u32[]{:S(2)}, u32[]{:S(2)}) collective-permute-start(f32[10,32,128]{2,1,0:T(8,128)S(1)} %collective-permute-done.3.refs_2_.refs_11_), channel_id=1, source_target_pairs={{0,1},{1,0},{2,3},{3,2},{4,5},{5,4},{6,7},{7,6},{8,9},{9,8},{10,11... | collective-permute-start | bytes 491528 | tf_op jit(solution)/shard_map/ppermute | solution.py:492
  18.8 1.6 %copy-start = (bf16[4,2,520,256]{3,2,1,0:T(8,128)(2,1)S(1)}, bf16[4,2,520,256]{3,2,1,0:T(8,128)(2,1)}, u32[]{:S(2)}) copy-start(bf16[4,2,520,256]{3,2,1,0:T(8,128)(2,1)} %refs_6_.1) | copy-start | bytes 6389764
  20.4 1.0 %copy-start.4 = (bf16[2,1,520,256]{3,2,1,0:T(8,128)(2,1)S(1)}, bf16[2,1,520,256]{3,2,1,0:T(8,128)(2,1)}, u32[]{:S(2)}) copy-start(bf16[2,1,520,256]{3,2,1,0:T(8,128)(2,1)} %refs_7_.1) | copy-start | bytes 1597444
  21.5 1.0 %copy-start.6 = (bf16[4,128,384]{2,1,0:T(8,128)(2,1)S(1)}, bf16[4,128,384]{2,1,0:T(8,128)(2,1)}, u32[]{:S(2)}) copy-start(bf16[4,128,384]{2,1,0:T(8,128)(2,1)} %constant.34.clone.refs_0_) | copy-start | bytes 1179652
  22.5 0.9 %copy-start.8 = (bf16[4,128,256]{2,1,0:T(8,128)(2,1)S(1)}, bf16[4,128,256]{2,1,0:T(8,128)(2,1)}, u32[]{:S(2)}) copy-start(bf16[4,128,256]{2,1,0:T(8,128)(2,1)} %constant.35.clone.refs_1_) | copy-start | bytes 786436
  23.4 0.9 %copy-start.9 = (bf16[4,256,128]{2,1,0:T(8,128)(2,1)S(1)}, bf16[4,256,128]{2,1,0:T(8,128)(2,1)}, u32[]{:S(2)}) copy-start(bf16[4,256,128]{2,1,0:T(8,128)(2,1)} %constant.37.clone.refs_3_) | copy-start | bytes 786436
  24.4 0.9 %copy-start.10 = (bf16[4,2,128,128]{3,2,1,0:T(8,128)(2,1)S(1)}, bf16[4,2,128,128]{3,2,1,0:T(8,128)(2,1)}, u32[]{:S(2)}) copy-start(bf16[4,2,128,128]{3,2,1,0:T(8,128)(2,1)} %constant.39.clone.refs_5_) | copy-start | bytes 786436
  25.3 0.9 %copy-start.14 = (bf16[4,128,128]{2,1,0:T(8,128)(2,1)S(1)}, bf16[4,128,128]{2,1,0:T(8,128)(2,1)}, u32[]{:S(2)}) copy-start(bf16[4,128,128]{2,1,0:T(8,128)(2,1)} %constant.36.clone.refs_2_) | copy-start | bytes 393220
  26.2 0.9 %copy-start.15 = (bf16[4,128,128]{2,1,0:T(8,128)(2,1)S(1)}, bf16[4,128,128]{2,1,0:T(8,128)(2,1)}, u32[]{:S(2)}) copy-start(bf16[4,128,128]{2,1,0:T(8,128)(2,1)} %constant.38.clone.refs_4_) | copy-start | bytes 393220
  27.1 0.9 %copy-start.19 = (bf16[1,1,264,128]{3,2,1,0:T(8,128)(2,1)S(1)}, bf16[1,1,264,128]{3,2,1,0:T(8,128)(2,1)}, u32[]{:S(2)}) copy-start(bf16[1,1,264,128]{3,2,1,0:T(8,128)(2,1)} %refs_8_.1) | copy-start | bytes 202756
  28.0 8.4 %copy-start.12 = (bf16[4,2,128,128]{3,2,1,0:T(8,128)(2,1)S(1)}, bf16[4,2,128,128]{3,2,1,0:T(8,128)(2,1)}, u32[]{:S(2)}) copy-start(bf16[4,2,128,128]{3,2,1,0:T(8,128)(2,1)} %constant.33.clone.place_ref) | copy-start | bytes 786436
  28.0 12.6 %copy-start.1 = (bf16[8,1,520,256]{3,2,1,0:T(8,128)(2,1)S(1)}, bf16[8,1,520,256]{3,2,1,0:T(8,128)(2,1)}, u32[]{:S(2)}) copy-start(bf16[8,1,520,256]{3,2,1,0:T(8,128)(2,1)} %factor_ref.1) | copy-start | bytes 6389764
  31.6 6.5 %copy-start.17 = (f32[8,32,128]{2,1,0:T(8,128)}, f32[8,32,128]{2,1,0:T(8,128)S(1)}, u32[]{:S(2)}) copy-start(f32[8,32,128]{2,1,0:T(8,128)S(1)} %get-tuple-element.16.one_ref) | copy-start | bytes 393220
  31.6 6.5 %copy-start.21 = (f32[4,32,128]{2,1,0:T(8,128)}, f32[4,32,128]{2,1,0:T(8,128)S(1)}, u32[]{:S(2)}) copy-start(f32[4,32,128]{2,1,0:T(8,128)S(1)} %get-tuple-element.17.two_ref) | copy-start | bytes 196612
  31.6 6.5 %copy-start.24 = (f32[2,32,128]{2,1,0:T(8,128)}, f32[2,32,128]{2,1,0:T(8,128)S(1)}, u32[]{:S(2)}) copy-start(f32[2,32,128]{2,1,0:T(8,128)S(1)} %get-tuple-element.18.three_ref) | copy-start | bytes 98308
  31.6 12.8 %collective-permute-start.5 = (f32[3,32,128]{2,1,0:T(8,128)}, f32[3,32,128]{2,1,0:T(8,128)}, u32[]{:S(2)}, u32[]{:S(2)}) collective-permute-start(f32[3,32,128]{2,1,0:T(8,128)} %get-tuple-element.19), channel_id=1, source_target_pairs={{0,4},{4,8},{8,12},{12,16},{16,20},{20,24},{24,28},{28,0},{1,5},{5... | collective-permute-start | bytes 147464 | tf_op jit(solution)/shard_map/ppermute | solution.py:489
  33.0 11.4 %collective-permute-start.6 = (f32[3,32,128]{2,1,0:T(8,128)}, f32[3,32,128]{2,1,0:T(8,128)}, u32[]{:S(2)}, u32[]{:S(2)}) collective-permute-start(f32[3,32,128]{2,1,0:T(8,128)} %get-tuple-element.20), channel_id=1, source_target_pairs={{0,28},{4,0},{8,4},{12,8},{16,12},{20,16},{24,20},{28,24},{1,29},{... | collective-permute-start | bytes 147464 | tf_op jit(solution)/shard_map/ppermute | solution.py:489
  37.4 7.0 %copy-start.16 = (bf16[512,64]{1,0:T(8,128)(2,1)S(1)}, bf16[512,64]{1,0:T(8,128)(2,1)}, u32[]{:S(2)}) copy-start(bf16[512,64]{1,0:T(8,128)(2,1)} %constant.42.clone.flat_ref) | copy-start | bytes 196612
  37.4 4.6 %collective-permute-start.7 = (f32[2,32,128]{2,1,0:T(8,128)}, f32[2,32,128]{2,1,0:T(8,128)}, u32[]{:S(2)}, u32[]{:S(2)}) collective-permute-start(f32[2,32,128]{2,1,0:T(8,128)} %shard_map.212.refs_0_), channel_id=1, source_target_pairs={{0,24},{4,28},{8,0},{12,4},{16,8},{20,12},{24,16},{28,20},{1,25},{... | collective-permute-start | bytes 98312 | tf_op jit(solution)/shard_map/ppermute | solution.py:489
  38.1 5.2 %collective-permute-start.8 = (f32[2,32,128]{2,1,0:T(8,128)}, f32[2,32,128]{2,1,0:T(8,128)}, u32[]{:S(2)}, u32[]{:S(2)}) collective-permute-start(f32[2,32,128]{2,1,0:T(8,128)} %shard_map.212.refs_0_), channel_id=1, source_target_pairs={{0,16},{4,20},{8,24},{12,28},{16,0},{20,4},{24,8},{28,12},{1,17},{... | collective-permute-start | bytes 98312 | tf_op jit(solution)/shard_map/ppermute | solution.py:489
  38.1 6.3 %collective-permute-start.9 = (f32[2,32,128]{2,1,0:T(8,128)}, f32[2,32,128]{2,1,0:T(8,128)}, u32[]{:S(2)}, u32[]{:S(2)}) collective-permute-start(f32[2,32,128]{2,1,0:T(8,128)} %shard_map.212.refs_0_), channel_id=1, source_target_pairs={{0,8},{4,12},{8,16},{12,20},{16,24},{20,28},{24,0},{28,4},{1,9},{5... | collective-permute-start | bytes 98312 | tf_op jit(solution)/shard_map/ppermute | solution.py:489
  40.6 3.8 %copy-start.5 = (bf16[4,4,128,128]{3,2,1,0:T(8,128)(2,1)S(1)}, bf16[4,4,128,128]{3,2,1,0:T(8,128)(2,1)}, u32[]{:S(2)}) copy-start(bf16[4,4,128,128]{3,2,1,0:T(8,128)(2,1)} %constant.44.clone.lift_ref) | copy-start | bytes 1572868
  40.6 3.8 %copy-start.18 = (f32[8,32,128]{2,1,0:T(8,128)S(1)}, f32[8,32,128]{2,1,0:T(8,128)}, u32[]{:S(2)}) copy-start(f32[8,32,128]{2,1,0:T(8,128)} %copy-done.17) | copy-start | bytes 393220
  40.6 3.8 %copy-start.20 = (bf16[2,128,128]{2,1,0:T(8,128)(2,1)S(1)}, bf16[2,128,128]{2,1,0:T(8,128)(2,1)}, u32[]{:S(2)}) copy-start(bf16[2,128,128]{2,1,0:T(8,128)(2,1)} %constant.41.clone.shrink_ref) | copy-start | bytes 196612
  40.6 3.8 %copy-start.22 = (f32[4,32,128]{2,1,0:T(8,128)S(1)}, f32[4,32,128]{2,1,0:T(8,128)}, u32[]{:S(2)}) copy-start(f32[4,32,128]{2,1,0:T(8,128)} %copy-done.21) | copy-start | bytes 196612
  40.6 3.8 %copy-start.23 = (bf16[64,256]{1,0:T(8,128)(2,1)S(1)}, bf16[64,256]{1,0:T(8,128)(2,1)}, u32[]{:S(2)}) copy-start(bf16[64,256]{1,0:T(8,128)(2,1)} %constant.43.clone.spread_ref) | copy-start | bytes 98308
  40.7 3.8 %copy-start.25 = (f32[2,32,128]{2,1,0:T(8,128)S(1)}, f32[2,32,128]{2,1,0:T(8,128)}, u32[]{:S(2)}) copy-start(f32[2,32,128]{2,1,0:T(8,128)} %copy-done.24) | copy-start | bytes 98308
  40.7 3.8 %copy-start.26 = (bf16[64,64]{1,0:T(8,128)(2,1)S(1)}, bf16[64,64]{1,0:T(8,128)(2,1)}, u32[]{:S(2)}) copy-start(bf16[64,64]{1,0:T(8,128)(2,1)} %inverse_ref.1) | copy-start | bytes 24580

commit v2 on v1

--- a/solution.py
+++ b/solution.py
@@ -1,4 +1,5 @@
 import functools
+import math
 
 import jax
 import jax.numpy as jnp
@@ -18,18 +19,6 @@
 
 def round_up(value, unit=LANES):
     return -(-value // unit) * unit
-
-
-def local_shrink(fine, coarse, halo_in, first, last):
-    out = np.zeros((fine + 2 * halo_in, coarse + 2))
-    for i in range(-1, coarse + 1):
-        if (i == -1 and first) or (i == coarse and last):
-            continue
-        for t, tap in enumerate(TAPS):
-            j = 2 * i - 1 + t
-            if -halo_in <= j < fine + halo_in:
-                out[j + halo_in, i + 1] = tap
-    return out
 
 
 def global_prolong(coarse):
@@ -62,31 +51,6 @@
         self.offset = [None, 0, self.w[1] + 2, self.w[1] + self.w[2] + 4]
         self.spare = self.w[1] + self.w[2] + self.w[3] + 6
 
-    def scale(self):
-        out = np.ones((1, LANES), np.float32)
-        for l in (1, 2, 3):
-            out[:, self.offset[l] : self.offset[l] + self.w[l] + 2] = SHRINK**l
-        return out
-
-    def shrink_columns(self):
-        out = np.zeros((self.m, 3, self.w0, LANES))
-        for c in range(self.m):
-            ends = (c == 0, c == self.m - 1)
-            now = local_shrink(self.w0, self.w[1], 0, *ends)
-            for l in (1, 2, 3):
-                if l > 1:
-                    now = now @ local_shrink(self.w[l - 1], self.w[l], 1, *ends)
-                o = self.offset[l]
-                out[c, l - 1, :, o : o + self.w[l] + 2] = now
-        return bf(out)
-
-    def pick_sides(self):
-        out = np.zeros((2, self.w0, LANES))
-        for k in range(2):
-            out[k, 0, self.spare + 2 * k] = 1
-            out[k, self.w0 - 1, self.spare + 2 * k + 1] = 1
-        return bf(out)
-
     def place(self, level, lead, width, at=0):
         out = np.zeros((self.m, LANES, width))
         for c in range(self.m):
@@ -126,7 +90,7 @@
         for side, taps in enumerate(((1, 3), (3, 1))):
             for j in range(2):
                 out[side, j, :, 1 : 1 + ny4] = taps[j] * columns
-        return bf(out.reshape(2, 2 * ny3, width))
+        return bf(out.reshape(4 * ny3, width))
 
     def coarsest_shrink(self):
         nx5, ny5, ny4 = self.nx[5], self.ny[5], self.ny[4]
@@ -156,6 +120,33 @@
         return bf(out), group
 
 
+class Blocks:
+    def __init__(self):
+        self.parts, self.places, self.count = [], {}, 0
+
+    def add(self, name, array):
+        lead, (rows, columns) = array.shape[:-2], array.shape[-2:]
+        high, wide = round_up(rows) // LANES, round_up(columns) // LANES
+        out = np.zeros((math.prod(lead), high * LANES, wide * LANES), np.float32)
+        out[:, :rows, :columns] = np.asarray(array, np.float32).reshape((-1, rows, columns))
+        out = out.reshape(-1, high, LANES, wide, LANES).transpose(0, 1, 3, 2, 4)
+        self.parts.append(out.reshape(-1, LANES, LANES))
+        self.places[name] = (self.count, high, wide)
+        self.count += len(self.parts[-1])
+
+    def array(self):
+        return jnp.asarray(bf(np.concatenate(self.parts, axis=0)))
+
+    def get(self, ref, name, lead=0):
+        base, high, wide = self.places[name]
+        base = base + lead * (high * wide)
+        rows = [
+            jnp.concatenate([ref[base + i * wide + j] for j in range(wide)], axis=1)
+            for i in range(high)
+        ]
+        return jnp.concatenate(rows, axis=0)
+
+
 def split(value):
     high = value.astype(BF16)
     return high, (value - high.astype(F32)).astype(BF16)
@@ -163,9 +154,11 @@
 
 def product(value, matrix):
     high, low = split(value)
-    return jnp.dot(high, matrix, preferred_element_type=F32) + jnp.dot(
-        low, matrix, preferred_element_type=F32
-    )
+    count = value.shape[0]
+    both = jnp.dot(
+        jnp.concatenate([high, low], axis=0), matrix, preferred_element_type=F32
+    )
+    return both[:count] + both[count:]
 
 
 def shrink_rows(rows, count, halo):
@@ -223,31 +216,74 @@
     return jnp.dot(lhs, factor, preferred_element_type=F32)
 
 
-def kernel_call(body, out_shape, scratch=()):
-    return pl.pallas_call(
-        body,
-        out_shape=out_shape,
-        scratch_shapes=list(scratch),
-        compiler_params=pltpu.CompilerParams(vmem_limit_bytes=VMEM_BYTES),
-    )
+def kernel_call(body, out_shape, scratch=(), cost_us=1.0):
+    whole = pl.BlockSpec(memory_space=pltpu.VMEM)
+
+    def call(*operands):
+        return pl.pallas_call(
+            body,
+            out_shape=out_shape,
+            in_specs=[whole] * len(operands),
+            out_specs=jax.tree.map(lambda _: whole, out_shape),
+            scratch_shapes=list(scratch),
+            compiler_params=pltpu.CompilerParams(vmem_limit_bytes=VMEM_BYTES),
+            cost_estimate=pl.CostEstimate(
+                flops=int(cost_us * 1e9), bytes_accessed=int(cost_us * 3e6), transcendentals=0
+            ),
+        )(*operands)
+
+    return call
 
 
 def shape(*dims):
     return jax.ShapeDtypeStruct(dims, F32)
 
 
-def restrict_kernel(plan, x_ref, shrink_ref, sides_ref, scale_ref, own_ref, down_ref, up_ref):
+def tap_matrix(row_lead, lane_lead, count, first, last):
+    row = lax.broadcasted_iota(jnp.int32, (LANES, LANES), 0) - row_lead
+    lane = lax.broadcasted_iota(jnp.int32, (LANES, LANES), 1) - lane_lead
+    tap = row - 2 * lane + 3
+    outer = jnp.logical_or(tap == 0, tap == 3)
+    inner = jnp.logical_or(tap == 1, tap == 2)
+    value = jnp.where(outer, 1.0, jnp.where(inner, 3.0, 0.0))
+    value = jnp.where(jnp.logical_or(lane < first, lane > count + 1 - last), 0.0, value)
+    return value.astype(BF16)
+
+
+def side_matrix(plan, k):
+    row = lax.broadcasted_iota(jnp.int32, (LANES, LANES), 0)
+    lane = lax.broadcasted_iota(jnp.int32, (LANES, LANES), 1) - plan.spare - 2 * k
+    left = jnp.logical_and(row == 0, lane == 0)
+    right = jnp.logical_and(row == plan.w0 - 1, lane == 1)
+    return jnp.where(jnp.logical_or(left, right), 1.0, 0.0).astype(BF16)
+
+
+def restrict_kernel(plan, x_ref, own_ref, down_ref, up_ref, rows_ref):
     r, c = lax.axis_index("px"), lax.axis_index("py")
     rhs, slots, h = plan.rhs, plan.slots, plan.h
+    first = jnp.where(c == 0, 1, 0)
+    last = jnp.where(c == plan.m - 1, 1, 0)
+    shrink = None
+    matrices = []
+    for level in (1, 2, 3):
+        lead = 0 if level == 1 else plan.offset[level - 1] + 1
+        step = tap_matrix(lead, plan.offset[level], plan.w[level], first, last)
+        if shrink is None:
+            shrink = step
+        else:
+            shrink = jnp.dot(shrink, step, preferred_element_type=F32).astype(BF16)
+        matrices.append(shrink)
     above = jnp.where(r > 0, 1.0, 0.0).astype(F32)
     below = jnp.where(r < plan.n - 1, 1.0, 0.0).astype(F32)
     x = [x_ref[pl.ds(row, rhs, stride=h[0]), :] for row in range(h[0])]
+    for i, row in enumerate(x):
+        rows_ref[i] = row
     rows, total = x, None
     for level in (1, 2, 3):
         rows = shrink_rows(rows, h[level - 1], 0 if level == 1 else 1)
         rows[0] = rows[0] * above
         rows[-1] = rows[-1] * below
-        part = product(jnp.concatenate(rows, axis=0), shrink_ref[c, level - 1])
+        part = product(jnp.concatenate(rows, axis=0), matrices[level - 1])
         if total is None:
             total = part
         else:
@@ -255,17 +291,20 @@
             total = jnp.concatenate([total[:count] + part, total[count:]], axis=0)
     sides = [jnp.zeros_like(x[0])] + x[: slots - 1]
     total = total + jnp.dot(
-        jnp.concatenate(sides, axis=0).astype(BF16), sides_ref[0], preferred_element_type=F32
+        jnp.concatenate(sides, axis=0).astype(BF16), side_matrix(plan, 0),
+        preferred_element_type=F32,
     )
     rest = jnp.concatenate(x[slots - 1 :], axis=0).astype(BF16)
-    more = jnp.dot(rest, sides_ref[1], preferred_element_type=F32)
+    more = jnp.dot(rest, side_matrix(plan, 1), preferred_element_type=F32)
     count = more.shape[0]
     total = jnp.concatenate([total[:count] + more, total[count:]], axis=0)
-    total = total * scale_ref[...]
+    lane = lane_index(slots * rhs)
+    one, two = plan.offset[2], plan.offset[3]
+    scale = jnp.where(lane < two, SHRINK**2, jnp.where(lane < plan.spare, SHRINK**3, 1.0))
+    total = total * jnp.where(lane < one, SHRINK, scale)
     own = total.reshape(slots, rhs, LANES)
     own_ref[...] = own
     lane = lane_index(rhs)
-    one, two = plan.offset[2], plan.offset[3]
     down_ref[0] = x[-1]
     up_ref[0] = x[0]
     for k in range(2):
@@ -276,7 +315,7 @@
         up_ref[1 + k] = own[k]
 
 
-def merge_kernel(plan, own_ref, down_ref, up_ref, sides_ref, out_ref):
+def merge_kernel(plan, own_ref, down_ref, up_ref, out_ref):
     r = lax.axis_index("px")
     rhs, h = plan.rhs, plan.h
     above = jnp.where(r > 0, 1.0, 0.0).astype(F32)
@@ -297,38 +336,43 @@
             chosen = jnp.logical_and(lane >= low, lane < high)
             out_ref[row] = out_ref[row] + jnp.where(chosen, piece, 0.0)
     top = (down_ref[0] * above).astype(BF16)
-    out_ref[0] = out_ref[0] + jnp.dot(top, sides_ref[0], preferred_element_type=F32)
+    out_ref[0] = out_ref[0] + jnp.dot(top, side_matrix(plan, 0), preferred_element_type=F32)
     bottom = (up_ref[0] * below).astype(BF16)
     at = h[0] + 1 - plan.slots
-    out_ref[at] = out_ref[at] + jnp.dot(bottom, sides_ref[1], preferred_element_type=F32)
-
-
-def gather_kernel(plan, place_ref, *refs):
+    out_ref[at] = out_ref[at] + jnp.dot(bottom, side_matrix(plan, 1), preferred_element_type=F32)
+
+
+def banded(bands, matrices):
+    return product(jnp.concatenate(bands, axis=1), jnp.concatenate(matrices, axis=0))
+
+
+def owners(plan):
+    c = lax.axis_index("py")
+    return [jnp.bitwise_xor(c, k) for k in range(plan.m)]
+
+
+def gather_kernel(plan, blocks, block_ref, *refs):
     band_refs, out_ref = refs[:-1], refs[-1]
-    c = lax.axis_index("py")
-    rhs, width = plan.rhs, 2 * plan.ny[3]
+    rhs = plan.rhs
+    values, matrices = [], []
+    for band, owner in zip(band_refs, owners(plan)):
+        for j in range(2):
+            values.append(jnp.concatenate([band[j], band[2 + j]], axis=0))
+            matrices.append(blocks.get(block_ref, "pairs", 2 * owner + j))
+    total = banded(values, matrices)
     for half in range(2):
-        total = jnp.zeros((rhs, width), F32)
-        for k, band in enumerate(band_refs):
-            owner = jnp.bitwise_xor(c, k)
-            for j in range(2):
-                total = total + product(band[2 * half + j], place_ref[owner, j])
-        out_ref[half] = total
-
-
-def level_rows(plan, level, band_refs, place_ref, c):
+        out_ref[half] = total[half * rhs : (half + 1) * rhs]
+
+
+def level_rows(plan, level, band_refs, blocks, block_ref):
     rhs, count = plan.rhs, plan.h[level] + 2
-    total = None
-    for k, band in enumerate(band_refs):
-        owner = jnp.bitwise_xor(c, k)
-        value = band[:count].reshape(count * rhs, LANES)
-        part = product(value, place_ref[owner])
-        total = part if total is None else total + part
-    return total
-
-
-def coarse_kernel(plan, places, lifts, factors, *refs):
-    bands, outs = refs[: plan.m], refs[plan.m :]
+    values = [band[:count].reshape(count * rhs, LANES) for band in band_refs]
+    matrices = [blocks.get(block_ref, f"place{level}", owner) for owner in owners(plan)]
+    return banded(values, matrices)
+
+
+def coarse_kernel(plan, blocks, block_ref, *refs):
+    factors, bands, outs = refs[:3], refs[3 : 3 + plan.m], refs[3 + plan.m :]
     r, c = lax.axis_index("px"), lax.axis_index("py")
     rhs = plan.rhs
     above = jnp.where(r > 0, 1.0, 0.0).astype(F32)
@@ -336,13 +380,13 @@
     down_ref, up_ref = outs[3], outs[4]
     for level in (1, 2, 3):
         w, tiles = plan.tile[level], plan.tiles[level]
-        whole = level_rows(plan, level, bands, places[level - 1], c)
+        whole = level_rows(plan, level, bands, blocks, block_ref)
         count = plan.h[level] + 2
         rows = [whole[i * rhs : (i + 1) * rhs] for i in range(count)]
         if level == 3:
             rows[0] = rows[0] * above
             rows[-1] = rows[-1] * below
-        lift_ref, factor_ref, out_ref = lifts[level - 1], factors[level - 1], outs[level - 1]
+        factor_ref, out_ref = factors[level - 1], outs[level - 1]
         solved = [[] for _ in range(tiles)]
         for b in range(plan.h[level] // 2):
             for t in range(tiles):
@@ -353,17 +397,16 @@
                     pieces.append([row[:, lo : lo + LANES] for lo in lanes])
                 solved[t].append(solve(assemble(pieces, w), factor_ref[b, t]))
         pairs = plan.h[level] // 2
-        lifted = [None, None]
-        for t in range(tiles):
-            stacked = jnp.concatenate(solved[t], axis=0)
-            for j in range(2):
-                if w % LANES == 0:
-                    part = product(
-                        stacked[:, j * w : (j + 1) * w], lift_ref[c, t * w : (t + 1) * w]
-                    )
-                else:
-                    part = product(stacked, lift_ref[c, j * tiles + t])
-                lifted[j] = part if lifted[j] is None else lifted[j] + part
+        stacked = [jnp.concatenate(solved[t], axis=0) for t in range(tiles)]
+        lifted = []
+        name = f"lift{level}"
+        for j in range(2):
+            if w % LANES == 0:
+                row = jnp.concatenate([v[:, j * w : (j + 1) * w] for v in stacked], axis=1)
+                lifted.append(product(row, blocks.get(block_ref, name, c)))
+            else:
+                row = jnp.concatenate(stacked, axis=1)
+                lifted.append(product(row, blocks.get(block_ref, name, 2 * c + j)))
         for b in range(pairs):
             for j in range(2):
                 out_ref[2 * b + j] = lifted[j][b * rhs : (b + 1) * rhs]
@@ -371,21 +414,24 @@
         up_ref[level - 1] = lifted[0][:rhs]
 
 
-def fine_kernel(plan, x_ref, down_ref, up_ref, halo_ref, factor_ref, *refs):
+def fine_kernel(plan, blocks, block_ref, rows_ref, down_ref, up_ref, factor_ref, *refs):
     bands, out_ref = refs[: plan.m], refs[plan.m]
     r, c = lax.axis_index("px"), lax.axis_index("py")
     rhs, h0, w0, slots = plan.rhs, plan.h0, plan.w0, plan.slots
     above = jnp.where(r > 0, 1.0, 0.0).astype(F32)
     below = jnp.where(r < plan.n - 1, 1.0, 0.0).astype(F32)
-    halo = None
-    for k, band in enumerate(bands):
-        owner = jnp.bitwise_xor(c, k)
+    values, matrices = [], []
+    left = blocks.get(block_ref, "halo", 0)
+    right = blocks.get(block_ref, "halo", 1)
+    for band, owner in zip(bands, owners(plan)):
         from_left = jnp.where(owner == c - 1, 1.0, 0.0).astype(BF16)
         from_right = jnp.where(owner == c + 1, 1.0, 0.0).astype(BF16)
-        matrix = halo_ref[0] * from_left + halo_ref[1] * from_right
-        value = band[...].reshape(slots * rhs, LANES).astype(BF16)
-        part = jnp.dot(value, matrix, preferred_element_type=F32)
-        halo = part if halo is None else halo + part
+        matrices.append(left * from_left + right * from_right)
+        values.append(band[...].reshape(slots * rhs, LANES).astype(BF16))
+    halo = jnp.dot(
+        jnp.concatenate(values, axis=1), jnp.concatenate(matrices, axis=0),
+        preferred_element_type=F32,
+    )
     lane = lane_index(rhs)
     rows, sides = [], []
     for row in range(-1, h0 + 1):
@@ -394,7 +440,7 @@
         elif row == h0:
             rows.append(up_ref[0] * below)
         else:
-            rows.append(x_ref[pl.ds(row, rhs, stride=h0), :])
+            rows.append(rows_ref[row])
         part, slot = divmod(row + 1, slots)
         sides.append(halo[slot * rhs : (slot + 1) * rhs, part * LANES : (part + 1) * LANES])
     for b in range(h0 // 2):
@@ -418,18 +464,15 @@
             out_ref[2 * b + j] = solved[:, j * w0 : (j + 1) * w0]
 
 
-def final_kernel(plan, group, fine_ref, one_ref, two_ref, three_ref, down_ref, up_ref, four_ref,
-                 inverse_ref, shrink_ref, flat_ref, spread_ref, lift_ref, *refs):
+def whole_kernel(plan, group, blocks, block_ref, four_ref, inverse_ref, *refs):
     count = plan.n // 2
     gathered, out_ref, pair_ref, four_rows = refs[:count], refs[count], refs[-2], refs[-1]
     r, c = lax.axis_index("px"), lax.axis_index("py")
     rhs, n, ny3, ny4 = plan.rhs, plan.n, plan.ny[3], plan.ny[4]
     nx4, nx5 = plan.nx[4], plan.nx[5]
-    above = jnp.where(r > 0, 1.0, 0.0).astype(F32)
-    below = jnp.where(r < n - 1, 1.0, 0.0).astype(F32)
     for k, block in enumerate(gathered):
         for half in range(2):
-            at = lax.rem(r + 2 * k + half, n)
+            at = lax.rem(jnp.bitwise_xor(r, 2 * k) + half, n)
             pair_ref[at] = block[half]
     lane = lax.broadcasted_iota(jnp.int32, (rhs, 2 * ny3), 1)
     ring = pair_ref[0]
@@ -437,13 +480,16 @@
     pair_ref[n] = jnp.where(lane < ny3, ring, 0.0)
     low = pair_ref[0:n].reshape(n * rhs, 2 * ny3)
     high = pair_ref[1 : n + 1].reshape(n * rhs, 2 * ny3)
-    four = (product(low, shrink_ref[0]) + product(high, shrink_ref[1])) * SHRINK
+    both = jnp.concatenate([low, high], axis=1)
+    four = product(both, blocks.get(block_ref, "shrink4")) * SHRINK
     zero = jnp.zeros((rhs, four.shape[1]), F32)
     rows = [zero] + [four[i * rhs : (i + 1) * rhs] for i in range(nx4)] + [zero]
     five = shrink_rows(rows, nx4, 1)[1:-1]
-    flat = product(jnp.concatenate(five, axis=1), flat_ref[...]) * SHRINK
+    flat = product(jnp.concatenate(five, axis=1), blocks.get(block_ref, "shrink5")) * SHRINK
+    flat = flat[:, : inverse_ref.shape[0]]
     part_five = jnp.dot(flat.astype(BF16), inverse_ref[...], preferred_element_type=F32)
-    lifted = product(part_five, spread_ref[...]) * SHRINK
+    spread = blocks.get(block_ref, "lift5")[: part_five.shape[1], : nx4 * ny4]
+    lifted = product(part_five, spread) * SHRINK
     w, tiles = plan.tile[4], plan.tiles[4]
     parts = []
     for b in range(nx4 // 2):
@@ -452,9 +498,14 @@
             for k in range(4):
                 lanes = range(t * w, t * w + w + 2, LANES)
                 pieces.append([rows[2 * b + k][:, lo : lo + LANES] for lo in lanes])
-            parts.append(solve(assemble(pieces, w), four_ref[b, t]))
+            lhs = assemble(pieces, w)
+            parts.append(
+                lax.dot_general(
+                    lhs, four_ref[b, t], (((1,), (1,)), ((), ())), preferred_element_type=F32
+                )
+            )
     correction = jnp.concatenate(parts, axis=1) + lifted
-    width = lift_ref.shape[3]
+    width = group * 2 * w * tiles
     bands = nx4 // 2 // group
     stacked = jnp.concatenate(
         [correction[:, i * width : (i + 1) * width] for i in range(bands)], axis=0
@@ -463,10 +514,18 @@
     four_rows[nx4 + 1] = jnp.zeros((rhs, LANES), F32)
     for g in range(group):
         for j in range(2):
-            value = product(stacked, lift_ref[c, 2 * g + j])
+            value = product(stacked, blocks.get(block_ref, "lift4", (c * group + g) * 2 + j))
             for i in range(bands):
                 four_rows[1 + 2 * (i * group + g) + j] = value[i * rhs : (i + 1) * rhs]
-    rows = [four_rows[r + k] for k in range(3)]
+    for k in range(3):
+        out_ref[k] = four_rows[r + k]
+
+
+def final_kernel(plan, fine_ref, one_ref, two_ref, three_ref, four_ref, down_ref, up_ref, out_ref):
+    r, rhs = lax.axis_index("px"), plan.rhs
+    above = jnp.where(r > 0, 1.0, 0.0).astype(F32)
+    below = jnp.where(r < plan.n - 1, 1.0, 0.0).astype(F32)
+    rows = [four_ref[k] for k in range(3)]
     for level, own_ref in ((3, three_ref), (2, two_ref), (1, one_ref)):
         height = plan.h[level]
         lifted = lift_rows(rows, -1, height + 1)
@@ -491,14 +550,33 @@
     def swap(value, bits):
         return lax.ppermute(value, "py", [(i, i ^ bits) for i in range(m)])
 
-    sides = jnp.asarray(plan.pick_sides())
-    own, down, up = kernel_call(
+    width3 = 2 * plan.ny[3]
+    blocks = Blocks()
+    pairs = [plan.place(3, 0, width3, j * plan.ny[3]) for j in range(2)]
+    blocks.add("pairs", np.stack(pairs, axis=1))
+    for l in (1, 2, 3):
+        blocks.add(f"place{l}", plan.place(l, 1, round_up(plan.ny[l] + 2)))
+        if plan.tile[l] % LANES == 0:
+            blocks.add(f"lift{l}", plan.lift_columns(l))
+        else:
+            lifted = plan.lift_rows_of(l)
+            blocks.add(f"lift{l}", lifted.reshape(m, 2, -1, plan.w0))
+    lifted, group = plan.level_four_lift()
+    blocks.add("lift4", lifted)
+    blocks.add("halo", plan.halo_lanes())
+    blocks.add("shrink4", plan.coarse_shrink())
+    blocks.add("shrink5", plan.coarsest_shrink())
+    blocks.add("lift5", plan.coarsest_lift())
+    matrices = blocks.array()
+
+    own, down, up, rows = kernel_call(
         functools.partial(restrict_kernel, plan),
-        (shape(plan.slots, rhs, LANES), shape(3, rhs, LANES), shape(3, rhs, LANES)),
-    )(x, jnp.asarray(plan.shrink_columns()), sides, jnp.asarray(plan.scale()))
+        (shape(plan.slots, rhs, LANES), shape(3, rhs, LANES), shape(3, rhs, LANES),
+         shape(h0, rhs, plan.w0)),
+    )(x)
     from_above, from_below = shift(down, 1), shift(up, -1)
     band = kernel_call(functools.partial(merge_kernel, plan), shape(plan.slots, rhs, LANES))(
-        own, from_above, from_below, sides
+        own, from_above, from_below
     )
     bands = {0: band}
     bit = m // 2
@@ -507,47 +585,40 @@
         bit //= 2
     bands = [bands[k] for k in range(m)]
 
-    width3 = 2 * plan.ny[3]
-    place = np.stack([plan.place(3, 0, width3, j * plan.ny[3]) for j in range(2)], axis=1)
-    pairs = kernel_call(functools.partial(gather_kernel, plan), shape(2, rhs, width3))(
-        jnp.asarray(bf(place)), *bands
-    )
-    gathered = [pairs] + [shift(pairs, -2 * k) for k in range(1, n // 2)]
-
-    places = [jnp.asarray(bf(plan.place(l, 1, round_up(plan.ny[l] + 2)))) for l in (1, 2, 3)]
-    lifts = []
-    for l in (1, 2, 3):
-        if plan.tile[l] % LANES == 0:
-            lifts.append(jnp.asarray(bf(plan.lift_columns(l))))
-        else:
-            rows = plan.lift_rows_of(l)
-            lifts.append(jnp.asarray(bf(rows.reshape((m, -1) + rows.shape[3:]))))
-
-    def coarse(*refs):
-        coarse_kernel(plan, refs[0:3], refs[3:6], refs[6:9], *refs[9:])
+    pairs = kernel_call(
+        functools.partial(gather_kernel, plan, blocks), shape(2, rhs, width3), cost_us=0.3
+    )(matrices, *bands)
+    gathered = {0: pairs}
+    bit = 1
+    while 2 * bit < n:
+        for k, value in list(gathered.items()):
+            gathered[k ^ bit] = lax.ppermute(value, "px", [(i, i ^ (2 * bit)) for i in range(n)])
+        bit *= 2
+    gathered = [gathered[k] for k in range(n // 2)]
+    bands, pairs = lax.optimization_barrier((bands, pairs))
 
     one, two, three, down, up = kernel_call(
-        coarse,
+        functools.partial(coarse_kernel, plan, blocks),
         tuple(shape(h[l], rhs, LANES) for l in (1, 2, 3))
         + (shape(3, rhs, LANES), shape(3, rhs, LANES)),
-    )(*places, *lifts, factor_one, factor_two, factor_three, *bands)
+        cost_us=2.5,
+    )(matrices, factor_one, factor_two, factor_three, *bands)
     down, up = shift(down, 1), shift(up, -1)
 
-    fine = kernel_call(functools.partial(fine_kernel, plan), shape(h0, rhs, plan.w0))(
-        x, from_above, from_below, jnp.asarray(plan.halo_lanes()), factor_fine, *bands
-    )
-    lift_four, group = plan.level_four_lift()
-    lift_four = lift_four.reshape((m, -1) + lift_four.shape[3:])
-    out = kernel_call(
-        functools.partial(final_kernel, plan, group),
-        shape(rhs * h0, plan.w0),
+    fine = kernel_call(
+        functools.partial(fine_kernel, plan, blocks), shape(h0, rhs, plan.w0)
+    )(matrices, rows, from_above, from_below, factor_fine, *bands)
+    four = kernel_call(
+        functools.partial(whole_kernel, plan, group, blocks),
+        shape(3, rhs, LANES),
         scratch=(
             pltpu.VMEM((n + 1, rhs, width3), F32),
             pltpu.VMEM((plan.nx[4] + 2, rhs, LANES), F32),
         ),
-    )(fine, one, two, three, down, up, factor_four, coarse_inverse,
-      jnp.asarray(plan.coarse_shrink()), jnp.asarray(plan.coarsest_shrink()),
-      jnp.asarray(plan.coarsest_lift()), jnp.asarray(lift_four), *gathered)
+    )(matrices, jnp.swapaxes(factor_four, 2, 3), coarse_inverse, *gathered)
+    out = kernel_call(functools.partial(final_kernel, plan), shape(rhs * h0, plan.w0))(
+        fine, one, two, three, four, down, up
+    )
     return out.reshape(rhs, h0, plan.w0)
 
 

time: 47.8 us -> 33.7 us (0.71); the launches traced: 47.2 us -> 33.6 us
  local copies, waits for them, and re-layouts: 13.7 us -> 0.99 us
  Pallas kernels: 8.78 us -> 5.65 us
  waiting for transfers between devices: 9.77 us -> 11.1 us
  starting transfers between devices: 14.7 us -> 15.7 us
    unnamed x57 -> x16, local copies, waits for them, and re-layouts: 13.7 us -> 0.99 us
    ppermute x0 -> x3, waiting for transfers between devices: none -> 3.99 us  [per_device(): lax.ppermute(value, 'px', [(i, i ^ 2 * bit) for i in range(n)])]
    ppermute x0 -> x3, starting transfers between devices: none -> 3.17 us  [per_device(): lax.ppermute(value, 'px', [(i, i ^ 2 * bit) for i in range(n)])]
    pallas_call x6 -> x7, Pallas kernels: 8.78 us -> 5.65 us  [call(): pl.pallas_call(body, out_shape=out_shape, in_specs=[whole] * len(operands...]
    ppermute x7 -> x4, waiting for transfers between devices: 4.68 us -> 2.05 us  [shift(): return lax.ppermute(value, 'px', [(i, (i + by) % n) for i in range(n)])]
    ppermute x7 -> x4, starting transfers between devices: 13.1 us -> 10.9 us  [shift(): return lax.ppermute(value, 'px', [(i, (i + by) % n) for i in range(n)])]
  transfers between devices with their start and end apart: 10 -> 10, of which waited for: 6 -> 4; matrix products, arithmetic and copies ran while one was open for 2% -> 0% of each run, Pallas kernels for 4% -> 12%
where the time goes in v2:
time: 33.7 us; the launch traced here: 33.6 us
  starting transfers between devices  15.7 us (47%)
  waiting for transfers between devices  11.1 us (33%)
  Pallas kernels  5.65 us (17%)
  local copies, waits for them, and re-layouts  0.99 us (3%)
    ppermute x4, starting transfers between devices, shift(): return lax.ppermute(value, 'px', [(i, (i + by) % n) for i in range(n)])  10.9 us
    pallas_call x7, Pallas kernels, call(): pl.pallas_call(body, out_shape=out_shape, in_specs=[whole] * len(operands...  5.65 us
    ppermute x3, waiting for transfers between devices, swap(): return lax.ppermute(value, 'py', [(i, i ^ bits) for i in range(m)])  5.09 us
    ppermute x3, waiting for transfers between devices, per_device(): lax.ppermute(value, 'px', [(i, i ^ 2 * bit) for i in range(n)])  3.99 us
    ppermute x3, starting transfers between devices, per_device(): lax.ppermute(value, 'px', [(i, i ^ 2 * bit) for i in range(n)])  3.17 us
    ppermute x4, waiting for transfers between devices, shift(): return lax.ppermute(value, 'px', [(i, (i + by) % n) for i in range(n)])  2.05 us
    ppermute x3, starting transfers between devices, swap(): return lax.ppermute(value, 'py', [(i, i ^ bits) for i in range(m)])  1.69 us
    unnamed x16, local copies, waits for them, and re-layouts  0.99 us
  transfers between devices with their start and end apart: 10, of which 4 were waited for; matrix products, arithmetic and copies ran while one was open for 0% of the time, Pallas kernels for 12%

profile of v2, /device:TPU:0, one launch (start us, length us, event | category | flops | bytes accessed | tf_op | source)
XLA Modules:
  0.0 33.6 jit_solution(7333281070147117029)
XLA Ops:
  0.0 0.0 copy-start.4
  0.0 0.9 %copy-done.4 = f32[32,16,128]{2,1,0:T(8,128)S(1)} copy-done((f32[32,16,128]{2,1,0:T(8,128)S(1)}, f32[32,16,128]{2,1,0:T(8,128)}, u32[]{:S(2)}) %copy-start.4) | copy-done | bytes 262168
  1.0 0.5 %shard_map.82 = (f32[10,32,128]{2,1,0:T(8,128)S(1)}, f32[3,32,128]{2,1,0:T(8,128)S(1)}, f32[3,32,128]{2,1,0:T(8,128)S(1)}, f32[16,32,128]{2,1,0:T(8,128)S(1)}) custom-call(f32[512,128]{1,0:T(8,128)S(1)} %bitcast.3), custom_call_target="tpu_custom_call" | custom-call | flops 1000000000 | bytes 3000000 | tf_op jit(solution)/shard_map/pallas_call | solution.py:223
  1.5 0.0 copy-start
  1.5 3.0 %collective-permute-start = (f32[3,32,128]{2,1,0:T(8,128)S(1)}, f32[3,32,128]{2,1,0:T(8,128)S(1)}, u32[]{:S(2)}, u32[]{:S(2)}) collective-permute-start(f32[3,32,128]{2,1,0:T(8,128)S(1)} %get-tuple-element.19), channel_id=1, source_target_pairs={{0,4},{4,8},{8,12},{12,16},{16,20},{20,24},{24,28},{28,0},{1,5},{5... | collective-permute-start | bytes 147464 | tf_op jit(solution)/shard_map/ppermute | solution.py:548
  4.5 3.1 %collective-permute-start.1 = (f32[3,32,128]{2,1,0:T(8,128)S(1)}, f32[3,32,128]{2,1,0:T(8,128)S(1)}, u32[]{:S(2)}, u32[]{:S(2)}) collective-permute-start(f32[3,32,128]{2,1,0:T(8,128)S(1)} %get-tuple-element.20), channel_id=1, source_target_pairs={{0,28},{4,0},{8,4},{12,8},{16,12},{20,16},{24,20},{28,24},{1,29},{... | collective-permute-start | bytes 147464 | tf_op jit(solution)/shard_map/ppermute | solution.py:548
  7.6 2.0 %collective-permute-done.down_ref = f32[3,32,128]{2,1,0:T(8,128)S(1)} collective-permute-done((f32[3,32,128]{2,1,0:T(8,128)S(1)}, f32[3,32,128]{2,1,0:T(8,128)S(1)}, u32[]{:S(2)}, u32[]{:S(2)}) %collective-permute-start) | collective-permute-done | bytes 49184 | tf_op jit(solution)/shard_map/ppermute | solution.py:548
  9.6 0.0 collective-permute-done.1.up_ref
  9.6 0.1 shard_map.83.refs_0_.refs_3_
  9.8 0.0 copy-start.2
  9.8 0.0 copy-start.3
  9.8 0.0 copy-start.6
  9.8 1.7 %collective-permute-start.3 = (f32[10,32,128]{2,1,0:T(8,128)S(1)}, f32[10,32,128]{2,1,0:T(8,128)S(1)}, u32[]{:S(2)}, u32[]{:S(2)}) collective-permute-start(f32[10,32,128]{2,1,0:T(8,128)S(1)} %shard_map.83.refs_0_.refs_3_), channel_id=1, source_target_pairs={{0,2},{1,3},{2,0},{3,1},{4,6},{5,7},{6,4},{7,5},{8,10},{9,11},{10,... | collective-permute-start | bytes 491528 | tf_op jit(solution)/shard_map/ppermute | solution.py:551
  11.5 0.0 collective-permute-start.2
  11.5 3.7 %collective-permute-done.3.refs_2_.refs_5_ = f32[10,32,128]{2,1,0:T(8,128)S(1)} collective-permute-done((f32[10,32,128]{2,1,0:T(8,128)S(1)}, f32[10,32,128]{2,1,0:T(8,128)S(1)}, u32[]{:S(2)}, u32[]{:S(2)}) %collective-permute-start.3) | collective-permute-done | bytes 163872 | tf_op jit(solution)/shard_map/ppermute | solution.py:551
  15.2 0.0 collective-permute-start.4
  15.2 0.0 collective-permute-done.2.refs_1_.refs_4_
  15.2 1.4 %collective-permute-done.4.refs_3_.refs_6_ = f32[10,32,128]{2,1,0:T(8,128)S(1)} collective-permute-done((f32[10,32,128]{2,1,0:T(8,128)S(1)}, f32[10,32,128]{2,1,0:T(8,128)S(1)}, u32[]{:S(2)}, u32[]{:S(2)}) %collective-permute-start.4) | collective-permute-done | bytes 163872 | tf_op jit(solution)/shard_map/ppermute | solution.py:551
  16.6 0.0 copy-done
  16.6 0.2 shard_map.84.refs_0_
  16.8 0.0 copy-start.1
  16.8 1.6 %collective-permute-start.6 = (f32[2,32,128]{2,1,0:T(8,128)S(1)}, f32[2,32,128]{2,1,0:T(8,128)S(1)}, u32[]{:S(2)}, u32[]{:S(2)}) collective-permute-start(f32[2,32,128]{2,1,0:T(8,128)S(1)} %shard_map.84.refs_0_), channel_id=1, source_target_pairs={{0,16},{4,20},{8,24},{12,28},{16,0},{20,4},{24,8},{28,12},{1,17},{... | collective-permute-start | bytes 98312 | tf_op jit(solution)/shard_map/ppermute | solution.py:595
  18.4 1.6 %collective-permute-start.5 = (f32[2,32,128]{2,1,0:T(8,128)S(1)}, f32[2,32,128]{2,1,0:T(8,128)S(1)}, u32[]{:S(2)}, u32[]{:S(2)}) collective-permute-start(f32[2,32,128]{2,1,0:T(8,128)S(1)} %shard_map.84.refs_0_), channel_id=1, source_target_pairs={{0,8},{4,12},{8,0},{12,4},{16,24},{20,28},{24,16},{28,20},{1,9},{5... | collective-permute-start | bytes 98312 | tf_op jit(solution)/shard_map/ppermute | solution.py:595
  20.0 0.0 copy-done.2
  20.0 0.0 copy-done.3
  20.0 0.0 copy-done.6
  20.0 2.2 %shard_map.86 = (f32[8,32,128]{2,1,0:T(8,128)S(1)}, f32[4,32,128]{2,1,0:T(8,128)S(1)}, f32[2,32,128]{2,1,0:T(8,128)S(1)}, f32[3,32,128]{2,1,0:T(8,128)S(1)}, f32[3,32,128]{2,1,0:T(8,128)S(1)}) custom-call(bf16[80,128,128]{2,1,0:T(8,128)(2,1)S(1)} %copy-done, bf16[4,2,520,256]{3,2,1,0:T(8,128)(2,1)S(1)} %copy-done.2, bf16[2,1,520,256]{3,2,1,0:T(8,128)(2,1)S(1)} %copy-done.3, ...), custom_call_target="tpu_custom_call" | custom-call | flops 2500000000 | bytes 7500000 | tf_op jit(solution)/shard_map/pallas_call | solution.py:223
  22.2 2.8 %collective-permute-start.8 = (f32[3,32,128]{2,1,0:T(8,128)S(1)}, f32[3,32,128]{2,1,0:T(8,128)S(1)}, u32[]{:S(2)}, u32[]{:S(2)}) collective-permute-start(f32[3,32,128]{2,1,0:T(8,128)S(1)} %get-tuple-element.29), channel_id=1, source_target_pairs={{0,4},{4,8},{8,12},{12,16},{16,20},{20,24},{24,28},{28,0},{1,5},{5... | collective-permute-start | bytes 147464 | tf_op jit(solution)/shard_map/ppermute | solution.py:548
  25.0 1.9 %collective-permute-start.9 = (f32[3,32,128]{2,1,0:T(8,128)S(1)}, f32[3,32,128]{2,1,0:T(8,128)S(1)}, u32[]{:S(2)}, u32[]{:S(2)}) collective-permute-start(f32[3,32,128]{2,1,0:T(8,128)S(1)} %get-tuple-element.30), channel_id=1, source_target_pairs={{0,28},{4,0},{8,4},{12,8},{16,12},{20,16},{24,20},{28,24},{1,29},{... | collective-permute-start | bytes 147464 | tf_op jit(solution)/shard_map/ppermute | solution.py:548
  26.9 0.0 collective-permute-done.5.refs_1_
  26.9 0.0 collective-permute-start.7
  26.9 0.0 copy-done.1
  26.9 0.0 copy-start.5
  26.9 0.0 copy-start.7
  27.0 0.8 %shard_map.85.fine_ref = f32[16,32,128]{2,1,0:T(8,128)S(1)} custom-call(bf16[80,128,128]{2,1,0:T(8,128)(2,1)S(1)} %copy-done, f32[16,32,128]{2,1,0:T(8,128)S(1)} %get-tuple-element.18.rows_ref, f32[3,32,128]{2,1,0:T(8,128)S(1)} %collective-permute-done.down_ref, f32[3,32,128]{2,1,0:T(8,128)S(1)} %collective-permute-done.1.up_ref, ...), custom_call_target="tpu_custom_call" | custom-call | flops 1000000000 | bytes 3000000 | tf_op jit(solution)/shard_map/pallas_call | solution.py:223
  27.7 0.0 collective-permute-done.6.refs_2_
  27.8 4.0 %collective-permute-done.7.refs_3_ = f32[2,32,128]{2,1,0:T(8,128)S(1)} collective-permute-done((f32[2,32,128]{2,1,0:T(8,128)S(1)}, f32[2,32,128]{2,1,0:T(8,128)S(1)}, u32[]{:S(2)}, u32[]{:S(2)}) %collective-permute-start.7) | collective-permute-done | bytes 32800 | tf_op jit(solution)/shard_map/ppermute | solution.py:595
  31.7 0.0 copy-done.5
  31.7 0.0 copy-done.7
  31.7 1.0 %shard_map.87.four_ref = f32[3,32,128]{2,1,0:T(8,128)S(1)} custom-call(bf16[80,128,128]{2,1,0:T(8,128)(2,1)S(1)} %copy-done, bf16[4,1,64,136]{3,2,1,0:T(8,128)(2,1)S(1)} %bitcast.4, bf16[64,64]{1,0:T(8,128)(2,1)S(1)} %copy-done.7, f32[2,32,128]{2,1,0:T(8,128)S(1)} %shard_map.84.refs_0_, f32[2,32,128]{2,1,0:T(8,128)S(1)} %collective-permute-done.5.refs_1_, ...), custom_call_target="tpu_custom_call" | custom-call | flops 1000000000 | bytes 3000000 | tf_op jit(solution)/shard_map/pallas_call | solution.py:223
  32.7 0.0 collective-permute-done.8.down_ref
  32.7 0.0 collective-permute-done.9.up_ref
  32.7 0.9 %shard_map.88 = f32[512,128]{1,0:T(8,128)} custom-call(f32[16,32,128]{2,1,0:T(8,128)S(1)} %shard_map.85.fine_ref, f32[8,32,128]{2,1,0:T(8,128)S(1)} %get-tuple-element.26.one_ref, f32[4,32,128]{2,1,0:T(8,128)S(1)} %get-tuple-element.27.two_ref, f32[2,32,128]{2,1,0:T(8,128)S(1)} %get-tuple-element.28.three_ref, f32[3,32,128]{2,1,0:T(8,128)S(1)} %shard_map.87.four_ref, ...), custom_call_target="tpu_custom_call" | custom-call | flops 1000000000 | bytes 3000000 | tf_op jit(solution)/shard_map/pallas_call | solution.py:223
Async XLA Ops:
  0.0 0.9 %copy-start.4 = (f32[32,16,128]{2,1,0:T(8,128)S(1)}, f32[32,16,128]{2,1,0:T(8,128)}, u32[]{:S(2)}) copy-start(f32[32,16,128]{2,1,0:T(8,128)} %param.8) | copy-start | bytes 786436
  1.5 15.1 %copy-start = (bf16[80,128,128]{2,1,0:T(8,128)(2,1)S(1)}, bf16[80,128,128]{2,1,0:T(8,128)(2,1)}, u32[]{:S(2)}) copy-start(bf16[80,128,128]{2,1,0:T(8,128)(2,1)} %constant.2.clone.block_ref) | copy-start | bytes 7864324
  1.5 8.2 %collective-permute-start = (f32[3,32,128]{2,1,0:T(8,128)S(1)}, f32[3,32,128]{2,1,0:T(8,128)S(1)}, u32[]{:S(2)}, u32[]{:S(2)}) collective-permute-start(f32[3,32,128]{2,1,0:T(8,128)S(1)} %get-tuple-element.19), channel_id=1, source_target_pairs={{0,4},{4,8},{8,12},{12,16},{16,20},{20,24},{24,28},{28,0},{1,5},{5... | collective-permute-start | bytes 147464 | tf_op jit(solution)/shard_map/ppermute | solution.py:548
  4.5 5.1 %collective-permute-start.1 = (f32[3,32,128]{2,1,0:T(8,128)S(1)}, f32[3,32,128]{2,1,0:T(8,128)S(1)}, u32[]{:S(2)}, u32[]{:S(2)}) collective-permute-start(f32[3,32,128]{2,1,0:T(8,128)S(1)} %get-tuple-element.20), channel_id=1, source_target_pairs={{0,28},{4,0},{8,4},{12,8},{16,12},{20,16},{24,20},{28,24},{1,29},{... | collective-permute-start | bytes 147464 | tf_op jit(solution)/shard_map/ppermute | solution.py:548
  9.8 10.2 %copy-start.2 = (bf16[4,2,520,256]{3,2,1,0:T(8,128)(2,1)S(1)}, bf16[4,2,520,256]{3,2,1,0:T(8,128)(2,1)}, u32[]{:S(2)}) copy-start(bf16[4,2,520,256]{3,2,1,0:T(8,128)(2,1)} %refs_0_.1) | copy-start | bytes 6389764
  9.8 10.2 %copy-start.3 = (bf16[2,1,520,256]{3,2,1,0:T(8,128)(2,1)S(1)}, bf16[2,1,520,256]{3,2,1,0:T(8,128)(2,1)}, u32[]{:S(2)}) copy-start(bf16[2,1,520,256]{3,2,1,0:T(8,128)(2,1)} %refs_1_.1) | copy-start | bytes 1597444
  9.8 10.2 %copy-start.6 = (bf16[1,1,264,128]{3,2,1,0:T(8,128)(2,1)S(1)}, bf16[1,1,264,128]{3,2,1,0:T(8,128)(2,1)}, u32[]{:S(2)}) copy-start(bf16[1,1,264,128]{3,2,1,0:T(8,128)(2,1)} %refs_2_.1) | copy-start | bytes 202756
  9.8 5.4 %collective-permute-start.3 = (f32[10,32,128]{2,1,0:T(8,128)S(1)}, f32[10,32,128]{2,1,0:T(8,128)S(1)}, u32[]{:S(2)}, u32[]{:S(2)}) collective-permute-start(f32[10,32,128]{2,1,0:T(8,128)S(1)} %shard_map.83.refs_0_.refs_3_), channel_id=1, source_target_pairs={{0,2},{1,3},{2,0},{3,1},{4,6},{5,7},{6,4},{7,5},{8,10},{9,11},{10,... | collective-permute-start | bytes 491528 | tf_op jit(solution)/shard_map/ppermute | solution.py:551
  11.5 3.7 %collective-permute-start.2 = (f32[10,32,128]{2,1,0:T(8,128)S(1)}, f32[10,32,128]{2,1,0:T(8,128)S(1)}, u32[]{:S(2)}, u32[]{:S(2)}) collective-permute-start(f32[10,32,128]{2,1,0:T(8,128)S(1)} %shard_map.83.refs_0_.refs_3_), channel_id=1, source_target_pairs={{0,1},{1,0},{2,3},{3,2},{4,5},{5,4},{6,7},{7,6},{8,9},{9,8},{10,11... | collective-permute-start | bytes 491528 | tf_op jit(solution)/shard_map/ppermute | solution.py:551
  15.2 1.4 %collective-permute-start.4 = (f32[10,32,128]{2,1,0:T(8,128)S(1)}, f32[10,32,128]{2,1,0:T(8,128)S(1)}, u32[]{:S(2)}, u32[]{:S(2)}) collective-permute-start(f32[10,32,128]{2,1,0:T(8,128)S(1)} %collective-permute-done.3.refs_2_.refs_5_), channel_id=1, source_target_pairs={{0,1},{1,0},{2,3},{3,2},{4,5},{5,4},{6,7},{7,6},{8,9},{9,8},{10,11... | collective-permute-start | bytes 491528 | tf_op jit(solution)/shard_map/ppermute | solution.py:551
  16.8 10.1 %copy-start.1 = (bf16[8,1,520,256]{3,2,1,0:T(8,128)(2,1)S(1)}, bf16[8,1,520,256]{3,2,1,0:T(8,128)(2,1)}, u32[]{:S(2)}) copy-start(bf16[8,1,520,256]{3,2,1,0:T(8,128)(2,1)} %factor_ref.1) | copy-start | bytes 6389764
  16.8 10.9 %collective-permute-start.6 = (f32[2,32,128]{2,1,0:T(8,128)S(1)}, f32[2,32,128]{2,1,0:T(8,128)S(1)}, u32[]{:S(2)}, u32[]{:S(2)}) collective-permute-start(f32[2,32,128]{2,1,0:T(8,128)S(1)} %shard_map.84.refs_0_), channel_id=1, source_target_pairs={{0,16},{4,20},{8,24},{12,28},{16,0},{20,4},{24,8},{28,12},{1,17},{... | collective-permute-start | bytes 98312 | tf_op jit(solution)/shard_map/ppermute | solution.py:595
  18.4 8.5 %collective-permute-start.5 = (f32[2,32,128]{2,1,0:T(8,128)S(1)}, f32[2,32,128]{2,1,0:T(8,128)S(1)}, u32[]{:S(2)}, u32[]{:S(2)}) collective-permute-start(f32[2,32,128]{2,1,0:T(8,128)S(1)} %shard_map.84.refs_0_), channel_id=1, source_target_pairs={{0,8},{4,12},{8,0},{12,4},{16,24},{20,28},{24,16},{28,20},{1,9},{5... | collective-permute-start | bytes 98312 | tf_op jit(solution)/shard_map/ppermute | solution.py:595
  22.2 10.5 %collective-permute-start.8 = (f32[3,32,128]{2,1,0:T(8,128)S(1)}, f32[3,32,128]{2,1,0:T(8,128)S(1)}, u32[]{:S(2)}, u32[]{:S(2)}) collective-permute-start(f32[3,32,128]{2,1,0:T(8,128)S(1)} %get-tuple-element.29), channel_id=1, source_target_pairs={{0,4},{4,8},{8,12},{12,16},{16,20},{20,24},{24,28},{28,0},{1,5},{5... | collective-permute-start | bytes 147464 | tf_op jit(solution)/shard_map/ppermute | solution.py:548
  25.0 7.8 %collective-permute-start.9 = (f32[3,32,128]{2,1,0:T(8,128)S(1)}, f32[3,32,128]{2,1,0:T(8,128)S(1)}, u32[]{:S(2)}, u32[]{:S(2)}) collective-permute-start(f32[3,32,128]{2,1,0:T(8,128)S(1)} %get-tuple-element.30), channel_id=1, source_target_pairs={{0,28},{4,0},{8,4},{12,8},{16,12},{20,16},{24,20},{28,24},{1,29},{... | collective-permute-start | bytes 147464 | tf_op jit(solution)/shard_map/ppermute | solution.py:548
  26.9 4.8 %collective-permute-start.7 = (f32[2,32,128]{2,1,0:T(8,128)S(1)}, f32[2,32,128]{2,1,0:T(8,128)S(1)}, u32[]{:S(2)}, u32[]{:S(2)}) collective-permute-start(f32[2,32,128]{2,1,0:T(8,128)S(1)} %collective-permute-done.5.refs_1_), channel_id=1, source_target_pairs={{0,16},{4,20},{8,24},{12,28},{16,0},{20,4},{24,8},{28,12},{1,17},{... | collective-permute-start | bytes 98312 | tf_op jit(solution)/shard_map/ppermute | solution.py:595
  26.9 4.8 %copy-start.5 = (bf16[4,1,136,64]{2,3,1,0:T(8,128)(2,1)S(1)}, bf16[4,1,136,64]{2,3,1,0:T(8,128)(2,1)}, u32[]{:S(2)}) copy-start(bf16[4,1,136,64]{2,3,1,0:T(8,128)(2,1)} %param.13) | copy-start | bytes 208900
  26.9 4.8 %copy-start.7 = (bf16[64,64]{1,0:T(8,128)(2,1)S(1)}, bf16[64,64]{1,0:T(8,128)(2,1)}, u32[]{:S(2)}) copy-start(bf16[64,64]{1,0:T(8,128)(2,1)} %inverse_ref.1) | copy-start | bytes 24580

commit v3 on v2

--- a/solution.py
+++ b/solution.py
@@ -470,9 +470,16 @@
     r, c = lax.axis_index("px"), lax.axis_index("py")
     rhs, n, ny3, ny4 = plan.rhs, plan.n, plan.ny[3], plan.ny[4]
     nx4, nx5 = plan.nx[4], plan.nx[5]
+    odd = jnp.bitwise_and(c, 1)
     for k, block in enumerate(gathered):
+        if k == 0 or (k == count - 1 and k % 2):
+            partner = 2 * k
+        elif k % 2:
+            partner = 2 * (k + odd)
+        else:
+            partner = 2 * (k - odd)
         for half in range(2):
-            at = lax.rem(jnp.bitwise_xor(r, 2 * k) + half, n)
+            at = lax.rem(jnp.bitwise_xor(r, partner) + half, n)
             pair_ref[at] = block[half]
     lane = lax.broadcasted_iota(jnp.int32, (rhs, 2 * ny3), 1)
     ring = pair_ref[0]
@@ -588,14 +595,22 @@
     pairs = kernel_call(
         functools.partial(gather_kernel, plan, blocks), shape(2, rhs, width3), cost_us=0.3
     )(matrices, *bands)
-    gathered = {0: pairs}
-    bit = 1
-    while 2 * bit < n:
-        for k, value in list(gathered.items()):
-            gathered[k ^ bit] = lax.ppermute(value, "px", [(i, i ^ (2 * bit)) for i in range(n)])
-        bit *= 2
-    gathered = [gathered[k] for k in range(n // 2)]
+    order, gathered = list(range(1, n // 2)), [pairs]
+    fetched = []
+    for k in range(0, len(order), 2):
+        even, odd = order[k], order[min(k + 1, len(order) - 1)]
+        fetched.append(
+            lax.ppermute(
+                pairs, ("px", "py"),
+                [(i * m + c, (i ^ (2 * (odd if c % 2 else even))) * m + c)
+                 for i in range(n) for c in range(m)],
+            )
+        )
     bands, pairs = lax.optimization_barrier((bands, pairs))
+    for k, value in enumerate(fetched):
+        gathered.append(value)
+        if 2 * k + 1 < len(order):
+            gathered.append(swap(value, 1))
 
     one, two, three, down, up = kernel_call(
         functools.partial(coarse_kernel, plan, blocks),

time: 33.7 us -> 30 us (0.89)
  waiting for transfers between devices: 11.1 us -> 7.91 us
  starting transfers between devices: 15.7 us -> 15.2 us
    ppermute x3 -> x2, waiting for transfers between devices: 3.99 us -> 0.01 us  [per_device(): lax.ppermute(pairs, ('px', 'py'), [(i * m + c, (i ^ 2 * (odd if c % 2 els...]
    ppermute x3 -> x2, starting transfers between devices: 3.17 us -> 2.61 us  [per_device(): lax.ppermute(pairs, ('px', 'py'), [(i * m + c, (i ^ 2 * (odd if c % 2 els...]
    ppermute x4, waiting for transfers between devices: 2.05 us -> 2.44 us  [shift(): return lax.ppermute(value, 'px', [(i, (i + by) % n) for i in range(n)])]
    ppermute x3 -> x4, waiting for transfers between devices: 5.09 us -> 5.47 us  [swap(): return lax.ppermute(value, 'py', [(i, i ^ bits) for i in range(m)])]
    ppermute x3 -> x4, starting transfers between devices: 1.69 us -> 1.69 us  [swap(): return lax.ppermute(value, 'py', [(i, i ^ bits) for i in range(m)])]
  transfers between devices with their start and end apart: 10 -> 10, of which waited for: 4 -> 5; matrix products, arithmetic and copies ran while one was open for 0% -> 0% of each run, Pallas kernels for 12% -> 13%
where the time goes in v3:
time: 30 us; the launch traced here: 29.8 us
  starting transfers between devices  15.2 us (51%)
  waiting for transfers between devices  7.91 us (26%)
  Pallas kernels  5.66 us (19%)
  local copies, waits for them, and re-layouts  0.99 us (3%)
    ppermute x4, starting transfers between devices, shift(): return lax.ppermute(value, 'px', [(i, (i + by) % n) for i in range(n)])  10.9 us
    pallas_call x7, Pallas kernels, call(): pl.pallas_call(body, out_shape=out_shape, in_specs=[whole] * len(operands...  5.66 us
    ppermute x4, waiting for transfers between devices, swap(): return lax.ppermute(value, 'py', [(i, i ^ bits) for i in range(m)])  5.47 us
    ppermute x2, starting transfers between devices, per_device(): lax.ppermute(pairs, ('px', 'py'), [(i * m + c, (i ^ 2 * (odd if c % 2 els...  2.61 us
    ppermute x4, waiting for transfers between devices, shift(): return lax.ppermute(value, 'px', [(i, (i + by) % n) for i in range(n)])  2.44 us
    ppermute x4, starting transfers between devices, swap(): return lax.ppermute(value, 'py', [(i, i ^ bits) for i in range(m)])  1.69 us
    unnamed x16, local copies, waits for them, and re-layouts  0.99 us
  transfers between devices with their start and end apart: 10, of which 5 were waited for; matrix products, arithmetic and copies ran while one was open for 0% of the time, Pallas kernels for 13%

profile of v3, /device:TPU:0, one launch (start us, length us, event | category | flops | bytes accessed | tf_op | source)
XLA Modules:
  0.0 29.8 jit_solution(16332757804408643054)
XLA Ops:
  0.0 0.0 copy-start.4
  0.0 0.9 %copy-done.4 = f32[32,16,128]{2,1,0:T(8,128)S(1)} copy-done((f32[32,16,128]{2,1,0:T(8,128)S(1)}, f32[32,16,128]{2,1,0:T(8,128)}, u32[]{:S(2)}) %copy-start.4) | copy-done | bytes 262168
  1.0 0.5 %shard_map.82 = (f32[10,32,128]{2,1,0:T(8,128)S(1)}, f32[3,32,128]{2,1,0:T(8,128)S(1)}, f32[3,32,128]{2,1,0:T(8,128)S(1)}, f32[16,32,128]{2,1,0:T(8,128)S(1)}) custom-call(f32[512,128]{1,0:T(8,128)S(1)} %bitcast.3), custom_call_target="tpu_custom_call" | custom-call | flops 1000000000 | bytes 3000000 | tf_op jit(solution)/shard_map/pallas_call | solution.py:223
  1.5 0.0 copy-start
  1.5 3.0 %collective-permute-start = (f32[3,32,128]{2,1,0:T(8,128)S(1)}, f32[3,32,128]{2,1,0:T(8,128)S(1)}, u32[]{:S(2)}, u32[]{:S(2)}) collective-permute-start(f32[3,32,128]{2,1,0:T(8,128)S(1)} %get-tuple-element.19), channel_id=1, source_target_pairs={{0,4},{4,8},{8,12},{12,16},{16,20},{20,24},{24,28},{28,0},{1,5},{5... | collective-permute-start | bytes 147464 | tf_op jit(solution)/shard_map/ppermute | solution.py:555
  4.5 3.1 %collective-permute-start.1 = (f32[3,32,128]{2,1,0:T(8,128)S(1)}, f32[3,32,128]{2,1,0:T(8,128)S(1)}, u32[]{:S(2)}, u32[]{:S(2)}) collective-permute-start(f32[3,32,128]{2,1,0:T(8,128)S(1)} %get-tuple-element.20), channel_id=1, source_target_pairs={{0,28},{4,0},{8,4},{12,8},{16,12},{20,16},{24,20},{28,24},{1,29},{... | collective-permute-start | bytes 147464 | tf_op jit(solution)/shard_map/ppermute | solution.py:555
  7.6 2.0 %collective-permute-done.down_ref = f32[3,32,128]{2,1,0:T(8,128)S(1)} collective-permute-done((f32[3,32,128]{2,1,0:T(8,128)S(1)}, f32[3,32,128]{2,1,0:T(8,128)S(1)}, u32[]{:S(2)}, u32[]{:S(2)}) %collective-permute-start) | collective-permute-done | bytes 49184 | tf_op jit(solution)/shard_map/ppermute | solution.py:555
  9.6 0.0 collective-permute-done.1.up_ref
  9.6 0.1 shard_map.83.refs_0_.refs_3_
  9.8 0.0 copy-start.2
  9.8 0.0 copy-start.3
  9.8 0.0 copy-start.6
  9.8 1.7 %collective-permute-start.3 = (f32[10,32,128]{2,1,0:T(8,128)S(1)}, f32[10,32,128]{2,1,0:T(8,128)S(1)}, u32[]{:S(2)}, u32[]{:S(2)}) collective-permute-start(f32[10,32,128]{2,1,0:T(8,128)S(1)} %shard_map.83.refs_0_.refs_3_), channel_id=1, source_target_pairs={{0,2},{1,3},{2,0},{3,1},{4,6},{5,7},{6,4},{7,5},{8,10},{9,11},{10,... | collective-permute-start | bytes 491528 | tf_op jit(solution)/shard_map/ppermute | solution.py:558
  11.5 0.0 collective-permute-start.2
  11.5 3.7 %collective-permute-done.3.refs_2_.refs_5_ = f32[10,32,128]{2,1,0:T(8,128)S(1)} collective-permute-done((f32[10,32,128]{2,1,0:T(8,128)S(1)}, f32[10,32,128]{2,1,0:T(8,128)S(1)}, u32[]{:S(2)}, u32[]{:S(2)}) %collective-permute-start.3) | collective-permute-done | bytes 163872 | tf_op jit(solution)/shard_map/ppermute | solution.py:558
  15.2 0.0 collective-permute-start.4
  15.2 0.0 collective-permute-done.2.refs_1_.refs_4_
  15.2 1.4 %collective-permute-done.4.refs_3_.refs_6_ = f32[10,32,128]{2,1,0:T(8,128)S(1)} collective-permute-done((f32[10,32,128]{2,1,0:T(8,128)S(1)}, f32[10,32,128]{2,1,0:T(8,128)S(1)}, u32[]{:S(2)}, u32[]{:S(2)}) %collective-permute-start.4) | collective-permute-done | bytes 163872 | tf_op jit(solution)/shard_map/ppermute | solution.py:558
  16.6 0.0 copy-done
  16.6 0.2 shard_map.84.refs_0_
  16.8 0.0 copy-start.1
  16.8 2.6 %collective-permute-start.7 = (f32[2,32,128]{2,1,0:T(8,128)S(1)}, f32[2,32,128]{2,1,0:T(8,128)S(1)}, u32[]{:S(2)}, u32[]{:S(2)}) collective-permute-start(f32[2,32,128]{2,1,0:T(8,128)S(1)} %shard_map.84.refs_0_), channel_id=1, source_target_pairs={{0,24},{1,25},{2,26},{3,27},{4,28},{5,29},{6,30},{7,31},{8,16},{9,... | collective-permute-start | bytes 98312 | tf_op jit(solution)/shard_map/ppermute | solution.py:603
  19.4 0.0 collective-permute-start.5
  19.4 0.0 copy-done.2
  19.4 0.0 copy-done.3
  19.5 0.0 copy-done.6
  19.5 2.2 %shard_map.86 = (f32[8,32,128]{2,1,0:T(8,128)S(1)}, f32[4,32,128]{2,1,0:T(8,128)S(1)}, f32[2,32,128]{2,1,0:T(8,128)S(1)}, f32[3,32,128]{2,1,0:T(8,128)S(1)}, f32[3,32,128]{2,1,0:T(8,128)S(1)}) custom-call(bf16[80,128,128]{2,1,0:T(8,128)(2,1)S(1)} %copy-done, bf16[4,2,520,256]{3,2,1,0:T(8,128)(2,1)S(1)} %copy-done.2, bf16[2,1,520,256]{3,2,1,0:T(8,128)(2,1)S(1)} %copy-done.3, ...), custom_call_target="tpu_custom_call" | custom-call | flops 2500000000 | bytes 7500000 | tf_op jit(solution)/shard_map/pallas_call | solution.py:223
  21.6 2.8 %collective-permute-start.8 = (f32[3,32,128]{2,1,0:T(8,128)S(1)}, f32[3,32,128]{2,1,0:T(8,128)S(1)}, u32[]{:S(2)}, u32[]{:S(2)}) collective-permute-start(f32[3,32,128]{2,1,0:T(8,128)S(1)} %get-tuple-element.29), channel_id=1, source_target_pairs={{0,4},{4,8},{8,12},{12,16},{16,20},{20,24},{24,28},{28,0},{1,5},{5... | collective-permute-start | bytes 147464 | tf_op jit(solution)/shard_map/ppermute | solution.py:555
  24.4 2.0 %collective-permute-start.9 = (f32[3,32,128]{2,1,0:T(8,128)S(1)}, f32[3,32,128]{2,1,0:T(8,128)S(1)}, u32[]{:S(2)}, u32[]{:S(2)}) collective-permute-start(f32[3,32,128]{2,1,0:T(8,128)S(1)} %get-tuple-element.30), channel_id=1, source_target_pairs={{0,28},{4,0},{8,4},{12,8},{16,12},{20,16},{24,20},{28,24},{1,29},{... | collective-permute-start | bytes 147464 | tf_op jit(solution)/shard_map/ppermute | solution.py:555
  26.4 0.0 collective-permute-done.5.refs_1_
  26.4 0.0 collective-permute-start.6
  26.4 0.0 copy-done.1
  26.4 0.0 copy-start.5
  26.4 0.0 copy-start.7
  26.4 0.8 %shard_map.85.fine_ref = f32[16,32,128]{2,1,0:T(8,128)S(1)} custom-call(bf16[80,128,128]{2,1,0:T(8,128)(2,1)S(1)} %copy-done, f32[16,32,128]{2,1,0:T(8,128)S(1)} %get-tuple-element.18.rows_ref, f32[3,32,128]{2,1,0:T(8,128)S(1)} %collective-permute-done.down_ref, f32[3,32,128]{2,1,0:T(8,128)S(1)} %collective-permute-done.1.up_ref, ...), custom_call_target="tpu_custom_call" | custom-call | flops 1000000000 | bytes 3000000 | tf_op jit(solution)/shard_map/pallas_call | solution.py:223
  27.2 0.0 collective-permute-done.7.refs_3_
  27.2 0.4 %collective-permute-done.6.refs_2_ = f32[2,32,128]{2,1,0:T(8,128)S(1)} collective-permute-done((f32[2,32,128]{2,1,0:T(8,128)S(1)}, f32[2,32,128]{2,1,0:T(8,128)S(1)}, u32[]{:S(2)}, u32[]{:S(2)}) %collective-permute-start.6) | collective-permute-done | bytes 32800 | tf_op jit(solution)/shard_map/ppermute | solution.py:558
  27.6 0.0 copy-done.5
  27.6 0.0 copy-done.7
  27.6 1.0 %shard_map.87.four_ref = f32[3,32,128]{2,1,0:T(8,128)S(1)} custom-call(bf16[80,128,128]{2,1,0:T(8,128)(2,1)S(1)} %copy-done, bf16[4,1,64,136]{3,2,1,0:T(8,128)(2,1)S(1)} %bitcast.4, bf16[64,64]{1,0:T(8,128)(2,1)S(1)} %copy-done.7, f32[2,32,128]{2,1,0:T(8,128)S(1)} %shard_map.84.refs_0_, f32[2,32,128]{2,1,0:T(8,128)S(1)} %collective-permute-done.5.refs_1_, ...), custom_call_target="tpu_custom_call" | custom-call | flops 1000000000 | bytes 3000000 | tf_op jit(solution)/shard_map/pallas_call | solution.py:223
  28.6 0.0 collective-permute-done.8.down_ref
  28.6 0.4 %collective-permute-done.9.up_ref = f32[3,32,128]{2,1,0:T(8,128)S(1)} collective-permute-done((f32[3,32,128]{2,1,0:T(8,128)S(1)}, f32[3,32,128]{2,1,0:T(8,128)S(1)}, u32[]{:S(2)}, u32[]{:S(2)}) %collective-permute-start.9) | collective-permute-done | bytes 49184 | tf_op jit(solution)/shard_map/ppermute | solution.py:555
  29.0 0.8 %shard_map.88 = f32[512,128]{1,0:T(8,128)} custom-call(f32[16,32,128]{2,1,0:T(8,128)S(1)} %shard_map.85.fine_ref, f32[8,32,128]{2,1,0:T(8,128)S(1)} %get-tuple-element.26.one_ref, f32[4,32,128]{2,1,0:T(8,128)S(1)} %get-tuple-element.27.two_ref, f32[2,32,128]{2,1,0:T(8,128)S(1)} %get-tuple-element.28.three_ref, f32[3,32,128]{2,1,0:T(8,128)S(1)} %shard_map.87.four_ref, ...), custom_call_target="tpu_custom_call" | custom-call | flops 1000000000 | bytes 3000000 | tf_op jit(solution)/shard_map/pallas_call | solution.py:223
Async XLA Ops:
  0.0 0.9 %copy-start.4 = (f32[32,16,128]{2,1,0:T(8,128)S(1)}, f32[32,16,128]{2,1,0:T(8,128)}, u32[]{:S(2)}) copy-start(f32[32,16,128]{2,1,0:T(8,128)} %param.8) | copy-start | bytes 786436
  1.5 15.1 %copy-start = (bf16[80,128,128]{2,1,0:T(8,128)(2,1)S(1)}, bf16[80,128,128]{2,1,0:T(8,128)(2,1)}, u32[]{:S(2)}) copy-start(bf16[80,128,128]{2,1,0:T(8,128)(2,1)} %constant.2.clone.block_ref) | copy-start | bytes 7864324
  1.5 8.2 %collective-permute-start = (f32[3,32,128]{2,1,0:T(8,128)S(1)}, f32[3,32,128]{2,1,0:T(8,128)S(1)}, u32[]{:S(2)}, u32[]{:S(2)}) collective-permute-start(f32[3,32,128]{2,1,0:T(8,128)S(1)} %get-tuple-element.19), channel_id=1, source_target_pairs={{0,4},{4,8},{8,12},{12,16},{16,20},{20,24},{24,28},{28,0},{1,5},{5... | collective-permute-start | bytes 147464 | tf_op jit(solution)/shard_map/ppermute | solution.py:555
  4.5 5.1 %collective-permute-start.1 = (f32[3,32,128]{2,1,0:T(8,128)S(1)}, f32[3,32,128]{2,1,0:T(8,128)S(1)}, u32[]{:S(2)}, u32[]{:S(2)}) collective-permute-start(f32[3,32,128]{2,1,0:T(8,128)S(1)} %get-tuple-element.20), channel_id=1, source_target_pairs={{0,28},{4,0},{8,4},{12,8},{16,12},{20,16},{24,20},{28,24},{1,29},{... | collective-permute-start | bytes 147464 | tf_op jit(solution)/shard_map/ppermute | solution.py:555
  9.8 9.7 %copy-start.2 = (bf16[4,2,520,256]{3,2,1,0:T(8,128)(2,1)S(1)}, bf16[4,2,520,256]{3,2,1,0:T(8,128)(2,1)}, u32[]{:S(2)}) copy-start(bf16[4,2,520,256]{3,2,1,0:T(8,128)(2,1)} %refs_0_.1) | copy-start | bytes 6389764
  9.8 9.7 %copy-start.3 = (bf16[2,1,520,256]{3,2,1,0:T(8,128)(2,1)S(1)}, bf16[2,1,520,256]{3,2,1,0:T(8,128)(2,1)}, u32[]{:S(2)}) copy-start(bf16[2,1,520,256]{3,2,1,0:T(8,128)(2,1)} %refs_1_.1) | copy-start | bytes 1597444
  9.8 9.7 %copy-start.6 = (bf16[1,1,264,128]{3,2,1,0:T(8,128)(2,1)S(1)}, bf16[1,1,264,128]{3,2,1,0:T(8,128)(2,1)}, u32[]{:S(2)}) copy-start(bf16[1,1,264,128]{3,2,1,0:T(8,128)(2,1)} %refs_2_.1) | copy-start | bytes 202756
  9.8 5.4 %collective-permute-start.3 = (f32[10,32,128]{2,1,0:T(8,128)S(1)}, f32[10,32,128]{2,1,0:T(8,128)S(1)}, u32[]{:S(2)}, u32[]{:S(2)}) collective-permute-start(f32[10,32,128]{2,1,0:T(8,128)S(1)} %shard_map.83.refs_0_.refs_3_), channel_id=1, source_target_pairs={{0,2},{1,3},{2,0},{3,1},{4,6},{5,7},{6,4},{7,5},{8,10},{9,11},{10,... | collective-permute-start | bytes 491528 | tf_op jit(solution)/shard_map/ppermute | solution.py:558
  11.5 3.7 %collective-permute-start.2 = (f32[10,32,128]{2,1,0:T(8,128)S(1)}, f32[10,32,128]{2,1,0:T(8,128)S(1)}, u32[]{:S(2)}, u32[]{:S(2)}) collective-permute-start(f32[10,32,128]{2,1,0:T(8,128)S(1)} %shard_map.83.refs_0_.refs_3_), channel_id=1, source_target_pairs={{0,1},{1,0},{2,3},{3,2},{4,5},{5,4},{6,7},{7,6},{8,9},{9,8},{10,11... | collective-permute-start | bytes 491528 | tf_op jit(solution)/shard_map/ppermute | solution.py:558
  15.2 1.4 %collective-permute-start.4 = (f32[10,32,128]{2,1,0:T(8,128)S(1)}, f32[10,32,128]{2,1,0:T(8,128)S(1)}, u32[]{:S(2)}, u32[]{:S(2)}) collective-permute-start(f32[10,32,128]{2,1,0:T(8,128)S(1)} %collective-permute-done.3.refs_2_.refs_5_), channel_id=1, source_target_pairs={{0,1},{1,0},{2,3},{3,2},{4,5},{5,4},{6,7},{7,6},{8,9},{9,8},{10,11... | collective-permute-start | bytes 491528 | tf_op jit(solution)/shard_map/ppermute | solution.py:558
  16.8 9.6 %copy-start.1 = (bf16[8,1,520,256]{3,2,1,0:T(8,128)(2,1)S(1)}, bf16[8,1,520,256]{3,2,1,0:T(8,128)(2,1)}, u32[]{:S(2)}) copy-start(bf16[8,1,520,256]{3,2,1,0:T(8,128)(2,1)} %factor_ref.1) | copy-start | bytes 6389764
  16.8 10.4 %collective-permute-start.7 = (f32[2,32,128]{2,1,0:T(8,128)S(1)}, f32[2,32,128]{2,1,0:T(8,128)S(1)}, u32[]{:S(2)}, u32[]{:S(2)}) collective-permute-start(f32[2,32,128]{2,1,0:T(8,128)S(1)} %shard_map.84.refs_0_), channel_id=1, source_target_pairs={{0,24},{1,25},{2,26},{3,27},{4,28},{5,29},{6,30},{7,31},{8,16},{9,... | collective-permute-start | bytes 98312 | tf_op jit(solution)/shard_map/ppermute | solution.py:603
  19.4 6.9 %collective-permute-start.5 = (f32[2,32,128]{2,1,0:T(8,128)S(1)}, f32[2,32,128]{2,1,0:T(8,128)S(1)}, u32[]{:S(2)}, u32[]{:S(2)}) collective-permute-start(f32[2,32,128]{2,1,0:T(8,128)S(1)} %shard_map.84.refs_0_), channel_id=1, source_target_pairs={{0,8},{1,17},{2,10},{3,19},{4,12},{5,21},{6,14},{7,23},{8,0},{9,25... | collective-permute-start | bytes 98312 | tf_op jit(solution)/shard_map/ppermute | solution.py:603
  21.6 6.9 %collective-permute-start.8 = (f32[3,32,128]{2,1,0:T(8,128)S(1)}, f32[3,32,128]{2,1,0:T(8,128)S(1)}, u32[]{:S(2)}, u32[]{:S(2)}) collective-permute-start(f32[3,32,128]{2,1,0:T(8,128)S(1)} %get-tuple-element.29), channel_id=1, source_target_pairs={{0,4},{4,8},{8,12},{12,16},{16,20},{20,24},{24,28},{28,0},{1,5},{5... | collective-permute-start | bytes 147464 | tf_op jit(solution)/shard_map/ppermute | solution.py:555
  24.4 4.5 %collective-permute-start.9 = (f32[3,32,128]{2,1,0:T(8,128)S(1)}, f32[3,32,128]{2,1,0:T(8,128)S(1)}, u32[]{:S(2)}, u32[]{:S(2)}) collective-permute-start(f32[3,32,128]{2,1,0:T(8,128)S(1)} %get-tuple-element.30), channel_id=1, source_target_pairs={{0,28},{4,0},{8,4},{12,8},{16,12},{20,16},{24,20},{28,24},{1,29},{... | collective-permute-start | bytes 147464 | tf_op jit(solution)/shard_map/ppermute | solution.py:555
  26.4 1.2 %collective-permute-start.6 = (f32[2,32,128]{2,1,0:T(8,128)S(1)}, f32[2,32,128]{2,1,0:T(8,128)S(1)}, u32[]{:S(2)}, u32[]{:S(2)}) collective-permute-start(f32[2,32,128]{2,1,0:T(8,128)S(1)} %collective-permute-done.5.refs_1_), channel_id=1, source_target_pairs={{0,1},{1,0},{2,3},{3,2},{4,5},{5,4},{6,7},{7,6},{8,9},{9,8},{10,11... | collective-permute-start | bytes 98312 | tf_op jit(solution)/shard_map/ppermute | solution.py:558
  26.4 1.2 %copy-start.5 = (bf16[4,1,136,64]{2,3,1,0:T(8,128)(2,1)S(1)}, bf16[4,1,136,64]{2,3,1,0:T(8,128)(2,1)}, u32[]{:S(2)}) copy-start(bf16[4,1,136,64]{2,3,1,0:T(8,128)(2,1)} %param.13) | copy-start | bytes 208900
  26.4 1.2 %copy-start.7 = (bf16[64,64]{1,0:T(8,128)(2,1)S(1)}, bf16[64,64]{1,0:T(8,128)(2,1)}, u32[]{:S(2)}) copy-start(bf16[64,64]{1,0:T(8,128)(2,1)} %inverse_ref.1) | copy-start | bytes 24580

commit v4 on v3

--- a/solution.py
+++ b/solution.py
@@ -258,7 +258,23 @@
     return jnp.where(jnp.logical_or(left, right), 1.0, 0.0).astype(BF16)
 
 
-def restrict_kernel(plan, x_ref, own_ref, down_ref, up_ref, rows_ref):
+def write_halos(c, down, up, first_ref, second_ref):
+    forward = jnp.bitwise_and(c, 2) == 0
+    for k, (low, high) in enumerate(zip(down, up)):
+        first_ref[k] = jnp.where(forward, low, high)
+        second_ref[k] = jnp.where(forward, high, low)
+
+
+def read_halos(plan, first_ref, second_ref):
+    r, c = lax.axis_index("px"), lax.axis_index("py")
+    forward = jnp.bitwise_and(c, 2) == 0
+    above = jnp.where(r > 0, 1.0, 0.0).astype(F32)
+    below = jnp.where(r < plan.n - 1, 1.0, 0.0).astype(F32)
+    first, second = first_ref[...], second_ref[...]
+    return jnp.where(forward, first, second) * above, jnp.where(forward, second, first) * below
+
+
+def restrict_kernel(plan, x_ref, own_ref, first_ref, second_ref, rows_ref):
     r, c = lax.axis_index("px"), lax.axis_index("py")
     rhs, slots, h = plan.rhs, plan.slots, plan.h
     first = jnp.where(c == 0, 1, 0)
@@ -305,39 +321,38 @@
     own = total.reshape(slots, rhs, LANES)
     own_ref[...] = own
     lane = lane_index(rhs)
-    down_ref[0] = x[-1]
-    up_ref[0] = x[0]
+    down, up = [x[-1]], [x[0]]
     for k in range(2):
         three_own = own[h[3] + k]
-        down_ref[1 + k] = jnp.where(
-            lane < one, own[h[1] + k], jnp.where(lane < two, own[h[2] + k], three_own)
+        down.append(
+            jnp.where(lane < one, own[h[1] + k], jnp.where(lane < two, own[h[2] + k], three_own))
         )
-        up_ref[1 + k] = own[k]
-
-
-def merge_kernel(plan, own_ref, down_ref, up_ref, out_ref):
+        up.append(own[k])
+    write_halos(c, down + [own[1]], up + [own[h[3]]], first_ref, second_ref)
+
+
+def merge_kernel(plan, own_ref, first_ref, second_ref, out_ref):
     r = lax.axis_index("px")
     rhs, h = plan.rhs, plan.h
-    above = jnp.where(r > 0, 1.0, 0.0).astype(F32)
-    below = jnp.where(r < plan.n - 1, 1.0, 0.0).astype(F32)
     lane = lane_index(rhs)
+    above, below = read_halos(plan, first_ref, second_ref)
     one, two, end = plan.offset[2], plan.offset[3], plan.spare
     out_ref[...] = own_ref[...]
-    wrapped = jnp.logical_and(lane >= two, lane < end)
-    in_band = lane < end
     for k in range(2):
-        piece = down_ref[1 + k]
-        piece = jnp.where(wrapped, piece, jnp.where(in_band, piece * above, 0.0))
-        out_ref[k] = out_ref[k] + piece
-        piece = up_ref[1 + k]
-        piece = jnp.where(wrapped, piece, jnp.where(in_band, piece * below, 0.0))
+        out_ref[k] = out_ref[k] + jnp.where(lane < end, above[1 + k], 0.0)
         for level, low, high in ((1, 0, one), (2, one, two), (3, two, end)):
             row = h[level] + k
             chosen = jnp.logical_and(lane >= low, lane < high)
-            out_ref[row] = out_ref[row] + jnp.where(chosen, piece, 0.0)
-    top = (down_ref[0] * above).astype(BF16)
+            out_ref[row] = out_ref[row] + jnp.where(chosen, below[1 + k], 0.0)
+    odd = lax.rem(r, 2) == 1
+    row = jnp.where(odd, above[3], below[3])
+    ends = jnp.where(r == jnp.where(odd, 1, plan.n - 2), 1.0, 0.0).astype(F32)
+    chosen = jnp.logical_and(lane >= two, lane < end)
+    at = h[3] + 2
+    out_ref[at] = out_ref[at] + jnp.where(chosen, row * ends, 0.0)
+    top = above[0].astype(BF16)
     out_ref[0] = out_ref[0] + jnp.dot(top, side_matrix(plan, 0), preferred_element_type=F32)
-    bottom = (up_ref[0] * below).astype(BF16)
+    bottom = below[0].astype(BF16)
     at = h[0] + 1 - plan.slots
     out_ref[at] = out_ref[at] + jnp.dot(bottom, side_matrix(plan, 1), preferred_element_type=F32)
 
@@ -357,10 +372,10 @@
     values, matrices = [], []
     for band, owner in zip(band_refs, owners(plan)):
         for j in range(2):
-            values.append(jnp.concatenate([band[j], band[2 + j]], axis=0))
+            values.append(jnp.concatenate([band[j], band[2 + j], band[4]], axis=0))
             matrices.append(blocks.get(block_ref, "pairs", 2 * owner + j))
     total = banded(values, matrices)
-    for half in range(2):
+    for half in range(3):
         out_ref[half] = total[half * rhs : (half + 1) * rhs]
 
 
@@ -373,19 +388,13 @@
 
 def coarse_kernel(plan, blocks, block_ref, *refs):
     factors, bands, outs = refs[:3], refs[3 : 3 + plan.m], refs[3 + plan.m :]
-    r, c = lax.axis_index("px"), lax.axis_index("py")
-    rhs = plan.rhs
-    above = jnp.where(r > 0, 1.0, 0.0).astype(F32)
-    below = jnp.where(r < plan.n - 1, 1.0, 0.0).astype(F32)
-    down_ref, up_ref = outs[3], outs[4]
+    c, rhs = lax.axis_index("py"), plan.rhs
+    down, up = [], []
     for level in (1, 2, 3):
         w, tiles = plan.tile[level], plan.tiles[level]
         whole = level_rows(plan, level, bands, blocks, block_ref)
         count = plan.h[level] + 2
         rows = [whole[i * rhs : (i + 1) * rhs] for i in range(count)]
-        if level == 3:
-            rows[0] = rows[0] * above
-            rows[-1] = rows[-1] * below
         factor_ref, out_ref = factors[level - 1], outs[level - 1]
         solved = [[] for _ in range(tiles)]
         for b in range(plan.h[level] // 2):
@@ -410,16 +419,16 @@
         for b in range(pairs):
             for j in range(2):
                 out_ref[2 * b + j] = lifted[j][b * rhs : (b + 1) * rhs]
-        down_ref[level - 1] = lifted[1][(pairs - 1) * rhs :]
-        up_ref[level - 1] = lifted[0][:rhs]
-
-
-def fine_kernel(plan, blocks, block_ref, rows_ref, down_ref, up_ref, factor_ref, *refs):
+        down.append(lifted[1][(pairs - 1) * rhs :])
+        up.append(lifted[0][:rhs])
+    write_halos(c, down, up, outs[3], outs[4])
+
+
+def fine_kernel(plan, blocks, block_ref, rows_ref, first_ref, second_ref, factor_ref, *refs):
     bands, out_ref = refs[: plan.m], refs[plan.m]
-    r, c = lax.axis_index("px"), lax.axis_index("py")
+    c = lax.axis_index("py")
     rhs, h0, w0, slots = plan.rhs, plan.h0, plan.w0, plan.slots
-    above = jnp.where(r > 0, 1.0, 0.0).astype(F32)
-    below = jnp.where(r < plan.n - 1, 1.0, 0.0).astype(F32)
+    above, below = read_halos(plan, first_ref, second_ref)
     values, matrices = [], []
     left = blocks.get(block_ref, "halo", 0)
     right = blocks.get(block_ref, "halo", 1)
@@ -436,9 +445,9 @@
     rows, sides = [], []
     for row in range(-1, h0 + 1):
         if row == -1:
-            rows.append(down_ref[0] * above)
+            rows.append(above[0])
         elif row == h0:
-            rows.append(up_ref[0] * below)
+            rows.append(below[0])
         else:
             rows.append(rows_ref[row])
         part, slot = divmod(row + 1, slots)
@@ -471,6 +480,8 @@
     rhs, n, ny3, ny4 = plan.rhs, plan.n, plan.ny[3], plan.ny[4]
     nx4, nx5 = plan.nx[4], plan.nx[5]
     odd = jnp.bitwise_and(c, 1)
+    even = lax.rem(r, 2) == 0
+    lane = lax.broadcasted_iota(jnp.int32, (rhs, 2 * ny3), 1)
     for k, block in enumerate(gathered):
         if k == 0 or (k == count - 1 and k % 2):
             partner = 2 * k
@@ -478,13 +489,11 @@
             partner = 2 * (k + odd)
         else:
             partner = 2 * (k - odd)
-        for half in range(2):
-            at = lax.rem(jnp.bitwise_xor(r, partner) + half, n)
-            pair_ref[at] = block[half]
-    lane = lax.broadcasted_iota(jnp.int32, (rhs, 2 * ny3), 1)
-    ring = pair_ref[0]
-    pair_ref[0] = jnp.where(lane < ny3, 0.0, ring)
-    pair_ref[n] = jnp.where(lane < ny3, ring, 0.0)
+        row = jnp.bitwise_xor(r, partner)
+        pair_ref[row] = block[0]
+        pair_ref[row + 1] = block[1]
+        at = jnp.where(even, jnp.where(row == n - 2, n, n + 1), jnp.where(row == 1, 0, n + 1))
+        pair_ref[at] = jnp.where((lane < ny3) == even, block[2], 0.0)
     low = pair_ref[0:n].reshape(n * rhs, 2 * ny3)
     high = pair_ref[1 : n + 1].reshape(n * rhs, 2 * ny3)
     both = jnp.concatenate([low, high], axis=1)
@@ -528,17 +537,19 @@
         out_ref[k] = four_rows[r + k]
 
 
-def final_kernel(plan, fine_ref, one_ref, two_ref, three_ref, four_ref, down_ref, up_ref, out_ref):
+def final_kernel(plan, fine_ref, one_ref, two_ref, three_ref, four_ref, first_ref, second_ref,
+                 out_ref):
     r, rhs = lax.axis_index("px"), plan.rhs
     above = jnp.where(r > 0, 1.0, 0.0).astype(F32)
     below = jnp.where(r < plan.n - 1, 1.0, 0.0).astype(F32)
+    from_above, from_below = read_halos(plan, first_ref, second_ref)
     rows = [four_ref[k] for k in range(3)]
     for level, own_ref in ((3, three_ref), (2, two_ref), (1, one_ref)):
         height = plan.h[level]
         lifted = lift_rows(rows, -1, height + 1)
-        rows = [(lifted[0] + down_ref[level - 1]) * above]
+        rows = [lifted[0] * above + from_above[level - 1]]
         rows += [lifted[i + 1] + own_ref[i] for i in range(height)]
-        rows += [(lifted[-1] + up_ref[level - 1]) * below]
+        rows += [lifted[-1] * below + from_below[level - 1]]
     lifted = lift_rows(rows, 0, plan.h0)
     for row in range(plan.h0):
         out_ref[pl.ds(row, rhs, stride=plan.h0), :] = lifted[row] + fine_ref[row]
@@ -551,8 +562,18 @@
     n, m, rhs, h, h0 = plan.n, plan.m, plan.rhs, plan.h, plan.h0
     x = residual.reshape(rhs * h0, plan.w0)
 
-    def shift(value, by):
-        return lax.ppermute(value, "px", [(i, (i + by) % n) for i in range(n)])
+    def trade(first, second):
+        def target(i, c):
+            after = i - 1 if c & 2 else i + 1
+            return (after, c) if 0 <= after < n else (i, c ^ 2)
+
+        ring = []
+        for i in range(n):
+            for c in range(m):
+                row, column = target(i, c)
+                ring.append((i * m + c, row * m + column))
+        back = [(b, a) for a, b in ring]
+        return lax.ppermute(first, ("px", "py"), ring), lax.ppermute(second, ("px", "py"), back)
 
     def swap(value, bits):
         return lax.ppermute(value, "py", [(i, i ^ bits) for i in range(m)])
@@ -576,14 +597,14 @@
     blocks.add("lift5", plan.coarsest_lift())
     matrices = blocks.array()
 
-    own, down, up, rows = kernel_call(
+    own, first, second, rows = kernel_call(
         functools.partial(restrict_kernel, plan),
-        (shape(plan.slots, rhs, LANES), shape(3, rhs, LANES), shape(3, rhs, LANES),
+        (shape(plan.slots, rhs, LANES), shape(4, rhs, LANES), shape(4, rhs, LANES),
          shape(h0, rhs, plan.w0)),
     )(x)
-    from_above, from_below = shift(down, 1), shift(up, -1)
+    first, second = trade(first, second)
     band = kernel_call(functools.partial(merge_kernel, plan), shape(plan.slots, rhs, LANES))(
-        own, from_above, from_below
+        own, first, second
     )
     bands = {0: band}
     bit = m // 2
@@ -593,7 +614,7 @@
     bands = [bands[k] for k in range(m)]
 
     pairs = kernel_call(
-        functools.partial(gather_kernel, plan, blocks), shape(2, rhs, width3), cost_us=0.3
+        functools.partial(gather_kernel, plan, blocks), shape(3, rhs, width3), cost_us=0.3
     )(matrices, *bands)
     order, gathered = list(range(1, n // 2)), [pairs]
     fetched = []
@@ -612,27 +633,27 @@
         if 2 * k + 1 < len(order):
             gathered.append(swap(value, 1))
 
-    one, two, three, down, up = kernel_call(
+    one, two, three, low, high = kernel_call(
         functools.partial(coarse_kernel, plan, blocks),
         tuple(shape(h[l], rhs, LANES) for l in (1, 2, 3))
         + (shape(3, rhs, LANES), shape(3, rhs, LANES)),
         cost_us=2.5,
     )(matrices, factor_one, factor_two, factor_three, *bands)
-    down, up = shift(down, 1), shift(up, -1)
+    low, high = trade(low, high)
 
     fine = kernel_call(
         functools.partial(fine_kernel, plan, blocks), shape(h0, rhs, plan.w0)
-    )(matrices, rows, from_above, from_below, factor_fine, *bands)
+    )(matrices, rows, first, second, factor_fine, *bands)
     four = kernel_call(
         functools.partial(whole_kernel, plan, group, blocks),
         shape(3, rhs, LANES),
         scratch=(
-            pltpu.VMEM((n + 1, rhs, width3), F32),
+            pltpu.VMEM((n + 2, rhs, width3), F32),
             pltpu.VMEM((plan.nx[4] + 2, rhs, LANES), F32),
         ),
     )(matrices, jnp.swapaxes(factor_four, 2, 3), coarse_inverse, *gathered)
     out = kernel_call(functools.partial(final_kernel, plan), shape(rhs * h0, plan.w0))(
-        fine, one, two, three, four, down, up
+        fine, one, two, three, four, low, high
     )
     return out.reshape(rhs, h0, plan.w0)
 

time: 30 us -> 29.1 us (0.970)
  starting transfers between devices: 15.2 us -> 9.79 us
  waiting for transfers between devices: 7.91 us -> 12.4 us
    ppermute x4, starting transfers between devices: 10.9 us -> 5.09 us  [the longest x2 4.27 us: trade(): lax.ppermute(first, ('px', 'py'), ring)]
    ppermute x4, waiting for transfers between devices: 2.44 us -> 5.35 us  [the longest x2 3.17 us: trade(): lax.ppermute(second, ('px', 'py'), back)]
    ppermute x2, starting transfers between devices: 2.61 us -> 4.38 us  [per_device(): lax.ppermute(pairs, ('px', 'py'), [(i * m + c, (i ^ 2 * (odd if c % 2 els...]
    ppermute x4, waiting for transfers between devices: 5.47 us -> 6.87 us  [swap(): return lax.ppermute(value, 'py', [(i, i ^ bits) for i in range(m)])]
    ppermute x4, starting transfers between devices: 1.69 us -> 0.32 us  [swap(): return lax.ppermute(value, 'py', [(i, i ^ bits) for i in range(m)])]
  transfers between devices with their start and end apart: 10 -> 10, of which waited for: 5 -> 7; matrix products, arithmetic and copies ran while one was open for 0% -> 0% of each run, Pallas kernels for 13% -> 14%
where the time goes in v4:
time: 29.1 us; the launch traced here: 28.9 us
  waiting for transfers between devices  12.4 us (43%)
  starting transfers between devices  9.79 us (34%)
  Pallas kernels  5.67 us (19%)
  local copies, waits for them, and re-layouts  0.98 us (3%)
    ppermute x4, waiting for transfers between devices, swap(): return lax.ppermute(value, 'py', [(i, i ^ bits) for i in range(m)])  6.87 us
    pallas_call x7, Pallas kernels, call(): pl.pallas_call(body, out_shape=out_shape, in_specs=[whole] * len(operands...  5.67 us
    ppermute x2, starting transfers between devices, per_device(): lax.ppermute(pairs, ('px', 'py'), [(i * m + c, (i ^ 2 * (odd if c % 2 els...  4.38 us
    ppermute x2, starting transfers between devices, trade(): lax.ppermute(first, ('px', 'py'), ring)  4.27 us
    ppermute x2, waiting for transfers between devices, trade(): lax.ppermute(second, ('px', 'py'), back)  3.17 us
    ppermute x2, waiting for transfers between devices, trade(): lax.ppermute(first, ('px', 'py'), ring)  2.18 us
    unnamed x16, local copies, waits for them, and re-layouts  0.98 us
    ppermute x2, starting transfers between devices, trade(): lax.ppermute(second, ('px', 'py'), back)  0.82 us
  transfers between devices with their start and end apart: 10, of which 7 were waited for; matrix products, arithmetic and copies ran while one was open for 0% of the time, Pallas kernels for 14%

profile of v4, /device:TPU:0, one launch (start us, length us, event | category | flops | bytes accessed | tf_op | source)
XLA Modules:
  0.0 28.9 jit_solution(3648543631054948645)
XLA Ops:
  0.0 0.0 copy-start.4
  0.0 0.9 %copy-done.4 = f32[32,16,128]{2,1,0:T(8,128)S(1)} copy-done((f32[32,16,128]{2,1,0:T(8,128)S(1)}, f32[32,16,128]{2,1,0:T(8,128)}, u32[]{:S(2)}) %copy-start.4) | copy-done | bytes 262168
  1.0 0.5 %shard_map.82 = (f32[10,32,128]{2,1,0:T(8,128)S(1)}, f32[4,32,128]{2,1,0:T(8,128)S(1)}, f32[4,32,128]{2,1,0:T(8,128)S(1)}, f32[16,32,128]{2,1,0:T(8,128)S(1)}) custom-call(f32[512,128]{1,0:T(8,128)S(1)} %bitcast.3), custom_call_target="tpu_custom_call" | custom-call | flops 1000000000 | bytes 3000000 | tf_op jit(solution)/shard_map/pallas_call | solution.py:223
  1.5 0.0 copy-start
  1.5 3.0 %collective-permute-start = (f32[4,32,128]{2,1,0:T(8,128)S(1)}, f32[4,32,128]{2,1,0:T(8,128)S(1)}, u32[]{:S(2)}, u32[]{:S(2)}) collective-permute-start(f32[4,32,128]{2,1,0:T(8,128)S(1)} %get-tuple-element.19), channel_id=1, source_target_pairs={{0,4},{1,5},{2,0},{3,1},{4,8},{5,9},{6,2},{7,3},{8,12},{9,13},{10,... | collective-permute-start | bytes 196616 | tf_op jit(solution)/shard_map/ppermute | solution.py:576
  4.5 0.0 collective-permute-start.1
  4.5 2.2 %collective-permute-done.first_ref = f32[4,32,128]{2,1,0:T(8,128)S(1)} collective-permute-done((f32[4,32,128]{2,1,0:T(8,128)S(1)}, f32[4,32,128]{2,1,0:T(8,128)S(1)}, u32[]{:S(2)}, u32[]{:S(2)}) %collective-permute-start) | collective-permute-done | bytes 65568 | tf_op jit(solution)/shard_map/ppermute | solution.py:576
  6.7 2.0 %collective-permute-done.1.second_ref = f32[4,32,128]{2,1,0:T(8,128)S(1)} collective-permute-done((f32[4,32,128]{2,1,0:T(8,128)S(1)}, f32[4,32,128]{2,1,0:T(8,128)S(1)}, u32[]{:S(2)}, u32[]{:S(2)}) %collective-permute-start.1) | collective-permute-done | bytes 65568 | tf_op jit(solution)/shard_map/ppermute | solution.py:576
  8.8 0.1 shard_map.83.refs_0_.refs_3_
  8.9 0.0 copy-start.2
  8.9 0.0 copy-start.3
  8.9 0.0 copy-start.6
  8.9 0.3 %collective-permute-start.3 = (f32[10,32,128]{2,1,0:T(8,128)S(1)}, f32[10,32,128]{2,1,0:T(8,128)S(1)}, u32[]{:S(2)}, u32[]{:S(2)}) collective-permute-start(f32[10,32,128]{2,1,0:T(8,128)S(1)} %shard_map.83.refs_0_.refs_3_), channel_id=1, source_target_pairs={{0,2},{1,3},{2,0},{3,1},{4,6},{5,7},{6,4},{7,5},{8,10},{9,11},{10,... | collective-permute-start | bytes 491528 | tf_op jit(solution)/shard_map/ppermute | solution.py:579
  9.2 0.0 collective-permute-start.2
  9.2 5.1 %collective-permute-done.3.refs_2_.refs_5_ = f32[10,32,128]{2,1,0:T(8,128)S(1)} collective-permute-done((f32[10,32,128]{2,1,0:T(8,128)S(1)}, f32[10,32,128]{2,1,0:T(8,128)S(1)}, u32[]{:S(2)}, u32[]{:S(2)}) %collective-permute-start.3) | collective-permute-done | bytes 163872 | tf_op jit(solution)/shard_map/ppermute | solution.py:579
  14.3 0.0 collective-permute-start.4
  14.3 0.0 collective-permute-done.2.refs_1_.refs_4_
  14.3 1.4 %collective-permute-done.4.refs_3_.refs_6_ = f32[10,32,128]{2,1,0:T(8,128)S(1)} collective-permute-done((f32[10,32,128]{2,1,0:T(8,128)S(1)}, f32[10,32,128]{2,1,0:T(8,128)S(1)}, u32[]{:S(2)}, u32[]{:S(2)}) %collective-permute-start.4) | collective-permute-done | bytes 163872 | tf_op jit(solution)/shard_map/ppermute | solution.py:579
  15.7 0.0 copy-done
  15.7 0.3 shard_map.84.refs_0_
  16.0 0.0 copy-start.1
  16.0 4.4 %collective-permute-start.7 = (f32[3,32,128]{2,1,0:T(8,128)S(1)}, f32[3,32,128]{2,1,0:T(8,128)S(1)}, u32[]{:S(2)}, u32[]{:S(2)}) collective-permute-start(f32[3,32,128]{2,1,0:T(8,128)S(1)} %shard_map.84.refs_0_), channel_id=1, source_target_pairs={{0,24},{1,25},{2,26},{3,27},{4,28},{5,29},{6,30},{7,31},{8,16},{9,... | collective-permute-start | bytes 147464 | tf_op jit(solution)/shard_map/ppermute | solution.py:624
  20.4 0.0 collective-permute-start.5
  20.4 0.0 copy-done.2
  20.4 0.0 copy-done.3
  20.4 0.0 copy-done.6
  20.4 2.2 %shard_map.86 = (f32[8,32,128]{2,1,0:T(8,128)S(1)}, f32[4,32,128]{2,1,0:T(8,128)S(1)}, f32[2,32,128]{2,1,0:T(8,128)S(1)}, f32[3,32,128]{2,1,0:T(8,128)S(1)}, f32[3,32,128]{2,1,0:T(8,128)S(1)}) custom-call(bf16[80,128,128]{2,1,0:T(8,128)(2,1)S(1)} %copy-done, bf16[4,2,520,256]{3,2,1,0:T(8,128)(2,1)S(1)} %copy-done.2, bf16[2,1,520,256]{3,2,1,0:T(8,128)(2,1)S(1)} %copy-done.3, ...), custom_call_target="tpu_custom_call" | custom-call | flops 2500000000 | bytes 7500000 | tf_op jit(solution)/shard_map/pallas_call | solution.py:223
  22.5 1.3 %collective-permute-start.8 = (f32[3,32,128]{2,1,0:T(8,128)S(1)}, f32[3,32,128]{2,1,0:T(8,128)S(1)}, u32[]{:S(2)}, u32[]{:S(2)}) collective-permute-start(f32[3,32,128]{2,1,0:T(8,128)S(1)} %get-tuple-element.29), channel_id=1, source_target_pairs={{0,4},{1,5},{2,0},{3,1},{4,8},{5,9},{6,2},{7,3},{8,12},{9,13},{10,... | collective-permute-start | bytes 147464 | tf_op jit(solution)/shard_map/ppermute | solution.py:576
  23.8 0.8 %collective-permute-start.9 = (f32[3,32,128]{2,1,0:T(8,128)S(1)}, f32[3,32,128]{2,1,0:T(8,128)S(1)}, u32[]{:S(2)}, u32[]{:S(2)}) collective-permute-start(f32[3,32,128]{2,1,0:T(8,128)S(1)} %get-tuple-element.30), channel_id=1, source_target_pairs={{4,0},{5,1},{0,2},{1,3},{8,4},{9,5},{2,6},{3,7},{12,8},{13,9},{6,1... | collective-permute-start | bytes 147464 | tf_op jit(solution)/shard_map/ppermute | solution.py:576
  24.6 0.2 collective-permute-done.5.refs_1_
  24.8 0.0 collective-permute-start.6
  24.8 0.0 copy-done.1
  24.8 0.0 copy-start.5
  24.8 0.0 copy-start.7
  24.8 0.8 %shard_map.85.fine_ref = f32[16,32,128]{2,1,0:T(8,128)S(1)} custom-call(bf16[80,128,128]{2,1,0:T(8,128)(2,1)S(1)} %copy-done, f32[16,32,128]{2,1,0:T(8,128)S(1)} %get-tuple-element.18.rows_ref, f32[4,32,128]{2,1,0:T(8,128)S(1)} %collective-permute-done.first_ref, f32[4,32,128]{2,1,0:T(8,128)S(1)} %collective-permute-done.1.second_ref, ...), custom_call_target="tpu_custom_call" | custom-call | flops 1000000000 | bytes 3000000 | tf_op jit(solution)/shard_map/pallas_call | solution.py:223
  25.6 0.0 collective-permute-done.7.refs_3_
  25.6 0.4 %collective-permute-done.6.refs_2_ = f32[3,32,128]{2,1,0:T(8,128)S(1)} collective-permute-done((f32[3,32,128]{2,1,0:T(8,128)S(1)}, f32[3,32,128]{2,1,0:T(8,128)S(1)}, u32[]{:S(2)}, u32[]{:S(2)}) %collective-permute-start.6) | collective-permute-done | bytes 49184 | tf_op jit(solution)/shard_map/ppermute | solution.py:579
  26.0 0.0 copy-done.5
  26.0 0.0 copy-done.7
  26.0 1.0 %shard_map.87.four_ref = f32[3,32,128]{2,1,0:T(8,128)S(1)} custom-call(bf16[80,128,128]{2,1,0:T(8,128)(2,1)S(1)} %copy-done, bf16[4,1,64,136]{3,2,1,0:T(8,128)(2,1)S(1)} %bitcast.4, bf16[64,64]{1,0:T(8,128)(2,1)S(1)} %copy-done.7, f32[3,32,128]{2,1,0:T(8,128)S(1)} %shard_map.84.refs_0_, f32[3,32,128]{2,1,0:T(8,128)S(1)} %collective-permute-done.5.refs_1_, ...), custom_call_target="tpu_custom_call" | custom-call | flops 1000000000 | bytes 3000000 | tf_op jit(solution)/shard_map/pallas_call | solution.py:223
  27.0 0.0 collective-permute-done.8.first_ref
  27.0 1.1 %collective-permute-done.9.second_ref = f32[3,32,128]{2,1,0:T(8,128)S(1)} collective-permute-done((f32[3,32,128]{2,1,0:T(8,128)S(1)}, f32[3,32,128]{2,1,0:T(8,128)S(1)}, u32[]{:S(2)}, u32[]{:S(2)}) %collective-permute-start.9) | collective-permute-done | bytes 49184 | tf_op jit(solution)/shard_map/ppermute | solution.py:576
  28.1 0.8 %shard_map.88 = f32[512,128]{1,0:T(8,128)} custom-call(f32[16,32,128]{2,1,0:T(8,128)S(1)} %shard_map.85.fine_ref, f32[8,32,128]{2,1,0:T(8,128)S(1)} %get-tuple-element.26.one_ref, f32[4,32,128]{2,1,0:T(8,128)S(1)} %get-tuple-element.27.two_ref, f32[2,32,128]{2,1,0:T(8,128)S(1)} %get-tuple-element.28.three_ref, f32[3,32,128]{2,1,0:T(8,128)S(1)} %shard_map.87.four_ref, ...), custom_call_target="tpu_custom_call" | custom-call | flops 1000000000 | bytes 3000000 | tf_op jit(solution)/shard_map/pallas_call | solution.py:223
Async XLA Ops:
  0.0 0.9 %copy-start.4 = (f32[32,16,128]{2,1,0:T(8,128)S(1)}, f32[32,16,128]{2,1,0:T(8,128)}, u32[]{:S(2)}) copy-start(f32[32,16,128]{2,1,0:T(8,128)} %param.8) | copy-start | bytes 786436
  1.5 14.2 %copy-start = (bf16[80,128,128]{2,1,0:T(8,128)(2,1)S(1)}, bf16[80,128,128]{2,1,0:T(8,128)(2,1)}, u32[]{:S(2)}) copy-start(bf16[80,128,128]{2,1,0:T(8,128)(2,1)} %constant.2.clone.block_ref) | copy-start | bytes 7864324
  1.5 5.2 %collective-permute-start = (f32[4,32,128]{2,1,0:T(8,128)S(1)}, f32[4,32,128]{2,1,0:T(8,128)S(1)}, u32[]{:S(2)}, u32[]{:S(2)}) collective-permute-start(f32[4,32,128]{2,1,0:T(8,128)S(1)} %get-tuple-element.19), channel_id=1, source_target_pairs={{0,4},{1,5},{2,0},{3,1},{4,8},{5,9},{6,2},{7,3},{8,12},{9,13},{10,... | collective-permute-start | bytes 196616 | tf_op jit(solution)/shard_map/ppermute | solution.py:576
  4.5 4.3 %collective-permute-start.1 = (f32[4,32,128]{2,1,0:T(8,128)S(1)}, f32[4,32,128]{2,1,0:T(8,128)S(1)}, u32[]{:S(2)}, u32[]{:S(2)}) collective-permute-start(f32[4,32,128]{2,1,0:T(8,128)S(1)} %get-tuple-element.20), channel_id=1, source_target_pairs={{4,0},{5,1},{0,2},{1,3},{8,4},{9,5},{2,6},{3,7},{12,8},{13,9},{6,1... | collective-permute-start | bytes 196616 | tf_op jit(solution)/shard_map/ppermute | solution.py:576
  8.9 11.5 %copy-start.2 = (bf16[4,2,520,256]{3,2,1,0:T(8,128)(2,1)S(1)}, bf16[4,2,520,256]{3,2,1,0:T(8,128)(2,1)}, u32[]{:S(2)}) copy-start(bf16[4,2,520,256]{3,2,1,0:T(8,128)(2,1)} %refs_0_.1) | copy-start | bytes 6389764
  8.9 11.5 %copy-start.3 = (bf16[2,1,520,256]{3,2,1,0:T(8,128)(2,1)S(1)}, bf16[2,1,520,256]{3,2,1,0:T(8,128)(2,1)}, u32[]{:S(2)}) copy-start(bf16[2,1,520,256]{3,2,1,0:T(8,128)(2,1)} %refs_1_.1) | copy-start | bytes 1597444
  8.9 11.5 %copy-start.6 = (bf16[1,1,264,128]{3,2,1,0:T(8,128)(2,1)S(1)}, bf16[1,1,264,128]{3,2,1,0:T(8,128)(2,1)}, u32[]{:S(2)}) copy-start(bf16[1,1,264,128]{3,2,1,0:T(8,128)(2,1)} %refs_2_.1) | copy-start | bytes 202756
  8.9 5.4 %collective-permute-start.3 = (f32[10,32,128]{2,1,0:T(8,128)S(1)}, f32[10,32,128]{2,1,0:T(8,128)S(1)}, u32[]{:S(2)}, u32[]{:S(2)}) collective-permute-start(f32[10,32,128]{2,1,0:T(8,128)S(1)} %shard_map.83.refs_0_.refs_3_), channel_id=1, source_target_pairs={{0,2},{1,3},{2,0},{3,1},{4,6},{5,7},{6,4},{7,5},{8,10},{9,11},{10,... | collective-permute-start | bytes 491528 | tf_op jit(solution)/shard_map/ppermute | solution.py:579
  9.2 5.1 %collective-permute-start.2 = (f32[10,32,128]{2,1,0:T(8,128)S(1)}, f32[10,32,128]{2,1,0:T(8,128)S(1)}, u32[]{:S(2)}, u32[]{:S(2)}) collective-permute-start(f32[10,32,128]{2,1,0:T(8,128)S(1)} %shard_map.83.refs_0_.refs_3_), channel_id=1, source_target_pairs={{0,1},{1,0},{2,3},{3,2},{4,5},{5,4},{6,7},{7,6},{8,9},{9,8},{10,11... | collective-permute-start | bytes 491528 | tf_op jit(solution)/shard_map/ppermute | solution.py:579
  14.3 1.4 %collective-permute-start.4 = (f32[10,32,128]{2,1,0:T(8,128)S(1)}, f32[10,32,128]{2,1,0:T(8,128)S(1)}, u32[]{:S(2)}, u32[]{:S(2)}) collective-permute-start(f32[10,32,128]{2,1,0:T(8,128)S(1)} %collective-permute-done.3.refs_2_.refs_5_), channel_id=1, source_target_pairs={{0,1},{1,0},{2,3},{3,2},{4,5},{5,4},{6,7},{7,6},{8,9},{9,8},{10,11... | collective-permute-start | bytes 491528 | tf_op jit(solution)/shard_map/ppermute | solution.py:579
  16.0 8.8 %copy-start.1 = (bf16[8,1,520,256]{3,2,1,0:T(8,128)(2,1)S(1)}, bf16[8,1,520,256]{3,2,1,0:T(8,128)(2,1)}, u32[]{:S(2)}) copy-start(bf16[8,1,520,256]{3,2,1,0:T(8,128)(2,1)} %factor_ref.1) | copy-start | bytes 6389764
  16.0 9.6 %collective-permute-start.7 = (f32[3,32,128]{2,1,0:T(8,128)S(1)}, f32[3,32,128]{2,1,0:T(8,128)S(1)}, u32[]{:S(2)}, u32[]{:S(2)}) collective-permute-start(f32[3,32,128]{2,1,0:T(8,128)S(1)} %shard_map.84.refs_0_), channel_id=1, source_target_pairs={{0,24},{1,25},{2,26},{3,27},{4,28},{5,29},{6,30},{7,31},{8,16},{9,... | collective-permute-start | bytes 147464 | tf_op jit(solution)/shard_map/ppermute | solution.py:624
  20.4 4.4 %collective-permute-start.5 = (f32[3,32,128]{2,1,0:T(8,128)S(1)}, f32[3,32,128]{2,1,0:T(8,128)S(1)}, u32[]{:S(2)}, u32[]{:S(2)}) collective-permute-start(f32[3,32,128]{2,1,0:T(8,128)S(1)} %shard_map.84.refs_0_), channel_id=1, source_target_pairs={{0,8},{1,17},{2,10},{3,19},{4,12},{5,21},{6,14},{7,23},{8,0},{9,25... | collective-permute-start | bytes 147464 | tf_op jit(solution)/shard_map/ppermute | solution.py:624
  22.5 4.4 %collective-permute-start.8 = (f32[3,32,128]{2,1,0:T(8,128)S(1)}, f32[3,32,128]{2,1,0:T(8,128)S(1)}, u32[]{:S(2)}, u32[]{:S(2)}) collective-permute-start(f32[3,32,128]{2,1,0:T(8,128)S(1)} %get-tuple-element.29), channel_id=1, source_target_pairs={{0,4},{1,5},{2,0},{3,1},{4,8},{5,9},{6,2},{7,3},{8,12},{9,13},{10,... | collective-permute-start | bytes 147464 | tf_op jit(solution)/shard_map/ppermute | solution.py:576
  23.8 4.3 %collective-permute-start.9 = (f32[3,32,128]{2,1,0:T(8,128)S(1)}, f32[3,32,128]{2,1,0:T(8,128)S(1)}, u32[]{:S(2)}, u32[]{:S(2)}) collective-permute-start(f32[3,32,128]{2,1,0:T(8,128)S(1)} %get-tuple-element.30), channel_id=1, source_target_pairs={{4,0},{5,1},{0,2},{1,3},{8,4},{9,5},{2,6},{3,7},{12,8},{13,9},{6,1... | collective-permute-start | bytes 147464 | tf_op jit(solution)/shard_map/ppermute | solution.py:576
  24.8 1.2 %collective-permute-start.6 = (f32[3,32,128]{2,1,0:T(8,128)S(1)}, f32[3,32,128]{2,1,0:T(8,128)S(1)}, u32[]{:S(2)}, u32[]{:S(2)}) collective-permute-start(f32[3,32,128]{2,1,0:T(8,128)S(1)} %collective-permute-done.5.refs_1_), channel_id=1, source_target_pairs={{0,1},{1,0},{2,3},{3,2},{4,5},{5,4},{6,7},{7,6},{8,9},{9,8},{10,11... | collective-permute-start | bytes 147464 | tf_op jit(solution)/shard_map/ppermute | solution.py:579
  24.8 1.2 %copy-start.5 = (bf16[4,1,136,64]{2,3,1,0:T(8,128)(2,1)S(1)}, bf16[4,1,136,64]{2,3,1,0:T(8,128)(2,1)}, u32[]{:S(2)}) copy-start(bf16[4,1,136,64]{2,3,1,0:T(8,128)(2,1)} %param.13) | copy-start | bytes 208900
  24.8 1.2 %copy-start.7 = (bf16[64,64]{1,0:T(8,128)(2,1)S(1)}, bf16[64,64]{1,0:T(8,128)(2,1)}, u32[]{:S(2)}) copy-start(bf16[64,64]{1,0:T(8,128)(2,1)} %inverse_ref.1) | copy-start | bytes 24580

commit v5 on v4

--- a/solution.py
+++ b/solution.py
@@ -48,8 +48,14 @@
         self.tile = [f[3] // 2 for f in factors]
         self.tiles = [f[1] for f in factors]
         self.slots = self.h[1] + 2
-        self.offset = [None, 0, self.w[1] + 2, self.w[1] + self.w[2] + 4]
-        self.spare = self.w[1] + self.w[2] + self.w[3] + 6
+        self.offset = [None, 0]
+        for l in (2, 3, 4):
+            self.offset.append(self.offset[-1] + self.w[l - 1] + 2)
+        self.whole = self.h[2] + 2
+        self.sent = self.whole + 2
+        self.sides = (self.h0 + 2) // 2
+        self.first = self.w[1] + 2
+        self.rest = LANES - self.first
 
     def place(self, level, lead, width, at=0):
         out = np.zeros((self.m, LANES, width))
@@ -60,13 +66,41 @@
                     out[c, self.offset[level] + k, at + column + lead] = 1
         return out
 
+    def place_tail(self):
+        whole = self.place(1, 1, round_up(self.ny[1] + 2))
+        out = np.zeros((self.m, 2) + whole.shape[1:])
+        out[:, 0, self.first :] = whole[:, : self.rest]
+        tail = self.first - self.rest
+        out[:, 1, self.offset[4] : self.offset[4] + tail] = whole[:, self.rest : self.first]
+        return out.reshape(self.m, 2 * LANES, -1)
+
+    def place_four(self):
+        rows = [self.place(4, 0, 4 * self.ny[4], j * self.ny[4]) for j in range(4)]
+        return np.stack(rows, axis=1)
+
     def halo_lanes(self):
-        out = np.zeros((2, LANES, 2 * LANES))
-        for k in range(2):
+        out = np.zeros((2, LANES, self.sides, LANES))
+        for j in range(self.sides):
             for position in range(4):
-                out[0, self.spare + 2 * k + 1, LANES * k + 2 * position] = 1
-                out[1, self.spare + 2 * k, LANES * k + 2 * position + 1] = 1
-        return bf(out)
+                out[0, self.offset[3] + 2 * j, j, 2 * position] = 1
+                out[1, self.offset[3] + 2 * j + 1, j, 2 * position + 1] = 1
+        return out.reshape(2, LANES, self.sides * LANES)
+
+    def pick_band(self):
+        out = []
+        for l in (1, 2, 3):
+            pick = np.zeros((self.m, round_up(self.ny[l]), LANES))
+            one = self.place(l, 0, self.ny[l])
+            pick[:, : self.ny[l]] = one.transpose(0, 2, 1)
+            out.append(pick)
+        return np.concatenate(out, axis=1)
+
+    def lift_band(self):
+        out = []
+        for l in (1, 2, 3):
+            one = self.place(l, 0, self.ny[l])
+            out.append(np.einsum("cki,cif->ckf", one, self.lift_columns(l)))
+        return np.concatenate(out, axis=2)
 
     def lift_columns(self, level):
         out = np.eye(self.ny[level])
@@ -81,16 +115,6 @@
         for j in range(2):
             out[:, j, :, j * w : (j + 1) * w] = full
         return out
-
-    def coarse_shrink(self):
-        ny3, ny4 = self.ny[3], self.ny[4]
-        columns = global_prolong(ny4).T
-        width = round_up(ny4 + 2)
-        out = np.zeros((2, 2, ny3, width))
-        for side, taps in enumerate(((1, 3), (3, 1))):
-            for j in range(2):
-                out[side, j, :, 1 : 1 + ny4] = taps[j] * columns
-        return bf(out.reshape(4 * ny3, width))
 
     def coarsest_shrink(self):
         nx5, ny5, ny4 = self.nx[5], self.ny[5], self.ny[4]
@@ -250,12 +274,16 @@
     return value.astype(BF16)
 
 
-def side_matrix(plan, k):
-    row = lax.broadcasted_iota(jnp.int32, (LANES, LANES), 0)
-    lane = lax.broadcasted_iota(jnp.int32, (LANES, LANES), 1) - plan.spare - 2 * k
-    left = jnp.logical_and(row == 0, lane == 0)
-    right = jnp.logical_and(row == plan.w0 - 1, lane == 1)
-    return jnp.where(jnp.logical_or(left, right), 1.0, 0.0).astype(BF16)
+def place_sides(plan, slot_value, row, index):
+    at = plan.offset[3] + 2 * (index % plan.sides)
+    lane = lane_index(plan.rhs)
+    chosen = jnp.logical_or(lane == at, lane == at + 1)
+    return jnp.where(chosen, pltpu.roll(row, (at + 1) % LANES, 1), slot_value)
+
+
+def column_ends(plan):
+    c = lax.axis_index("py")
+    return jnp.where(c == 0, 1, 0), jnp.where(c == plan.m - 1, 1, 0)
 
 
 def write_halos(c, down, up, first_ref, second_ref):
@@ -277,11 +305,10 @@
 def restrict_kernel(plan, x_ref, own_ref, first_ref, second_ref, rows_ref):
     r, c = lax.axis_index("px"), lax.axis_index("py")
     rhs, slots, h = plan.rhs, plan.slots, plan.h
-    first = jnp.where(c == 0, 1, 0)
-    last = jnp.where(c == plan.m - 1, 1, 0)
+    first, last = column_ends(plan)
     shrink = None
     matrices = []
-    for level in (1, 2, 3):
+    for level in (1, 2, 3, 4):
         lead = 0 if level == 1 else plan.offset[level - 1] + 1
         step = tap_matrix(lead, plan.offset[level], plan.w[level], first, last)
         if shrink is None:
@@ -295,7 +322,7 @@
     for i, row in enumerate(x):
         rows_ref[i] = row
     rows, total = x, None
-    for level in (1, 2, 3):
+    for level in (1, 2, 3, 4):
         rows = shrink_rows(rows, h[level - 1], 0 if level == 1 else 1)
         rows[0] = rows[0] * above
         rows[-1] = rows[-1] * below
@@ -305,56 +332,70 @@
         else:
             count = part.shape[0]
             total = jnp.concatenate([total[:count] + part, total[count:]], axis=0)
-    sides = [jnp.zeros_like(x[0])] + x[: slots - 1]
-    total = total + jnp.dot(
-        jnp.concatenate(sides, axis=0).astype(BF16), side_matrix(plan, 0),
-        preferred_element_type=F32,
-    )
-    rest = jnp.concatenate(x[slots - 1 :], axis=0).astype(BF16)
-    more = jnp.dot(rest, side_matrix(plan, 1), preferred_element_type=F32)
-    count = more.shape[0]
-    total = jnp.concatenate([total[:count] + more, total[count:]], axis=0)
     lane = lane_index(slots * rhs)
-    one, two = plan.offset[2], plan.offset[3]
-    scale = jnp.where(lane < two, SHRINK**2, jnp.where(lane < plan.spare, SHRINK**3, 1.0))
-    total = total * jnp.where(lane < one, SHRINK, scale)
-    own = total.reshape(slots, rhs, LANES)
-    own_ref[...] = own
+    scale = jnp.where(lane < plan.offset[2], SHRINK, SHRINK**2)
+    scale = jnp.where(lane < plan.offset[3], scale, SHRINK**3)
+    total = total * jnp.where(lane < plan.offset[4], scale, SHRINK**4)
+    own = [total[i * rhs : (i + 1) * rhs] for i in range(slots)]
+    for i, row in enumerate(x):
+        slot = plan.h[2] + (i + 1) // plan.sides
+        own[slot] = place_sides(plan, own[slot], row, i + 1)
+    for i, value in enumerate(own):
+        own_ref[i] = value
     lane = lane_index(rhs)
-    down, up = [x[-1]], [x[0]]
+    one, two, three = plan.offset[2:]
+    third = pltpu.roll(own[2], LANES - three, 1)
+    down = [x[-1]]
     for k in range(2):
-        three_own = own[h[3] + k]
-        down.append(
-            jnp.where(lane < one, own[h[1] + k], jnp.where(lane < two, own[h[2] + k], three_own))
-        )
-        up.append(own[k])
-    write_halos(c, down + [own[1]], up + [own[h[3]]], first_ref, second_ref)
+        value = jnp.where(lane < three, own[h[3] + k], own[k])
+        value = jnp.where(lane < two, own[h[2] + k], value)
+        down.append(jnp.where(lane < one, third if k else own[h[1]], value))
+    up = [x[0], jnp.where(lane < one, third, own[0]), own[1]]
+    write_halos(c, down, up, first_ref, second_ref)
 
 
 def merge_kernel(plan, own_ref, first_ref, second_ref, out_ref):
-    r = lax.axis_index("px")
-    rhs, h = plan.rhs, plan.h
+    r, h, rhs = lax.axis_index("px"), plan.h, plan.rhs
     lane = lane_index(rhs)
     above, below = read_halos(plan, first_ref, second_ref)
-    one, two, end = plan.offset[2], plan.offset[3], plan.spare
-    out_ref[...] = own_ref[...]
+    one, two, three = plan.offset[2:]
+    slot = [own_ref[i] for i in range(plan.slots)]
+    matrix = tap_matrix(0, 0, plan.w[1], *column_ends(plan))
+    outer = product(jnp.concatenate([above[0], below[0]], axis=0), matrix) * SHRINK
+    from_above, from_below = outer[:rhs], outer[rhs:]
+    slot[0] = slot[0] + jnp.where(lane < three, above[1], 0.0)
+    value = jnp.where(lane < one, from_above, above[2])
+    slot[1] = slot[1] + jnp.where(lane < three, value, 0.0)
     for k in range(2):
-        out_ref[k] = out_ref[k] + jnp.where(lane < end, above[1 + k], 0.0)
-        for level, low, high in ((1, 0, one), (2, one, two), (3, two, end)):
+        value = from_below if k == 0 else below[2]
+        pieces = ((1, 0, one, value), (2, one, two, below[1 + k]), (3, two, three, below[1 + k]))
+        for level, low, high, piece in pieces:
+            chosen = jnp.logical_and(lane >= low, lane < high)
             row = h[level] + k
-            chosen = jnp.logical_and(lane >= low, lane < high)
-            out_ref[row] = out_ref[row] + jnp.where(chosen, below[1 + k], 0.0)
-    odd = lax.rem(r, 2) == 1
-    row = jnp.where(odd, above[3], below[3])
-    ends = jnp.where(r == jnp.where(odd, 1, plan.n - 2), 1.0, 0.0).astype(F32)
-    chosen = jnp.logical_and(lane >= two, lane < end)
-    at = h[3] + 2
-    out_ref[at] = out_ref[at] + jnp.where(chosen, row * ends, 0.0)
-    top = above[0].astype(BF16)
-    out_ref[0] = out_ref[0] + jnp.dot(top, side_matrix(plan, 0), preferred_element_type=F32)
-    bottom = below[0].astype(BF16)
-    at = h[0] + 1 - plan.slots
-    out_ref[at] = out_ref[at] + jnp.dot(bottom, side_matrix(plan, 1), preferred_element_type=F32)
+            slot[row] = slot[row] + jnp.where(chosen, piece, 0.0)
+    even = lax.rem(r, 2) == 0
+    own = [own_ref[k] for k in range(3)]
+    partner = [jnp.where(even, below[k], above[k]) for k in (1, 2)]
+    third = jnp.where(even, below[1], above[2])
+    partner.append(pltpu.roll(third, three, 1))
+    low = [jnp.where(even, a, b) for a, b in zip(own, partner)]
+    high = [jnp.where(even, b, a) for a, b in zip(own, partner)]
+    sums = [low[0], low[1] + high[0], low[2] + high[1], high[2]]
+    for k in range(4):
+        slot[k] = jnp.where(lane < three, slot[k], sums[k])
+    sides = plan.h[2]
+    slot[sides] = place_sides(plan, slot[sides], above[0], 0)
+    slot[sides + 1] = place_sides(plan, slot[sides + 1], below[0], plan.h0 + 1)
+    tail = plan.first - plan.rest
+    for k in range(2):
+        even_row, odd_row = slot[plan.whole + 2 * k], slot[plan.whole + 2 * k + 1]
+        chosen = jnp.logical_and(lane >= three, lane < three + tail)
+        moved = pltpu.roll(odd_row, (three - plan.rest) % LANES, 1)
+        slot[sides + k] = jnp.where(chosen, moved, slot[sides + k])
+        moved = pltpu.roll(odd_row, plan.first, 1)
+        out_ref[plan.whole + k] = jnp.where(lane < plan.first, even_row, moved)
+    for k in range(plan.whole):
+        out_ref[k] = slot[k]
 
 
 def banded(bands, matrices):
@@ -368,22 +409,30 @@
 
 def gather_kernel(plan, blocks, block_ref, *refs):
     band_refs, out_ref = refs[:-1], refs[-1]
-    rhs = plan.rhs
     values, matrices = [], []
     for band, owner in zip(band_refs, owners(plan)):
-        for j in range(2):
-            values.append(jnp.concatenate([band[j], band[2 + j], band[4]], axis=0))
-            matrices.append(blocks.get(block_ref, "pairs", 2 * owner + j))
-    total = banded(values, matrices)
-    for half in range(3):
-        out_ref[half] = total[half * rhs : (half + 1) * rhs]
+        for j in range(4):
+            values.append(band[j])
+            matrices.append(blocks.get(block_ref, "four", 4 * owner + j))
+    out_ref[...] = banded(values, matrices)
 
 
 def level_rows(plan, level, band_refs, blocks, block_ref):
-    rhs, count = plan.rhs, plan.h[level] + 2
+    rhs = plan.rhs
+    count = plan.sent if level == 1 else plan.h[level] + 2
     values = [band[:count].reshape(count * rhs, LANES) for band in band_refs]
     matrices = [blocks.get(block_ref, f"place{level}", owner) for owner in owners(plan)]
-    return banded(values, matrices)
+    whole = banded(values, matrices)
+    rows = [whole[i * rhs : (i + 1) * rhs] for i in range(count)]
+    if level > 1:
+        return rows
+    values, at = [], plan.whole
+    for band in band_refs:
+        pair = [band[at : at + 2], band[at - 2 : at]]
+        values.append(jnp.concatenate([v.reshape(2 * rhs, LANES) for v in pair], axis=1))
+    matrices = [blocks.get(block_ref, "tail", owner) for owner in owners(plan)]
+    odd = banded(values, matrices)
+    return rows[:at] + [rows[at], odd[:rhs], rows[at + 1], odd[rhs:]]
 
 
 def coarse_kernel(plan, blocks, block_ref, *refs):
@@ -392,9 +441,7 @@
     down, up = [], []
     for level in (1, 2, 3):
         w, tiles = plan.tile[level], plan.tiles[level]
-        whole = level_rows(plan, level, bands, blocks, block_ref)
-        count = plan.h[level] + 2
-        rows = [whole[i * rhs : (i + 1) * rhs] for i in range(count)]
+        rows = level_rows(plan, level, bands, blocks, block_ref)
         factor_ref, out_ref = factors[level - 1], outs[level - 1]
         solved = [[] for _ in range(tiles)]
         for b in range(plan.h[level] // 2):
@@ -419,24 +466,31 @@
         for b in range(pairs):
             for j in range(2):
                 out_ref[2 * b + j] = lifted[j][b * rhs : (b + 1) * rhs]
-        down.append(lifted[1][(pairs - 1) * rhs :])
-        up.append(lifted[0][:rhs])
-    write_halos(c, down, up, outs[3], outs[4])
+        for j, (edge, at) in enumerate(((up, 0), (down, pairs - 1))):
+            for value in solved:
+                if w % LANES == 0:
+                    edge.append(value[at][:, j * w : (j + 1) * w])
+                else:
+                    edge.append(pltpu.roll(value[at], LANES - w, 1) if j else value[at])
+    edges = [jnp.concatenate(edge, axis=1) for edge in (down, up)]
+    picked = product(jnp.concatenate(edges, axis=0), blocks.get(block_ref, "pick", c))
+    write_halos(c, [picked[:rhs]], [picked[rhs:]], outs[3], outs[4])
 
 
 def fine_kernel(plan, blocks, block_ref, rows_ref, first_ref, second_ref, factor_ref, *refs):
     bands, out_ref = refs[: plan.m], refs[plan.m]
     c = lax.axis_index("py")
-    rhs, h0, w0, slots = plan.rhs, plan.h0, plan.w0, plan.slots
+    rhs, h0, w0 = plan.rhs, plan.h0, plan.w0
     above, below = read_halos(plan, first_ref, second_ref)
     values, matrices = [], []
     left = blocks.get(block_ref, "halo", 0)
     right = blocks.get(block_ref, "halo", 1)
+    at = plan.h[2]
     for band, owner in zip(bands, owners(plan)):
         from_left = jnp.where(owner == c - 1, 1.0, 0.0).astype(BF16)
         from_right = jnp.where(owner == c + 1, 1.0, 0.0).astype(BF16)
         matrices.append(left * from_left + right * from_right)
-        values.append(band[...].reshape(slots * rhs, LANES).astype(BF16))
+        values.append(band[at : at + 2].reshape(2 * rhs, LANES).astype(BF16))
     halo = jnp.dot(
         jnp.concatenate(values, axis=1), jnp.concatenate(matrices, axis=0),
         preferred_element_type=F32,
@@ -450,7 +504,7 @@
             rows.append(below[0])
         else:
             rows.append(rows_ref[row])
-        part, slot = divmod(row + 1, slots)
+        slot, part = divmod(row + 1, plan.sides)
         sides.append(halo[slot * rhs : (slot + 1) * rhs, part * LANES : (part + 1) * LANES])
     for b in range(h0 // 2):
         tiles, before = [], None
@@ -477,11 +531,9 @@
     count = plan.n // 2
     gathered, out_ref, pair_ref, four_rows = refs[:count], refs[count], refs[-2], refs[-1]
     r, c = lax.axis_index("px"), lax.axis_index("py")
-    rhs, n, ny3, ny4 = plan.rhs, plan.n, plan.ny[3], plan.ny[4]
+    rhs, ny4 = plan.rhs, plan.ny[4]
     nx4, nx5 = plan.nx[4], plan.nx[5]
     odd = jnp.bitwise_and(c, 1)
-    even = lax.rem(r, 2) == 0
-    lane = lax.broadcasted_iota(jnp.int32, (rhs, 2 * ny3), 1)
     for k, block in enumerate(gathered):
         if k == 0 or (k == count - 1 and k % 2):
             partner = 2 * k
@@ -489,17 +541,25 @@
             partner = 2 * (k + odd)
         else:
             partner = 2 * (k - odd)
-        row = jnp.bitwise_xor(r, partner)
-        pair_ref[row] = block[0]
-        pair_ref[row + 1] = block[1]
-        at = jnp.where(even, jnp.where(row == n - 2, n, n + 1), jnp.where(row == 1, 0, n + 1))
-        pair_ref[at] = jnp.where((lane < ny3) == even, block[2], 0.0)
-    low = pair_ref[0:n].reshape(n * rhs, 2 * ny3)
-    high = pair_ref[1 : n + 1].reshape(n * rhs, 2 * ny3)
-    both = jnp.concatenate([low, high], axis=1)
-    four = product(both, blocks.get(block_ref, "shrink4")) * SHRINK
-    zero = jnp.zeros((rhs, four.shape[1]), F32)
-    rows = [zero] + [four[i * rhs : (i + 1) * rhs] for i in range(nx4)] + [zero]
+        pair_ref[jnp.bitwise_xor(r, partner) // 2] = block[...]
+    lane = lane_index(rhs)
+    inside = jnp.logical_and(lane >= 1, lane <= ny4)
+
+    def part_row(pair, j):
+        tile, start = divmod(j * ny4, LANES)
+        value = pair_ref[pair, :, tile * LANES : (tile + 1) * LANES]
+        return jnp.where(inside, pltpu.roll(value, (1 - start) % LANES, 1), 0.0)
+
+    zero = jnp.zeros((rhs, LANES), F32)
+    rows = [zero]
+    for i in range(nx4):
+        value = part_row(i // 2, 1 + i % 2)
+        if i % 2 == 0 and i > 0:
+            value = value + part_row(i // 2 - 1, 3)
+        if i % 2 == 1 and i < nx4 - 1:
+            value = value + part_row(i // 2 + 1, 0)
+        rows.append(value)
+    rows.append(zero)
     five = shrink_rows(rows, nx4, 1)[1:-1]
     flat = product(jnp.concatenate(five, axis=1), blocks.get(block_ref, "shrink5")) * SHRINK
     flat = flat[:, : inverse_ref.shape[0]]
@@ -537,12 +597,20 @@
         out_ref[k] = four_rows[r + k]
 
 
-def final_kernel(plan, fine_ref, one_ref, two_ref, three_ref, four_ref, first_ref, second_ref,
-                 out_ref):
+def final_kernel(plan, blocks, block_ref, fine_ref, one_ref, two_ref, three_ref, four_ref,
+                 first_ref, second_ref, out_ref):
     r, rhs = lax.axis_index("px"), plan.rhs
     above = jnp.where(r > 0, 1.0, 0.0).astype(F32)
     below = jnp.where(r < plan.n - 1, 1.0, 0.0).astype(F32)
-    from_above, from_below = read_halos(plan, first_ref, second_ref)
+    halos = read_halos(plan, first_ref, second_ref)
+    halo = product(
+        jnp.concatenate([halos[0][0], halos[1][0]], axis=0),
+        blocks.get(block_ref, "band", lax.axis_index("py")),
+    )
+    from_above, from_below = [
+        [halo[k * rhs : (k + 1) * rhs, l * plan.w0 : (l + 1) * plan.w0] for l in range(3)]
+        for k in range(2)
+    ]
     rows = [four_ref[k] for k in range(3)]
     for level, own_ref in ((3, three_ref), (2, two_ref), (1, one_ref)):
         height = plan.h[level]
@@ -578,10 +646,11 @@
     def swap(value, bits):
         return lax.ppermute(value, "py", [(i, i ^ bits) for i in range(m)])
 
-    width3 = 2 * plan.ny[3]
     blocks = Blocks()
-    pairs = [plan.place(3, 0, width3, j * plan.ny[3]) for j in range(2)]
-    blocks.add("pairs", np.stack(pairs, axis=1))
+    blocks.add("four", plan.place_four())
+    blocks.add("tail", plan.place_tail())
+    blocks.add("pick", plan.pick_band())
+    blocks.add("band", plan.lift_band())
     for l in (1, 2, 3):
         blocks.add(f"place{l}", plan.place(l, 1, round_up(plan.ny[l] + 2)))
         if plan.tile[l] % LANES == 0:
@@ -592,18 +661,17 @@
     lifted, group = plan.level_four_lift()
     blocks.add("lift4", lifted)
     blocks.add("halo", plan.halo_lanes())
-    blocks.add("shrink4", plan.coarse_shrink())
     blocks.add("shrink5", plan.coarsest_shrink())
     blocks.add("lift5", plan.coarsest_lift())
     matrices = blocks.array()
 
     own, first, second, rows = kernel_call(
         functools.partial(restrict_kernel, plan),
-        (shape(plan.slots, rhs, LANES), shape(4, rhs, LANES), shape(4, rhs, LANES),
+        (shape(plan.slots, rhs, LANES), shape(3, rhs, LANES), shape(3, rhs, LANES),
          shape(h0, rhs, plan.w0)),
     )(x)
     first, second = trade(first, second)
-    band = kernel_call(functools.partial(merge_kernel, plan), shape(plan.slots, rhs, LANES))(
+    band = kernel_call(functools.partial(merge_kernel, plan), shape(plan.sent, rhs, LANES))(
         own, first, second
     )
     bands = {0: band}
@@ -614,7 +682,7 @@
     bands = [bands[k] for k in range(m)]
 
     pairs = kernel_call(
-        functools.partial(gather_kernel, plan, blocks), shape(3, rhs, width3), cost_us=0.3
+        functools.partial(gather_kernel, plan, blocks), shape(rhs, 4 * plan.ny[4]), cost_us=0.3
     )(matrices, *bands)
     order, gathered = list(range(1, n // 2)), [pairs]
     fetched = []
@@ -636,7 +704,7 @@
     one, two, three, low, high = kernel_call(
         functools.partial(coarse_kernel, plan, blocks),
         tuple(shape(h[l], rhs, LANES) for l in (1, 2, 3))
-        + (shape(3, rhs, LANES), shape(3, rhs, LANES)),
+        + (shape(1, rhs, LANES), shape(1, rhs, LANES)),
         cost_us=2.5,
     )(matrices, factor_one, factor_two, factor_three, *bands)
     low, high = trade(low, high)
@@ -648,12 +716,12 @@
         functools.partial(whole_kernel, plan, group, blocks),
         shape(3, rhs, LANES),
         scratch=(
-            pltpu.VMEM((n + 2, rhs, width3), F32),
+            pltpu.VMEM((n // 2, rhs, 4 * plan.ny[4]), F32),
             pltpu.VMEM((plan.nx[4] + 2, rhs, LANES), F32),
         ),
     )(matrices, jnp.swapaxes(factor_four, 2, 3), coarse_inverse, *gathered)
-    out = kernel_call(functools.partial(final_kernel, plan), shape(rhs * h0, plan.w0))(
-        fine, one, two, three, four, low, high
+    out = kernel_call(functools.partial(final_kernel, plan, blocks), shape(rhs * h0, plan.w0))(
+        matrices, fine, one, two, three, four, low, high
     )
     return out.reshape(rhs, h0, plan.w0)
 

time: 29.1 us -> 28.2 us (0.969)
  starting transfers between devices: 9.79 us -> 9.22 us
  waiting for transfers between devices: 12.4 us -> 12 us
    ppermute x2, starting transfers between devices: 4.27 us -> 4.73 us  [trade(): lax.ppermute(first, ('px', 'py'), ring)]
    ppermute x2, starting transfers between devices: 4.38 us -> 3.93 us  [per_device(): lax.ppermute(pairs, ('px', 'py'), [(i * m + c, (i ^ 2 * (odd if c % 2 els...]
    ppermute x2, starting transfers between devices: 0.82 us -> 0.41 us  [trade(): lax.ppermute(second, ('px', 'py'), back)]
  transfers between devices with their start and end apart: 10 -> 10, of which waited for: 7 -> 6; matrix products, arithmetic and copies ran while one was open for 0% -> 0% of each run, Pallas kernels for 14% -> 13%
where the time goes in v5:
time: 28.2 us; the launch traced here: 28.1 us
  waiting for transfers between devices  12 us (43%)
  starting transfers between devices  9.22 us (33%)
  Pallas kernels  5.7 us (20%)
  local copies, waits for them, and re-layouts  0.99 us (4%)
    ppermute x4, waiting for transfers between devices, swap(): return lax.ppermute(value, 'py', [(i, i ^ bits) for i in range(m)])  6.6 us
    pallas_call x7, Pallas kernels, call(): pl.pallas_call(body, out_shape=out_shape, in_specs=[whole] * len(operands...  5.7 us
    ppermute x2, starting transfers between devices, trade(): lax.ppermute(first, ('px', 'py'), ring)  4.73 us
    ppermute x2, starting transfers between devices, per_device(): lax.ppermute(pairs, ('px', 'py'), [(i * m + c, (i ^ 2 * (odd if c % 2 els...  3.93 us
    ppermute x2, waiting for transfers between devices, trade(): lax.ppermute(second, ('px', 'py'), back)  3.42 us
    ppermute x2, waiting for transfers between devices, trade(): lax.ppermute(first, ('px', 'py'), ring)  2.02 us
    unnamed x16, local copies, waits for them, and re-layouts  0.99 us
  transfers between devices with their start and end apart: 10, of which 6 were waited for; matrix products, arithmetic and copies ran while one was open for 0% of the time, Pallas kernels for 13%

profile of v5, /device:TPU:0, one launch (start us, length us, event | category | flops | bytes accessed | tf_op | source)
XLA Modules:
  0.0 28.1 jit_solution(5455981711258700224)
XLA Ops:
  0.0 0.0 copy-start.6
  0.0 0.9 %copy-done.6 = f32[32,16,128]{2,1,0:T(8,128)S(1)} copy-done((f32[32,16,128]{2,1,0:T(8,128)S(1)}, f32[32,16,128]{2,1,0:T(8,128)}, u32[]{:S(2)}) %copy-start.6) | copy-done | bytes 262168
  1.0 0.0 copy-start
  1.0 0.6 %shard_map.82 = (f32[10,32,128]{2,1,0:T(8,128)S(1)}, f32[3,32,128]{2,1,0:T(8,128)S(1)}, f32[3,32,128]{2,1,0:T(8,128)S(1)}, f32[16,32,128]{2,1,0:T(8,128)S(1)}) custom-call(f32[512,128]{1,0:T(8,128)S(1)} %bitcast.4), custom_call_target="tpu_custom_call" | custom-call | flops 1000000000 | bytes 3000000 | tf_op jit(solution)/shard_map/pallas_call | solution.py:247
  1.6 3.0 %collective-permute-start = (f32[3,32,128]{2,1,0:T(8,128)S(1)}, f32[3,32,128]{2,1,0:T(8,128)S(1)}, u32[]{:S(2)}, u32[]{:S(2)}) collective-permute-start(f32[3,32,128]{2,1,0:T(8,128)S(1)} %get-tuple-element.19), channel_id=1, source_target_pairs={{0,4},{1,5},{2,0},{3,1},{4,8},{5,9},{6,2},{7,3},{8,12},{9,13},{10,... | collective-permute-start | bytes 147464 | tf_op jit(solution)/shard_map/ppermute | solution.py:644
  4.5 0.0 collective-permute-start.1
  4.6 2.0 %collective-permute-done.first_ref = f32[3,32,128]{2,1,0:T(8,128)S(1)} collective-permute-done((f32[3,32,128]{2,1,0:T(8,128)S(1)}, f32[3,32,128]{2,1,0:T(8,128)S(1)}, u32[]{:S(2)}, u32[]{:S(2)}) %collective-permute-start) | collective-permute-done | bytes 49184 | tf_op jit(solution)/shard_map/ppermute | solution.py:644
  6.6 2.1 %collective-permute-done.1.second_ref = f32[3,32,128]{2,1,0:T(8,128)S(1)} collective-permute-done((f32[3,32,128]{2,1,0:T(8,128)S(1)}, f32[3,32,128]{2,1,0:T(8,128)S(1)}, u32[]{:S(2)}, u32[]{:S(2)}) %collective-permute-start.1) | collective-permute-done | bytes 49184 | tf_op jit(solution)/shard_map/ppermute | solution.py:644
  8.6 0.2 shard_map.83.refs_0_.refs_3_
  8.8 0.0 copy-start.4
  8.8 0.0 copy-start.5
  8.8 0.0 copy-start.7
  8.8 0.1 collective-permute-start.3
  8.9 0.1 collective-permute-start.2
  9.0 4.9 %collective-permute-done.3.refs_2_.refs_5_ = f32[8,32,128]{2,1,0:T(8,128)S(1)} collective-permute-done((f32[8,32,128]{2,1,0:T(8,128)S(1)}, f32[8,32,128]{2,1,0:T(8,128)S(1)}, u32[]{:S(2)}, u32[]{:S(2)}) %collective-permute-start.3) | collective-permute-done | bytes 131104 | tf_op jit(solution)/shard_map/ppermute | solution.py:647
  13.9 0.0 collective-permute-start.4
  13.9 0.0 collective-permute-done.2.refs_1_.refs_4_
  13.9 1.3 %collective-permute-done.4.refs_3_.refs_6_ = f32[8,32,128]{2,1,0:T(8,128)S(1)} collective-permute-done((f32[8,32,128]{2,1,0:T(8,128)S(1)}, f32[8,32,128]{2,1,0:T(8,128)S(1)}, u32[]{:S(2)}, u32[]{:S(2)}) %collective-permute-start.4) | collective-permute-done | bytes 131104 | tf_op jit(solution)/shard_map/ppermute | solution.py:647
  15.2 0.0 copy-done
  15.2 0.2 shard_map.84.refs_0_
  15.4 0.0 copy-start.1
  15.5 3.9 %collective-permute-start.7 = (f32[32,128]{1,0:T(8,128)S(1)}, f32[32,128]{1,0:T(8,128)S(1)}, u32[]{:S(2)}, u32[]{:S(2)}) collective-permute-start(f32[32,128]{1,0:T(8,128)S(1)} %shard_map.84.refs_0_), channel_id=1, source_target_pairs={{0,24},{1,25},{2,26},{3,27},{4,28},{5,29},{6,30},{7,31},{8,16},{9,... | collective-permute-start | bytes 49160 | tf_op jit(solution)/shard_map/ppermute | solution.py:692
  19.4 0.0 collective-permute-start.5
  19.4 0.0 copy-done.4
  19.4 0.0 copy-done.5
  19.4 0.0 copy-done.7
  19.4 2.2 %shard_map.86 = (f32[8,32,128]{2,1,0:T(8,128)S(1)}, f32[4,32,128]{2,1,0:T(8,128)S(1)}, f32[2,32,128]{2,1,0:T(8,128)S(1)}, f32[1,32,128]{2,1,0:T(8,128)S(1)}, f32[1,32,128]{2,1,0:T(8,128)S(1)}) custom-call(bf16[152,128,128]{2,1,0:T(8,128)(2,1)S(1)} %copy-done, bf16[4,2,520,256]{3,2,1,0:T(8,128)(2,1)S(1)} %copy-done.4, bf16[2,1,520,256]{3,2,1,0:T(8,128)(2,1)S(1)} %copy-done.5, ...), custom_call_target="tpu_custom_call" | custom-call | flops 2500000000 | bytes 7500000 | tf_op jit(solution)/shard_map/pallas_call | solution.py:247
  21.6 1.8 %collective-permute-start.8 = (f32[1,32,128]{2,1,0:T(8,128)S(1)}, f32[1,32,128]{2,1,0:T(8,128)S(1)}, u32[]{:S(2)}, u32[]{:S(2)}) collective-permute-start(f32[1,32,128]{2,1,0:T(8,128)S(1)} %get-tuple-element.29), channel_id=1, source_target_pairs={{0,4},{1,5},{2,0},{3,1},{4,8},{5,9},{6,2},{7,3},{8,12},{9,13},{10,... | collective-permute-start | bytes 49160 | tf_op jit(solution)/shard_map/ppermute | solution.py:644
  23.4 0.4 %collective-permute-start.9 = (f32[1,32,128]{2,1,0:T(8,128)S(1)}, f32[1,32,128]{2,1,0:T(8,128)S(1)}, u32[]{:S(2)}, u32[]{:S(2)}) collective-permute-start(f32[1,32,128]{2,1,0:T(8,128)S(1)} %get-tuple-element.30), channel_id=1, source_target_pairs={{4,0},{5,1},{0,2},{1,3},{8,4},{9,5},{2,6},{3,7},{12,8},{13,9},{6,1... | collective-permute-start | bytes 49160 | tf_op jit(solution)/shard_map/ppermute | solution.py:644
  23.8 0.0 collective-permute-done.5.refs_1_
  23.8 0.0 collective-permute-start.6
  23.8 0.0 copy-done.1
  23.8 0.0 copy-start.2
  23.8 0.0 copy-start.3
  23.8 0.8 %shard_map.85.fine_ref = f32[16,32,128]{2,1,0:T(8,128)S(1)} custom-call(bf16[152,128,128]{2,1,0:T(8,128)(2,1)S(1)} %copy-done, f32[16,32,128]{2,1,0:T(8,128)S(1)} %get-tuple-element.18.rows_ref, f32[3,32,128]{2,1,0:T(8,128)S(1)} %collective-permute-done.first_ref, f32[3,32,128]{2,1,0:T(8,128)S(1)} %collective-permute-done.1.second_ref, ...), custom_call_target="tpu_custom_call" | custom-call | flops 1000000000 | bytes 3000000 | tf_op jit(solution)/shard_map/pallas_call | solution.py:247
  24.6 0.0 collective-permute-done.7.refs_3_
  24.6 0.4 %collective-permute-done.6.refs_2_ = f32[32,128]{1,0:T(8,128)S(1)} collective-permute-done((f32[32,128]{1,0:T(8,128)S(1)}, f32[32,128]{1,0:T(8,128)S(1)}, u32[]{:S(2)}, u32[]{:S(2)}) %collective-permute-start.6) | collective-permute-done | bytes 16416 | tf_op jit(solution)/shard_map/ppermute | solution.py:647
  25.0 0.0 copy-done.2
  25.0 0.0 copy-done.3
  25.0 0.8 %shard_map.87.four_ref = f32[3,32,128]{2,1,0:T(8,128)S(1)} custom-call(bf16[152,128,128]{2,1,0:T(8,128)(2,1)S(1)} %copy-done, bf16[4,1,64,136]{3,2,1,0:T(8,128)(2,1)S(1)} %bitcast.3, bf16[64,64]{1,0:T(8,128)(2,1)S(1)} %copy-done.3, f32[32,128]{1,0:T(8,128)S(1)} %shard_map.84.refs_0_, f32[32,128]{1,0:T(8,128)S(1)} %collective-permute-done.5.refs_1_, ...), custom_call_target="tpu_custom_call" | custom-call | flops 1000000000 | bytes 3000000 | tf_op jit(solution)/shard_map/pallas_call | solution.py:247
  25.7 0.0 collective-permute-done.8.first_ref
  25.7 1.4 %collective-permute-done.9.second_ref = f32[1,32,128]{2,1,0:T(8,128)S(1)} collective-permute-done((f32[1,32,128]{2,1,0:T(8,128)S(1)}, f32[1,32,128]{2,1,0:T(8,128)S(1)}, u32[]{:S(2)}, u32[]{:S(2)}) %collective-permute-start.9) | collective-permute-done | bytes 16416 | tf_op jit(solution)/shard_map/ppermute | solution.py:644
  27.1 1.0 %shard_map.88 = f32[512,128]{1,0:T(8,128)} custom-call(bf16[152,128,128]{2,1,0:T(8,128)(2,1)S(1)} %copy-done, f32[16,32,128]{2,1,0:T(8,128)S(1)} %shard_map.85.fine_ref, f32[8,32,128]{2,1,0:T(8,128)S(1)} %get-tuple-element.26.one_ref, f32[4,32,128]{2,1,0:T(8,128)S(1)} %get-tuple-element.27.two_ref, f32[2,32,128]{2,1,0:T(8,128)S(1)} %get-tuple-element.28.three_ref, ...), custom_call_target="tpu_custom_call" | custom-call | flops 1000000000 | bytes 3000000 | tf_op jit(solution)/shard_map/pallas_call | solution.py:247
Async XLA Ops:
  0.0 0.9 %copy-start.6 = (f32[32,16,128]{2,1,0:T(8,128)S(1)}, f32[32,16,128]{2,1,0:T(8,128)}, u32[]{:S(2)}) copy-start(f32[32,16,128]{2,1,0:T(8,128)} %param.8) | copy-start | bytes 786436
  1.0 14.3 %copy-start = (bf16[152,128,128]{2,1,0:T(8,128)(2,1)S(1)}, bf16[152,128,128]{2,1,0:T(8,128)(2,1)}, u32[]{:S(2)}) copy-start(bf16[152,128,128]{2,1,0:T(8,128)(2,1)} %constant.2.clone.block_ref) | copy-start | bytes 14942212
  1.6 5.0 %collective-permute-start = (f32[3,32,128]{2,1,0:T(8,128)S(1)}, f32[3,32,128]{2,1,0:T(8,128)S(1)}, u32[]{:S(2)}, u32[]{:S(2)}) collective-permute-start(f32[3,32,128]{2,1,0:T(8,128)S(1)} %get-tuple-element.19), channel_id=1, source_target_pairs={{0,4},{1,5},{2,0},{3,1},{4,8},{5,9},{6,2},{7,3},{8,12},{9,13},{10,... | collective-permute-start | bytes 147464 | tf_op jit(solution)/shard_map/ppermute | solution.py:644
  4.5 4.1 %collective-permute-start.1 = (f32[3,32,128]{2,1,0:T(8,128)S(1)}, f32[3,32,128]{2,1,0:T(8,128)S(1)}, u32[]{:S(2)}, u32[]{:S(2)}) collective-permute-start(f32[3,32,128]{2,1,0:T(8,128)S(1)} %get-tuple-element.20), channel_id=1, source_target_pairs={{4,0},{5,1},{0,2},{1,3},{8,4},{9,5},{2,6},{3,7},{12,8},{13,9},{6,1... | collective-permute-start | bytes 147464 | tf_op jit(solution)/shard_map/ppermute | solution.py:644
  8.8 10.6 %copy-start.4 = (bf16[4,2,520,256]{3,2,1,0:T(8,128)(2,1)S(1)}, bf16[4,2,520,256]{3,2,1,0:T(8,128)(2,1)}, u32[]{:S(2)}) copy-start(bf16[4,2,520,256]{3,2,1,0:T(8,128)(2,1)} %refs_0_.1) | copy-start | bytes 6389764
  8.8 10.6 %copy-start.5 = (bf16[2,1,520,256]{3,2,1,0:T(8,128)(2,1)S(1)}, bf16[2,1,520,256]{3,2,1,0:T(8,128)(2,1)}, u32[]{:S(2)}) copy-start(bf16[2,1,520,256]{3,2,1,0:T(8,128)(2,1)} %refs_1_.1) | copy-start | bytes 1597444
  8.8 10.6 %copy-start.7 = (bf16[1,1,264,128]{3,2,1,0:T(8,128)(2,1)S(1)}, bf16[1,1,264,128]{3,2,1,0:T(8,128)(2,1)}, u32[]{:S(2)}) copy-start(bf16[1,1,264,128]{3,2,1,0:T(8,128)(2,1)} %refs_2_.1) | copy-start | bytes 202756
  8.8 5.0 %collective-permute-start.3 = (f32[8,32,128]{2,1,0:T(8,128)S(1)}, f32[8,32,128]{2,1,0:T(8,128)S(1)}, u32[]{:S(2)}, u32[]{:S(2)}) collective-permute-start(f32[8,32,128]{2,1,0:T(8,128)S(1)} %shard_map.83.refs_0_.refs_3_), channel_id=1, source_target_pairs={{0,2},{1,3},{2,0},{3,1},{4,6},{5,7},{6,4},{7,5},{8,10},{9,11},{10,... | collective-permute-start | bytes 393224 | tf_op jit(solution)/shard_map/ppermute | solution.py:647
  8.9 4.9 %collective-permute-start.2 = (f32[8,32,128]{2,1,0:T(8,128)S(1)}, f32[8,32,128]{2,1,0:T(8,128)S(1)}, u32[]{:S(2)}, u32[]{:S(2)}) collective-permute-start(f32[8,32,128]{2,1,0:T(8,128)S(1)} %shard_map.83.refs_0_.refs_3_), channel_id=1, source_target_pairs={{0,1},{1,0},{2,3},{3,2},{4,5},{5,4},{6,7},{7,6},{8,9},{9,8},{10,11... | collective-permute-start | bytes 393224 | tf_op jit(solution)/shard_map/ppermute | solution.py:647
  13.9 1.3 %collective-permute-start.4 = (f32[8,32,128]{2,1,0:T(8,128)S(1)}, f32[8,32,128]{2,1,0:T(8,128)S(1)}, u32[]{:S(2)}, u32[]{:S(2)}) collective-permute-start(f32[8,32,128]{2,1,0:T(8,128)S(1)} %collective-permute-done.3.refs_2_.refs_5_), channel_id=1, source_target_pairs={{0,1},{1,0},{2,3},{3,2},{4,5},{5,4},{6,7},{7,6},{8,9},{9,8},{10,11... | collective-permute-start | bytes 393224 | tf_op jit(solution)/shard_map/ppermute | solution.py:647
  15.4 8.3 %copy-start.1 = (bf16[8,1,520,256]{3,2,1,0:T(8,128)(2,1)S(1)}, bf16[8,1,520,256]{3,2,1,0:T(8,128)(2,1)}, u32[]{:S(2)}) copy-start(bf16[8,1,520,256]{3,2,1,0:T(8,128)(2,1)} %factor_ref.1) | copy-start | bytes 6389764
  15.5 9.1 %collective-permute-start.7 = (f32[32,128]{1,0:T(8,128)S(1)}, f32[32,128]{1,0:T(8,128)S(1)}, u32[]{:S(2)}, u32[]{:S(2)}) collective-permute-start(f32[32,128]{1,0:T(8,128)S(1)} %shard_map.84.refs_0_), channel_id=1, source_target_pairs={{0,24},{1,25},{2,26},{3,27},{4,28},{5,29},{6,30},{7,31},{8,16},{9,... | collective-permute-start | bytes 49160 | tf_op jit(solution)/shard_map/ppermute | solution.py:692
  19.4 4.4 %collective-permute-start.5 = (f32[32,128]{1,0:T(8,128)S(1)}, f32[32,128]{1,0:T(8,128)S(1)}, u32[]{:S(2)}, u32[]{:S(2)}) collective-permute-start(f32[32,128]{1,0:T(8,128)S(1)} %shard_map.84.refs_0_), channel_id=1, source_target_pairs={{0,8},{1,17},{2,10},{3,19},{4,12},{5,21},{6,14},{7,23},{8,0},{9,25... | collective-permute-start | bytes 49160 | tf_op jit(solution)/shard_map/ppermute | solution.py:692
  21.6 4.1 %collective-permute-start.8 = (f32[1,32,128]{2,1,0:T(8,128)S(1)}, f32[1,32,128]{2,1,0:T(8,128)S(1)}, u32[]{:S(2)}, u32[]{:S(2)}) collective-permute-start(f32[1,32,128]{2,1,0:T(8,128)S(1)} %get-tuple-element.29), channel_id=1, source_target_pairs={{0,4},{1,5},{2,0},{3,1},{4,8},{5,9},{6,2},{7,3},{8,12},{9,13},{10,... | collective-permute-start | bytes 49160 | tf_op jit(solution)/shard_map/ppermute | solution.py:644
  23.4 3.7 %collective-permute-start.9 = (f32[1,32,128]{2,1,0:T(8,128)S(1)}, f32[1,32,128]{2,1,0:T(8,128)S(1)}, u32[]{:S(2)}, u32[]{:S(2)}) collective-permute-start(f32[1,32,128]{2,1,0:T(8,128)S(1)} %get-tuple-element.30), channel_id=1, source_target_pairs={{4,0},{5,1},{0,2},{1,3},{8,4},{9,5},{2,6},{3,7},{12,8},{13,9},{6,1... | collective-permute-start | bytes 49160 | tf_op jit(solution)/shard_map/ppermute | solution.py:644
  23.8 1.2 %collective-permute-start.6 = (f32[32,128]{1,0:T(8,128)S(1)}, f32[32,128]{1,0:T(8,128)S(1)}, u32[]{:S(2)}, u32[]{:S(2)}) collective-permute-start(f32[32,128]{1,0:T(8,128)S(1)} %collective-permute-done.5.refs_1_), channel_id=1, source_target_pairs={{0,1},{1,0},{2,3},{3,2},{4,5},{5,4},{6,7},{7,6},{8,9},{9,8},{10,11... | collective-permute-start | bytes 49160 | tf_op jit(solution)/shard_map/ppermute | solution.py:647
  23.8 1.2 %copy-start.2 = (bf16[4,1,136,64]{2,3,1,0:T(8,128)(2,1)S(1)}, bf16[4,1,136,64]{2,3,1,0:T(8,128)(2,1)}, u32[]{:S(2)}) copy-start(bf16[4,1,136,64]{2,3,1,0:T(8,128)(2,1)} %param.13) | copy-start | bytes 208900
  23.8 1.2 %copy-start.3 = (bf16[64,64]{1,0:T(8,128)(2,1)S(1)}, bf16[64,64]{1,0:T(8,128)(2,1)}, u32[]{:S(2)}) copy-start(bf16[64,64]{1,0:T(8,128)(2,1)} %inverse_ref.1) | copy-start | bytes 24580

commit v6 on v5

--- a/solution.py
+++ b/solution.py
@@ -51,11 +51,10 @@
         self.offset = [None, 0]
         for l in (2, 3, 4):
             self.offset.append(self.offset[-1] + self.w[l - 1] + 2)
-        self.whole = self.h[2] + 2
-        self.sent = self.whole + 2
-        self.sides = (self.h0 + 2) // 2
+        self.sides = self.h0 // 2 + 1
         self.first = self.w[1] + 2
         self.rest = LANES - self.first
+        self.tail = self.offset[3] + 2 * self.sides
 
     def place(self, level, lead, width, at=0):
         out = np.zeros((self.m, LANES, width))
@@ -66,13 +65,10 @@
                     out[c, self.offset[level] + k, at + column + lead] = 1
         return out
 
-    def place_tail(self):
-        whole = self.place(1, 1, round_up(self.ny[1] + 2))
-        out = np.zeros((self.m, 2) + whole.shape[1:])
-        out[:, 0, self.first :] = whole[:, : self.rest]
-        tail = self.first - self.rest
-        out[:, 1, self.offset[4] : self.offset[4] + tail] = whole[:, self.rest : self.first]
-        return out.reshape(self.m, 2 * LANES, -1)
+    def place_whole(self, level):
+        if self.tile[level] == LANES:
+            return self.place(level, 0, self.ny[level])
+        return self.place(level, 1, round_up(self.ny[level] + 2))
 
     def place_four(self):
         rows = [self.place(4, 0, 4 * self.ny[4], j * self.ny[4]) for j in range(4)]
@@ -240,15 +236,16 @@
     return jnp.dot(lhs, factor, preferred_element_type=F32)
 
 
-def kernel_call(body, out_shape, scratch=(), cost_us=1.0):
+def kernel_call(body, out_shape, scratch=(), cost_us=1.0, out_space=pltpu.VMEM):
     whole = pl.BlockSpec(memory_space=pltpu.VMEM)
+    result = pl.BlockSpec(memory_space=out_space)
 
     def call(*operands):
         return pl.pallas_call(
             body,
             out_shape=out_shape,
             in_specs=[whole] * len(operands),
-            out_specs=jax.tree.map(lambda _: whole, out_shape),
+            out_specs=jax.tree.map(lambda _: result, out_shape),
             scratch_shapes=list(scratch),
             compiler_params=pltpu.CompilerParams(vmem_limit_bytes=VMEM_BYTES),
             cost_estimate=pl.CostEstimate(
@@ -274,8 +271,7 @@
     return value.astype(BF16)
 
 
-def place_sides(plan, slot_value, row, index):
-    at = plan.offset[3] + 2 * (index % plan.sides)
+def place_sides(plan, slot_value, row, at):
     lane = lane_index(plan.rhs)
     chosen = jnp.logical_or(lane == at, lane == at + 1)
     return jnp.where(chosen, pltpu.roll(row, (at + 1) % LANES, 1), slot_value)
@@ -302,12 +298,9 @@
     return jnp.where(forward, first, second) * above, jnp.where(forward, second, first) * below
 
 
-def restrict_kernel(plan, x_ref, own_ref, first_ref, second_ref, rows_ref):
-    r, c = lax.axis_index("px"), lax.axis_index("py")
-    rhs, slots, h = plan.rhs, plan.slots, plan.h
+def shrink_kernel(plan, out_ref):
     first, last = column_ends(plan)
     shrink = None
-    matrices = []
     for level in (1, 2, 3, 4):
         lead = 0 if level == 1 else plan.offset[level - 1] + 1
         step = tap_matrix(lead, plan.offset[level], plan.w[level], first, last)
@@ -315,18 +308,21 @@
             shrink = step
         else:
             shrink = jnp.dot(shrink, step, preferred_element_type=F32).astype(BF16)
-        matrices.append(shrink)
+        out_ref[level - 1] = shrink
+
+
+def restrict_kernel(plan, x_ref, shrink_ref, early_ref, outer_ref, first_ref, second_ref, rows_ref):
+    r, c = lax.axis_index("px"), lax.axis_index("py")
+    rhs, slots, h = plan.rhs, plan.slots, plan.h
     above = jnp.where(r > 0, 1.0, 0.0).astype(F32)
     below = jnp.where(r < plan.n - 1, 1.0, 0.0).astype(F32)
     x = [x_ref[pl.ds(row, rhs, stride=h[0]), :] for row in range(h[0])]
-    for i, row in enumerate(x):
-        rows_ref[i] = row
     rows, total = x, None
     for level in (1, 2, 3, 4):
         rows = shrink_rows(rows, h[level - 1], 0 if level == 1 else 1)
         rows[0] = rows[0] * above
         rows[-1] = rows[-1] * below
-        part = product(jnp.concatenate(rows, axis=0), matrices[level - 1])
+        part = product(jnp.concatenate(rows, axis=0), shrink_ref[level - 1])
         if total is None:
             total = part
         else:
@@ -337,44 +333,49 @@
     scale = jnp.where(lane < plan.offset[3], scale, SHRINK**3)
     total = total * jnp.where(lane < plan.offset[4], scale, SHRINK**4)
     own = [total[i * rhs : (i + 1) * rhs] for i in range(slots)]
-    for i, row in enumerate(x):
-        slot = plan.h[2] + (i + 1) // plan.sides
-        own[slot] = place_sides(plan, own[slot], row, i + 1)
-    for i, value in enumerate(own):
-        own_ref[i] = value
     lane = lane_index(rhs)
     one, two, three = plan.offset[2:]
+    inner = [own[2], own[3], own[4], own[5]]
+    for k in range(2):
+        value = inner[k]
+        value = jnp.where(lane < two, value, 0.0)
+        for j in range(h[0] // 2):
+            value = place_sides(plan, value, x[k * (h[0] // 2) + j], two + 2 * j)
+        odd_row, end = own[6 + k], plan.tail + plan.first - plan.rest
+        moved = pltpu.roll(odd_row, (plan.tail - plan.rest) % LANES, 1)
+        chosen = jnp.logical_and(lane >= plan.tail, lane < end)
+        early_ref[k] = jnp.where(chosen, moved, value)
+        moved = pltpu.roll(odd_row, plan.first, 1)
+        early_ref[2 + k] = jnp.where(lane < plan.first, inner[2 + k], moved)
+    outer = [own[0], own[1]]
+    for k in range(2):
+        value = jnp.where(lane < two, own[h[2] + k], own[h[3] + k])
+        outer.append(jnp.where(lane < one, own[h[1] + k], value))
+    for k in range(4):
+        outer_ref[k] = outer[k]
     third = pltpu.roll(own[2], LANES - three, 1)
-    down = [x[-1]]
-    for k in range(2):
-        value = jnp.where(lane < three, own[h[3] + k], own[k])
-        value = jnp.where(lane < two, own[h[2] + k], value)
-        down.append(jnp.where(lane < one, third if k else own[h[1]], value))
+    down = [x[-1], jnp.where(lane < three, outer[2], own[0])]
+    down.append(jnp.where(lane < one, third, jnp.where(lane < three, outer[3], own[1])))
     up = [x[0], jnp.where(lane < one, third, own[0]), own[1]]
     write_halos(c, down, up, first_ref, second_ref)
-
-
-def merge_kernel(plan, own_ref, first_ref, second_ref, out_ref):
-    r, h, rhs = lax.axis_index("px"), plan.h, plan.rhs
+    for i, row in enumerate(x):
+        rows_ref[i] = row
+
+
+def merge_kernel(plan, outer_ref, shrink_ref, first_ref, second_ref, out_ref):
+    r, rhs = lax.axis_index("px"), plan.rhs
     lane = lane_index(rhs)
     above, below = read_halos(plan, first_ref, second_ref)
     one, two, three = plan.offset[2:]
-    slot = [own_ref[i] for i in range(plan.slots)]
-    matrix = tap_matrix(0, 0, plan.w[1], *column_ends(plan))
-    outer = product(jnp.concatenate([above[0], below[0]], axis=0), matrix) * SHRINK
-    from_above, from_below = outer[:rhs], outer[rhs:]
-    slot[0] = slot[0] + jnp.where(lane < three, above[1], 0.0)
-    value = jnp.where(lane < one, from_above, above[2])
-    slot[1] = slot[1] + jnp.where(lane < three, value, 0.0)
-    for k in range(2):
-        value = from_below if k == 0 else below[2]
-        pieces = ((1, 0, one, value), (2, one, two, below[1 + k]), (3, two, three, below[1 + k]))
-        for level, low, high, piece in pieces:
-            chosen = jnp.logical_and(lane >= low, lane < high)
-            row = h[level] + k
-            slot[row] = slot[row] + jnp.where(chosen, piece, 0.0)
+    edge = product(jnp.concatenate([above[0], below[0]], axis=0), shrink_ref[0]) * SHRINK
+    added = [
+        above[1],
+        jnp.where(lane < one, edge[:rhs], above[2]),
+        jnp.where(lane < one, edge[rhs:], below[1]),
+        below[2],
+    ]
     even = lax.rem(r, 2) == 0
-    own = [own_ref[k] for k in range(3)]
+    own = [outer_ref[k] for k in range(3)]
     partner = [jnp.where(even, below[k], above[k]) for k in (1, 2)]
     third = jnp.where(even, below[1], above[2])
     partner.append(pltpu.roll(third, three, 1))
@@ -382,20 +383,16 @@
     high = [jnp.where(even, b, a) for a, b in zip(own, partner)]
     sums = [low[0], low[1] + high[0], low[2] + high[1], high[2]]
     for k in range(4):
-        slot[k] = jnp.where(lane < three, slot[k], sums[k])
-    sides = plan.h[2]
-    slot[sides] = place_sides(plan, slot[sides], above[0], 0)
-    slot[sides + 1] = place_sides(plan, slot[sides + 1], below[0], plan.h0 + 1)
-    tail = plan.first - plan.rest
-    for k in range(2):
-        even_row, odd_row = slot[plan.whole + 2 * k], slot[plan.whole + 2 * k + 1]
-        chosen = jnp.logical_and(lane >= three, lane < three + tail)
-        moved = pltpu.roll(odd_row, (three - plan.rest) % LANES, 1)
-        slot[sides + k] = jnp.where(chosen, moved, slot[sides + k])
-        moved = pltpu.roll(odd_row, plan.first, 1)
-        out_ref[plan.whole + k] = jnp.where(lane < plan.first, even_row, moved)
-    for k in range(plan.whole):
-        out_ref[k] = slot[k]
+        value = jnp.where(lane < three, outer_ref[k] + added[k], sums[k])
+        out_ref[k * rhs : (k + 1) * rhs] = value
+    sides = place_sides(plan, jnp.zeros((rhs, LANES), F32), above[0], 0)
+    sides = place_sides(plan, sides, below[0], 2)
+    total = None
+    for k in range(rhs // 8):
+        part = sides[8 * k : 8 * (k + 1)]
+        part = pltpu.roll(part, 4 * k, 1) if k else part
+        total = part if total is None else total + part
+    out_ref[4 * rhs :] = total
 
 
 def banded(bands, matrices):
@@ -412,57 +409,88 @@
     values, matrices = [], []
     for band, owner in zip(band_refs, owners(plan)):
         for j in range(4):
-            values.append(band[j])
+            values.append(band[j * plan.rhs : (j + 1) * plan.rhs])
             matrices.append(blocks.get(block_ref, "four", 4 * owner + j))
     out_ref[...] = banded(values, matrices)
 
 
-def level_rows(plan, level, band_refs, blocks, block_ref):
-    rhs = plan.rhs
-    count = plan.sent if level == 1 else plan.h[level] + 2
-    values = [band[:count].reshape(count * rhs, LANES) for band in band_refs]
+def level_rows(plan, level, early_refs, late_refs, blocks, block_ref):
+    rhs, values = plan.rhs, []
+    lane = lane_index(rhs)
+    for early, late in zip(early_refs, late_refs):
+        outer = [late[i * rhs : (i + 1) * rhs] for i in range(4)]
+        inner = []
+        if level == 1:
+            inner = [early[k] for k in range(4)]
+            for k in range(2):
+                begin = pltpu.roll(early[2 + k], plan.rest, 1)
+                end = pltpu.roll(early[k], (plan.rest - plan.tail) % LANES, 1)
+                inner.append(jnp.where(lane < plan.rest, begin, end))
+        elif level == 2:
+            inner = [early[k] for k in range(2)]
+        values.append(jnp.concatenate(outer[:2] + inner + outer[2:], axis=0))
     matrices = [blocks.get(block_ref, f"place{level}", owner) for owner in owners(plan)]
-    whole = banded(values, matrices)
-    rows = [whole[i * rhs : (i + 1) * rhs] for i in range(count)]
-    if level > 1:
-        return rows
-    values, at = [], plan.whole
-    for band in band_refs:
-        pair = [band[at : at + 2], band[at - 2 : at]]
-        values.append(jnp.concatenate([v.reshape(2 * rhs, LANES) for v in pair], axis=1))
-    matrices = [blocks.get(block_ref, "tail", owner) for owner in owners(plan)]
-    odd = banded(values, matrices)
-    return rows[:at] + [rows[at], odd[:rhs], rows[at + 1], odd[rhs:]]
+    whole = jnp.dot(
+        jnp.concatenate(values, axis=1).astype(BF16), jnp.concatenate(matrices, axis=0),
+        preferred_element_type=F32,
+    )
+    return [whole[i * rhs : (i + 1) * rhs] for i in range(plan.h[level] + 2)]
+
+
+def assemble_tiles(rows, t):
+    rhs, count = rows[0].shape[0], rows[0].shape[1] // LANES
+    lane = lane_index(rhs)
+
+    def rolled(k, tile):
+        if not 0 <= tile < count:
+            return jnp.zeros((rhs, LANES), F32)
+        return pltpu.roll(rows[k][:, tile * LANES : (tile + 1) * LANES], 2 * k + 1, 1)
+
+    out = []
+    for k in range(5):
+        if k < 4:
+            value = jnp.where(lane == 2 * k, rolled(k, t - 1), rolled(k, t))
+        else:
+            value = jnp.zeros((rhs, LANES), F32)
+        if k > 0:
+            value = jnp.where(lane == 2 * k - 1, rolled(k - 1, t + 1), value)
+            value = jnp.where(lane < 2 * k - 1, rolled(k - 1, t), value)
+        out.append(value)
+    return jnp.concatenate(out, axis=1).astype(BF16)[:, : 4 * (LANES + 2)]
 
 
 def coarse_kernel(plan, blocks, block_ref, *refs):
-    factors, bands, outs = refs[:3], refs[3 : 3 + plan.m], refs[3 + plan.m :]
+    factors, outs = refs[:3], refs[3 + 2 * plan.m :]
+    early, late = refs[3 : 3 + plan.m], refs[3 + plan.m : 3 + 2 * plan.m]
     c, rhs = lax.axis_index("py"), plan.rhs
     down, up = [], []
     for level in (1, 2, 3):
         w, tiles = plan.tile[level], plan.tiles[level]
-        rows = level_rows(plan, level, bands, blocks, block_ref)
+        rows = level_rows(plan, level, early, late, blocks, block_ref)
         factor_ref, out_ref = factors[level - 1], outs[level - 1]
         solved = [[] for _ in range(tiles)]
         for b in range(plan.h[level] // 2):
             for t in range(tiles):
-                pieces = []
-                for k in range(4):
-                    row = rows[2 * b + k]
-                    lanes = range(t * w, t * w + w + 2, LANES)
-                    pieces.append([row[:, lo : lo + LANES] for lo in lanes])
-                solved[t].append(solve(assemble(pieces, w), factor_ref[b, t]))
+                window = rows[2 * b : 2 * b + 4]
+                if w == LANES:
+                    lhs = assemble_tiles(window, t)
+                else:
+                    lhs = assemble([[row] for row in window], w)
+                solved[t].append(solve(lhs, factor_ref[b, t]))
         pairs = plan.h[level] // 2
         stacked = [jnp.concatenate(solved[t], axis=0) for t in range(tiles)]
         lifted = []
         name = f"lift{level}"
-        for j in range(2):
-            if w % LANES == 0:
-                row = jnp.concatenate([v[:, j * w : (j + 1) * w] for v in stacked], axis=1)
-                lifted.append(product(row, blocks.get(block_ref, name, c)))
-            else:
-                row = jnp.concatenate(stacked, axis=1)
-                lifted.append(product(row, blocks.get(block_ref, name, 2 * c + j)))
+        if w % LANES == 0:
+            both = [
+                jnp.concatenate([v[:, j * w : (j + 1) * w] for v in stacked], axis=1)
+                for j in range(2)
+            ]
+            both = product(jnp.concatenate(both, axis=0), blocks.get(block_ref, name, c))
+            lifted = [both[: pairs * rhs], both[pairs * rhs :]]
+        else:
+            row = jnp.concatenate(stacked, axis=1)
+            lifted = [product(row, blocks.get(block_ref, name, 2 * c + j)) for j in range(2)]
         for b in range(pairs):
             for j in range(2):
                 out_ref[2 * b + j] = lifted[j][b * rhs : (b + 1) * rhs]
@@ -478,19 +506,28 @@
 
 
 def fine_kernel(plan, blocks, block_ref, rows_ref, first_ref, second_ref, factor_ref, *refs):
-    bands, out_ref = refs[: plan.m], refs[plan.m]
+    early, late, out_ref = refs[: plan.m], refs[plan.m : 2 * plan.m], refs[2 * plan.m]
     c = lax.axis_index("py")
     rhs, h0, w0 = plan.rhs, plan.h0, plan.w0
     above, below = read_halos(plan, first_ref, second_ref)
     values, matrices = [], []
     left = blocks.get(block_ref, "halo", 0)
     right = blocks.get(block_ref, "halo", 1)
-    at = plan.h[2]
-    for band, owner in zip(bands, owners(plan)):
+    lane = lane_index(rhs)
+    spot = plan.offset[3] + plan.h0
+    for inner, outer, owner in zip(early, late, owners(plan)):
         from_left = jnp.where(owner == c - 1, 1.0, 0.0).astype(BF16)
         from_right = jnp.where(owner == c + 1, 1.0, 0.0).astype(BF16)
         matrices.append(left * from_left + right * from_right)
-        values.append(band[at : at + 2].reshape(2 * rhs, LANES).astype(BF16))
+        packed = outer[4 * rhs :]
+        sides = [pltpu.roll(packed, (spot - 4 * k) % LANES, 1) for k in range(rhs // 8)]
+        sides = jnp.concatenate(sides, axis=0)
+        pair = []
+        for k in range(2):
+            moved = pltpu.roll(sides, LANES - 2 * k, 1) if k else sides
+            chosen = jnp.logical_or(lane == spot, lane == spot + 1)
+            pair.append(jnp.where(chosen, moved, inner[k]))
+        values.append(jnp.concatenate(pair, axis=0).astype(BF16))
     halo = jnp.dot(
         jnp.concatenate(values, axis=1), jnp.concatenate(matrices, axis=0),
         preferred_element_type=F32,
@@ -504,7 +541,10 @@
             rows.append(below[0])
         else:
             rows.append(rows_ref[row])
-        slot, part = divmod(row + 1, plan.sides)
+        if row < 0 or row == h0:
+            slot, part = (0 if row < 0 else 1), plan.sides - 1
+        else:
+            slot, part = divmod(row, h0 // 2)
         sides.append(halo[slot * rhs : (slot + 1) * rhs, part * LANES : (part + 1) * LANES])
     for b in range(h0 // 2):
         tiles, before = [], None
@@ -598,7 +638,7 @@
 
 
 def final_kernel(plan, blocks, block_ref, fine_ref, one_ref, two_ref, three_ref, four_ref,
-                 first_ref, second_ref, out_ref):
+                 first_ref, second_ref, out_ref, whole_ref, semaphores):
     r, rhs = lax.axis_index("px"), plan.rhs
     above = jnp.where(r > 0, 1.0, 0.0).astype(F32)
     below = jnp.where(r < plan.n - 1, 1.0, 0.0).astype(F32)
@@ -611,16 +651,28 @@
         [halo[k * rhs : (k + 1) * rhs, l * plan.w0 : (l + 1) * plan.w0] for l in range(3)]
         for k in range(2)
     ]
-    rows = [four_ref[k] for k in range(3)]
-    for level, own_ref in ((3, three_ref), (2, two_ref), (1, one_ref)):
-        height = plan.h[level]
-        lifted = lift_rows(rows, -1, height + 1)
-        rows = [lifted[0] * above + from_above[level - 1]]
-        rows += [lifted[i + 1] + own_ref[i] for i in range(height)]
-        rows += [lifted[-1] * below + from_below[level - 1]]
-    lifted = lift_rows(rows, 0, plan.h0)
-    for row in range(plan.h0):
-        out_ref[pl.ds(row, rhs, stride=plan.h0), :] = lifted[row] + fine_ref[row]
+    copies = []
+    for part in range(rhs // 8):
+        own = slice(8 * part, 8 * (part + 1))
+        rows = [four_ref[k, own] for k in range(3)]
+        for level, own_ref in ((3, three_ref), (2, two_ref), (1, one_ref)):
+            height = plan.h[level]
+            lifted = lift_rows(rows, -1, height + 1)
+            rows = [lifted[0] * above + from_above[level - 1][own]]
+            rows += [lifted[i + 1] + own_ref[i, own] for i in range(height)]
+            rows += [lifted[-1] * below + from_below[level - 1][own]]
+        lifted = lift_rows(rows, 0, plan.h0)
+        start, count = 8 * part * plan.h0, 8 * plan.h0
+        for row in range(plan.h0):
+            value = lifted[row] + fine_ref[row, own]
+            whole_ref[pl.ds(start + row, 8, stride=plan.h0), :] = value
+        span = pl.ds(start, count)
+        copies.append(
+            pltpu.make_async_copy(whole_ref.at[span], out_ref.at[span], semaphores.at[part])
+        )
+        copies[-1].start()
+    for copy in copies:
+        copy.wait()
 
 
 def per_device(mesh_shape, residual, factor_fine, factor_one, factor_two, factor_three,
@@ -648,11 +700,10 @@
 
     blocks = Blocks()
     blocks.add("four", plan.place_four())
-    blocks.add("tail", plan.place_tail())
     blocks.add("pick", plan.pick_band())
     blocks.add("band", plan.lift_band())
     for l in (1, 2, 3):
-        blocks.add(f"place{l}", plan.place(l, 1, round_up(plan.ny[l] + 2)))
+        blocks.add(f"place{l}", plan.place_whole(l))
         if plan.tile[l] % LANES == 0:
             blocks.add(f"lift{l}", plan.lift_columns(l))
         else:
@@ -665,25 +716,33 @@
     blocks.add("lift5", plan.coarsest_lift())
     matrices = blocks.array()
 
-    own, first, second, rows = kernel_call(
+    shrink = kernel_call(
+        functools.partial(shrink_kernel, plan),
+        jax.ShapeDtypeStruct((4, LANES, LANES), BF16), cost_us=4.0,
+    )()
+    early, outer, first, second, rows = kernel_call(
         functools.partial(restrict_kernel, plan),
-        (shape(plan.slots, rhs, LANES), shape(3, rhs, LANES), shape(3, rhs, LANES),
+        (shape(4, rhs, LANES), shape(4, rhs, LANES), shape(3, rhs, LANES), shape(3, rhs, LANES),
          shape(h0, rhs, plan.w0)),
-    )(x)
+    )(x, shrink)
     first, second = trade(first, second)
-    band = kernel_call(functools.partial(merge_kernel, plan), shape(plan.sent, rhs, LANES))(
-        own, first, second
+    late = kernel_call(functools.partial(merge_kernel, plan), shape(4 * rhs + 8, LANES))(
+        outer, shrink, first, second
     )
-    bands = {0: band}
-    bit = m // 2
-    while bit:
-        bands.update({k ^ bit: swap(value, bit) for k, value in list(bands.items())})
-        bit //= 2
-    bands = [bands[k] for k in range(m)]
+
+    def spread(value):
+        bands = {0: value}
+        bit = m // 2
+        while bit:
+            bands.update({k ^ bit: swap(band, bit) for k, band in list(bands.items())})
+            bit //= 2
+        return [bands[k] for k in range(m)]
+
+    early, late = spread(early), spread(late)
 
     pairs = kernel_call(
         functools.partial(gather_kernel, plan, blocks), shape(rhs, 4 * plan.ny[4]), cost_us=0.3
-    )(matrices, *bands)
+    )(matrices, *late)
     order, gathered = list(range(1, n // 2)), [pairs]
     fetched = []
     for k in range(0, len(order), 2):
@@ -695,7 +754,7 @@
                  for i in range(n) for c in range(m)],
             )
         )
-    bands, pairs = lax.optimization_barrier((bands, pairs))
+    late, pairs = lax.optimization_barrier((late, pairs))
     for k, value in enumerate(fetched):
         gathered.append(value)
         if 2 * k + 1 < len(order):
@@ -706,12 +765,12 @@
         tuple(shape(h[l], rhs, LANES) for l in (1, 2, 3))
         + (shape(1, rhs, LANES), shape(1, rhs, LANES)),
         cost_us=2.5,
-    )(matrices, factor_one, factor_two, factor_three, *bands)
+    )(matrices, factor_one, factor_two, factor_three, *early, *late)
     low, high = trade(low, high)
 
     fine = kernel_call(
         functools.partial(fine_kernel, plan, blocks), shape(h0, rhs, plan.w0)
-    )(matrices, rows, first, second, factor_fine, *bands)
+    )(matrices, rows, first, second, factor_fine, *early, *late)
     four = kernel_call(
         functools.partial(whole_kernel, plan, group, blocks),
         shape(3, rhs, LANES),
@@ -720,7 +779,11 @@
             pltpu.VMEM((plan.nx[4] + 2, rhs, LANES), F32),
         ),
     )(matrices, jnp.swapaxes(factor_four, 2, 3), coarse_inverse, *gathered)
-    out = kernel_call(functools.partial(final_kernel, plan, blocks), shape(rhs * h0, plan.w0))(
+    out = kernel_call(
+        functools.partial(final_kernel, plan, blocks), shape(rhs * h0, plan.w0),
+        scratch=(pltpu.VMEM((rhs * h0, plan.w0), F32), pltpu.SemaphoreType.DMA((rhs // 8,))),
+        out_space=pl.ANY,
+    )(
         matrices, fine, one, two, three, four, low, high
     )
     return out.reshape(rhs, h0, plan.w0)

time: 28.2 us -> 27.3 us (0.968)
  waiting for transfers between devices: 12 us -> 8.58 us
  starting transfers between devices: 9.22 us -> 12.4 us
  local copies, waits for them, and re-layouts: 0.99 us -> 0.59 us
    ppermute x4 -> x7, waiting for transfers between devices: 6.6 us -> 3.32 us  [swap(): return lax.ppermute(value, 'py', [(i, i ^ bits) for i in range(m)])]
    ppermute x4 -> x7, starting transfers between devices: 0.15 us -> 2.61 us  [swap(): return lax.ppermute(value, 'py', [(i, i ^ bits) for i in range(m)])]
    ppermute x2, starting transfers between devices: 3.93 us -> 4.67 us  [per_device(): lax.ppermute(pairs, ('px', 'py'), [(i * m + c, (i ^ 2 * (odd if c % 2 els...]
    ppermute x2, starting transfers between devices: 4.73 us -> 4.02 us  [trade(): lax.ppermute(first, ('px', 'py'), ring)]
    ppermute x2, starting transfers between devices: 0.41 us -> 1.1 us  [trade(): lax.ppermute(second, ('px', 'py'), back)]
    unnamed x16, local copies, waits for them, and re-layouts: 0.99 us -> 0.59 us
    pallas_call x7 -> x8, Pallas kernels: 5.7 us -> 5.45 us  [call(): pl.pallas_call(body, out_shape=out_shape, in_specs=[whole] * len(operands...]
  transfers between devices with their start and end apart: 10 -> 13, of which waited for: 6 -> 7; matrix products, arithmetic and copies ran while one was open for 0% -> 0% of each run, Pallas kernels for 13% -> 13%
where the time goes in v6:
time: 27.3 us; the launch traced here: 27.1 us
  starting transfers between devices  12.4 us (45%)
  waiting for transfers between devices  8.58 us (31%)
  Pallas kernels  5.45 us (20%)
  local copies, waits for them, and re-layouts  0.59 us (2%)
    pallas_call x8, Pallas kernels, call(): pl.pallas_call(body, out_shape=out_shape, in_specs=[whole] * len(operands...  5.45 us
    ppermute x2, starting transfers between devices, per_device(): lax.ppermute(pairs, ('px', 'py'), [(i * m + c, (i ^ 2 * (odd if c % 2 els...  4.67 us
    ppermute x2, starting transfers between devices, trade(): lax.ppermute(first, ('px', 'py'), ring)  4.02 us
    ppermute x7, waiting for transfers between devices, swap(): return lax.ppermute(value, 'py', [(i, i ^ bits) for i in range(m)])  3.32 us
    ppermute x2, waiting for transfers between devices, trade(): lax.ppermute(second, ('px', 'py'), back)  3.23 us
    ppermute x7, starting transfers between devices, swap(): return lax.ppermute(value, 'py', [(i, i ^ bits) for i in range(m)])  2.61 us
    ppermute x2, waiting for transfers between devices, trade(): lax.ppermute(first, ('px', 'py'), ring)  2.01 us
    ppermute x2, starting transfers between devices, trade(): lax.ppermute(second, ('px', 'py'), back)  1.1 us
  transfers between devices with their start and end apart: 13, of which 7 were waited for; matrix products, arithmetic and copies ran while one was open for 0% of the time, Pallas kernels for 13%

profile of v6, /device:TPU:0, one launch (start us, length us, event | category | flops | bytes accessed | tf_op | source)
XLA Modules:
  0.0 27.1 jit_solution(5285929452844775288)
XLA Ops:
  0.0 0.0 copy-start.6
  0.0 0.4 %shard_map.82.shrink_ref = bf16[4,128,128]{2,1,0:T(8,128)(2,1)S(1)} custom-call(), custom_call_target="tpu_custom_call" | custom-call | flops 4000000000 | bytes 12000000 | tf_op jit(solution)/shard_map/pallas_call | solution.py:244
  0.4 0.5 %copy-done.6 = f32[32,16,128]{2,1,0:T(8,128)S(1)} copy-done((f32[32,16,128]{2,1,0:T(8,128)S(1)}, f32[32,16,128]{2,1,0:T(8,128)}, u32[]{:S(2)}) %copy-start.6) | copy-done | bytes 262168
  1.0 0.4 %shard_map.83 = (f32[4,32,128]{2,1,0:T(8,128)S(1)}, f32[4,32,128]{2,1,0:T(8,128)S(1)}, f32[3,32,128]{2,1,0:T(8,128)S(1)}, f32[3,32,128]{2,1,0:T(8,128)S(1)}, f32[16,32,128]{2,1,0:T(8,128)S(1)}) custom-call(f32[512,128]{1,0:T(8,128)S(1)} %bitcast.4, bf16[4,128,128]{2,1,0:T(8,128)(2,1)S(1)} %shard_map.82.shrink_ref), custom_call_target="tpu_custom_call" | custom-call | flops 1000000000 | bytes 3000000 | tf_op jit(solution)/shard_map/pallas_call | solution.py:244
  1.3 3.0 %collective-permute-start = (f32[3,32,128]{2,1,0:T(8,128)S(1)}, f32[3,32,128]{2,1,0:T(8,128)S(1)}, u32[]{:S(2)}, u32[]{:S(2)}) collective-permute-start(f32[3,32,128]{2,1,0:T(8,128)S(1)} %get-tuple-element.20), channel_id=1, source_target_pairs={{0,4},{1,5},{2,0},{3,1},{4,8},{5,9},{6,2},{7,3},{8,12},{9,13},{10,... | collective-permute-start | bytes 147464 | tf_op jit(solution)/shard_map/ppermute | solution.py:696
  4.4 0.0 collective-permute-start.1
  4.4 2.0 %collective-permute-done.first_ref = f32[3,32,128]{2,1,0:T(8,128)S(1)} collective-permute-done((f32[3,32,128]{2,1,0:T(8,128)S(1)}, f32[3,32,128]{2,1,0:T(8,128)S(1)}, u32[]{:S(2)}, u32[]{:S(2)}) %collective-permute-start) | collective-permute-done | bytes 49184 | tf_op jit(solution)/shard_map/ppermute | solution.py:696
  6.4 2.0 %collective-permute-done.1.second_ref = f32[3,32,128]{2,1,0:T(8,128)S(1)} collective-permute-done((f32[3,32,128]{2,1,0:T(8,128)S(1)}, f32[3,32,128]{2,1,0:T(8,128)S(1)}, u32[]{:S(2)}, u32[]{:S(2)}) %collective-permute-start.1) | collective-permute-done | bytes 49184 | tf_op jit(solution)/shard_map/ppermute | solution.py:696
  8.4 0.2 shard_map.84.refs_0_.refs_4_.refs_7_
  8.6 0.0 copy-start.5
  8.6 0.0 copy-start.7
  8.6 0.1 collective-permute-start.6
  8.7 2.0 %collective-permute-start.3 = (f32[4,32,128]{2,1,0:T(8,128)S(1)}, f32[4,32,128]{2,1,0:T(8,128)S(1)}, u32[]{:S(2)}, u32[]{:S(2)}) collective-permute-start(f32[4,32,128]{2,1,0:T(8,128)S(1)} %get-tuple-element.22.refs_0_.refs_3_), channel_id=1, source_target_pairs={{0,2},{1,3},{2,0},{3,1},{4,6},{5,7},{6,4},{7,5},{8,10},{9,11},{10,... | collective-permute-start | bytes 196616 | tf_op jit(solution)/shard_map/ppermute | solution.py:699
  10.7 0.0 collective-permute-start.5
  10.7 2.3 %collective-permute-done.6.refs_2_.refs_6_.refs_9_ = f32[136,128]{1,0:T(8,128)S(1)} collective-permute-done((f32[136,128]{1,0:T(8,128)S(1)}, f32[136,128]{1,0:T(8,128)S(1)}, u32[]{:S(2)}, u32[]{:S(2)}) %collective-permute-start.6) | collective-permute-done | bytes 69664 | tf_op jit(solution)/shard_map/ppermute | solution.py:699
  13.0 0.0 collective-permute-start.7
  13.0 0.5 %collective-permute-start.2 = (f32[4,32,128]{2,1,0:T(8,128)S(1)}, f32[4,32,128]{2,1,0:T(8,128)S(1)}, u32[]{:S(2)}, u32[]{:S(2)}) collective-permute-start(f32[4,32,128]{2,1,0:T(8,128)S(1)} %get-tuple-element.22.refs_0_.refs_3_), channel_id=1, source_target_pairs={{0,1},{1,0},{2,3},{3,2},{4,5},{5,4},{6,7},{7,6},{8,9},{9,8},{10,11... | collective-permute-start | bytes 196616 | tf_op jit(solution)/shard_map/ppermute | solution.py:699
  13.5 0.2 collective-permute-done.3.refs_2_.refs_5_
  13.7 0.0 collective-permute-start.4
  13.7 0.0 collective-permute-done.5.refs_1_.refs_5_.refs_8_
  13.7 0.6 %collective-permute-done.7.refs_3_.refs_7_.refs_10_ = f32[136,128]{1,0:T(8,128)S(1)} collective-permute-done((f32[136,128]{1,0:T(8,128)S(1)}, f32[136,128]{1,0:T(8,128)S(1)}, u32[]{:S(2)}, u32[]{:S(2)}) %collective-permute-start.7) | collective-permute-done | bytes 69664 | tf_op jit(solution)/shard_map/ppermute | solution.py:699
  14.3 0.0 copy-done
  14.3 0.2 shard_map.85.refs_0_
  14.5 0.0 copy-start.1
  14.5 4.7 %collective-permute-start.10 = (f32[32,128]{1,0:T(8,128)S(1)}, f32[32,128]{1,0:T(8,128)S(1)}, u32[]{:S(2)}, u32[]{:S(2)}) collective-permute-start(f32[32,128]{1,0:T(8,128)S(1)} %shard_map.85.refs_0_), channel_id=1, source_target_pairs={{0,24},{1,25},{2,26},{3,27},{4,28},{5,29},{6,30},{7,31},{8,16},{9,... | collective-permute-start | bytes 49160 | tf_op jit(solution)/shard_map/ppermute | solution.py:751
  19.2 0.0 collective-permute-start.8
  19.2 0.0 collective-permute-done.2.refs_1_.refs_4_
  19.2 0.0 collective-permute-done.4.refs_3_.refs_6_
  19.2 0.0 copy-done.4
  19.2 0.0 copy-done.5
  19.2 0.0 copy-done.7
  19.2 1.7 %shard_map.87 = (f32[8,32,128]{2,1,0:T(8,128)S(1)}, f32[4,32,128]{2,1,0:T(8,128)S(1)}, f32[2,32,128]{2,1,0:T(8,128)S(1)}, f32[1,32,128]{2,1,0:T(8,128)S(1)}, f32[1,32,128]{2,1,0:T(8,128)S(1)}) custom-call(bf16[120,128,128]{2,1,0:T(8,128)(2,1)S(1)} %copy-done, bf16[4,2,520,256]{3,2,1,0:T(8,128)(2,1)S(1)} %copy-done.4, bf16[2,1,520,256]{3,2,1,0:T(8,128)(2,1)S(1)} %copy-done.5, ...), custom_call_target="tpu_custom_call" | custom-call | flops 2500000000 | bytes 7500000 | tf_op jit(solution)/shard_map/pallas_call | solution.py:244
  21.0 1.0 %collective-permute-start.11 = (f32[1,32,128]{2,1,0:T(8,128)S(1)}, f32[1,32,128]{2,1,0:T(8,128)S(1)}, u32[]{:S(2)}, u32[]{:S(2)}) collective-permute-start(f32[1,32,128]{2,1,0:T(8,128)S(1)} %get-tuple-element.31), channel_id=1, source_target_pairs={{0,4},{1,5},{2,0},{3,1},{4,8},{5,9},{6,2},{7,3},{8,12},{9,13},{10,... | collective-permute-start | bytes 49160 | tf_op jit(solution)/shard_map/ppermute | solution.py:696
  22.0 1.1 %collective-permute-start.12 = (f32[1,32,128]{2,1,0:T(8,128)S(1)}, f32[1,32,128]{2,1,0:T(8,128)S(1)}, u32[]{:S(2)}, u32[]{:S(2)}) collective-permute-start(f32[1,32,128]{2,1,0:T(8,128)S(1)} %get-tuple-element.32), channel_id=1, source_target_pairs={{4,0},{5,1},{0,2},{1,3},{8,4},{9,5},{2,6},{3,7},{12,8},{13,9},{6,1... | collective-permute-start | bytes 49160 | tf_op jit(solution)/shard_map/ppermute | solution.py:696
  23.0 0.0 collective-permute-done.8.refs_1_
  23.0 0.0 collective-permute-start.9
  23.1 0.0 copy-done.1
  23.1 0.0 copy-start.2
  23.1 0.0 copy-start.3
  23.1 0.9 %shard_map.86.fine_ref = f32[16,32,128]{2,1,0:T(8,128)S(1)} custom-call(bf16[120,128,128]{2,1,0:T(8,128)(2,1)S(1)} %copy-done, f32[16,32,128]{2,1,0:T(8,128)S(1)} %get-tuple-element.19.rows_ref, f32[3,32,128]{2,1,0:T(8,128)S(1)} %collective-permute-done.first_ref, f32[3,32,128]{2,1,0:T(8,128)S(1)} %collective-permute-done.1.second_ref, ...), custom_call_target="tpu_custom_call" | custom-call | flops 1000000000 | bytes 3000000 | tf_op jit(solution)/shard_map/pallas_call | solution.py:244
  23.9 0.0 collective-permute-done.10.refs_3_
  23.9 0.3 %collective-permute-done.9.refs_2_ = f32[32,128]{1,0:T(8,128)S(1)} collective-permute-done((f32[32,128]{1,0:T(8,128)S(1)}, f32[32,128]{1,0:T(8,128)S(1)}, u32[]{:S(2)}, u32[]{:S(2)}) %collective-permute-start.9) | collective-permute-done | bytes 16416 | tf_op jit(solution)/shard_map/ppermute | solution.py:699
  24.2 0.0 copy-done.2
  24.2 0.0 copy-done.3
  24.2 0.8 %shard_map.88.four_ref = f32[3,32,128]{2,1,0:T(8,128)S(1)} custom-call(bf16[120,128,128]{2,1,0:T(8,128)(2,1)S(1)} %copy-done, bf16[4,1,64,136]{3,2,1,0:T(8,128)(2,1)S(1)} %bitcast.3, bf16[64,64]{1,0:T(8,128)(2,1)S(1)} %copy-done.3, f32[32,128]{1,0:T(8,128)S(1)} %shard_map.85.refs_0_, f32[32,128]{1,0:T(8,128)S(1)} %collective-permute-done.8.refs_1_, ...), custom_call_target="tpu_custom_call" | custom-call | flops 1000000000 | bytes 3000000 | tf_op jit(solution)/shard_map/pallas_call | solution.py:244
  25.0 0.0 collective-permute-done.11.first_ref
  25.0 1.2 %collective-permute-done.12.second_ref = f32[1,32,128]{2,1,0:T(8,128)S(1)} collective-permute-done((f32[1,32,128]{2,1,0:T(8,128)S(1)}, f32[1,32,128]{2,1,0:T(8,128)S(1)}, u32[]{:S(2)}, u32[]{:S(2)}) %collective-permute-start.12) | collective-permute-done | bytes 16416 | tf_op jit(solution)/shard_map/ppermute | solution.py:696
  26.2 0.9 %shard_map.89 = f32[512,128]{1,0:T(8,128)} custom-call(bf16[120,128,128]{2,1,0:T(8,128)(2,1)S(1)} %copy-done, f32[16,32,128]{2,1,0:T(8,128)S(1)} %shard_map.86.fine_ref, f32[8,32,128]{2,1,0:T(8,128)S(1)} %get-tuple-element.28.one_ref, f32[4,32,128]{2,1,0:T(8,128)S(1)} %get-tuple-element.29.two_ref, f32[2,32,128]{2,1,0:T(8,128)S(1)} %get-tuple-element.30.three_ref, ...), custom_call_target="tpu_custom_call" | custom-call | flops 1000000000 | bytes 3000000 | tf_op jit(solution)/shard_map/pallas_call | solution.py:244
  (2 shorter events, 0.0 us)
Async XLA Ops:
  0.0 0.9 %copy-start.6 = (f32[32,16,128]{2,1,0:T(8,128)S(1)}, f32[32,16,128]{2,1,0:T(8,128)}, u32[]{:S(2)}) copy-start(f32[32,16,128]{2,1,0:T(8,128)} %param.8) | copy-start | bytes 786436
  1.0 13.3 %copy-start = (bf16[120,128,128]{2,1,0:T(8,128)(2,1)S(1)}, bf16[120,128,128]{2,1,0:T(8,128)(2,1)}, u32[]{:S(2)}) copy-start(bf16[120,128,128]{2,1,0:T(8,128)(2,1)} %constant.2.clone.block_ref) | copy-start | bytes 11796484
  1.3 5.0 %collective-permute-start = (f32[3,32,128]{2,1,0:T(8,128)S(1)}, f32[3,32,128]{2,1,0:T(8,128)S(1)}, u32[]{:S(2)}, u32[]{:S(2)}) collective-permute-start(f32[3,32,128]{2,1,0:T(8,128)S(1)} %get-tuple-element.20), channel_id=1, source_target_pairs={{0,4},{1,5},{2,0},{3,1},{4,8},{5,9},{6,2},{7,3},{8,12},{9,13},{10,... | collective-permute-start | bytes 147464 | tf_op jit(solution)/shard_map/ppermute | solution.py:696
  4.4 4.1 %collective-permute-start.1 = (f32[3,32,128]{2,1,0:T(8,128)S(1)}, f32[3,32,128]{2,1,0:T(8,128)S(1)}, u32[]{:S(2)}, u32[]{:S(2)}) collective-permute-start(f32[3,32,128]{2,1,0:T(8,128)S(1)} %get-tuple-element.21), channel_id=1, source_target_pairs={{4,0},{5,1},{0,2},{1,3},{8,4},{9,5},{2,6},{3,7},{12,8},{13,9},{6,1... | collective-permute-start | bytes 147464 | tf_op jit(solution)/shard_map/ppermute | solution.py:696
  8.6 10.6 %copy-start.4 = (bf16[4,2,520,256]{3,2,1,0:T(8,128)(2,1)S(1)}, bf16[4,2,520,256]{3,2,1,0:T(8,128)(2,1)}, u32[]{:S(2)}) copy-start(bf16[4,2,520,256]{3,2,1,0:T(8,128)(2,1)} %refs_0_.1) | copy-start | bytes 6389764
  8.6 10.6 %copy-start.5 = (bf16[2,1,520,256]{3,2,1,0:T(8,128)(2,1)S(1)}, bf16[2,1,520,256]{3,2,1,0:T(8,128)(2,1)}, u32[]{:S(2)}) copy-start(bf16[2,1,520,256]{3,2,1,0:T(8,128)(2,1)} %refs_1_.1) | copy-start | bytes 1597444
  8.6 10.6 %copy-start.7 = (bf16[1,1,264,128]{3,2,1,0:T(8,128)(2,1)S(1)}, bf16[1,1,264,128]{3,2,1,0:T(8,128)(2,1)}, u32[]{:S(2)}) copy-start(bf16[1,1,264,128]{3,2,1,0:T(8,128)(2,1)} %refs_2_.1) | copy-start | bytes 202756
  8.6 4.4 %collective-permute-start.6 = (f32[136,128]{1,0:T(8,128)S(1)}, f32[136,128]{1,0:T(8,128)S(1)}, u32[]{:S(2)}, u32[]{:S(2)}) collective-permute-start(f32[136,128]{1,0:T(8,128)S(1)} %shard_map.84.refs_0_.refs_4_.refs_7_), channel_id=1, source_target_pairs={{0,2},{1,3},{2,0},{3,1},{4,6},{5,7},{6,4},{7,5},{8,10},{9,11},{10,... | collective-permute-start | bytes 208904 | tf_op jit(solution)/shard_map/ppermute | solution.py:699
  8.7 5.0 %collective-permute-start.3 = (f32[4,32,128]{2,1,0:T(8,128)S(1)}, f32[4,32,128]{2,1,0:T(8,128)S(1)}, u32[]{:S(2)}, u32[]{:S(2)}) collective-permute-start(f32[4,32,128]{2,1,0:T(8,128)S(1)} %get-tuple-element.22.refs_0_.refs_3_), channel_id=1, source_target_pairs={{0,2},{1,3},{2,0},{3,1},{4,6},{5,7},{6,4},{7,5},{8,10},{9,11},{10,... | collective-permute-start | bytes 196616 | tf_op jit(solution)/shard_map/ppermute | solution.py:699
  10.7 3.0 %collective-permute-start.5 = (f32[136,128]{1,0:T(8,128)S(1)}, f32[136,128]{1,0:T(8,128)S(1)}, u32[]{:S(2)}, u32[]{:S(2)}) collective-permute-start(f32[136,128]{1,0:T(8,128)S(1)} %shard_map.84.refs_0_.refs_4_.refs_7_), channel_id=1, source_target_pairs={{0,1},{1,0},{2,3},{3,2},{4,5},{5,4},{6,7},{7,6},{8,9},{9,8},{10,11... | collective-permute-start | bytes 208904 | tf_op jit(solution)/shard_map/ppermute | solution.py:699
  13.0 1.3 %collective-permute-start.7 = (f32[136,128]{1,0:T(8,128)S(1)}, f32[136,128]{1,0:T(8,128)S(1)}, u32[]{:S(2)}, u32[]{:S(2)}) collective-permute-start(f32[136,128]{1,0:T(8,128)S(1)} %collective-permute-done.6.refs_2_.refs_6_.refs_9_), channel_id=1, source_target_pairs={{0,1},{1,0},{2,3},{3,2},{4,5},{5,4},{6,7},{7,6},{8,9},{9,8},{10,11... | collective-permute-start | bytes 208904 | tf_op jit(solution)/shard_map/ppermute | solution.py:699
  13.0 6.2 %collective-permute-start.2 = (f32[4,32,128]{2,1,0:T(8,128)S(1)}, f32[4,32,128]{2,1,0:T(8,128)S(1)}, u32[]{:S(2)}, u32[]{:S(2)}) collective-permute-start(f32[4,32,128]{2,1,0:T(8,128)S(1)} %get-tuple-element.22.refs_0_.refs_3_), channel_id=1, source_target_pairs={{0,1},{1,0},{2,3},{3,2},{4,5},{5,4},{6,7},{7,6},{8,9},{9,8},{10,11... | collective-permute-start | bytes 196616 | tf_op jit(solution)/shard_map/ppermute | solution.py:699
  13.7 5.5 %collective-permute-start.4 = (f32[4,32,128]{2,1,0:T(8,128)S(1)}, f32[4,32,128]{2,1,0:T(8,128)S(1)}, u32[]{:S(2)}, u32[]{:S(2)}) collective-permute-start(f32[4,32,128]{2,1,0:T(8,128)S(1)} %collective-permute-done.3.refs_2_.refs_5_), channel_id=1, source_target_pairs={{0,1},{1,0},{2,3},{3,2},{4,5},{5,4},{6,7},{7,6},{8,9},{9,8},{10,11... | collective-permute-start | bytes 196616 | tf_op jit(solution)/shard_map/ppermute | solution.py:699
  14.5 8.5 %copy-start.1 = (bf16[8,1,520,256]{3,2,1,0:T(8,128)(2,1)S(1)}, bf16[8,1,520,256]{3,2,1,0:T(8,128)(2,1)}, u32[]{:S(2)}) copy-start(bf16[8,1,520,256]{3,2,1,0:T(8,128)(2,1)} %factor_ref.1) | copy-start | bytes 6389764
  14.5 9.4 %collective-permute-start.10 = (f32[32,128]{1,0:T(8,128)S(1)}, f32[32,128]{1,0:T(8,128)S(1)}, u32[]{:S(2)}, u32[]{:S(2)}) collective-permute-start(f32[32,128]{1,0:T(8,128)S(1)} %shard_map.85.refs_0_), channel_id=1, source_target_pairs={{0,24},{1,25},{2,26},{3,27},{4,28},{5,29},{6,30},{7,31},{8,16},{9,... | collective-permute-start | bytes 49160 | tf_op jit(solution)/shard_map/ppermute | solution.py:751
  19.2 3.9 %collective-permute-start.8 = (f32[32,128]{1,0:T(8,128)S(1)}, f32[32,128]{1,0:T(8,128)S(1)}, u32[]{:S(2)}, u32[]{:S(2)}) collective-permute-start(f32[32,128]{1,0:T(8,128)S(1)} %shard_map.85.refs_0_), channel_id=1, source_target_pairs={{0,8},{1,17},{2,10},{3,19},{4,12},{5,21},{6,14},{7,23},{8,0},{9,25... | collective-permute-start | bytes 49160 | tf_op jit(solution)/shard_map/ppermute | solution.py:751
  21.0 4.1 %collective-permute-start.11 = (f32[1,32,128]{2,1,0:T(8,128)S(1)}, f32[1,32,128]{2,1,0:T(8,128)S(1)}, u32[]{:S(2)}, u32[]{:S(2)}) collective-permute-start(f32[1,32,128]{2,1,0:T(8,128)S(1)} %get-tuple-element.31), channel_id=1, source_target_pairs={{0,4},{1,5},{2,0},{3,1},{4,8},{5,9},{6,2},{7,3},{8,12},{9,13},{10,... | collective-permute-start | bytes 49160 | tf_op jit(solution)/shard_map/ppermute | solution.py:696
  22.0 4.2 %collective-permute-start.12 = (f32[1,32,128]{2,1,0:T(8,128)S(1)}, f32[1,32,128]{2,1,0:T(8,128)S(1)}, u32[]{:S(2)}, u32[]{:S(2)}) collective-permute-start(f32[1,32,128]{2,1,0:T(8,128)S(1)} %get-tuple-element.32), channel_id=1, source_target_pairs={{4,0},{5,1},{0,2},{1,3},{8,4},{9,5},{2,6},{3,7},{12,8},{13,9},{6,1... | collective-permute-start | bytes 49160 | tf_op jit(solution)/shard_map/ppermute | solution.py:696
  23.0 1.2 %collective-permute-start.9 = (f32[32,128]{1,0:T(8,128)S(1)}, f32[32,128]{1,0:T(8,128)S(1)}, u32[]{:S(2)}, u32[]{:S(2)}) collective-permute-start(f32[32,128]{1,0:T(8,128)S(1)} %collective-permute-done.8.refs_1_), channel_id=1, source_target_pairs={{0,1},{1,0},{2,3},{3,2},{4,5},{5,4},{6,7},{7,6},{8,9},{9,8},{10,11... | collective-permute-start | bytes 49160 | tf_op jit(solution)/shard_map/ppermute | solution.py:699
  23.1 1.2 %copy-start.2 = (bf16[4,1,136,64]{2,3,1,0:T(8,128)(2,1)S(1)}, bf16[4,1,136,64]{2,3,1,0:T(8,128)(2,1)}, u32[]{:S(2)}) copy-start(bf16[4,1,136,64]{2,3,1,0:T(8,128)(2,1)} %param.13) | copy-start | bytes 208900
  23.1 1.2 %copy-start.3 = (bf16[64,64]{1,0:T(8,128)(2,1)S(1)}, bf16[64,64]{1,0:T(8,128)(2,1)}, u32[]{:S(2)}) copy-start(bf16[64,64]{1,0:T(8,128)(2,1)} %inverse_ref.1) | copy-start | bytes 24580

commit v7 on v6

--- a/solution.py
+++ b/solution.py
@@ -283,7 +283,7 @@
 
 
 def write_halos(c, down, up, first_ref, second_ref):
-    forward = jnp.bitwise_and(c, 2) == 0
+    forward = jnp.bitwise_and(c, 2) != 0
     for k, (low, high) in enumerate(zip(down, up)):
         first_ref[k] = jnp.where(forward, low, high)
         second_ref[k] = jnp.where(forward, high, low)
@@ -291,7 +291,7 @@
 
 def read_halos(plan, first_ref, second_ref):
     r, c = lax.axis_index("px"), lax.axis_index("py")
-    forward = jnp.bitwise_and(c, 2) == 0
+    forward = jnp.bitwise_and(c, 2) != 0
     above = jnp.where(r > 0, 1.0, 0.0).astype(F32)
     below = jnp.where(r < plan.n - 1, 1.0, 0.0).astype(F32)
     first, second = first_ref[...], second_ref[...]
@@ -459,42 +459,55 @@
     return jnp.concatenate(out, axis=1).astype(BF16)[:, : 4 * (LANES + 2)]
 
 
+def solve_pairs(plan, level, rows, pairs, factor_ref):
+    w, solved = plan.tile[level], []
+    for t in range(plan.tiles[level]):
+        solved.append([])
+        for at, b in pairs:
+            window = rows[at : at + 4]
+            if w == LANES:
+                lhs = assemble_tiles(window, t)
+            else:
+                lhs = assemble([[row] for row in window], w)
+            solved[t].append(solve(lhs, factor_ref[b, t]))
+    return solved
+
+
+def lift_pairs(plan, level, solved, blocks, block_ref):
+    c, w = lax.axis_index("py"), plan.tile[level]
+    name, count = f"lift{level}", len(solved[0]) * plan.rhs
+    stacked = [jnp.concatenate(values, axis=0) for values in solved]
+    if w % LANES == 0:
+        both = [
+            jnp.concatenate([v[:, j * w : (j + 1) * w] for v in stacked], axis=1)
+            for j in range(2)
+        ]
+        both = product(jnp.concatenate(both, axis=0), blocks.get(block_ref, name, c))
+        return [both[:count], both[count:]]
+    row = jnp.concatenate(stacked, axis=1)
+    return [product(row, blocks.get(block_ref, name, 2 * c + j)) for j in range(2)]
+
+
 def coarse_kernel(plan, blocks, block_ref, *refs):
     factors, outs = refs[:3], refs[3 + 2 * plan.m :]
     early, late = refs[3 : 3 + plan.m], refs[3 + plan.m : 3 + 2 * plan.m]
     c, rhs = lax.axis_index("py"), plan.rhs
     down, up = [], []
     for level in (1, 2, 3):
-        w, tiles = plan.tile[level], plan.tiles[level]
         rows = level_rows(plan, level, early, late, blocks, block_ref)
-        factor_ref, out_ref = factors[level - 1], outs[level - 1]
-        solved = [[] for _ in range(tiles)]
-        for b in range(plan.h[level] // 2):
-            for t in range(tiles):
-                window = rows[2 * b : 2 * b + 4]
-                if w == LANES:
-                    lhs = assemble_tiles(window, t)
-                else:
-                    lhs = assemble([[row] for row in window], w)
-                solved[t].append(solve(lhs, factor_ref[b, t]))
-        pairs = plan.h[level] // 2
-        stacked = [jnp.concatenate(solved[t], axis=0) for t in range(tiles)]
-        lifted = []
-        name = f"lift{level}"
-        if w % LANES == 0:
-            both = [
-                jnp.concatenate([v[:, j * w : (j + 1) * w] for v in stacked], axis=1)
-                for j in range(2)
-            ]
-            both = product(jnp.concatenate(both, axis=0), blocks.get(block_ref, name, c))
-            lifted = [both[: pairs * rhs], both[pairs * rhs :]]
+        w, count = plan.tile[level], plan.h[level] // 2
+        pairs = [(2 * b, b) for b in sorted({0, count - 1})]
+        if level == 1:
+            for i, row in enumerate(rows[2:-2]):
+                outs[3][i] = row
         else:
-            row = jnp.concatenate(stacked, axis=1)
-            lifted = [product(row, blocks.get(block_ref, name, 2 * c + j)) for j in range(2)]
-        for b in range(pairs):
+            pairs = [(2 * b, b) for b in range(count)]
+        solved = solve_pairs(plan, level, rows, pairs, factors[level - 1])
+        lifted = lift_pairs(plan, level, solved, blocks, block_ref)
+        for b in range(len(pairs)):
             for j in range(2):
-                out_ref[2 * b + j] = lifted[j][b * rhs : (b + 1) * rhs]
-        for j, (edge, at) in enumerate(((up, 0), (down, pairs - 1))):
+                outs[level - 1][2 * b + j] = lifted[j][b * rhs : (b + 1) * rhs]
+        for j, (edge, at) in enumerate(((up, 0), (down, -1))):
             for value in solved:
                 if w % LANES == 0:
                     edge.append(value[at][:, j * w : (j + 1) * w])
@@ -502,7 +515,18 @@
                     edge.append(pltpu.roll(value[at], LANES - w, 1) if j else value[at])
     edges = [jnp.concatenate(edge, axis=1) for edge in (down, up)]
     picked = product(jnp.concatenate(edges, axis=0), blocks.get(block_ref, "pick", c))
-    write_halos(c, [picked[:rhs]], [picked[rhs:]], outs[3], outs[4])
+    write_halos(c, [picked[:rhs]], [picked[rhs:]], outs[4], outs[5])
+
+
+def inner_kernel(plan, blocks, block_ref, factor_ref, rows_ref, out_ref):
+    rhs, count = plan.rhs, plan.h[1] // 2
+    rows = [rows_ref[i] for i in range(rows_ref.shape[0])]
+    pairs = [(2 * (b - 1), b) for b in range(1, count - 1)]
+    solved = solve_pairs(plan, 1, rows, pairs, factor_ref)
+    lifted = lift_pairs(plan, 1, solved, blocks, block_ref)
+    for b in range(len(pairs)):
+        for j in range(2):
+            out_ref[2 * b + j] = lifted[j][b * rhs : (b + 1) * rhs]
 
 
 def fine_kernel(plan, blocks, block_ref, rows_ref, first_ref, second_ref, factor_ref, *refs):
@@ -637,8 +661,8 @@
         out_ref[k] = four_rows[r + k]
 
 
-def final_kernel(plan, blocks, block_ref, fine_ref, one_ref, two_ref, three_ref, four_ref,
-                 first_ref, second_ref, out_ref, whole_ref, semaphores):
+def final_kernel(plan, blocks, block_ref, fine_ref, one_ref, inner_ref, two_ref, three_ref,
+                 four_ref, first_ref, second_ref, out_ref, whole_ref, semaphores):
     r, rhs = lax.axis_index("px"), plan.rhs
     above = jnp.where(r > 0, 1.0, 0.0).astype(F32)
     below = jnp.where(r < plan.n - 1, 1.0, 0.0).astype(F32)
@@ -659,7 +683,10 @@
             height = plan.h[level]
             lifted = lift_rows(rows, -1, height + 1)
             rows = [lifted[0] * above + from_above[level - 1][own]]
-            rows += [lifted[i + 1] + own_ref[i, own] for i in range(height)]
+            parts = [own_ref[i, own] for i in range(own_ref.shape[0])]
+            if level == 1:
+                parts[2:2] = [inner_ref[i, own] for i in range(inner_ref.shape[0])]
+            rows += [lifted[i + 1] + parts[i] for i in range(height)]
             rows += [lifted[-1] * below + from_below[level - 1][own]]
         lifted = lift_rows(rows, 0, plan.h0)
         start, count = 8 * part * plan.h0, 8 * plan.h0
@@ -684,7 +711,7 @@
 
     def trade(first, second):
         def target(i, c):
-            after = i - 1 if c & 2 else i + 1
+            after = i + 1 if c & 2 else i - 1
             return (after, c) if 0 <= after < n else (i, c ^ 2)
 
         ring = []
@@ -760,13 +787,17 @@
         if 2 * k + 1 < len(order):
             gathered.append(swap(value, 1))
 
-    one, two, three, low, high = kernel_call(
+    one, two, three, inner, low, high = kernel_call(
         functools.partial(coarse_kernel, plan, blocks),
-        tuple(shape(h[l], rhs, LANES) for l in (1, 2, 3))
+        (shape(4, rhs, LANES), shape(h[2], rhs, LANES), shape(h[3], rhs, LANES),
+         shape(h[1] - 2, rhs, plan.ny[1]))
         + (shape(1, rhs, LANES), shape(1, rhs, LANES)),
         cost_us=2.5,
     )(matrices, factor_one, factor_two, factor_three, *early, *late)
     low, high = trade(low, high)
+    inner = kernel_call(
+        functools.partial(inner_kernel, plan, blocks), shape(h[1] - 4, rhs, LANES), cost_us=0.6
+    )(matrices, factor_one, inner)
 
     fine = kernel_call(
         functools.partial(fine_kernel, plan, blocks), shape(h0, rhs, plan.w0)
@@ -784,7 +815,7 @@
         scratch=(pltpu.VMEM((rhs * h0, plan.w0), F32), pltpu.SemaphoreType.DMA((rhs // 8,))),
         out_space=pl.ANY,
     )(
-        matrices, fine, one, two, three, four, low, high
+        matrices, fine, one, inner, two, three, four, low, high
     )
     return out.reshape(rhs, h0, plan.w0)
 

time: 27.3 us -> 26.6 us (0.974)
  waiting for transfers between devices: 8.58 us -> 7.89 us
  starting transfers between devices: 12.4 us -> 12.1 us
  Pallas kernels: 5.45 us -> 5.75 us
    ppermute x2, waiting for transfers between devices: 3.23 us -> 1.99 us  [trade(): lax.ppermute(second, ('px', 'py'), back)]
    ppermute x7, waiting for transfers between devices: 3.32 us -> 3.87 us  [swap(): return lax.ppermute(value, 'py', [(i, i ^ bits) for i in range(m)])]
    ppermute x2, starting transfers between devices: 4.67 us -> 4.24 us  [per_device(): lax.ppermute(pairs, ('px', 'py'), [(i * m + c, (i ^ 2 * (odd if c % 2 els...]
    pallas_call x8 -> x9, Pallas kernels: 5.45 us -> 5.75 us  [call(): pl.pallas_call(body, out_shape=out_shape, in_specs=[whole] * len(operands...]
  transfers between devices with their start and end apart: 13 -> 13, of which waited for: 7 -> 5; matrix products, arithmetic and copies ran while one was open for 0% -> 0% of each run, Pallas kernels for 13% -> 15%
where the time goes in v7:
time: 26.6 us; the launch traced here: 26.5 us
  starting transfers between devices  12.1 us (45%)
  waiting for transfers between devices  7.89 us (30%)
  Pallas kernels  5.75 us (22%)
  local copies, waits for them, and re-layouts  0.59 us (2%)
    pallas_call x9, Pallas kernels, call(): pl.pallas_call(body, out_shape=out_shape, in_specs=[whole] * len(operands...  5.75 us
    ppermute x2, starting transfers between devices, per_device(): lax.ppermute(pairs, ('px', 'py'), [(i * m + c, (i ^ 2 * (odd if c % 2 els...  4.24 us
    ppermute x7, waiting for transfers between devices, swap(): return lax.ppermute(value, 'py', [(i, i ^ bits) for i in range(m)])  3.87 us
    ppermute x2, starting transfers between devices, trade(): lax.ppermute(first, ('px', 'py'), ring)  3.77 us
    ppermute x7, starting transfers between devices, swap(): return lax.ppermute(value, 'py', [(i, i ^ bits) for i in range(m)])  2.67 us
    ppermute x2, waiting for transfers between devices, trade(): lax.ppermute(first, ('px', 'py'), ring)  2.02 us
    ppermute x2, waiting for transfers between devices, trade(): lax.ppermute(second, ('px', 'py'), back)  1.99 us
    ppermute x2, starting transfers between devices, trade(): lax.ppermute(second, ('px', 'py'), back)  1.37 us
  transfers between devices with their start and end apart: 13, of which 5 were waited for; matrix products, arithmetic and copies ran while one was open for 0% of the time, Pallas kernels for 15%

profile of v7, /device:TPU:0, one launch (start us, length us, event | category | flops | bytes accessed | tf_op | source)
XLA Modules:
  0.0 26.5 jit_solution(8565324605008399275)
XLA Ops:
  0.0 0.4 %shard_map.82.shrink_ref = bf16[4,128,128]{2,1,0:T(8,128)(2,1)S(1)} custom-call(), custom_call_target="tpu_custom_call" | custom-call | flops 4000000000 | bytes 12000000 | tf_op jit(solution)/shard_map/pallas_call | solution.py:244
  0.4 0.5 %copy-done.6 = f32[32,16,128]{2,1,0:T(8,128)S(1)} copy-done((f32[32,16,128]{2,1,0:T(8,128)S(1)}, f32[32,16,128]{2,1,0:T(8,128)}, u32[]{:S(2)}) %copy-start.6) | copy-done | bytes 262168
  1.0 0.4 %shard_map.83 = (f32[4,32,128]{2,1,0:T(8,128)S(1)}, f32[4,32,128]{2,1,0:T(8,128)S(1)}, f32[3,32,128]{2,1,0:T(8,128)S(1)}, f32[3,32,128]{2,1,0:T(8,128)S(1)}, f32[16,32,128]{2,1,0:T(8,128)S(1)}) custom-call(f32[512,128]{1,0:T(8,128)S(1)} %bitcast.4, bf16[4,128,128]{2,1,0:T(8,128)(2,1)S(1)} %shard_map.82.shrink_ref), custom_call_target="tpu_custom_call" | custom-call | flops 1000000000 | bytes 3000000 | tf_op jit(solution)/shard_map/pallas_call | solution.py:244
  1.3 3.0 %collective-permute-start = (f32[3,32,128]{2,1,0:T(8,128)S(1)}, f32[3,32,128]{2,1,0:T(8,128)S(1)}, u32[]{:S(2)}, u32[]{:S(2)}) collective-permute-start(f32[3,32,128]{2,1,0:T(8,128)S(1)} %get-tuple-element.21), channel_id=1, source_target_pairs={{0,2},{1,3},{2,6},{3,7},{4,0},{5,1},{6,10},{7,11},{8,4},{9,5},{10,... | collective-permute-start | bytes 147464 | tf_op jit(solution)/shard_map/ppermute | solution.py:723
  4.3 0.1 collective-permute-start.1
  4.4 2.0 %collective-permute-done.first_ref = f32[3,32,128]{2,1,0:T(8,128)S(1)} collective-permute-done((f32[3,32,128]{2,1,0:T(8,128)S(1)}, f32[3,32,128]{2,1,0:T(8,128)S(1)}, u32[]{:S(2)}, u32[]{:S(2)}) %collective-permute-start) | collective-permute-done | bytes 49184 | tf_op jit(solution)/shard_map/ppermute | solution.py:723
  6.4 2.0 %collective-permute-done.1.second_ref = f32[3,32,128]{2,1,0:T(8,128)S(1)} collective-permute-done((f32[3,32,128]{2,1,0:T(8,128)S(1)}, f32[3,32,128]{2,1,0:T(8,128)S(1)}, u32[]{:S(2)}, u32[]{:S(2)}) %collective-permute-start.1) | collective-permute-done | bytes 49184 | tf_op jit(solution)/shard_map/ppermute | solution.py:723
  8.4 0.2 shard_map.84.refs_0_.refs_4_.refs_7_
  8.6 0.0 copy-start.5
  8.6 0.0 copy-start.7
  8.6 1.6 %collective-permute-start.6 = (f32[136,128]{1,0:T(8,128)S(1)}, f32[136,128]{1,0:T(8,128)S(1)}, u32[]{:S(2)}, u32[]{:S(2)}) collective-permute-start(f32[136,128]{1,0:T(8,128)S(1)} %shard_map.84.refs_0_.refs_4_.refs_7_), channel_id=1, source_target_pairs={{0,2},{1,3},{2,0},{3,1},{4,6},{5,7},{6,4},{7,5},{8,10},{9,11},{10,... | collective-permute-start | bytes 208904 | tf_op jit(solution)/shard_map/ppermute | solution.py:726
  10.2 0.5 %collective-permute-start.3 = (f32[4,32,128]{2,1,0:T(8,128)S(1)}, f32[4,32,128]{2,1,0:T(8,128)S(1)}, u32[]{:S(2)}, u32[]{:S(2)}) collective-permute-start(f32[4,32,128]{2,1,0:T(8,128)S(1)} %get-tuple-element.23.refs_0_.refs_3_), channel_id=1, source_target_pairs={{0,2},{1,3},{2,0},{3,1},{4,6},{5,7},{6,4},{7,5},{8,10},{9,11},{10,... | collective-permute-start | bytes 196616 | tf_op jit(solution)/shard_map/ppermute | solution.py:726
  10.7 0.0 collective-permute-start.5
  10.7 2.3 %collective-permute-done.6.refs_2_.refs_6_.refs_9_ = f32[136,128]{1,0:T(8,128)S(1)} collective-permute-done((f32[136,128]{1,0:T(8,128)S(1)}, f32[136,128]{1,0:T(8,128)S(1)}, u32[]{:S(2)}, u32[]{:S(2)}) %collective-permute-start.6) | collective-permute-done | bytes 69664 | tf_op jit(solution)/shard_map/ppermute | solution.py:726
  13.0 0.0 collective-permute-start.7
  13.0 0.5 %collective-permute-start.2 = (f32[4,32,128]{2,1,0:T(8,128)S(1)}, f32[4,32,128]{2,1,0:T(8,128)S(1)}, u32[]{:S(2)}, u32[]{:S(2)}) collective-permute-start(f32[4,32,128]{2,1,0:T(8,128)S(1)} %get-tuple-element.23.refs_0_.refs_3_), channel_id=1, source_target_pairs={{0,1},{1,0},{2,3},{3,2},{4,5},{5,4},{6,7},{7,6},{8,9},{9,8},{10,11... | collective-permute-start | bytes 196616 | tf_op jit(solution)/shard_map/ppermute | solution.py:726
  13.5 1.0 %collective-permute-done.3.refs_2_.refs_5_ = f32[4,32,128]{2,1,0:T(8,128)S(1)} collective-permute-done((f32[4,32,128]{2,1,0:T(8,128)S(1)}, f32[4,32,128]{2,1,0:T(8,128)S(1)}, u32[]{:S(2)}, u32[]{:S(2)}) %collective-permute-start.3) | collective-permute-done | bytes 65568 | tf_op jit(solution)/shard_map/ppermute | solution.py:726
  14.5 0.0 collective-permute-start.4
  14.5 0.0 collective-permute-done.5.refs_1_.refs_5_.refs_8_
  14.5 0.0 collective-permute-done.7.refs_3_.refs_7_.refs_10_
  14.5 0.0 copy-done
  14.5 0.2 shard_map.85.refs_0_
  14.7 0.0 copy-start.1
  14.7 4.2 %collective-permute-start.10 = (f32[32,128]{1,0:T(8,128)S(1)}, f32[32,128]{1,0:T(8,128)S(1)}, u32[]{:S(2)}, u32[]{:S(2)}) collective-permute-start(f32[32,128]{1,0:T(8,128)S(1)} %shard_map.85.refs_0_), channel_id=1, source_target_pairs={{0,24},{1,25},{2,26},{3,27},{4,28},{5,29},{6,30},{7,31},{8,16},{9,... | collective-permute-start | bytes 49160 | tf_op jit(solution)/shard_map/ppermute | solution.py:778
  19.0 0.0 collective-permute-start.8
  19.0 0.0 collective-permute-done.2.refs_1_.refs_4_
  19.0 0.0 collective-permute-done.4.refs_3_.refs_6_
  19.0 0.0 copy-done.2
  19.0 0.0 copy-done.5
  19.0 0.0 copy-done.7
  19.0 1.5 %shard_map.87 = (f32[4,32,128]{2,1,0:T(8,128)S(1)}, f32[4,32,128]{2,1,0:T(8,128)S(1)}, f32[2,32,128]{2,1,0:T(8,128)S(1)}, f32[6,32,256]{2,1,0:T(8,128)S(1)}, f32...) custom-call(bf16[120,128,128]{2,1,0:T(8,128)(2,1)S(1)} %copy-done, bf16[4,2,520,256]{3,2,1,0:T(8,128)(2,1)S(1)} %copy-done.2, ...), custom_call_target="tpu_custom_call" | custom-call | flops 2500000000 | bytes 7500000 | tf_op jit(solution)/shard_map/pallas_call | solution.py:244
  20.5 0.8 %collective-permute-start.11 = (f32[1,32,128]{2,1,0:T(8,128)S(1)}, f32[1,32,128]{2,1,0:T(8,128)S(1)}, u32[]{:S(2)}, u32[]{:S(2)}) collective-permute-start(f32[1,32,128]{2,1,0:T(8,128)S(1)} %get-tuple-element.33), channel_id=1, source_target_pairs={{0,2},{1,3},{2,6},{3,7},{4,0},{5,1},{6,10},{7,11},{8,4},{9,5},{10,... | collective-permute-start | bytes 49160 | tf_op jit(solution)/shard_map/ppermute | solution.py:723
  21.3 1.3 %collective-permute-start.12 = (f32[1,32,128]{2,1,0:T(8,128)S(1)}, f32[1,32,128]{2,1,0:T(8,128)S(1)}, u32[]{:S(2)}, u32[]{:S(2)}) collective-permute-start(f32[1,32,128]{2,1,0:T(8,128)S(1)} %get-tuple-element.34), channel_id=1, source_target_pairs={{2,0},{3,1},{6,2},{7,3},{0,4},{1,5},{10,6},{11,7},{4,8},{5,9},{14,... | collective-permute-start | bytes 49160 | tf_op jit(solution)/shard_map/ppermute | solution.py:723
  22.6 0.0 copy-done.1
  22.6 0.8 %shard_map.86.fine_ref = f32[16,32,128]{2,1,0:T(8,128)S(1)} custom-call(bf16[120,128,128]{2,1,0:T(8,128)(2,1)S(1)} %copy-done, f32[16,32,128]{2,1,0:T(8,128)S(1)} %get-tuple-element.20.rows_ref, f32[3,32,128]{2,1,0:T(8,128)S(1)} %collective-permute-done.first_ref, f32[3,32,128]{2,1,0:T(8,128)S(1)} %collective-permute-done.1.second_ref, ...), custom_call_target="tpu_custom_call" | custom-call | flops 1000000000 | bytes 3000000 | tf_op jit(solution)/shard_map/pallas_call | solution.py:244
  23.5 0.0 collective-permute-done.8.refs_1_
  23.5 0.1 collective-permute-start.9
  23.5 0.0 copy-start.3
  23.6 0.0 copy-start.4
  23.6 0.5 %shard_map.88.inner_ref = f32[4,32,128]{2,1,0:T(8,128)S(1)} custom-call(bf16[120,128,128]{2,1,0:T(8,128)(2,1)S(1)} %copy-done, bf16[4,2,520,256]{3,2,1,0:T(8,128)(2,1)S(1)} %copy-done.2, f32[6,32,256]{2,1,0:T(8,128)S(1)} %get-tuple-element.30.rows_ref), custom_call_target="tpu_custom_call" | custom-call | flops 600000000 | bytes 1800000 | tf_op jit(solution)/shard_map/pallas_call | solution.py:244
  24.1 0.0 collective-permute-done.10.refs_3_
  24.1 0.6 %collective-permute-done.9.refs_2_ = f32[32,128]{1,0:T(8,128)S(1)} collective-permute-done((f32[32,128]{1,0:T(8,128)S(1)}, f32[32,128]{1,0:T(8,128)S(1)}, u32[]{:S(2)}, u32[]{:S(2)}) %collective-permute-start.9) | collective-permute-done | bytes 16416 | tf_op jit(solution)/shard_map/ppermute | solution.py:726
  24.7 0.0 copy-done.3
  24.7 0.0 copy-done.4
  24.7 0.8 %shard_map.89.four_ref = f32[3,32,128]{2,1,0:T(8,128)S(1)} custom-call(bf16[120,128,128]{2,1,0:T(8,128)(2,1)S(1)} %copy-done, bf16[4,1,64,136]{3,2,1,0:T(8,128)(2,1)S(1)} %bitcast.3, bf16[64,64]{1,0:T(8,128)(2,1)S(1)} %copy-done.4, f32[32,128]{1,0:T(8,128)S(1)} %shard_map.85.refs_0_, f32[32,128]{1,0:T(8,128)S(1)} %collective-permute-done.8.refs_1_, ...), custom_call_target="tpu_custom_call" | custom-call | flops 1000000000 | bytes 3000000 | tf_op jit(solution)/shard_map/pallas_call | solution.py:244
  25.5 0.0 collective-permute-done.11.first_ref
  25.5 0.0 collective-permute-done.12.second_ref
  25.5 0.9 %shard_map.90 = f32[512,128]{1,0:T(8,128)} custom-call(bf16[120,128,128]{2,1,0:T(8,128)(2,1)S(1)} %copy-done, f32[16,32,128]{2,1,0:T(8,128)S(1)} %shard_map.86.fine_ref, f32[4,32,128]{2,1,0:T(8,128)S(1)} %get-tuple-element.29.one_ref, f32[4,32,128]{2,1,0:T(8,128)S(1)} %shard_map.88.inner_ref, f32[4,32,128]{2,1,0:T(8,128)S(1)} %get-tuple-element.31.two_ref, ...), custom_call_target="tpu_custom_call" | custom-call | flops 1000000000 | bytes 3000000 | tf_op jit(solution)/shard_map/pallas_call | solution.py:244
  (3 shorter events, 0.0 us)
Async XLA Ops:
  0.0 0.9 %copy-start.6 = (f32[32,16,128]{2,1,0:T(8,128)S(1)}, f32[32,16,128]{2,1,0:T(8,128)}, u32[]{:S(2)}) copy-start(f32[32,16,128]{2,1,0:T(8,128)} %param.8) | copy-start | bytes 786436
  1.0 13.5 %copy-start = (bf16[120,128,128]{2,1,0:T(8,128)(2,1)S(1)}, bf16[120,128,128]{2,1,0:T(8,128)(2,1)}, u32[]{:S(2)}) copy-start(bf16[120,128,128]{2,1,0:T(8,128)(2,1)} %constant.2.clone.block_ref) | copy-start | bytes 11796484
  1.3 5.1 %collective-permute-start = (f32[3,32,128]{2,1,0:T(8,128)S(1)}, f32[3,32,128]{2,1,0:T(8,128)S(1)}, u32[]{:S(2)}, u32[]{:S(2)}) collective-permute-start(f32[3,32,128]{2,1,0:T(8,128)S(1)} %get-tuple-element.21), channel_id=1, source_target_pairs={{0,2},{1,3},{2,6},{3,7},{4,0},{5,1},{6,10},{7,11},{8,4},{9,5},{10,... | collective-permute-start | bytes 147464 | tf_op jit(solution)/shard_map/ppermute | solution.py:723
  4.3 4.1 %collective-permute-start.1 = (f32[3,32,128]{2,1,0:T(8,128)S(1)}, f32[3,32,128]{2,1,0:T(8,128)S(1)}, u32[]{:S(2)}, u32[]{:S(2)}) collective-permute-start(f32[3,32,128]{2,1,0:T(8,128)S(1)} %get-tuple-element.22), channel_id=1, source_target_pairs={{2,0},{3,1},{6,2},{7,3},{0,4},{1,5},{10,6},{11,7},{4,8},{5,9},{14,... | collective-permute-start | bytes 147464 | tf_op jit(solution)/shard_map/ppermute | solution.py:723
  8.6 10.4 %copy-start.2 = (bf16[4,2,520,256]{3,2,1,0:T(8,128)(2,1)S(1)}, bf16[4,2,520,256]{3,2,1,0:T(8,128)(2,1)}, u32[]{:S(2)}) copy-start(bf16[4,2,520,256]{3,2,1,0:T(8,128)(2,1)} %factor_ref.3) | copy-start | bytes 6389764
  8.6 10.4 %copy-start.5 = (bf16[2,1,520,256]{3,2,1,0:T(8,128)(2,1)S(1)}, bf16[2,1,520,256]{3,2,1,0:T(8,128)(2,1)}, u32[]{:S(2)}) copy-start(bf16[2,1,520,256]{3,2,1,0:T(8,128)(2,1)} %refs_1_.1) | copy-start | bytes 1597444
  8.6 10.4 %copy-start.7 = (bf16[1,1,264,128]{3,2,1,0:T(8,128)(2,1)S(1)}, bf16[1,1,264,128]{3,2,1,0:T(8,128)(2,1)}, u32[]{:S(2)}) copy-start(bf16[1,1,264,128]{3,2,1,0:T(8,128)(2,1)} %refs_2_.1) | copy-start | bytes 202756
  8.6 4.4 %collective-permute-start.6 = (f32[136,128]{1,0:T(8,128)S(1)}, f32[136,128]{1,0:T(8,128)S(1)}, u32[]{:S(2)}, u32[]{:S(2)}) collective-permute-start(f32[136,128]{1,0:T(8,128)S(1)} %shard_map.84.refs_0_.refs_4_.refs_7_), channel_id=1, source_target_pairs={{0,2},{1,3},{2,0},{3,1},{4,6},{5,7},{6,4},{7,5},{8,10},{9,11},{10,... | collective-permute-start | bytes 208904 | tf_op jit(solution)/shard_map/ppermute | solution.py:726
  10.2 4.3 %collective-permute-start.3 = (f32[4,32,128]{2,1,0:T(8,128)S(1)}, f32[4,32,128]{2,1,0:T(8,128)S(1)}, u32[]{:S(2)}, u32[]{:S(2)}) collective-permute-start(f32[4,32,128]{2,1,0:T(8,128)S(1)} %get-tuple-element.23.refs_0_.refs_3_), channel_id=1, source_target_pairs={{0,2},{1,3},{2,0},{3,1},{4,6},{5,7},{6,4},{7,5},{8,10},{9,11},{10,... | collective-permute-start | bytes 196616 | tf_op jit(solution)/shard_map/ppermute | solution.py:726
  10.7 3.8 %collective-permute-start.5 = (f32[136,128]{1,0:T(8,128)S(1)}, f32[136,128]{1,0:T(8,128)S(1)}, u32[]{:S(2)}, u32[]{:S(2)}) collective-permute-start(f32[136,128]{1,0:T(8,128)S(1)} %shard_map.84.refs_0_.refs_4_.refs_7_), channel_id=1, source_target_pairs={{0,1},{1,0},{2,3},{3,2},{4,5},{5,4},{6,7},{7,6},{8,9},{9,8},{10,11... | collective-permute-start | bytes 208904 | tf_op jit(solution)/shard_map/ppermute | solution.py:726
  13.0 1.5 %collective-permute-start.7 = (f32[136,128]{1,0:T(8,128)S(1)}, f32[136,128]{1,0:T(8,128)S(1)}, u32[]{:S(2)}, u32[]{:S(2)}) collective-permute-start(f32[136,128]{1,0:T(8,128)S(1)} %collective-permute-done.6.refs_2_.refs_6_.refs_9_), channel_id=1, source_target_pairs={{0,1},{1,0},{2,3},{3,2},{4,5},{5,4},{6,7},{7,6},{8,9},{9,8},{10,11... | collective-permute-start | bytes 208904 | tf_op jit(solution)/shard_map/ppermute | solution.py:726
  13.0 6.0 %collective-permute-start.2 = (f32[4,32,128]{2,1,0:T(8,128)S(1)}, f32[4,32,128]{2,1,0:T(8,128)S(1)}, u32[]{:S(2)}, u32[]{:S(2)}) collective-permute-start(f32[4,32,128]{2,1,0:T(8,128)S(1)} %get-tuple-element.23.refs_0_.refs_3_), channel_id=1, source_target_pairs={{0,1},{1,0},{2,3},{3,2},{4,5},{5,4},{6,7},{7,6},{8,9},{9,8},{10,11... | collective-permute-start | bytes 196616 | tf_op jit(solution)/shard_map/ppermute | solution.py:726
  14.5 4.5 %collective-permute-start.4 = (f32[4,32,128]{2,1,0:T(8,128)S(1)}, f32[4,32,128]{2,1,0:T(8,128)S(1)}, u32[]{:S(2)}, u32[]{:S(2)}) collective-permute-start(f32[4,32,128]{2,1,0:T(8,128)S(1)} %collective-permute-done.3.refs_2_.refs_5_), channel_id=1, source_target_pairs={{0,1},{1,0},{2,3},{3,2},{4,5},{5,4},{6,7},{7,6},{8,9},{9,8},{10,11... | collective-permute-start | bytes 196616 | tf_op jit(solution)/shard_map/ppermute | solution.py:726
  14.7 7.9 %copy-start.1 = (bf16[8,1,520,256]{3,2,1,0:T(8,128)(2,1)S(1)}, bf16[8,1,520,256]{3,2,1,0:T(8,128)(2,1)}, u32[]{:S(2)}) copy-start(bf16[8,1,520,256]{3,2,1,0:T(8,128)(2,1)} %factor_ref.2) | copy-start | bytes 6389764
  14.7 9.4 %collective-permute-start.10 = (f32[32,128]{1,0:T(8,128)S(1)}, f32[32,128]{1,0:T(8,128)S(1)}, u32[]{:S(2)}, u32[]{:S(2)}) collective-permute-start(f32[32,128]{1,0:T(8,128)S(1)} %shard_map.85.refs_0_), channel_id=1, source_target_pairs={{0,24},{1,25},{2,26},{3,27},{4,28},{5,29},{6,30},{7,31},{8,16},{9,... | collective-permute-start | bytes 49160 | tf_op jit(solution)/shard_map/ppermute | solution.py:778
  19.0 4.5 %collective-permute-start.8 = (f32[32,128]{1,0:T(8,128)S(1)}, f32[32,128]{1,0:T(8,128)S(1)}, u32[]{:S(2)}, u32[]{:S(2)}) collective-permute-start(f32[32,128]{1,0:T(8,128)S(1)} %shard_map.85.refs_0_), channel_id=1, source_target_pairs={{0,8},{1,17},{2,10},{3,19},{4,12},{5,21},{6,14},{7,23},{8,0},{9,25... | collective-permute-start | bytes 49160 | tf_op jit(solution)/shard_map/ppermute | solution.py:778
  20.5 5.0 %collective-permute-start.11 = (f32[1,32,128]{2,1,0:T(8,128)S(1)}, f32[1,32,128]{2,1,0:T(8,128)S(1)}, u32[]{:S(2)}, u32[]{:S(2)}) collective-permute-start(f32[1,32,128]{2,1,0:T(8,128)S(1)} %get-tuple-element.33), channel_id=1, source_target_pairs={{0,2},{1,3},{2,6},{3,7},{4,0},{5,1},{6,10},{7,11},{8,4},{9,5},{10,... | collective-permute-start | bytes 49160 | tf_op jit(solution)/shard_map/ppermute | solution.py:723
  21.3 4.2 %collective-permute-start.12 = (f32[1,32,128]{2,1,0:T(8,128)S(1)}, f32[1,32,128]{2,1,0:T(8,128)S(1)}, u32[]{:S(2)}, u32[]{:S(2)}) collective-permute-start(f32[1,32,128]{2,1,0:T(8,128)S(1)} %get-tuple-element.34), channel_id=1, source_target_pairs={{2,0},{3,1},{6,2},{7,3},{0,4},{1,5},{10,6},{11,7},{4,8},{5,9},{14,... | collective-permute-start | bytes 49160 | tf_op jit(solution)/shard_map/ppermute | solution.py:723
  23.5 1.2 %collective-permute-start.9 = (f32[32,128]{1,0:T(8,128)S(1)}, f32[32,128]{1,0:T(8,128)S(1)}, u32[]{:S(2)}, u32[]{:S(2)}) collective-permute-start(f32[32,128]{1,0:T(8,128)S(1)} %collective-permute-done.8.refs_1_), channel_id=1, source_target_pairs={{0,1},{1,0},{2,3},{3,2},{4,5},{5,4},{6,7},{7,6},{8,9},{9,8},{10,11... | collective-permute-start | bytes 49160 | tf_op jit(solution)/shard_map/ppermute | solution.py:726
  23.5 1.2 %copy-start.3 = (bf16[4,1,136,64]{2,3,1,0:T(8,128)(2,1)S(1)}, bf16[4,1,136,64]{2,3,1,0:T(8,128)(2,1)}, u32[]{:S(2)}) copy-start(bf16[4,1,136,64]{2,3,1,0:T(8,128)(2,1)} %param.13) | copy-start | bytes 208900
  23.6 1.2 %copy-start.4 = (bf16[64,64]{1,0:T(8,128)(2,1)S(1)}, bf16[64,64]{1,0:T(8,128)(2,1)}, u32[]{:S(2)}) copy-start(bf16[64,64]{1,0:T(8,128)(2,1)} %inverse_ref.1) | copy-start | bytes 24580

commit v8 on v7

--- a/solution.py
+++ b/solution.py
@@ -73,14 +73,6 @@
     def place_four(self):
         rows = [self.place(4, 0, 4 * self.ny[4], j * self.ny[4]) for j in range(4)]
         return np.stack(rows, axis=1)
-
-    def halo_lanes(self):
-        out = np.zeros((2, LANES, self.sides, LANES))
-        for j in range(self.sides):
-            for position in range(4):
-                out[0, self.offset[3] + 2 * j, j, 2 * position] = 1
-                out[1, self.offset[3] + 2 * j + 1, j, 2 * position + 1] = 1
-        return out.reshape(2, LANES, self.sides * LANES)
 
     def pick_band(self):
         out = []
@@ -503,10 +495,9 @@
         else:
             pairs = [(2 * b, b) for b in range(count)]
         solved = solve_pairs(plan, level, rows, pairs, factors[level - 1])
-        lifted = lift_pairs(plan, level, solved, blocks, block_ref)
-        for b in range(len(pairs)):
-            for j in range(2):
-                outs[level - 1][2 * b + j] = lifted[j][b * rhs : (b + 1) * rhs]
+        for t, values in enumerate(solved):
+            for k, value in enumerate(values):
+                outs[level - 1][t, k] = value
         for j, (edge, at) in enumerate(((up, 0), (down, -1))):
             for value in solved:
                 if w % LANES == 0:
@@ -518,93 +509,100 @@
     write_halos(c, [picked[:rhs]], [picked[rhs:]], outs[4], outs[5])
 
 
-def inner_kernel(plan, blocks, block_ref, factor_ref, rows_ref, out_ref):
+def inner_kernel(plan, blocks, block_ref, factor_ref, rows_ref, one_ref, two_ref, three_ref,
+                 main_ref, picked_ref, *refs):
+    early, late = refs[: plan.m], refs[plan.m : 2 * plan.m]
+    outs, fine_ref = refs[2 * plan.m : -1], refs[-1]
     rhs, count = plan.rhs, plan.h[1] // 2
     rows = [rows_ref[i] for i in range(rows_ref.shape[0])]
     pairs = [(2 * (b - 1), b) for b in range(1, count - 1)]
-    solved = solve_pairs(plan, 1, rows, pairs, factor_ref)
-    lifted = lift_pairs(plan, 1, solved, blocks, block_ref)
-    for b in range(len(pairs)):
+    inner = solve_pairs(plan, 1, rows, pairs, factor_ref)
+    for level, ref in ((1, one_ref), (2, two_ref), (3, three_ref)):
+        solved = []
+        for t in range(ref.shape[0]):
+            values = [ref[t, k] for k in range(ref.shape[1])]
+            if level == 1:
+                values[1:1] = inner[t]
+            solved.append(values)
+        lifted = lift_pairs(plan, level, solved, blocks, block_ref)
+        for b in range(plan.h[level] // 2):
+            for j in range(2):
+                outs[level - 1][2 * b + j] = lifted[j][b * rhs : (b + 1) * rhs]
+    sides, w0 = side_columns(plan, early, late), plan.w0
+    lane = lane_index(rhs)
+    for b in range(plan.h0 // 2):
+        value = pltpu.roll(sides, (LANES - 4 * b) % LANES, 1) if b else sides
+        value = jnp.where(lane < 8, value, 0.0)[:, :16].astype(BF16)
+        added = jnp.dot(value, picked_ref[b], preferred_element_type=F32)
         for j in range(2):
-            out_ref[2 * b + j] = lifted[j][b * rhs : (b + 1) * rhs]
-
-
-def fine_kernel(plan, blocks, block_ref, rows_ref, first_ref, second_ref, factor_ref, *refs):
-    early, late, out_ref = refs[: plan.m], refs[plan.m : 2 * plan.m], refs[2 * plan.m]
-    c = lax.axis_index("py")
+            fine_ref[2 * b + j] = main_ref[2 * b + j] + added[:, j * w0 : (j + 1) * w0]
+
+
+def fine_kernel(plan, rows_ref, first_ref, second_ref, factor_ref, out_ref, picked_ref):
     rhs, h0, w0 = plan.rhs, plan.h0, plan.w0
     above, below = read_halos(plan, first_ref, second_ref)
-    values, matrices = [], []
-    left = blocks.get(block_ref, "halo", 0)
-    right = blocks.get(block_ref, "halo", 1)
     lane = lane_index(rhs)
-    spot = plan.offset[3] + plan.h0
-    for inner, outer, owner in zip(early, late, owners(plan)):
-        from_left = jnp.where(owner == c - 1, 1.0, 0.0).astype(BF16)
-        from_right = jnp.where(owner == c + 1, 1.0, 0.0).astype(BF16)
-        matrices.append(left * from_left + right * from_right)
-        packed = outer[4 * rhs :]
-        sides = [pltpu.roll(packed, (spot - 4 * k) % LANES, 1) for k in range(rhs // 8)]
-        sides = jnp.concatenate(sides, axis=0)
-        pair = []
-        for k in range(2):
-            moved = pltpu.roll(sides, LANES - 2 * k, 1) if k else sides
-            chosen = jnp.logical_or(lane == spot, lane == spot + 1)
-            pair.append(jnp.where(chosen, moved, inner[k]))
-        values.append(jnp.concatenate(pair, axis=0).astype(BF16))
-    halo = jnp.dot(
-        jnp.concatenate(values, axis=1), jnp.concatenate(matrices, axis=0),
-        preferred_element_type=F32,
-    )
-    lane = lane_index(rhs)
-    rows, sides = [], []
-    for row in range(-1, h0 + 1):
-        if row == -1:
-            rows.append(above[0])
-        elif row == h0:
-            rows.append(below[0])
-        else:
-            rows.append(rows_ref[row])
-        if row < 0 or row == h0:
-            slot, part = (0 if row < 0 else 1), plan.sides - 1
-        else:
-            slot, part = divmod(row, h0 // 2)
-        sides.append(halo[slot * rhs : (slot + 1) * rhs, part * LANES : (part + 1) * LANES])
+    rows = [above[0]] + [rows_ref[row] for row in range(h0)] + [below[0]]
+    length = 4 * (w0 + 2)
+    side = lax.broadcasted_iota(jnp.int32, (16, length), 0)
+    at = lax.broadcasted_iota(jnp.int32, (16, length), 1)
+    wanted = (side // 2) * (w0 + 2) + (side % 2) * (w0 + 1)
+    pick = jnp.where(at == wanted, 1.0, 0.0).astype(BF16)
     for b in range(h0 // 2):
         tiles, before = [], None
         for k in range(5):
             if k < 4:
-                row, side = rows[2 * b + k], sides[2 * b + k]
-                rolled = pltpu.roll(row, 2 * k + 1, 1)
-                value = jnp.where(lane == 2 * k, side, rolled)
+                rolled = pltpu.roll(rows[2 * b + k], 2 * k + 1, 1)
+                value = jnp.where(lane > 2 * k, rolled, 0.0)
             else:
                 value = jnp.zeros((rhs, LANES), F32)
             if before is not None:
-                old, old_side = before
-                value = jnp.where(lane == 2 * k - 1, old_side, value)
-                value = jnp.where(lane < 2 * k - 1, old, value)
+                value = jnp.where(lane < 2 * k - 1, before, value)
             tiles.append(value)
-            before = (rolled, side)
-        lhs = jnp.concatenate(tiles, axis=1).astype(BF16)[:, : 4 * (w0 + 2)]
-        solved = solve(lhs, factor_ref[b, 0])
+            before = rolled
+        lhs = jnp.concatenate(tiles, axis=1).astype(BF16)[:, :length]
+        solved = solve(jnp.concatenate([lhs, pick], axis=0), factor_ref[b, 0])
         for j in range(2):
-            out_ref[2 * b + j] = solved[:, j * w0 : (j + 1) * w0]
-
-
-def whole_kernel(plan, group, blocks, block_ref, four_ref, inverse_ref, *refs):
+            out_ref[2 * b + j] = solved[:rhs, j * w0 : (j + 1) * w0]
+        picked_ref[b] = solved[rhs:].astype(BF16)
+
+
+def side_columns(plan, early_refs, late_refs):
+    c, rhs, h0 = lax.axis_index("py"), plan.rhs, plan.h0
+    found = []
+    for offset in (-1, 1):
+        total = None
+        for early, late, owner in zip(early_refs, late_refs, owners(plan)):
+            chosen = jnp.where(owner == c + offset, 1.0, 0.0).astype(F32)
+            parts = [early[0] * chosen, early[1] * chosen, late[4 * rhs :] * chosen]
+            total = parts if total is None else [a + b for a, b in zip(total, parts)]
+        found.append(total)
+    slots = []
+    for left, right in zip(*found):
+        even = lane_index(left.shape[0]) % 2 == 0
+        slots.append(jnp.where(even, left, right))
+    packed = slots.pop()
+    outer = [pltpu.roll(packed, LANES - 4 * k, 1) if k else packed for k in range(rhs // 8)]
+    outer = jnp.concatenate(outer, axis=0)
+    lane, start = lane_index(rhs), plan.offset[3]
+    inner = [
+        pltpu.roll(slot, (2 + k * h0 - start) % LANES, 1) for k, slot in enumerate(slots)
+    ]
+    value = jnp.where(lane < 2 * h0 + 4, pltpu.roll(outer, 2 * h0, 1), 0.0)
+    value = jnp.where(lane < 2 * h0 + 2, inner[1], value)
+    value = jnp.where(lane < h0 + 2, inner[0], value)
+    return jnp.where(lane < 2, outer, value)
+
+
+def whole_kernel(plan, group, partners, blocks, block_ref, four_ref, inverse_ref, *refs):
     count = plan.n // 2
     gathered, out_ref, pair_ref, four_rows = refs[:count], refs[count], refs[-2], refs[-1]
     r, c = lax.axis_index("px"), lax.axis_index("py")
     rhs, ny4 = plan.rhs, plan.ny[4]
     nx4, nx5 = plan.nx[4], plan.nx[5]
     odd = jnp.bitwise_and(c, 1)
-    for k, block in enumerate(gathered):
-        if k == 0 or (k == count - 1 and k % 2):
-            partner = 2 * k
-        elif k % 2:
-            partner = 2 * (k + odd)
-        else:
-            partner = 2 * (k - odd)
+    for block, (left, right) in zip(gathered, partners):
+        partner = jnp.where(odd == 1, right, left)
         pair_ref[jnp.bitwise_xor(r, partner) // 2] = block[...]
     lane = lane_index(rhs)
     inside = jnp.logical_and(lane >= 1, lane <= ny4)
@@ -661,8 +659,8 @@
         out_ref[k] = four_rows[r + k]
 
 
-def final_kernel(plan, blocks, block_ref, fine_ref, one_ref, inner_ref, two_ref, three_ref,
-                 four_ref, first_ref, second_ref, out_ref, whole_ref, semaphores):
+def final_kernel(plan, blocks, block_ref, fine_ref, one_ref, two_ref, three_ref, four_ref,
+                 first_ref, second_ref, out_ref, whole_ref, semaphores):
     r, rhs = lax.axis_index("px"), plan.rhs
     above = jnp.where(r > 0, 1.0, 0.0).astype(F32)
     below = jnp.where(r < plan.n - 1, 1.0, 0.0).astype(F32)
@@ -683,10 +681,7 @@
             height = plan.h[level]
             lifted = lift_rows(rows, -1, height + 1)
             rows = [lifted[0] * above + from_above[level - 1][own]]
-            parts = [own_ref[i, own] for i in range(own_ref.shape[0])]
-            if level == 1:
-                parts[2:2] = [inner_ref[i, own] for i in range(inner_ref.shape[0])]
-            rows += [lifted[i + 1] + parts[i] for i in range(height)]
+            rows += [lifted[i + 1] + own_ref[i, own] for i in range(height)]
             rows += [lifted[-1] * below + from_below[level - 1][own]]
         lifted = lift_rows(rows, 0, plan.h0)
         start, count = 8 * part * plan.h0, 8 * plan.h0
@@ -738,7 +733,6 @@
             blocks.add(f"lift{l}", lifted.reshape(m, 2, -1, plan.w0))
     lifted, group = plan.level_four_lift()
     blocks.add("lift4", lifted)
-    blocks.add("halo", plan.halo_lanes())
     blocks.add("shrink5", plan.coarsest_shrink())
     blocks.add("lift5", plan.coarsest_lift())
     matrices = blocks.array()
@@ -757,53 +751,60 @@
         outer, shrink, first, second
     )
 
-    def spread(value):
-        bands = {0: value}
-        bit = m // 2
-        while bit:
+    main, picked = kernel_call(
+        functools.partial(fine_kernel, plan),
+        (shape(h0, rhs, plan.w0), jax.ShapeDtypeStruct((h0 // 2, 16, 2 * plan.w0), BF16)),
+        cost_us=0.7,
+    )(rows, first, second, factor_fine)
+    def spread(bands, bits):
+        for bit in bits:
             bands.update({k ^ bit: swap(band, bit) for k, band in list(bands.items())})
-            bit //= 2
-        return [bands[k] for k in range(m)]
-
-    early, late = spread(early), spread(late)
+        return bands
+
+    bits = [1 << k for k in reversed(range(m.bit_length() - 1))]
+    late = spread({0: late}, bits[:1])
+    late, main, picked = lax.optimization_barrier((late, main, picked))
+    early, late = spread({0: early}, bits), spread(late, bits[1:])
+    early, late = [early[k] for k in range(m)], [late[k] for k in range(m)]
 
     pairs = kernel_call(
         functools.partial(gather_kernel, plan, blocks), shape(rhs, 4 * plan.ny[4]), cost_us=0.3
     )(matrices, *late)
-    order, gathered = list(range(1, n // 2)), [pairs]
-    fetched = []
+    order, fetched, gathered, partners = list(range(n // 2 - 1, 0, -1)), [], [pairs], [(0, 0)]
     for k in range(0, len(order), 2):
         even, odd = order[k], order[min(k + 1, len(order) - 1)]
-        fetched.append(
-            lax.ppermute(
-                pairs, ("px", "py"),
-                [(i * m + c, (i ^ (2 * (odd if c % 2 else even))) * m + c)
-                 for i in range(n) for c in range(m)],
-            )
-        )
+        routes = [
+            (i * m + c, (i ^ (2 * (odd if c % 2 else even))) * m + c)
+            for i in range(n) for c in range(m)
+        ]
+        fetched.append((lax.ppermute(pairs, ("px", "py"), routes), even, odd))
     late, pairs = lax.optimization_barrier((late, pairs))
-    for k, value in enumerate(fetched):
+    for value, even, odd in fetched:
         gathered.append(value)
-        if 2 * k + 1 < len(order):
+        partners.append((2 * even, 2 * odd))
+        if even != odd:
             gathered.append(swap(value, 1))
+            partners.append((2 * odd, 2 * even))
+
 
     one, two, three, inner, low, high = kernel_call(
         functools.partial(coarse_kernel, plan, blocks),
-        (shape(4, rhs, LANES), shape(h[2], rhs, LANES), shape(h[3], rhs, LANES),
-         shape(h[1] - 2, rhs, plan.ny[1]))
+        tuple(
+            shape(plan.tiles[l], count, rhs, 2 * plan.tile[l])
+            for l, count in ((1, 2), (2, h[2] // 2), (3, h[3] // 2))
+        )
+        + (shape(h[1] - 2, rhs, plan.ny[1]),)
         + (shape(1, rhs, LANES), shape(1, rhs, LANES)),
         cost_us=2.5,
     )(matrices, factor_one, factor_two, factor_three, *early, *late)
     low, high = trade(low, high)
-    inner = kernel_call(
-        functools.partial(inner_kernel, plan, blocks), shape(h[1] - 4, rhs, LANES), cost_us=0.6
-    )(matrices, factor_one, inner)
-
-    fine = kernel_call(
-        functools.partial(fine_kernel, plan, blocks), shape(h0, rhs, plan.w0)
-    )(matrices, rows, first, second, factor_fine, *early, *late)
+    one, two, three, fine = kernel_call(
+        functools.partial(inner_kernel, plan, blocks),
+        tuple(shape(h[l], rhs, LANES) for l in (1, 2, 3)) + (shape(h0, rhs, plan.w0),),
+        cost_us=1.2,
+    )(matrices, factor_one, inner, one, two, three, main, picked, *early, *late)
     four = kernel_call(
-        functools.partial(whole_kernel, plan, group, blocks),
+        functools.partial(whole_kernel, plan, group, partners, blocks),
         shape(3, rhs, LANES),
         scratch=(
             pltpu.VMEM((n // 2, rhs, 4 * plan.ny[4]), F32),
@@ -815,7 +816,7 @@
         scratch=(pltpu.VMEM((rhs * h0, plan.w0), F32), pltpu.SemaphoreType.DMA((rhs // 8,))),
         out_space=pl.ANY,
     )(
-        matrices, fine, one, inner, two, three, four, low, high
+        matrices, fine, one, two, three, four, low, high
     )
     return out.reshape(rhs, h0, plan.w0)
 

time: 26.6 us -> 26.1 us (0.981)
  Pallas kernels: 5.75 us -> 5.47 us
  waiting for transfers between devices: 7.89 us -> 7.61 us
    ppermute x7, waiting for transfers between devices: 3.87 us -> 3.15 us  [swap(): return lax.ppermute(value, 'py', [(i, i ^ bits) for i in range(m)])]
    ppermute x2, waiting for transfers between devices: 1.99 us -> 2.44 us  [trade(): lax.ppermute(second, ('px', 'py'), back)]
    pallas_call x9, Pallas kernels: 5.75 us -> 5.47 us  [call(): pl.pallas_call(body, out_shape=out_shape, in_specs=[whole] * len(operands...]
  transfers between devices with their start and end apart: 13 -> 13, of which waited for: 5 -> 6; matrix products, arithmetic and copies ran while one was open for 0% -> 0% of each run, Pallas kernels for 15% -> 14%
where the time goes in v8:
time: 26.1 us; the launch traced here: 26 us
  starting transfers between devices  12.2 us (47%)
  waiting for transfers between devices  7.61 us (29%)
  Pallas kernels  5.47 us (21%)
  local copies, waits for them, and re-layouts  0.58 us (2%)
    pallas_call x9, Pallas kernels, call(): pl.pallas_call(body, out_shape=out_shape, in_specs=[whole] * len(operands...  5.47 us
    ppermute x2, starting transfers between devices, per_device(): fetched.append((lax.ppermute(pairs, ('px', 'py'), routes), even, odd))  4.4 us
    ppermute x2, starting transfers between devices, trade(): lax.ppermute(first, ('px', 'py'), ring)  3.77 us
    ppermute x7, waiting for transfers between devices, swap(): return lax.ppermute(value, 'py', [(i, i ^ bits) for i in range(m)])  3.15 us
    ppermute x7, starting transfers between devices, swap(): return lax.ppermute(value, 'py', [(i, i ^ bits) for i in range(m)])  2.61 us
    ppermute x2, waiting for transfers between devices, trade(): lax.ppermute(second, ('px', 'py'), back)  2.44 us
    ppermute x2, waiting for transfers between devices, trade(): lax.ppermute(first, ('px', 'py'), ring)  2.01 us
    ppermute x2, starting transfers between devices, trade(): lax.ppermute(second, ('px', 'py'), back)  1.39 us
  transfers between devices with their start and end apart: 13, of which 6 were waited for; matrix products, arithmetic and copies ran while one was open for 0% of the time, Pallas kernels for 14%

profile of v8, /device:TPU:0, one launch (start us, length us, event | category | flops | bytes accessed | tf_op | source)
XLA Modules:
  0.0 26.0 jit_solution(17152383825258684230)
XLA Ops:
  0.0 0.0 copy-start.4
  0.0 0.4 %shard_map.82.shrink_ref = bf16[4,128,128]{2,1,0:T(8,128)(2,1)S(1)} custom-call(), custom_call_target="tpu_custom_call" | custom-call | flops 4000000000 | bytes 12000000 | tf_op jit(solution)/shard_map/pallas_call | solution.py:236
  0.4 0.5 %copy-done.4 = f32[32,16,128]{2,1,0:T(8,128)S(1)} copy-done((f32[32,16,128]{2,1,0:T(8,128)S(1)}, f32[32,16,128]{2,1,0:T(8,128)}, u32[]{:S(2)}) %copy-start.4) | copy-done | bytes 262168
  1.0 0.4 %shard_map.83 = (f32[4,32,128]{2,1,0:T(8,128)S(1)}, f32[4,32,128]{2,1,0:T(8,128)S(1)}, f32[3,32,128]{2,1,0:T(8,128)S(1)}, f32[3,32,128]{2,1,0:T(8,128)S(1)}, f32[16,32,128]{2,1,0:T(8,128)S(1)}) custom-call(f32[512,128]{1,0:T(8,128)S(1)} %bitcast.3, bf16[4,128,128]{2,1,0:T(8,128)(2,1)S(1)} %shard_map.82.shrink_ref), custom_call_target="tpu_custom_call" | custom-call | flops 1000000000 | bytes 3000000 | tf_op jit(solution)/shard_map/pallas_call | solution.py:236
  1.4 3.0 %collective-permute-start.3 = (f32[3,32,128]{2,1,0:T(8,128)S(1)}, f32[3,32,128]{2,1,0:T(8,128)S(1)}, u32[]{:S(2)}, u32[]{:S(2)}) collective-permute-start(f32[3,32,128]{2,1,0:T(8,128)S(1)} %get-tuple-element.32), channel_id=1, source_target_pairs={{0,2},{1,3},{2,6},{3,7},{4,0},{5,1},{6,10},{7,11},{8,4},{9,5},{10,... | collective-permute-start | bytes 147464 | tf_op jit(solution)/shard_map/ppermute | solution.py:718
  4.3 0.1 collective-permute-start.4
  4.4 2.0 %collective-permute-done.3.first_ref = f32[3,32,128]{2,1,0:T(8,128)S(1)} collective-permute-done((f32[3,32,128]{2,1,0:T(8,128)S(1)}, f32[3,32,128]{2,1,0:T(8,128)S(1)}, u32[]{:S(2)}, u32[]{:S(2)}) %collective-permute-start.3) | collective-permute-done | bytes 49184 | tf_op jit(solution)/shard_map/ppermute | solution.py:718
  6.4 2.0 %collective-permute-done.4.second_ref = f32[3,32,128]{2,1,0:T(8,128)S(1)} collective-permute-done((f32[3,32,128]{2,1,0:T(8,128)S(1)}, f32[3,32,128]{2,1,0:T(8,128)S(1)}, u32[]{:S(2)}, u32[]{:S(2)}) %collective-permute-start.4) | collective-permute-done | bytes 49184 | tf_op jit(solution)/shard_map/ppermute | solution.py:718
  8.4 0.2 shard_map.84.refs_0_.refs_7_.refs_4_
  8.6 1.6 %collective-permute-start.5 = (f32[136,128]{1,0:T(8,128)S(1)}, f32[136,128]{1,0:T(8,128)S(1)}, u32[]{:S(2)}, u32[]{:S(2)}) collective-permute-start(f32[136,128]{1,0:T(8,128)S(1)} %shard_map.84.refs_0_.refs_7_.refs_4_), channel_id=1, source_target_pairs={{0,2},{1,3},{2,0},{3,1},{4,6},{5,7},{6,4},{7,5},{8,10},{9,11},{10,... | collective-permute-start | bytes 208904 | tf_op jit(solution)/shard_map/ppermute | solution.py:721
  10.2 0.5 %collective-permute-start.1 = (f32[4,32,128]{2,1,0:T(8,128)S(1)}, f32[4,32,128]{2,1,0:T(8,128)S(1)}, u32[]{:S(2)}, u32[]{:S(2)}) collective-permute-start(f32[4,32,128]{2,1,0:T(8,128)S(1)} %get-tuple-element.30.refs_3_.refs_0_), channel_id=1, source_target_pairs={{0,2},{1,3},{2,0},{3,1},{4,6},{5,7},{6,4},{7,5},{8,10},{9,11},{10,... | collective-permute-start | bytes 196616 | tf_op jit(solution)/shard_map/ppermute | solution.py:721
  10.7 0.0 copy-done.2
  10.7 0.6 %shard_map.85 = (f32[16,32,128]{2,1,0:T(8,128)S(1)}, bf16[8,16,256]{2,1,0:T(8,128)(2,1)S(1)}) custom-call(f32[16,32,128]{2,1,0:T(8,128)S(1)} %get-tuple-element.34.rows_ref, f32[3,32,128]{2,1,0:T(8,128)S(1)} %collective-permute-done.3.first_ref, f32[3,32,128]{2,1,0:T(8,128)S(1)} %collective-permute-done.4.second_ref, bf16[8,1,520,256]{3,2,1,0:T(8,128)(2,1)S(1)} %copy-done.2), custom_call_target="tpu_custom_call" | custom-call | flops 700000000 | bytes 2100000 | tf_op jit(solution)/shard_map/pallas_call | solution.py:236
  11.3 0.0 copy-start.1
  11.3 0.0 copy-start.3
  11.3 0.0 copy-start.6
  11.3 1.6 %collective-permute-done.5.refs_2_.refs_9_.refs_6_ = f32[136,128]{1,0:T(8,128)S(1)} collective-permute-done((f32[136,128]{1,0:T(8,128)S(1)}, f32[136,128]{1,0:T(8,128)S(1)}, u32[]{:S(2)}, u32[]{:S(2)}) %collective-permute-start.5) | collective-permute-done | bytes 69664 | tf_op jit(solution)/shard_map/ppermute | solution.py:721
  13.0 0.0 collective-permute-start.6
  13.0 0.5 %collective-permute-start.7 = (f32[136,128]{1,0:T(8,128)S(1)}, f32[136,128]{1,0:T(8,128)S(1)}, u32[]{:S(2)}, u32[]{:S(2)}) collective-permute-start(f32[136,128]{1,0:T(8,128)S(1)} %collective-permute-done.5.refs_2_.refs_9_.refs_6_), channel_id=1, source_target_pairs={{0,1},{1,0},{2,3},{3,2},{4,5},{5,4},{6,7},{7,6},{8,9},{9,8},{10,11... | collective-permute-start | bytes 208904 | tf_op jit(solution)/shard_map/ppermute | solution.py:721
  13.5 0.0 collective-permute-start
  13.5 1.0 %collective-permute-done.1.refs_5_.refs_2_ = f32[4,32,128]{2,1,0:T(8,128)S(1)} collective-permute-done((f32[4,32,128]{2,1,0:T(8,128)S(1)}, f32[4,32,128]{2,1,0:T(8,128)S(1)}, u32[]{:S(2)}, u32[]{:S(2)}) %collective-permute-start.1) | collective-permute-done | bytes 65568 | tf_op jit(solution)/shard_map/ppermute | solution.py:721
  14.4 0.0 collective-permute-start.2
  14.4 0.0 collective-permute-done.6.refs_1_.refs_8_.refs_5_
  14.4 0.0 collective-permute-done.7.refs_3_.refs_10_.refs_7_
  14.4 0.0 copy-done
  14.5 0.2 shard_map.86.refs_0_
  14.7 4.4 %collective-permute-start.8 = (f32[32,128]{1,0:T(8,128)S(1)}, f32[32,128]{1,0:T(8,128)S(1)}, u32[]{:S(2)}, u32[]{:S(2)}) collective-permute-start(f32[32,128]{1,0:T(8,128)S(1)} %shard_map.86.refs_0_), channel_id=1, source_target_pairs={{0,24},{1,17},{2,26},{3,19},{4,28},{5,21},{6,30},{7,23},{8,16},{9,... | collective-permute-start | bytes 49160 | tf_op jit(solution)/shard_map/ppermute | solution.py:780
  19.1 0.0 collective-permute-start.10
  19.1 0.0 collective-permute-done.refs_4_.refs_1_
  19.1 0.0 collective-permute-done.2.refs_6_.refs_3_
  19.1 0.0 copy-done.1
  19.1 0.0 copy-done.3
  19.1 0.0 copy-done.6
  19.1 1.4 %shard_map.87 = (f32[2,2,32,256]{3,2,1,0:T(8,128)S(1)}, f32[1,2,32,256]{3,2,1,0:T(8,128)S(1)}, f32[1,1,32,128]{3,2,1,0:T(8,128)S(1)}, f32[6,32,256]{2,1,0:T(8,12...) custom-call(bf16[102,128,128]{2,1,0:T(8,128)(2,1)S(1)} %copy-done, bf16[4,2,520,256]{3,2,1,0:T(8,128)(2,1)S(1)} %copy-done.1, ...), custom_call_target="tpu_custom_call" | custom-call | flops 2500000000 | bytes 7500000 | tf_op jit(solution)/shard_map/pallas_call | solution.py:236
  20.5 0.8 %collective-permute-start.11 = (f32[1,32,128]{2,1,0:T(8,128)S(1)}, f32[1,32,128]{2,1,0:T(8,128)S(1)}, u32[]{:S(2)}, u32[]{:S(2)}) collective-permute-start(f32[1,32,128]{2,1,0:T(8,128)S(1)} %get-tuple-element.53), channel_id=1, source_target_pairs={{0,2},{1,3},{2,6},{3,7},{4,0},{5,1},{6,10},{7,11},{8,4},{9,5},{10,... | collective-permute-start | bytes 49160 | tf_op jit(solution)/shard_map/ppermute | solution.py:718
  21.3 1.3 %collective-permute-start.12 = (f32[1,32,128]{2,1,0:T(8,128)S(1)}, f32[1,32,128]{2,1,0:T(8,128)S(1)}, u32[]{:S(2)}, u32[]{:S(2)}) collective-permute-start(f32[1,32,128]{2,1,0:T(8,128)S(1)} %get-tuple-element.54), channel_id=1, source_target_pairs={{2,0},{3,1},{6,2},{7,3},{0,4},{1,5},{10,6},{11,7},{4,8},{5,9},{14,... | collective-permute-start | bytes 49160 | tf_op jit(solution)/shard_map/ppermute | solution.py:718
  22.6 0.0 collective-permute-done.8.refs_1_
  22.6 0.0 collective-permute-start.9
  22.6 0.0 copy-start.7
  22.6 0.6 %shard_map.88 = (f32[8,32,128]{2,1,0:T(8,128)S(1)}, f32[4,32,128]{2,1,0:T(8,128)S(1)}, f32[2,32,128]{2,1,0:T(8,128)S(1)}, f32[16,32,128]{2,1,0:T(8,128)S(1)}) custom-call(bf16[102,128,128]{2,1,0:T(8,128)(2,1)S(1)} %copy-done, bf16[4,2,520,256]{3,2,1,0:T(8,128)(2,1)S(1)} %copy-done.1, f32[6,32,256]{2,1,0:T(8,128)S(1)} %get-tuple-element.43.rows_ref, ...), custom_call_target="tpu_custom_call" | custom-call | flops 1200000000 | bytes 3600000 | tf_op jit(solution)/shard_map/pallas_call | solution.py:236
  23.2 0.0 collective-permute-done.10.refs_3_
  23.3 0.5 %collective-permute-done.9.refs_2_ = f32[32,128]{1,0:T(8,128)S(1)} collective-permute-done((f32[32,128]{1,0:T(8,128)S(1)}, f32[32,128]{1,0:T(8,128)S(1)}, u32[]{:S(2)}, u32[]{:S(2)}) %collective-permute-start.9) | collective-permute-done | bytes 16416 | tf_op jit(solution)/shard_map/ppermute | solution.py:721
  23.8 0.0 copy-done.5
  23.8 0.0 copy-done.7
  23.8 0.8 %shard_map.89.four_ref = f32[3,32,128]{2,1,0:T(8,128)S(1)} custom-call(bf16[102,128,128]{2,1,0:T(8,128)(2,1)S(1)} %copy-done, bf16[4,1,64,136]{3,2,1,0:T(8,128)(2,1)S(1)} %bitcast.4, bf16[64,64]{1,0:T(8,128)(2,1)S(1)} %copy-done.7, f32[32,128]{1,0:T(8,128)S(1)} %shard_map.86.refs_0_, f32[32,128]{1,0:T(8,128)S(1)} %collective-permute-done.8.refs_1_, ...), custom_call_target="tpu_custom_call" | custom-call | flops 1000000000 | bytes 3000000 | tf_op jit(solution)/shard_map/pallas_call | solution.py:236
  24.6 0.0 collective-permute-done.11.first_ref
  24.6 0.5 %collective-permute-done.12.second_ref = f32[1,32,128]{2,1,0:T(8,128)S(1)} collective-permute-done((f32[1,32,128]{2,1,0:T(8,128)S(1)}, f32[1,32,128]{2,1,0:T(8,128)S(1)}, u32[]{:S(2)}, u32[]{:S(2)}) %collective-permute-start.12) | collective-permute-done | bytes 16416 | tf_op jit(solution)/shard_map/ppermute | solution.py:718
  25.0 0.9 %shard_map.90 = f32[512,128]{1,0:T(8,128)} custom-call(bf16[102,128,128]{2,1,0:T(8,128)(2,1)S(1)} %copy-done, f32[16,32,128]{2,1,0:T(8,128)S(1)} %get-tuple-element.49.fine_ref, f32[8,32,128]{2,1,0:T(8,128)S(1)} %get-tuple-element.50.one_ref, f32[4,32,128]{2,1,0:T(8,128)S(1)} %get-tuple-element.51.two_ref, f32[2,32,128]{2,1,0:T(8,128)S(1)} %get-tuple-element.52.three_ref, ...), custom_call_target="tpu_custom_call" | custom-call | flops 1000000000 | bytes 3000000 | tf_op jit(solution)/shard_map/pallas_call | solution.py:236
  (3 shorter events, 0.0 us)
Async XLA Ops:
  0.0 0.9 %copy-start.4 = (f32[32,16,128]{2,1,0:T(8,128)S(1)}, f32[32,16,128]{2,1,0:T(8,128)}, u32[]{:S(2)}) copy-start(f32[32,16,128]{2,1,0:T(8,128)} %param.8) | copy-start | bytes 786436
  1.3 9.3 %copy-start.2 = (bf16[8,1,520,256]{3,2,1,0:T(8,128)(2,1)S(1)}, bf16[8,1,520,256]{3,2,1,0:T(8,128)(2,1)}, u32[]{:S(2)}) copy-start(bf16[8,1,520,256]{3,2,1,0:T(8,128)(2,1)} %factor_ref.2) | copy-start | bytes 6389764
  1.4 5.1 %collective-permute-start.3 = (f32[3,32,128]{2,1,0:T(8,128)S(1)}, f32[3,32,128]{2,1,0:T(8,128)S(1)}, u32[]{:S(2)}, u32[]{:S(2)}) collective-permute-start(f32[3,32,128]{2,1,0:T(8,128)S(1)} %get-tuple-element.32), channel_id=1, source_target_pairs={{0,2},{1,3},{2,6},{3,7},{4,0},{5,1},{6,10},{7,11},{8,4},{9,5},{10,... | collective-permute-start | bytes 147464 | tf_op jit(solution)/shard_map/ppermute | solution.py:718
  4.3 4.1 %collective-permute-start.4 = (f32[3,32,128]{2,1,0:T(8,128)S(1)}, f32[3,32,128]{2,1,0:T(8,128)S(1)}, u32[]{:S(2)}, u32[]{:S(2)}) collective-permute-start(f32[3,32,128]{2,1,0:T(8,128)S(1)} %get-tuple-element.33), channel_id=1, source_target_pairs={{2,0},{3,1},{6,2},{7,3},{0,4},{1,5},{10,6},{11,7},{4,8},{5,9},{14,... | collective-permute-start | bytes 147464 | tf_op jit(solution)/shard_map/ppermute | solution.py:718
  8.4 6.0 %copy-start = (bf16[102,128,128]{2,1,0:T(8,128)(2,1)S(1)}, bf16[102,128,128]{2,1,0:T(8,128)(2,1)}, u32[]{:S(2)}) copy-start(bf16[102,128,128]{2,1,0:T(8,128)(2,1)} %constant.2.clone.block_ref) | copy-start | bytes 10027012
  8.6 4.4 %collective-permute-start.5 = (f32[136,128]{1,0:T(8,128)S(1)}, f32[136,128]{1,0:T(8,128)S(1)}, u32[]{:S(2)}, u32[]{:S(2)}) collective-permute-start(f32[136,128]{1,0:T(8,128)S(1)} %shard_map.84.refs_0_.refs_7_.refs_4_), channel_id=1, source_target_pairs={{0,2},{1,3},{2,0},{3,1},{4,6},{5,7},{6,4},{7,5},{8,10},{9,11},{10,... | collective-permute-start | bytes 208904 | tf_op jit(solution)/shard_map/ppermute | solution.py:721
  10.2 4.3 %collective-permute-start.1 = (f32[4,32,128]{2,1,0:T(8,128)S(1)}, f32[4,32,128]{2,1,0:T(8,128)S(1)}, u32[]{:S(2)}, u32[]{:S(2)}) collective-permute-start(f32[4,32,128]{2,1,0:T(8,128)S(1)} %get-tuple-element.30.refs_3_.refs_0_), channel_id=1, source_target_pairs={{0,2},{1,3},{2,0},{3,1},{4,6},{5,7},{6,4},{7,5},{8,10},{9,11},{10,... | collective-permute-start | bytes 196616 | tf_op jit(solution)/shard_map/ppermute | solution.py:721
  11.3 7.8 %copy-start.1 = (bf16[4,2,520,256]{3,2,1,0:T(8,128)(2,1)S(1)}, bf16[4,2,520,256]{3,2,1,0:T(8,128)(2,1)}, u32[]{:S(2)}) copy-start(bf16[4,2,520,256]{3,2,1,0:T(8,128)(2,1)} %factor_ref.3) | copy-start | bytes 6389764
  11.3 7.8 %copy-start.3 = (bf16[2,1,520,256]{3,2,1,0:T(8,128)(2,1)S(1)}, bf16[2,1,520,256]{3,2,1,0:T(8,128)(2,1)}, u32[]{:S(2)}) copy-start(bf16[2,1,520,256]{3,2,1,0:T(8,128)(2,1)} %refs_1_.1) | copy-start | bytes 1597444
  11.3 7.8 %copy-start.6 = (bf16[1,1,264,128]{3,2,1,0:T(8,128)(2,1)S(1)}, bf16[1,1,264,128]{3,2,1,0:T(8,128)(2,1)}, u32[]{:S(2)}) copy-start(bf16[1,1,264,128]{3,2,1,0:T(8,128)(2,1)} %refs_2_.1) | copy-start | bytes 202756
  13.0 1.5 %collective-permute-start.6 = (f32[136,128]{1,0:T(8,128)S(1)}, f32[136,128]{1,0:T(8,128)S(1)}, u32[]{:S(2)}, u32[]{:S(2)}) collective-permute-start(f32[136,128]{1,0:T(8,128)S(1)} %shard_map.84.refs_0_.refs_7_.refs_4_), channel_id=1, source_target_pairs={{0,1},{1,0},{2,3},{3,2},{4,5},{5,4},{6,7},{7,6},{8,9},{9,8},{10,11... | collective-permute-start | bytes 208904 | tf_op jit(solution)/shard_map/ppermute | solution.py:721
  13.0 1.5 %collective-permute-start.7 = (f32[136,128]{1,0:T(8,128)S(1)}, f32[136,128]{1,0:T(8,128)S(1)}, u32[]{:S(2)}, u32[]{:S(2)}) collective-permute-start(f32[136,128]{1,0:T(8,128)S(1)} %collective-permute-done.5.refs_2_.refs_9_.refs_6_), channel_id=1, source_target_pairs={{0,1},{1,0},{2,3},{3,2},{4,5},{5,4},{6,7},{7,6},{8,9},{9,8},{10,11... | collective-permute-start | bytes 208904 | tf_op jit(solution)/shard_map/ppermute | solution.py:721
  13.5 5.6 %collective-permute-start = (f32[4,32,128]{2,1,0:T(8,128)S(1)}, f32[4,32,128]{2,1,0:T(8,128)S(1)}, u32[]{:S(2)}, u32[]{:S(2)}) collective-permute-start(f32[4,32,128]{2,1,0:T(8,128)S(1)} %get-tuple-element.30.refs_3_.refs_0_), channel_id=1, source_target_pairs={{0,1},{1,0},{2,3},{3,2},{4,5},{5,4},{6,7},{7,6},{8,9},{9,8},{10,11... | collective-permute-start | bytes 196616 | tf_op jit(solution)/shard_map/ppermute | solution.py:721
  14.4 4.7 %collective-permute-start.2 = (f32[4,32,128]{2,1,0:T(8,128)S(1)}, f32[4,32,128]{2,1,0:T(8,128)S(1)}, u32[]{:S(2)}, u32[]{:S(2)}) collective-permute-start(f32[4,32,128]{2,1,0:T(8,128)S(1)} %collective-permute-done.1.refs_5_.refs_2_), channel_id=1, source_target_pairs={{0,1},{1,0},{2,3},{3,2},{4,5},{5,4},{6,7},{7,6},{8,9},{9,8},{10,11... | collective-permute-start | bytes 196616 | tf_op jit(solution)/shard_map/ppermute | solution.py:721
  14.7 7.9 %collective-permute-start.8 = (f32[32,128]{1,0:T(8,128)S(1)}, f32[32,128]{1,0:T(8,128)S(1)}, u32[]{:S(2)}, u32[]{:S(2)}) collective-permute-start(f32[32,128]{1,0:T(8,128)S(1)} %shard_map.86.refs_0_), channel_id=1, source_target_pairs={{0,24},{1,17},{2,26},{3,19},{4,28},{5,21},{6,30},{7,23},{8,16},{9,... | collective-permute-start | bytes 49160 | tf_op jit(solution)/shard_map/ppermute | solution.py:780
  19.1 4.2 %collective-permute-start.10 = (f32[32,128]{1,0:T(8,128)S(1)}, f32[32,128]{1,0:T(8,128)S(1)}, u32[]{:S(2)}, u32[]{:S(2)}) collective-permute-start(f32[32,128]{1,0:T(8,128)S(1)} %shard_map.86.refs_0_), channel_id=1, source_target_pairs={{0,8},{1,9},{2,10},{3,11},{4,12},{5,13},{6,14},{7,15},{8,0},{9,1},... | collective-permute-start | bytes 49160 | tf_op jit(solution)/shard_map/ppermute | solution.py:780
  20.5 4.1 %collective-permute-start.11 = (f32[1,32,128]{2,1,0:T(8,128)S(1)}, f32[1,32,128]{2,1,0:T(8,128)S(1)}, u32[]{:S(2)}, u32[]{:S(2)}) collective-permute-start(f32[1,32,128]{2,1,0:T(8,128)S(1)} %get-tuple-element.53), channel_id=1, source_target_pairs={{0,2},{1,3},{2,6},{3,7},{4,0},{5,1},{6,10},{7,11},{8,4},{9,5},{10,... | collective-permute-start | bytes 49160 | tf_op jit(solution)/shard_map/ppermute | solution.py:718
  21.3 3.7 %collective-permute-start.12 = (f32[1,32,128]{2,1,0:T(8,128)S(1)}, f32[1,32,128]{2,1,0:T(8,128)S(1)}, u32[]{:S(2)}, u32[]{:S(2)}) collective-permute-start(f32[1,32,128]{2,1,0:T(8,128)S(1)} %get-tuple-element.54), channel_id=1, source_target_pairs={{2,0},{3,1},{6,2},{7,3},{0,4},{1,5},{10,6},{11,7},{4,8},{5,9},{14,... | collective-permute-start | bytes 49160 | tf_op jit(solution)/shard_map/ppermute | solution.py:718
  22.6 1.2 %collective-permute-start.9 = (f32[32,128]{1,0:T(8,128)S(1)}, f32[32,128]{1,0:T(8,128)S(1)}, u32[]{:S(2)}, u32[]{:S(2)}) collective-permute-start(f32[32,128]{1,0:T(8,128)S(1)} %collective-permute-done.8.refs_1_), channel_id=1, source_target_pairs={{0,1},{1,0},{2,3},{3,2},{4,5},{5,4},{6,7},{7,6},{8,9},{9,8},{10,11... | collective-permute-start | bytes 49160 | tf_op jit(solution)/shard_map/ppermute | solution.py:721
  22.6 1.2 %copy-start.5 = (bf16[4,1,136,64]{2,3,1,0:T(8,128)(2,1)S(1)}, bf16[4,1,136,64]{2,3,1,0:T(8,128)(2,1)}, u32[]{:S(2)}) copy-start(bf16[4,1,136,64]{2,3,1,0:T(8,128)(2,1)} %param.13) | copy-start | bytes 208900
  22.6 1.2 %copy-start.7 = (bf16[64,64]{1,0:T(8,128)(2,1)S(1)}, bf16[64,64]{1,0:T(8,128)(2,1)}, u32[]{:S(2)}) copy-start(bf16[64,64]{1,0:T(8,128)(2,1)} %inverse_ref.1) | copy-start | bytes 24580

commit v9 on v8

--- a/solution.py
+++ b/solution.py
@@ -327,18 +327,8 @@
     own = [total[i * rhs : (i + 1) * rhs] for i in range(slots)]
     lane = lane_index(rhs)
     one, two, three = plan.offset[2:]
-    inner = [own[2], own[3], own[4], own[5]]
-    for k in range(2):
-        value = inner[k]
-        value = jnp.where(lane < two, value, 0.0)
-        for j in range(h[0] // 2):
-            value = place_sides(plan, value, x[k * (h[0] // 2) + j], two + 2 * j)
-        odd_row, end = own[6 + k], plan.tail + plan.first - plan.rest
-        moved = pltpu.roll(odd_row, (plan.tail - plan.rest) % LANES, 1)
-        chosen = jnp.logical_and(lane >= plan.tail, lane < end)
-        early_ref[k] = jnp.where(chosen, moved, value)
-        moved = pltpu.roll(odd_row, plan.first, 1)
-        early_ref[2 + k] = jnp.where(lane < plan.first, inner[2 + k], moved)
+    for k in range(6):
+        early_ref[k] = own[2 + k]
     outer = [own[0], own[1]]
     for k in range(2):
         value = jnp.where(lane < two, own[h[2] + k], own[h[3] + k])
@@ -352,6 +342,26 @@
     write_halos(c, down, up, first_ref, second_ref)
     for i, row in enumerate(x):
         rows_ref[i] = row
+
+
+def inner_rows_kernel(plan, own_ref, rows_ref, early_ref):
+    h, rhs = plan.h, plan.rhs
+    lane = lane_index(rhs)
+    two = plan.offset[3]
+    own = [None, None] + [own_ref[k] for k in range(6)]
+    x = [rows_ref[k] for k in range(h[0])]
+    inner = [own[2], own[3], own[4], own[5]]
+    for k in range(2):
+        value = inner[k]
+        value = jnp.where(lane < two, value, 0.0)
+        for j in range(h[0] // 2):
+            value = place_sides(plan, value, x[k * (h[0] // 2) + j], two + 2 * j)
+        odd_row, end = own[6 + k], plan.tail + plan.first - plan.rest
+        moved = pltpu.roll(odd_row, (plan.tail - plan.rest) % LANES, 1)
+        chosen = jnp.logical_and(lane >= plan.tail, lane < end)
+        early_ref[k] = jnp.where(chosen, moved, value)
+        moved = pltpu.roll(odd_row, plan.first, 1)
+        early_ref[2 + k] = jnp.where(lane < plan.first, inner[2 + k], moved)
 
 
 def merge_kernel(plan, outer_ref, shrink_ref, first_ref, second_ref, out_ref):
@@ -485,21 +495,20 @@
     early, late = refs[3 : 3 + plan.m], refs[3 + plan.m : 3 + 2 * plan.m]
     c, rhs = lax.axis_index("py"), plan.rhs
     down, up = [], []
+    rows = {
+        level: level_rows(plan, level, early, late, blocks, block_ref) for level in (1, 2, 3)
+    }
+    solved = {}
     for level in (1, 2, 3):
-        rows = level_rows(plan, level, early, late, blocks, block_ref)
-        w, count = plan.tile[level], plan.h[level] // 2
-        pairs = [(2 * b, b) for b in sorted({0, count - 1})]
-        if level == 1:
-            for i, row in enumerate(rows[2:-2]):
-                outs[3][i] = row
-        else:
-            pairs = [(2 * b, b) for b in range(count)]
-        solved = solve_pairs(plan, level, rows, pairs, factors[level - 1])
-        for t, values in enumerate(solved):
-            for k, value in enumerate(values):
-                outs[level - 1][t, k] = value
+        count = plan.h[level] // 2
+        pairs = range(count) if level > 1 else sorted({0, count - 1})
+        solved[level] = solve_pairs(
+            plan, level, rows[level], [(2 * b, b) for b in pairs], factors[level - 1]
+        )
+    for level in (1, 2, 3):
+        w = plan.tile[level]
         for j, (edge, at) in enumerate(((up, 0), (down, -1))):
-            for value in solved:
+            for value in solved[level]:
                 if w % LANES == 0:
                     edge.append(value[at][:, j * w : (j + 1) * w])
                 else:
@@ -507,6 +516,12 @@
     edges = [jnp.concatenate(edge, axis=1) for edge in (down, up)]
     picked = product(jnp.concatenate(edges, axis=0), blocks.get(block_ref, "pick", c))
     write_halos(c, [picked[:rhs]], [picked[rhs:]], outs[4], outs[5])
+    for level in (1, 2, 3):
+        for t, values in enumerate(solved[level]):
+            for k, value in enumerate(values):
+                outs[level - 1][t, k] = value
+    for i, row in enumerate(rows[1][2:-2]):
+        outs[3][i] = row
 
 
 def inner_kernel(plan, blocks, block_ref, factor_ref, rows_ref, one_ref, two_ref, three_ref,
@@ -743,10 +758,22 @@
     )()
     early, outer, first, second, rows = kernel_call(
         functools.partial(restrict_kernel, plan),
-        (shape(4, rhs, LANES), shape(4, rhs, LANES), shape(3, rhs, LANES), shape(3, rhs, LANES),
+        (shape(6, rhs, LANES), shape(4, rhs, LANES), shape(3, rhs, LANES), shape(3, rhs, LANES),
          shape(h0, rhs, plan.w0)),
     )(x, shrink)
     first, second = trade(first, second)
+    early = kernel_call(
+        functools.partial(inner_rows_kernel, plan), shape(4, rhs, LANES), cost_us=0.3
+    )(early, rows)
+
+    def spread(bands, bits):
+        for bit in bits:
+            bands.update({k ^ bit: swap(band, bit) for k, band in list(bands.items())})
+        return bands
+
+    bits = [1 << k for k in reversed(range(m.bit_length() - 1))]
+    early, first, second = lax.optimization_barrier((early, first, second))
+    early = spread({0: early}, bits[:1])
     late = kernel_call(functools.partial(merge_kernel, plan), shape(4 * rhs + 8, LANES))(
         outer, shrink, first, second
     )
@@ -756,15 +783,9 @@
         (shape(h0, rhs, plan.w0), jax.ShapeDtypeStruct((h0 // 2, 16, 2 * plan.w0), BF16)),
         cost_us=0.7,
     )(rows, first, second, factor_fine)
-    def spread(bands, bits):
-        for bit in bits:
-            bands.update({k ^ bit: swap(band, bit) for k, band in list(bands.items())})
-        return bands
-
-    bits = [1 << k for k in reversed(range(m.bit_length() - 1))]
     late = spread({0: late}, bits[:1])
     late, main, picked = lax.optimization_barrier((late, main, picked))
-    early, late = spread({0: early}, bits), spread(late, bits[1:])
+    early, late = spread(early, bits[1:]), spread(late, bits[1:])
     early, late = [early[k] for k in range(m)], [late[k] for k in range(m)]
 
     pairs = kernel_call(

time: 26.1 us -> 25.6 us (0.981)
  Pallas kernels: 5.47 us -> 5.17 us
    pallas_call x9 -> x10, Pallas kernels: 5.47 us -> 5.17 us  [call(): pl.pallas_call(body, out_shape=out_shape, in_specs=[whole] * len(operands...]
  transfers between devices with their start and end apart: 13 -> 13, of which waited for: 6 -> 6; matrix products, arithmetic and copies ran while one was open for 0% -> 0% of each run, Pallas kernels for 14% -> 13%
where the time goes in v9:
time: 25.6 us; the launch traced here: 25.5 us
  starting transfers between devices  12.1 us (47%)
  waiting for transfers between devices  7.47 us (29%)
  Pallas kernels  5.17 us (20%)
  local copies, waits for them, and re-layouts  0.58 us (2%)
    pallas_call x10, Pallas kernels, call(): pl.pallas_call(body, out_shape=out_shape, in_specs=[whole] * len(operands...  5.17 us
    ppermute x2, starting transfers between devices, per_device(): fetched.append((lax.ppermute(pairs, ('px', 'py'), routes), even, odd))  4.41 us
    ppermute x2, starting transfers between devices, trade(): lax.ppermute(first, ('px', 'py'), ring)  3.71 us
    ppermute x7, waiting for transfers between devices, swap(): return lax.ppermute(value, 'py', [(i, i ^ bits) for i in range(m)])  3.14 us
    ppermute x7, starting transfers between devices, swap(): return lax.ppermute(value, 'py', [(i, i ^ bits) for i in range(m)])  2.61 us
    ppermute x2, waiting for transfers between devices, trade(): lax.ppermute(second, ('px', 'py'), back)  2.44 us
    ppermute x2, waiting for transfers between devices, trade(): lax.ppermute(first, ('px', 'py'), ring)  1.87 us
    ppermute x2, starting transfers between devices, trade(): lax.ppermute(second, ('px', 'py'), back)  1.39 us
  transfers between devices with their start and end apart: 13, of which 6 were waited for; matrix products, arithmetic and copies ran while one was open for 0% of the time, Pallas kernels for 13%

profile of v9, /device:TPU:0, one launch (start us, length us, event | category | flops | bytes accessed | tf_op | source)
XLA Modules:
  0.0 25.5 jit_solution(6670049841117609215)
XLA Ops:
  0.0 0.4 %shard_map.82.shrink_ref = bf16[4,128,128]{2,1,0:T(8,128)(2,1)S(1)} custom-call(), custom_call_target="tpu_custom_call" | custom-call | flops 4000000000 | bytes 12000000 | tf_op jit(solution)/shard_map/pallas_call | solution.py:236
  0.4 0.5 %copy-done.4 = f32[32,16,128]{2,1,0:T(8,128)S(1)} copy-done((f32[32,16,128]{2,1,0:T(8,128)S(1)}, f32[32,16,128]{2,1,0:T(8,128)}, u32[]{:S(2)}) %copy-start.4) | copy-done | bytes 262168
  1.0 0.4 %shard_map.83 = (f32[6,32,128]{2,1,0:T(8,128)S(1)}, f32[4,32,128]{2,1,0:T(8,128)S(1)}, f32[3,32,128]{2,1,0:T(8,128)S(1)}, f32[3,32,128]{2,1,0:T(8,128)S(1)}, f32[16,32,128]{2,1,0:T(8,128)S(1)}) custom-call(f32[512,128]{1,0:T(8,128)S(1)} %bitcast.3, bf16[4,128,128]{2,1,0:T(8,128)(2,1)S(1)} %shard_map.82.shrink_ref), custom_call_target="tpu_custom_call" | custom-call | flops 1000000000 | bytes 3000000 | tf_op jit(solution)/shard_map/pallas_call | solution.py:236
  1.3 2.9 %collective-permute-start = (f32[3,32,128]{2,1,0:T(8,128)S(1)}, f32[3,32,128]{2,1,0:T(8,128)S(1)}, u32[]{:S(2)}, u32[]{:S(2)}) collective-permute-start(f32[3,32,128]{2,1,0:T(8,128)S(1)} %get-tuple-element.35), channel_id=1, source_target_pairs={{0,2},{1,3},{2,6},{3,7},{4,0},{5,1},{6,10},{7,11},{8,4},{9,5},{10,... | collective-permute-start | bytes 147464 | tf_op jit(solution)/shard_map/ppermute | solution.py:733
  4.3 0.1 collective-permute-start.1
  4.4 0.1 shard_map.84.refs_3_.refs_0_
  4.5 1.9 %collective-permute-done.first_ref = f32[3,32,128]{2,1,0:T(8,128)S(1)} collective-permute-done((f32[3,32,128]{2,1,0:T(8,128)S(1)}, f32[3,32,128]{2,1,0:T(8,128)S(1)}, u32[]{:S(2)}, u32[]{:S(2)}) %collective-permute-start) | collective-permute-done | bytes 49184 | tf_op jit(solution)/shard_map/ppermute | solution.py:733
  6.4 2.0 %collective-permute-done.1.second_ref = f32[3,32,128]{2,1,0:T(8,128)S(1)} collective-permute-done((f32[3,32,128]{2,1,0:T(8,128)S(1)}, f32[3,32,128]{2,1,0:T(8,128)S(1)}, u32[]{:S(2)}, u32[]{:S(2)}) %collective-permute-start.1) | collective-permute-done | bytes 49184 | tf_op jit(solution)/shard_map/ppermute | solution.py:733
  8.4 0.2 shard_map.85.refs_0_.refs_7_.refs_4_
  8.5 1.6 %collective-permute-start.5 = (f32[136,128]{1,0:T(8,128)S(1)}, f32[136,128]{1,0:T(8,128)S(1)}, u32[]{:S(2)}, u32[]{:S(2)}) collective-permute-start(f32[136,128]{1,0:T(8,128)S(1)} %shard_map.85.refs_0_.refs_7_.refs_4_), channel_id=1, source_target_pairs={{0,2},{1,3},{2,0},{3,1},{4,6},{5,7},{6,4},{7,5},{8,10},{9,11},{10,... | collective-permute-start | bytes 208904 | tf_op jit(solution)/shard_map/ppermute | solution.py:736
  10.1 0.5 %collective-permute-start.3 = (f32[4,32,128]{2,1,0:T(8,128)S(1)}, f32[4,32,128]{2,1,0:T(8,128)S(1)}, u32[]{:S(2)}, u32[]{:S(2)}) collective-permute-start(f32[4,32,128]{2,1,0:T(8,128)S(1)} %shard_map.84.refs_3_.refs_0_), channel_id=1, source_target_pairs={{0,2},{1,3},{2,0},{3,1},{4,6},{5,7},{6,4},{7,5},{8,10},{9,11},{10,... | collective-permute-start | bytes 196616 | tf_op jit(solution)/shard_map/ppermute | solution.py:736
  10.6 0.0 copy-done.2
  10.6 0.6 %shard_map.86 = (f32[16,32,128]{2,1,0:T(8,128)S(1)}, bf16[8,16,256]{2,1,0:T(8,128)(2,1)S(1)}) custom-call(f32[16,32,128]{2,1,0:T(8,128)S(1)} %get-tuple-element.34.rows_ref, f32[3,32,128]{2,1,0:T(8,128)S(1)} %collective-permute-done.first_ref, f32[3,32,128]{2,1,0:T(8,128)S(1)} %collective-permute-done.1.second_ref, bf16[8,1,520,256]{3,2,1,0:T(8,128)(2,1)S(1)} %copy-done.2), custom_call_target="tpu_custom_call" | custom-call | flops 700000000 | bytes 2100000 | tf_op jit(solution)/shard_map/pallas_call | solution.py:236
  11.2 0.0 copy-start.1
  11.2 0.0 copy-start.3
  11.2 0.0 copy-start.6
  11.3 1.6 %collective-permute-done.5.refs_2_.refs_9_.refs_6_ = f32[136,128]{1,0:T(8,128)S(1)} collective-permute-done((f32[136,128]{1,0:T(8,128)S(1)}, f32[136,128]{1,0:T(8,128)S(1)}, u32[]{:S(2)}, u32[]{:S(2)}) %collective-permute-start.5) | collective-permute-done | bytes 69664 | tf_op jit(solution)/shard_map/ppermute | solution.py:736
  12.9 0.0 collective-permute-start.6
  12.9 0.5 %collective-permute-start.7 = (f32[136,128]{1,0:T(8,128)S(1)}, f32[136,128]{1,0:T(8,128)S(1)}, u32[]{:S(2)}, u32[]{:S(2)}) collective-permute-start(f32[136,128]{1,0:T(8,128)S(1)} %collective-permute-done.5.refs_2_.refs_9_.refs_6_), channel_id=1, source_target_pairs={{0,1},{1,0},{2,3},{3,2},{4,5},{5,4},{6,7},{7,6},{8,9},{9,8},{10,11... | collective-permute-start | bytes 208904 | tf_op jit(solution)/shard_map/ppermute | solution.py:736
  13.4 0.0 collective-permute-start.2
  13.4 1.0 %collective-permute-done.3.refs_5_.refs_2_ = f32[4,32,128]{2,1,0:T(8,128)S(1)} collective-permute-done((f32[4,32,128]{2,1,0:T(8,128)S(1)}, f32[4,32,128]{2,1,0:T(8,128)S(1)}, u32[]{:S(2)}, u32[]{:S(2)}) %collective-permute-start.3) | collective-permute-done | bytes 65568 | tf_op jit(solution)/shard_map/ppermute | solution.py:736
  14.4 0.0 collective-permute-start.4
  14.4 0.0 collective-permute-done.6.refs_1_.refs_8_.refs_5_
  14.4 0.0 collective-permute-done.7.refs_3_.refs_10_.refs_7_
  14.4 0.0 copy-done
  14.4 0.2 shard_map.87.refs_0_
  14.6 4.4 %collective-permute-start.8 = (f32[32,128]{1,0:T(8,128)S(1)}, f32[32,128]{1,0:T(8,128)S(1)}, u32[]{:S(2)}, u32[]{:S(2)}) collective-permute-start(f32[32,128]{1,0:T(8,128)S(1)} %shard_map.87.refs_0_), channel_id=1, source_target_pairs={{0,24},{1,17},{2,26},{3,19},{4,28},{5,21},{6,30},{7,23},{8,16},{9,... | collective-permute-start | bytes 49160 | tf_op jit(solution)/shard_map/ppermute | solution.py:801
  19.0 0.0 collective-permute-start.10
  19.0 0.0 collective-permute-done.2.refs_4_.refs_1_
  19.0 0.0 collective-permute-done.4.refs_6_.refs_3_
  19.1 0.0 copy-done.1
  19.1 0.0 copy-done.3
  19.1 0.0 copy-done.6
  19.1 0.9 %shard_map.88 = (f32[2,2,32,256]{3,2,1,0:T(8,128)S(1)}, f32[1,2,32,256]{3,2,1,0:T(8,128)S(1)}, f32[1,1,32,128]{3,2,1,0:T(8,128)S(1)}, f32[6,32,256]{2,1,0:T(8,12...) custom-call(bf16[102,128,128]{2,1,0:T(8,128)(2,1)S(1)} %copy-done, bf16[4,2,520,256]{3,2,1,0:T(8,128)(2,1)S(1)} %copy-done.1, ...), custom_call_target="tpu_custom_call" | custom-call | flops 2500000000 | bytes 7500000 | tf_op jit(solution)/shard_map/pallas_call | solution.py:236
  20.0 0.8 %collective-permute-start.11 = (f32[1,32,128]{2,1,0:T(8,128)S(1)}, f32[1,32,128]{2,1,0:T(8,128)S(1)}, u32[]{:S(2)}, u32[]{:S(2)}) collective-permute-start(f32[1,32,128]{2,1,0:T(8,128)S(1)} %get-tuple-element.59), channel_id=1, source_target_pairs={{0,2},{1,3},{2,6},{3,7},{4,0},{5,1},{6,10},{7,11},{8,4},{9,5},{10,... | collective-permute-start | bytes 49160 | tf_op jit(solution)/shard_map/ppermute | solution.py:733
  20.8 1.3 %collective-permute-start.12 = (f32[1,32,128]{2,1,0:T(8,128)S(1)}, f32[1,32,128]{2,1,0:T(8,128)S(1)}, u32[]{:S(2)}, u32[]{:S(2)}) collective-permute-start(f32[1,32,128]{2,1,0:T(8,128)S(1)} %get-tuple-element.60), channel_id=1, source_target_pairs={{2,0},{3,1},{6,2},{7,3},{0,4},{1,5},{10,6},{11,7},{4,8},{5,9},{14,... | collective-permute-start | bytes 49160 | tf_op jit(solution)/shard_map/ppermute | solution.py:733
  22.1 0.0 collective-permute-done.8.refs_1_
  22.1 0.0 collective-permute-start.9
  22.1 0.0 copy-start.7
  22.1 0.6 %shard_map.89 = (f32[8,32,128]{2,1,0:T(8,128)S(1)}, f32[4,32,128]{2,1,0:T(8,128)S(1)}, f32[2,32,128]{2,1,0:T(8,128)S(1)}, f32[16,32,128]{2,1,0:T(8,128)S(1)}) custom-call(bf16[102,128,128]{2,1,0:T(8,128)(2,1)S(1)} %copy-done, bf16[4,2,520,256]{3,2,1,0:T(8,128)(2,1)S(1)} %copy-done.1, f32[6,32,256]{2,1,0:T(8,128)S(1)} %get-tuple-element.49.rows_ref, ...), custom_call_target="tpu_custom_call" | custom-call | flops 1200000000 | bytes 3600000 | tf_op jit(solution)/shard_map/pallas_call | solution.py:236
  22.8 0.0 collective-permute-done.10.refs_3_
  22.8 0.5 %collective-permute-done.9.refs_2_ = f32[32,128]{1,0:T(8,128)S(1)} collective-permute-done((f32[32,128]{1,0:T(8,128)S(1)}, f32[32,128]{1,0:T(8,128)S(1)}, u32[]{:S(2)}, u32[]{:S(2)}) %collective-permute-start.9) | collective-permute-done | bytes 16416 | tf_op jit(solution)/shard_map/ppermute | solution.py:736
  23.3 0.0 copy-done.5
  23.3 0.0 copy-done.7
  23.3 0.8 %shard_map.90.four_ref = f32[3,32,128]{2,1,0:T(8,128)S(1)} custom-call(bf16[102,128,128]{2,1,0:T(8,128)(2,1)S(1)} %copy-done, bf16[4,1,64,136]{3,2,1,0:T(8,128)(2,1)S(1)} %bitcast.4, bf16[64,64]{1,0:T(8,128)(2,1)S(1)} %copy-done.7, f32[32,128]{1,0:T(8,128)S(1)} %shard_map.87.refs_0_, f32[32,128]{1,0:T(8,128)S(1)} %collective-permute-done.8.refs_1_, ...), custom_call_target="tpu_custom_call" | custom-call | flops 1000000000 | bytes 3000000 | tf_op jit(solution)/shard_map/pallas_call | solution.py:236
  24.1 0.0 collective-permute-done.11.first_ref
  24.1 0.4 %collective-permute-done.12.second_ref = f32[1,32,128]{2,1,0:T(8,128)S(1)} collective-permute-done((f32[1,32,128]{2,1,0:T(8,128)S(1)}, f32[1,32,128]{2,1,0:T(8,128)S(1)}, u32[]{:S(2)}, u32[]{:S(2)}) %collective-permute-start.12) | collective-permute-done | bytes 16416 | tf_op jit(solution)/shard_map/ppermute | solution.py:733
  24.6 0.9 %shard_map.91 = f32[512,128]{1,0:T(8,128)} custom-call(bf16[102,128,128]{2,1,0:T(8,128)(2,1)S(1)} %copy-done, f32[16,32,128]{2,1,0:T(8,128)S(1)} %get-tuple-element.55.fine_ref, f32[8,32,128]{2,1,0:T(8,128)S(1)} %get-tuple-element.56.one_ref, f32[4,32,128]{2,1,0:T(8,128)S(1)} %get-tuple-element.57.two_ref, f32[2,32,128]{2,1,0:T(8,128)S(1)} %get-tuple-element.58.three_ref, ...), custom_call_target="tpu_custom_call" | custom-call | flops 1000000000 | bytes 3000000 | tf_op jit(solution)/shard_map/pallas_call | solution.py:236
  (4 shorter events, 0.0 us)
Async XLA Ops:
  0.0 0.9 %copy-start.4 = (f32[32,16,128]{2,1,0:T(8,128)S(1)}, f32[32,16,128]{2,1,0:T(8,128)}, u32[]{:S(2)}) copy-start(f32[32,16,128]{2,1,0:T(8,128)} %param.8) | copy-start | bytes 786436
  1.3 5.0 %collective-permute-start = (f32[3,32,128]{2,1,0:T(8,128)S(1)}, f32[3,32,128]{2,1,0:T(8,128)S(1)}, u32[]{:S(2)}, u32[]{:S(2)}) collective-permute-start(f32[3,32,128]{2,1,0:T(8,128)S(1)} %get-tuple-element.35), channel_id=1, source_target_pairs={{0,2},{1,3},{2,6},{3,7},{4,0},{5,1},{6,10},{7,11},{8,4},{9,5},{10,... | collective-permute-start | bytes 147464 | tf_op jit(solution)/shard_map/ppermute | solution.py:733
  4.3 4.1 %collective-permute-start.1 = (f32[3,32,128]{2,1,0:T(8,128)S(1)}, f32[3,32,128]{2,1,0:T(8,128)S(1)}, u32[]{:S(2)}, u32[]{:S(2)}) collective-permute-start(f32[3,32,128]{2,1,0:T(8,128)S(1)} %get-tuple-element.36), channel_id=1, source_target_pairs={{2,0},{3,1},{6,2},{7,3},{0,4},{1,5},{10,6},{11,7},{4,8},{5,9},{14,... | collective-permute-start | bytes 147464 | tf_op jit(solution)/shard_map/ppermute | solution.py:733
  4.4 6.2 %copy-start.2 = (bf16[8,1,520,256]{3,2,1,0:T(8,128)(2,1)S(1)}, bf16[8,1,520,256]{3,2,1,0:T(8,128)(2,1)}, u32[]{:S(2)}) copy-start(bf16[8,1,520,256]{3,2,1,0:T(8,128)(2,1)} %factor_ref.2) | copy-start | bytes 6389764
  8.4 6.0 %copy-start = (bf16[102,128,128]{2,1,0:T(8,128)(2,1)S(1)}, bf16[102,128,128]{2,1,0:T(8,128)(2,1)}, u32[]{:S(2)}) copy-start(bf16[102,128,128]{2,1,0:T(8,128)(2,1)} %constant.2.clone.block_ref) | copy-start | bytes 10027012
  8.5 4.4 %collective-permute-start.5 = (f32[136,128]{1,0:T(8,128)S(1)}, f32[136,128]{1,0:T(8,128)S(1)}, u32[]{:S(2)}, u32[]{:S(2)}) collective-permute-start(f32[136,128]{1,0:T(8,128)S(1)} %shard_map.85.refs_0_.refs_7_.refs_4_), channel_id=1, source_target_pairs={{0,2},{1,3},{2,0},{3,1},{4,6},{5,7},{6,4},{7,5},{8,10},{9,11},{10,... | collective-permute-start | bytes 208904 | tf_op jit(solution)/shard_map/ppermute | solution.py:736
  10.1 4.3 %collective-permute-start.3 = (f32[4,32,128]{2,1,0:T(8,128)S(1)}, f32[4,32,128]{2,1,0:T(8,128)S(1)}, u32[]{:S(2)}, u32[]{:S(2)}) collective-permute-start(f32[4,32,128]{2,1,0:T(8,128)S(1)} %shard_map.84.refs_3_.refs_0_), channel_id=1, source_target_pairs={{0,2},{1,3},{2,0},{3,1},{4,6},{5,7},{6,4},{7,5},{8,10},{9,11},{10,... | collective-permute-start | bytes 196616 | tf_op jit(solution)/shard_map/ppermute | solution.py:736
  11.2 7.8 %copy-start.1 = (bf16[4,2,520,256]{3,2,1,0:T(8,128)(2,1)S(1)}, bf16[4,2,520,256]{3,2,1,0:T(8,128)(2,1)}, u32[]{:S(2)}) copy-start(bf16[4,2,520,256]{3,2,1,0:T(8,128)(2,1)} %factor_ref.3) | copy-start | bytes 6389764
  11.2 7.8 %copy-start.3 = (bf16[2,1,520,256]{3,2,1,0:T(8,128)(2,1)S(1)}, bf16[2,1,520,256]{3,2,1,0:T(8,128)(2,1)}, u32[]{:S(2)}) copy-start(bf16[2,1,520,256]{3,2,1,0:T(8,128)(2,1)} %refs_1_.1) | copy-start | bytes 1597444
  11.2 7.8 %copy-start.6 = (bf16[1,1,264,128]{3,2,1,0:T(8,128)(2,1)S(1)}, bf16[1,1,264,128]{3,2,1,0:T(8,128)(2,1)}, u32[]{:S(2)}) copy-start(bf16[1,1,264,128]{3,2,1,0:T(8,128)(2,1)} %refs_2_.1) | copy-start | bytes 202756
  12.9 1.5 %collective-permute-start.6 = (f32[136,128]{1,0:T(8,128)S(1)}, f32[136,128]{1,0:T(8,128)S(1)}, u32[]{:S(2)}, u32[]{:S(2)}) collective-permute-start(f32[136,128]{1,0:T(8,128)S(1)} %shard_map.85.refs_0_.refs_7_.refs_4_), channel_id=1, source_target_pairs={{0,1},{1,0},{2,3},{3,2},{4,5},{5,4},{6,7},{7,6},{8,9},{9,8},{10,11... | collective-permute-start | bytes 208904 | tf_op jit(solution)/shard_map/ppermute | solution.py:736
  12.9 1.5 %collective-permute-start.7 = (f32[136,128]{1,0:T(8,128)S(1)}, f32[136,128]{1,0:T(8,128)S(1)}, u32[]{:S(2)}, u32[]{:S(2)}) collective-permute-start(f32[136,128]{1,0:T(8,128)S(1)} %collective-permute-done.5.refs_2_.refs_9_.refs_6_), channel_id=1, source_target_pairs={{0,1},{1,0},{2,3},{3,2},{4,5},{5,4},{6,7},{7,6},{8,9},{9,8},{10,11... | collective-permute-start | bytes 208904 | tf_op jit(solution)/shard_map/ppermute | solution.py:736
  13.4 5.6 %collective-permute-start.2 = (f32[4,32,128]{2,1,0:T(8,128)S(1)}, f32[4,32,128]{2,1,0:T(8,128)S(1)}, u32[]{:S(2)}, u32[]{:S(2)}) collective-permute-start(f32[4,32,128]{2,1,0:T(8,128)S(1)} %shard_map.84.refs_3_.refs_0_), channel_id=1, source_target_pairs={{0,1},{1,0},{2,3},{3,2},{4,5},{5,4},{6,7},{7,6},{8,9},{9,8},{10,11... | collective-permute-start | bytes 196616 | tf_op jit(solution)/shard_map/ppermute | solution.py:736
  14.4 4.7 %collective-permute-start.4 = (f32[4,32,128]{2,1,0:T(8,128)S(1)}, f32[4,32,128]{2,1,0:T(8,128)S(1)}, u32[]{:S(2)}, u32[]{:S(2)}) collective-permute-start(f32[4,32,128]{2,1,0:T(8,128)S(1)} %collective-permute-done.3.refs_5_.refs_2_), channel_id=1, source_target_pairs={{0,1},{1,0},{2,3},{3,2},{4,5},{5,4},{6,7},{7,6},{8,9},{9,8},{10,11... | collective-permute-start | bytes 196616 | tf_op jit(solution)/shard_map/ppermute | solution.py:736
  14.6 7.5 %collective-permute-start.8 = (f32[32,128]{1,0:T(8,128)S(1)}, f32[32,128]{1,0:T(8,128)S(1)}, u32[]{:S(2)}, u32[]{:S(2)}) collective-permute-start(f32[32,128]{1,0:T(8,128)S(1)} %shard_map.87.refs_0_), channel_id=1, source_target_pairs={{0,24},{1,17},{2,26},{3,19},{4,28},{5,21},{6,30},{7,23},{8,16},{9,... | collective-permute-start | bytes 49160 | tf_op jit(solution)/shard_map/ppermute | solution.py:801
  19.0 3.7 %collective-permute-start.10 = (f32[32,128]{1,0:T(8,128)S(1)}, f32[32,128]{1,0:T(8,128)S(1)}, u32[]{:S(2)}, u32[]{:S(2)}) collective-permute-start(f32[32,128]{1,0:T(8,128)S(1)} %shard_map.87.refs_0_), channel_id=1, source_target_pairs={{0,8},{1,9},{2,10},{3,11},{4,12},{5,13},{6,14},{7,15},{8,0},{9,1},... | collective-permute-start | bytes 49160 | tf_op jit(solution)/shard_map/ppermute | solution.py:801
  20.0 4.1 %collective-permute-start.11 = (f32[1,32,128]{2,1,0:T(8,128)S(1)}, f32[1,32,128]{2,1,0:T(8,128)S(1)}, u32[]{:S(2)}, u32[]{:S(2)}) collective-permute-start(f32[1,32,128]{2,1,0:T(8,128)S(1)} %get-tuple-element.59), channel_id=1, source_target_pairs={{0,2},{1,3},{2,6},{3,7},{4,0},{5,1},{6,10},{7,11},{8,4},{9,5},{10,... | collective-permute-start | bytes 49160 | tf_op jit(solution)/shard_map/ppermute | solution.py:733
  20.8 3.7 %collective-permute-start.12 = (f32[1,32,128]{2,1,0:T(8,128)S(1)}, f32[1,32,128]{2,1,0:T(8,128)S(1)}, u32[]{:S(2)}, u32[]{:S(2)}) collective-permute-start(f32[1,32,128]{2,1,0:T(8,128)S(1)} %get-tuple-element.60), channel_id=1, source_target_pairs={{2,0},{3,1},{6,2},{7,3},{0,4},{1,5},{10,6},{11,7},{4,8},{5,9},{14,... | collective-permute-start | bytes 49160 | tf_op jit(solution)/shard_map/ppermute | solution.py:733
  22.1 1.2 %collective-permute-start.9 = (f32[32,128]{1,0:T(8,128)S(1)}, f32[32,128]{1,0:T(8,128)S(1)}, u32[]{:S(2)}, u32[]{:S(2)}) collective-permute-start(f32[32,128]{1,0:T(8,128)S(1)} %collective-permute-done.8.refs_1_), channel_id=1, source_target_pairs={{0,1},{1,0},{2,3},{3,2},{4,5},{5,4},{6,7},{7,6},{8,9},{9,8},{10,11... | collective-permute-start | bytes 49160 | tf_op jit(solution)/shard_map/ppermute | solution.py:736
  22.1 1.2 %copy-start.5 = (bf16[4,1,136,64]{2,3,1,0:T(8,128)(2,1)S(1)}, bf16[4,1,136,64]{2,3,1,0:T(8,128)(2,1)}, u32[]{:S(2)}) copy-start(bf16[4,1,136,64]{2,3,1,0:T(8,128)(2,1)} %param.13) | copy-start | bytes 208900
  22.1 1.2 %copy-start.7 = (bf16[64,64]{1,0:T(8,128)(2,1)S(1)}, bf16[64,64]{1,0:T(8,128)(2,1)}, u32[]{:S(2)}) copy-start(bf16[64,64]{1,0:T(8,128)(2,1)} %inverse_ref.1) | copy-start | bytes 24580

commit v10 on v9

--- a/solution.py
+++ b/solution.py
@@ -274,16 +274,20 @@
     return jnp.where(c == 0, 1, 0), jnp.where(c == plan.m - 1, 1, 0)
 
 
-def write_halos(c, down, up, first_ref, second_ref):
+def write_halos(c, down, up, first_ref, second_ref, pairs=False):
     forward = jnp.bitwise_and(c, 2) != 0
+    if pairs:
+        forward = lax.rem(lax.axis_index("px"), 2) == 1
     for k, (low, high) in enumerate(zip(down, up)):
         first_ref[k] = jnp.where(forward, low, high)
         second_ref[k] = jnp.where(forward, high, low)
 
 
-def read_halos(plan, first_ref, second_ref):
+def read_halos(plan, first_ref, second_ref, pairs=False):
     r, c = lax.axis_index("px"), lax.axis_index("py")
     forward = jnp.bitwise_and(c, 2) != 0
+    if pairs:
+        forward = lax.rem(r, 2) == 0
     above = jnp.where(r > 0, 1.0, 0.0).astype(F32)
     below = jnp.where(r < plan.n - 1, 1.0, 0.0).astype(F32)
     first, second = first_ref[...], second_ref[...]
@@ -339,7 +343,7 @@
     down = [x[-1], jnp.where(lane < three, outer[2], own[0])]
     down.append(jnp.where(lane < one, third, jnp.where(lane < three, outer[3], own[1])))
     up = [x[0], jnp.where(lane < one, third, own[0]), own[1]]
-    write_halos(c, down, up, first_ref, second_ref)
+    write_halos(c, down, up, first_ref, second_ref, True)
     for i, row in enumerate(x):
         rows_ref[i] = row
 
@@ -367,7 +371,7 @@
 def merge_kernel(plan, outer_ref, shrink_ref, first_ref, second_ref, out_ref):
     r, rhs = lax.axis_index("px"), plan.rhs
     lane = lane_index(rhs)
-    above, below = read_halos(plan, first_ref, second_ref)
+    above, below = read_halos(plan, first_ref, second_ref, True)
     one, two, three = plan.offset[2:]
     edge = product(jnp.concatenate([above[0], below[0]], axis=0), shrink_ref[0]) * SHRINK
     added = [
@@ -515,7 +519,7 @@
                     edge.append(pltpu.roll(value[at], LANES - w, 1) if j else value[at])
     edges = [jnp.concatenate(edge, axis=1) for edge in (down, up)]
     picked = product(jnp.concatenate(edges, axis=0), blocks.get(block_ref, "pick", c))
-    write_halos(c, [picked[:rhs]], [picked[rhs:]], outs[4], outs[5])
+    write_halos(c, [picked[:rhs]], [picked[rhs:]], outs[4], outs[5], False)
     for level in (1, 2, 3):
         for t, values in enumerate(solved[level]):
             for k, value in enumerate(values):
@@ -555,7 +559,7 @@
 
 def fine_kernel(plan, rows_ref, first_ref, second_ref, factor_ref, out_ref, picked_ref):
     rhs, h0, w0 = plan.rhs, plan.h0, plan.w0
-    above, below = read_halos(plan, first_ref, second_ref)
+    above, below = read_halos(plan, first_ref, second_ref, True)
     lane = lane_index(rhs)
     rows = [above[0]] + [rows_ref[row] for row in range(h0)] + [below[0]]
     length = 4 * (w0 + 2)
@@ -679,7 +683,7 @@
     r, rhs = lax.axis_index("px"), plan.rhs
     above = jnp.where(r > 0, 1.0, 0.0).astype(F32)
     below = jnp.where(r < plan.n - 1, 1.0, 0.0).astype(F32)
-    halos = read_halos(plan, first_ref, second_ref)
+    halos = read_halos(plan, first_ref, second_ref, False)
     halo = product(
         jnp.concatenate([halos[0][0], halos[1][0]], axis=0),
         blocks.get(block_ref, "band", lax.axis_index("py")),
@@ -732,6 +736,16 @@
         back = [(b, a) for a, b in ring]
         return lax.ppermute(first, ("px", "py"), ring), lax.ppermute(second, ("px", "py"), back)
 
+    def trade_pairs(first, second):
+        far = []
+        for i in range(n):
+            for c in range(m):
+                j = ((i + 1) ^ 1) - 1
+                at = j * m + c if 0 <= j < n else i * m + (c ^ 2)
+                far.append((i * m + c, at))
+        near = [(i, i ^ 1) for i in range(n)]
+        return lax.ppermute(first, ("px", "py"), far), lax.ppermute(second, "px", near)
+
     def swap(value, bits):
         return lax.ppermute(value, "py", [(i, i ^ bits) for i in range(m)])
 
@@ -761,7 +775,7 @@
         (shape(6, rhs, LANES), shape(4, rhs, LANES), shape(3, rhs, LANES), shape(3, rhs, LANES),
          shape(h0, rhs, plan.w0)),
     )(x, shrink)
-    first, second = trade(first, second)
+    first, second = trade_pairs(first, second)
     early = kernel_call(
         functools.partial(inner_rows_kernel, plan), shape(4, rhs, LANES), cost_us=0.3
     )(early, rows)

time: 25.6 us -> 25.5 us (level)
  waiting for transfers between devices: 7.47 us -> 6.6 us
  starting transfers between devices: 12.1 us -> 12.9 us
    ppermute x0 -> x2, starting transfers between devices: none -> 4.5 us  [the longest x1 2.94 us: trade_pairs(): lax.ppermute(first, ('px', 'py'), far)]
    ppermute x0 -> x2, waiting for transfers between devices: none -> 2.38 us  [the longest x1 2.02 us: trade_pairs(): lax.ppermute(second, 'px', near)]
    ppermute x2 -> x1, starting transfers between devices: 3.71 us -> 1.48 us  [trade(): lax.ppermute(first, ('px', 'py'), ring)]
    ppermute x2 -> x1, waiting for transfers between devices: 1.87 us -> 0.01 us  [trade(): lax.ppermute(first, ('px', 'py'), ring)]
    ppermute x2 -> x1, waiting for transfers between devices: 2.44 us -> 1.16 us  [trade(): lax.ppermute(second, ('px', 'py'), back)]
    ppermute x2 -> x1, starting transfers between devices: 1.39 us -> 0.6 us  [trade(): lax.ppermute(second, ('px', 'py'), back)]
    ppermute x2, starting transfers between devices: 4.41 us -> 3.67 us  [per_device(): fetched.append((lax.ppermute(pairs, ('px', 'py'), routes), even, odd))]
  transfers between devices with their start and end apart: 13 -> 13, of which waited for: 6 -> 8; matrix products, arithmetic and copies ran while one was open for 0% -> 0% of each run, Pallas kernels for 13% -> 13%
where the time goes in v10:
time: 25.5 us; the launch traced here: 25.4 us
  starting transfers between devices  12.9 us (51%)
  waiting for transfers between devices  6.6 us (26%)
  Pallas kernels  5.17 us (20%)
  local copies, waits for them, and re-layouts  0.58 us (2%)
    pallas_call x10, Pallas kernels, call(): pl.pallas_call(body, out_shape=out_shape, in_specs=[whole] * len(operands...  5.17 us
    ppermute x2, starting transfers between devices, per_device(): fetched.append((lax.ppermute(pairs, ('px', 'py'), routes), even, odd))  3.67 us
    ppermute x7, waiting for transfers between devices, swap(): return lax.ppermute(value, 'py', [(i, i ^ bits) for i in range(m)])  3.03 us
    ppermute x1, starting transfers between devices, trade_pairs(): lax.ppermute(first, ('px', 'py'), far)  2.94 us
    ppermute x7, starting transfers between devices, swap(): return lax.ppermute(value, 'py', [(i, i ^ bits) for i in range(m)])  2.65 us
    ppermute x1, waiting for transfers between devices, trade_pairs(): lax.ppermute(second, 'px', near)  2.02 us
    ppermute x1, starting transfers between devices, trade_pairs(): lax.ppermute(second, 'px', near)  1.55 us
    ppermute x1, starting transfers between devices, trade(): lax.ppermute(first, ('px', 'py'), ring)  1.48 us
  transfers between devices with their start and end apart: 13, of which 8 were waited for; matrix products, arithmetic and copies ran while one was open for 0% of the time, Pallas kernels for 13%

profile of v10, /device:TPU:0, one launch (start us, length us, event | category | flops | bytes accessed | tf_op | source)
XLA Modules:
  0.0 25.4 jit_solution(10263373881619314174)
XLA Ops:
  0.0 0.4 %shard_map.82.shrink_ref = bf16[4,128,128]{2,1,0:T(8,128)(2,1)S(1)} custom-call(), custom_call_target="tpu_custom_call" | custom-call | flops 4000000000 | bytes 12000000 | tf_op jit(solution)/shard_map/pallas_call | solution.py:236
  0.4 0.5 %copy-done.4 = f32[32,16,128]{2,1,0:T(8,128)S(1)} copy-done((f32[32,16,128]{2,1,0:T(8,128)S(1)}, f32[32,16,128]{2,1,0:T(8,128)}, u32[]{:S(2)}) %copy-start.4) | copy-done | bytes 262168
  1.0 0.4 %shard_map.83 = (f32[6,32,128]{2,1,0:T(8,128)S(1)}, f32[4,32,128]{2,1,0:T(8,128)S(1)}, f32[3,32,128]{2,1,0:T(8,128)S(1)}, f32[3,32,128]{2,1,0:T(8,128)S(1)}, f32[16,32,128]{2,1,0:T(8,128)S(1)}) custom-call(f32[512,128]{1,0:T(8,128)S(1)} %bitcast.3, bf16[4,128,128]{2,1,0:T(8,128)(2,1)S(1)} %shard_map.82.shrink_ref), custom_call_target="tpu_custom_call" | custom-call | flops 1000000000 | bytes 3000000 | tf_op jit(solution)/shard_map/pallas_call | solution.py:236
  1.3 2.9 %collective-permute-start = (f32[3,32,128]{2,1,0:T(8,128)S(1)}, f32[3,32,128]{2,1,0:T(8,128)S(1)}, u32[]{:S(2)}, u32[]{:S(2)}) collective-permute-start(f32[3,32,128]{2,1,0:T(8,128)S(1)} %get-tuple-element.35), channel_id=1, source_target_pairs={{0,2},{1,3},{2,0},{3,1},{4,8},{5,9},{6,10},{7,11},{8,4},{9,5},{10,... | collective-permute-start | bytes 147464 | tf_op jit(solution)/shard_map/ppermute | solution.py:747
  4.3 1.6 %collective-permute-start.1 = (f32[3,32,128]{2,1,0:T(8,128)S(1)}, f32[3,32,128]{2,1,0:T(8,128)S(1)}, u32[]{:S(2)}, u32[]{:S(2)}) collective-permute-start(f32[3,32,128]{2,1,0:T(8,128)S(1)} %get-tuple-element.36), channel_id=1, source_target_pairs={{0,4},{4,0},{8,12},{12,8},{16,20},{20,16},{24,28},{28,24},{1,5},{5... | collective-permute-start | bytes 147464 | tf_op jit(solution)/shard_map/ppermute | solution.py:747
  5.8 0.1 shard_map.84.refs_3_.refs_0_
  6.0 0.4 %collective-permute-done.first_ref = f32[3,32,128]{2,1,0:T(8,128)S(1)} collective-permute-done((f32[3,32,128]{2,1,0:T(8,128)S(1)}, f32[3,32,128]{2,1,0:T(8,128)S(1)}, u32[]{:S(2)}, u32[]{:S(2)}) %collective-permute-start) | collective-permute-done | bytes 49184 | tf_op jit(solution)/shard_map/ppermute | solution.py:747
  6.4 2.0 %collective-permute-done.1.second_ref = f32[3,32,128]{2,1,0:T(8,128)S(1)} collective-permute-done((f32[3,32,128]{2,1,0:T(8,128)S(1)}, f32[3,32,128]{2,1,0:T(8,128)S(1)}, u32[]{:S(2)}, u32[]{:S(2)}) %collective-permute-start.1) | collective-permute-done | bytes 49184 | tf_op jit(solution)/shard_map/ppermute | solution.py:747
  8.4 0.2 shard_map.85.refs_0_.refs_7_.refs_4_
  8.5 1.1 %collective-permute-start.5 = (f32[136,128]{1,0:T(8,128)S(1)}, f32[136,128]{1,0:T(8,128)S(1)}, u32[]{:S(2)}, u32[]{:S(2)}) collective-permute-start(f32[136,128]{1,0:T(8,128)S(1)} %shard_map.85.refs_0_.refs_7_.refs_4_), channel_id=1, source_target_pairs={{0,2},{1,3},{2,0},{3,1},{4,6},{5,7},{6,4},{7,5},{8,10},{9,11},{10,... | collective-permute-start | bytes 208904 | tf_op jit(solution)/shard_map/ppermute | solution.py:750
  9.6 1.0 %collective-permute-start.3 = (f32[4,32,128]{2,1,0:T(8,128)S(1)}, f32[4,32,128]{2,1,0:T(8,128)S(1)}, u32[]{:S(2)}, u32[]{:S(2)}) collective-permute-start(f32[4,32,128]{2,1,0:T(8,128)S(1)} %shard_map.84.refs_3_.refs_0_), channel_id=1, source_target_pairs={{0,2},{1,3},{2,0},{3,1},{4,6},{5,7},{6,4},{7,5},{8,10},{9,11},{10,... | collective-permute-start | bytes 196616 | tf_op jit(solution)/shard_map/ppermute | solution.py:750
  10.6 0.0 copy-done.2
  10.6 0.6 %shard_map.86 = (f32[16,32,128]{2,1,0:T(8,128)S(1)}, bf16[8,16,256]{2,1,0:T(8,128)(2,1)S(1)}) custom-call(f32[16,32,128]{2,1,0:T(8,128)S(1)} %get-tuple-element.34.rows_ref, f32[3,32,128]{2,1,0:T(8,128)S(1)} %collective-permute-done.first_ref, f32[3,32,128]{2,1,0:T(8,128)S(1)} %collective-permute-done.1.second_ref, bf16[8,1,520,256]{3,2,1,0:T(8,128)(2,1)S(1)} %copy-done.2), custom_call_target="tpu_custom_call" | custom-call | flops 700000000 | bytes 2100000 | tf_op jit(solution)/shard_map/pallas_call | solution.py:236
  11.2 0.0 copy-start.1
  11.2 0.0 copy-start.3
  11.3 0.0 copy-start.6
  11.3 1.6 %collective-permute-done.5.refs_2_.refs_9_.refs_6_ = f32[136,128]{1,0:T(8,128)S(1)} collective-permute-done((f32[136,128]{1,0:T(8,128)S(1)}, f32[136,128]{1,0:T(8,128)S(1)}, u32[]{:S(2)}, u32[]{:S(2)}) %collective-permute-start.5) | collective-permute-done | bytes 69664 | tf_op jit(solution)/shard_map/ppermute | solution.py:750
  12.9 0.0 collective-permute-start.6
  12.9 0.5 %collective-permute-start.7 = (f32[136,128]{1,0:T(8,128)S(1)}, f32[136,128]{1,0:T(8,128)S(1)}, u32[]{:S(2)}, u32[]{:S(2)}) collective-permute-start(f32[136,128]{1,0:T(8,128)S(1)} %collective-permute-done.5.refs_2_.refs_9_.refs_6_), channel_id=1, source_target_pairs={{0,1},{1,0},{2,3},{3,2},{4,5},{5,4},{6,7},{7,6},{8,9},{9,8},{10,11... | collective-permute-start | bytes 208904 | tf_op jit(solution)/shard_map/ppermute | solution.py:750
  13.4 0.0 collective-permute-start.2
  13.4 0.5 %collective-permute-done.3.refs_5_.refs_2_ = f32[4,32,128]{2,1,0:T(8,128)S(1)} collective-permute-done((f32[4,32,128]{2,1,0:T(8,128)S(1)}, f32[4,32,128]{2,1,0:T(8,128)S(1)}, u32[]{:S(2)}, u32[]{:S(2)}) %collective-permute-start.3) | collective-permute-done | bytes 65568 | tf_op jit(solution)/shard_map/ppermute | solution.py:750
  13.9 0.0 collective-permute-start.4
  13.9 0.2 collective-permute-done.6.refs_1_.refs_8_.refs_5_
  14.2 0.2 collective-permute-done.7.refs_3_.refs_10_.refs_7_
  14.3 0.0 copy-done
  14.3 0.2 shard_map.87.refs_0_
  14.6 3.7 %collective-permute-start.8 = (f32[32,128]{1,0:T(8,128)S(1)}, f32[32,128]{1,0:T(8,128)S(1)}, u32[]{:S(2)}, u32[]{:S(2)}) collective-permute-start(f32[32,128]{1,0:T(8,128)S(1)} %shard_map.87.refs_0_), channel_id=1, source_target_pairs={{0,24},{1,17},{2,26},{3,19},{4,28},{5,21},{6,30},{7,23},{8,16},{9,... | collective-permute-start | bytes 49160 | tf_op jit(solution)/shard_map/ppermute | solution.py:815
  18.2 0.0 collective-permute-start.10
  18.2 0.0 collective-permute-done.2.refs_4_.refs_1_
  18.2 0.0 collective-permute-done.4.refs_6_.refs_3_
  18.2 0.0 copy-done.1
  18.3 0.0 copy-done.3
  18.3 0.0 copy-done.6
  18.3 0.9 %shard_map.88 = (f32[2,2,32,256]{3,2,1,0:T(8,128)S(1)}, f32[1,2,32,256]{3,2,1,0:T(8,128)S(1)}, f32[1,1,32,128]{3,2,1,0:T(8,128)S(1)}, f32[6,32,256]{2,1,0:T(8,12...) custom-call(bf16[102,128,128]{2,1,0:T(8,128)(2,1)S(1)} %copy-done, bf16[4,2,520,256]{3,2,1,0:T(8,128)(2,1)S(1)} %copy-done.1, ...), custom_call_target="tpu_custom_call" | custom-call | flops 2500000000 | bytes 7500000 | tf_op jit(solution)/shard_map/pallas_call | solution.py:236
  19.2 1.5 %collective-permute-start.11 = (f32[1,32,128]{2,1,0:T(8,128)S(1)}, f32[1,32,128]{2,1,0:T(8,128)S(1)}, u32[]{:S(2)}, u32[]{:S(2)}) collective-permute-start(f32[1,32,128]{2,1,0:T(8,128)S(1)} %get-tuple-element.59), channel_id=1, source_target_pairs={{0,2},{1,3},{2,6},{3,7},{4,0},{5,1},{6,10},{7,11},{8,4},{9,5},{10,... | collective-permute-start | bytes 49160 | tf_op jit(solution)/shard_map/ppermute | solution.py:737
  20.7 0.6 %collective-permute-start.12 = (f32[1,32,128]{2,1,0:T(8,128)S(1)}, f32[1,32,128]{2,1,0:T(8,128)S(1)}, u32[]{:S(2)}, u32[]{:S(2)}) collective-permute-start(f32[1,32,128]{2,1,0:T(8,128)S(1)} %get-tuple-element.60), channel_id=1, source_target_pairs={{2,0},{3,1},{6,2},{7,3},{0,4},{1,5},{10,6},{11,7},{4,8},{5,9},{14,... | collective-permute-start | bytes 49160 | tf_op jit(solution)/shard_map/ppermute | solution.py:737
  21.3 0.0 collective-permute-done.8.refs_1_
  21.3 0.0 collective-permute-start.9
  21.3 0.0 copy-start.7
  21.3 0.6 %shard_map.89 = (f32[8,32,128]{2,1,0:T(8,128)S(1)}, f32[4,32,128]{2,1,0:T(8,128)S(1)}, f32[2,32,128]{2,1,0:T(8,128)S(1)}, f32[16,32,128]{2,1,0:T(8,128)S(1)}) custom-call(bf16[102,128,128]{2,1,0:T(8,128)(2,1)S(1)} %copy-done, bf16[4,2,520,256]{3,2,1,0:T(8,128)(2,1)S(1)} %copy-done.1, f32[6,32,256]{2,1,0:T(8,128)S(1)} %get-tuple-element.49.rows_ref, ...), custom_call_target="tpu_custom_call" | custom-call | flops 1200000000 | bytes 3600000 | tf_op jit(solution)/shard_map/pallas_call | solution.py:236
  22.0 0.0 collective-permute-done.10.refs_3_
  22.0 0.5 %collective-permute-done.9.refs_2_ = f32[32,128]{1,0:T(8,128)S(1)} collective-permute-done((f32[32,128]{1,0:T(8,128)S(1)}, f32[32,128]{1,0:T(8,128)S(1)}, u32[]{:S(2)}, u32[]{:S(2)}) %collective-permute-start.9) | collective-permute-done | bytes 16416 | tf_op jit(solution)/shard_map/ppermute | solution.py:750
  22.5 0.0 copy-done.5
  22.5 0.0 copy-done.7
  22.5 0.8 %shard_map.90.four_ref = f32[3,32,128]{2,1,0:T(8,128)S(1)} custom-call(bf16[102,128,128]{2,1,0:T(8,128)(2,1)S(1)} %copy-done, bf16[4,1,64,136]{3,2,1,0:T(8,128)(2,1)S(1)} %bitcast.4, bf16[64,64]{1,0:T(8,128)(2,1)S(1)} %copy-done.7, f32[32,128]{1,0:T(8,128)S(1)} %shard_map.87.refs_0_, f32[32,128]{1,0:T(8,128)S(1)} %collective-permute-done.8.refs_1_, ...), custom_call_target="tpu_custom_call" | custom-call | flops 1000000000 | bytes 3000000 | tf_op jit(solution)/shard_map/pallas_call | solution.py:236
  23.3 0.0 collective-permute-done.11.first_ref
  23.3 1.2 %collective-permute-done.12.second_ref = f32[1,32,128]{2,1,0:T(8,128)S(1)} collective-permute-done((f32[1,32,128]{2,1,0:T(8,128)S(1)}, f32[1,32,128]{2,1,0:T(8,128)S(1)}, u32[]{:S(2)}, u32[]{:S(2)}) %collective-permute-start.12) | collective-permute-done | bytes 16416 | tf_op jit(solution)/shard_map/ppermute | solution.py:737
  24.5 0.9 %shard_map.91 = f32[512,128]{1,0:T(8,128)} custom-call(bf16[102,128,128]{2,1,0:T(8,128)(2,1)S(1)} %copy-done, f32[16,32,128]{2,1,0:T(8,128)S(1)} %get-tuple-element.55.fine_ref, f32[8,32,128]{2,1,0:T(8,128)S(1)} %get-tuple-element.56.one_ref, f32[4,32,128]{2,1,0:T(8,128)S(1)} %get-tuple-element.57.two_ref, f32[2,32,128]{2,1,0:T(8,128)S(1)} %get-tuple-element.58.three_ref, ...), custom_call_target="tpu_custom_call" | custom-call | flops 1000000000 | bytes 3000000 | tf_op jit(solution)/shard_map/pallas_call | solution.py:236
  (4 shorter events, 0.0 us)
Async XLA Ops:
  0.0 0.9 %copy-start.4 = (f32[32,16,128]{2,1,0:T(8,128)S(1)}, f32[32,16,128]{2,1,0:T(8,128)}, u32[]{:S(2)}) copy-start(f32[32,16,128]{2,1,0:T(8,128)} %param.8) | copy-start | bytes 786436
  1.3 5.0 %collective-permute-start = (f32[3,32,128]{2,1,0:T(8,128)S(1)}, f32[3,32,128]{2,1,0:T(8,128)S(1)}, u32[]{:S(2)}, u32[]{:S(2)}) collective-permute-start(f32[3,32,128]{2,1,0:T(8,128)S(1)} %get-tuple-element.35), channel_id=1, source_target_pairs={{0,2},{1,3},{2,0},{3,1},{4,8},{5,9},{6,10},{7,11},{8,4},{9,5},{10,... | collective-permute-start | bytes 147464 | tf_op jit(solution)/shard_map/ppermute | solution.py:747
  4.3 4.1 %collective-permute-start.1 = (f32[3,32,128]{2,1,0:T(8,128)S(1)}, f32[3,32,128]{2,1,0:T(8,128)S(1)}, u32[]{:S(2)}, u32[]{:S(2)}) collective-permute-start(f32[3,32,128]{2,1,0:T(8,128)S(1)} %get-tuple-element.36), channel_id=1, source_target_pairs={{0,4},{4,0},{8,12},{12,8},{16,20},{20,16},{24,28},{28,24},{1,5},{5... | collective-permute-start | bytes 147464 | tf_op jit(solution)/shard_map/ppermute | solution.py:747
  5.8 4.8 %copy-start.2 = (bf16[8,1,520,256]{3,2,1,0:T(8,128)(2,1)S(1)}, bf16[8,1,520,256]{3,2,1,0:T(8,128)(2,1)}, u32[]{:S(2)}) copy-start(bf16[8,1,520,256]{3,2,1,0:T(8,128)(2,1)} %factor_ref.2) | copy-start | bytes 6389764
  8.4 6.0 %copy-start = (bf16[102,128,128]{2,1,0:T(8,128)(2,1)S(1)}, bf16[102,128,128]{2,1,0:T(8,128)(2,1)}, u32[]{:S(2)}) copy-start(bf16[102,128,128]{2,1,0:T(8,128)(2,1)} %constant.2.clone.block_ref) | copy-start | bytes 10027012
  8.5 4.4 %collective-permute-start.5 = (f32[136,128]{1,0:T(8,128)S(1)}, f32[136,128]{1,0:T(8,128)S(1)}, u32[]{:S(2)}, u32[]{:S(2)}) collective-permute-start(f32[136,128]{1,0:T(8,128)S(1)} %shard_map.85.refs_0_.refs_7_.refs_4_), channel_id=1, source_target_pairs={{0,2},{1,3},{2,0},{3,1},{4,6},{5,7},{6,4},{7,5},{8,10},{9,11},{10,... | collective-permute-start | bytes 208904 | tf_op jit(solution)/shard_map/ppermute | solution.py:750
  9.6 4.3 %collective-permute-start.3 = (f32[4,32,128]{2,1,0:T(8,128)S(1)}, f32[4,32,128]{2,1,0:T(8,128)S(1)}, u32[]{:S(2)}, u32[]{:S(2)}) collective-permute-start(f32[4,32,128]{2,1,0:T(8,128)S(1)} %shard_map.84.refs_3_.refs_0_), channel_id=1, source_target_pairs={{0,2},{1,3},{2,0},{3,1},{4,6},{5,7},{6,4},{7,5},{8,10},{9,11},{10,... | collective-permute-start | bytes 196616 | tf_op jit(solution)/shard_map/ppermute | solution.py:750
  11.2 7.0 %copy-start.1 = (bf16[4,2,520,256]{3,2,1,0:T(8,128)(2,1)S(1)}, bf16[4,2,520,256]{3,2,1,0:T(8,128)(2,1)}, u32[]{:S(2)}) copy-start(bf16[4,2,520,256]{3,2,1,0:T(8,128)(2,1)} %factor_ref.3) | copy-start | bytes 6389764
  11.2 7.0 %copy-start.3 = (bf16[2,1,520,256]{3,2,1,0:T(8,128)(2,1)S(1)}, bf16[2,1,520,256]{3,2,1,0:T(8,128)(2,1)}, u32[]{:S(2)}) copy-start(bf16[2,1,520,256]{3,2,1,0:T(8,128)(2,1)} %refs_1_.1) | copy-start | bytes 1597444
  11.3 7.0 %copy-start.6 = (bf16[1,1,264,128]{3,2,1,0:T(8,128)(2,1)S(1)}, bf16[1,1,264,128]{3,2,1,0:T(8,128)(2,1)}, u32[]{:S(2)}) copy-start(bf16[1,1,264,128]{3,2,1,0:T(8,128)(2,1)} %refs_2_.1) | copy-start | bytes 202756
  12.9 1.3 %collective-permute-start.6 = (f32[136,128]{1,0:T(8,128)S(1)}, f32[136,128]{1,0:T(8,128)S(1)}, u32[]{:S(2)}, u32[]{:S(2)}) collective-permute-start(f32[136,128]{1,0:T(8,128)S(1)} %shard_map.85.refs_0_.refs_7_.refs_4_), channel_id=1, source_target_pairs={{0,1},{1,0},{2,3},{3,2},{4,5},{5,4},{6,7},{7,6},{8,9},{9,8},{10,11... | collective-permute-start | bytes 208904 | tf_op jit(solution)/shard_map/ppermute | solution.py:750
  12.9 1.4 %collective-permute-start.7 = (f32[136,128]{1,0:T(8,128)S(1)}, f32[136,128]{1,0:T(8,128)S(1)}, u32[]{:S(2)}, u32[]{:S(2)}) collective-permute-start(f32[136,128]{1,0:T(8,128)S(1)} %collective-permute-done.5.refs_2_.refs_9_.refs_6_), channel_id=1, source_target_pairs={{0,1},{1,0},{2,3},{3,2},{4,5},{5,4},{6,7},{7,6},{8,9},{9,8},{10,11... | collective-permute-start | bytes 208904 | tf_op jit(solution)/shard_map/ppermute | solution.py:750
  13.4 4.8 %collective-permute-start.2 = (f32[4,32,128]{2,1,0:T(8,128)S(1)}, f32[4,32,128]{2,1,0:T(8,128)S(1)}, u32[]{:S(2)}, u32[]{:S(2)}) collective-permute-start(f32[4,32,128]{2,1,0:T(8,128)S(1)} %shard_map.84.refs_3_.refs_0_), channel_id=1, source_target_pairs={{0,1},{1,0},{2,3},{3,2},{4,5},{5,4},{6,7},{7,6},{8,9},{9,8},{10,11... | collective-permute-start | bytes 196616 | tf_op jit(solution)/shard_map/ppermute | solution.py:750
  13.9 4.4 %collective-permute-start.4 = (f32[4,32,128]{2,1,0:T(8,128)S(1)}, f32[4,32,128]{2,1,0:T(8,128)S(1)}, u32[]{:S(2)}, u32[]{:S(2)}) collective-permute-start(f32[4,32,128]{2,1,0:T(8,128)S(1)} %collective-permute-done.3.refs_5_.refs_2_), channel_id=1, source_target_pairs={{0,1},{1,0},{2,3},{3,2},{4,5},{5,4},{6,7},{7,6},{8,9},{9,8},{10,11... | collective-permute-start | bytes 196616 | tf_op jit(solution)/shard_map/ppermute | solution.py:750
  14.6 6.7 %collective-permute-start.8 = (f32[32,128]{1,0:T(8,128)S(1)}, f32[32,128]{1,0:T(8,128)S(1)}, u32[]{:S(2)}, u32[]{:S(2)}) collective-permute-start(f32[32,128]{1,0:T(8,128)S(1)} %shard_map.87.refs_0_), channel_id=1, source_target_pairs={{0,24},{1,17},{2,26},{3,19},{4,28},{5,21},{6,30},{7,23},{8,16},{9,... | collective-permute-start | bytes 49160 | tf_op jit(solution)/shard_map/ppermute | solution.py:815
  18.2 3.7 %collective-permute-start.10 = (f32[32,128]{1,0:T(8,128)S(1)}, f32[32,128]{1,0:T(8,128)S(1)}, u32[]{:S(2)}, u32[]{:S(2)}) collective-permute-start(f32[32,128]{1,0:T(8,128)S(1)} %shard_map.87.refs_0_), channel_id=1, source_target_pairs={{0,8},{1,9},{2,10},{3,11},{4,12},{5,13},{6,14},{7,15},{8,0},{9,1},... | collective-permute-start | bytes 49160 | tf_op jit(solution)/shard_map/ppermute | solution.py:815
  19.2 4.1 %collective-permute-start.11 = (f32[1,32,128]{2,1,0:T(8,128)S(1)}, f32[1,32,128]{2,1,0:T(8,128)S(1)}, u32[]{:S(2)}, u32[]{:S(2)}) collective-permute-start(f32[1,32,128]{2,1,0:T(8,128)S(1)} %get-tuple-element.59), channel_id=1, source_target_pairs={{0,2},{1,3},{2,6},{3,7},{4,0},{5,1},{6,10},{7,11},{8,4},{9,5},{10,... | collective-permute-start | bytes 49160 | tf_op jit(solution)/shard_map/ppermute | solution.py:737
  20.7 3.7 %collective-permute-start.12 = (f32[1,32,128]{2,1,0:T(8,128)S(1)}, f32[1,32,128]{2,1,0:T(8,128)S(1)}, u32[]{:S(2)}, u32[]{:S(2)}) collective-permute-start(f32[1,32,128]{2,1,0:T(8,128)S(1)} %get-tuple-element.60), channel_id=1, source_target_pairs={{2,0},{3,1},{6,2},{7,3},{0,4},{1,5},{10,6},{11,7},{4,8},{5,9},{14,... | collective-permute-start | bytes 49160 | tf_op jit(solution)/shard_map/ppermute | solution.py:737
  21.3 1.2 %collective-permute-start.9 = (f32[32,128]{1,0:T(8,128)S(1)}, f32[32,128]{1,0:T(8,128)S(1)}, u32[]{:S(2)}, u32[]{:S(2)}) collective-permute-start(f32[32,128]{1,0:T(8,128)S(1)} %collective-permute-done.8.refs_1_), channel_id=1, source_target_pairs={{0,1},{1,0},{2,3},{3,2},{4,5},{5,4},{6,7},{7,6},{8,9},{9,8},{10,11... | collective-permute-start | bytes 49160 | tf_op jit(solution)/shard_map/ppermute | solution.py:750
  21.3 1.2 %copy-start.5 = (bf16[4,1,136,64]{2,3,1,0:T(8,128)(2,1)S(1)}, bf16[4,1,136,64]{2,3,1,0:T(8,128)(2,1)}, u32[]{:S(2)}) copy-start(bf16[4,1,136,64]{2,3,1,0:T(8,128)(2,1)} %param.13) | copy-start | bytes 208900
  21.3 1.2 %copy-start.7 = (bf16[64,64]{1,0:T(8,128)(2,1)S(1)}, bf16[64,64]{1,0:T(8,128)(2,1)}, u32[]{:S(2)}) copy-start(bf16[64,64]{1,0:T(8,128)(2,1)} %inverse_ref.1) | copy-start | bytes 24580

commit v11 on v10

--- a/solution.py
+++ b/solution.py
@@ -275,7 +275,7 @@
 
 
 def write_halos(c, down, up, first_ref, second_ref, pairs=False):
-    forward = jnp.bitwise_and(c, 2) != 0
+    forward = jnp.bitwise_and(c, 1) != 0
     if pairs:
         forward = lax.rem(lax.axis_index("px"), 2) == 1
     for k, (low, high) in enumerate(zip(down, up)):
@@ -285,7 +285,7 @@
 
 def read_halos(plan, first_ref, second_ref, pairs=False):
     r, c = lax.axis_index("px"), lax.axis_index("py")
-    forward = jnp.bitwise_and(c, 2) != 0
+    forward = jnp.bitwise_and(c, 1) != 0
     if pairs:
         forward = lax.rem(r, 2) == 0
     above = jnp.where(r > 0, 1.0, 0.0).astype(F32)
@@ -725,8 +725,8 @@
 
     def trade(first, second):
         def target(i, c):
-            after = i + 1 if c & 2 else i - 1
-            return (after, c) if 0 <= after < n else (i, c ^ 2)
+            after = i + 1 if c & 1 else i - 1
+            return (after, c) if 0 <= after < n else (i, c ^ 1)
 
         ring = []
         for i in range(n):
@@ -741,7 +741,7 @@
         for i in range(n):
             for c in range(m):
                 j = ((i + 1) ^ 1) - 1
-                at = j * m + c if 0 <= j < n else i * m + (c ^ 2)
+                at = j * m + c if 0 <= j < n else i * m + (c ^ 1)
                 far.append((i * m + c, at))
         near = [(i, i ^ 1) for i in range(n)]
         return lax.ppermute(first, ("px", "py"), far), lax.ppermute(second, "px", near)

time: 25.5 us -> 24.6 us (0.965)
  waiting for transfers between devices: 6.6 us -> 5.05 us
  starting transfers between devices: 12.9 us -> 13.3 us
    ppermute x1, starting transfers between devices: 2.94 us -> 0.46 us  [trade_pairs(): lax.ppermute(first, ('px', 'py'), far)]
    ppermute x1, starting transfers between devices: 1.55 us -> 4.03 us  [trade_pairs(): lax.ppermute(second, 'px', near)]
    ppermute x1, waiting for transfers between devices: 1.16 us -> 0.01 us  [trade(): lax.ppermute(second, ('px', 'py'), back)]
    ppermute x1, starting transfers between devices: 0.6 us -> 1.54 us  [trade(): lax.ppermute(second, ('px', 'py'), back)]
    ppermute x1, starting transfers between devices: 1.48 us -> 0.54 us  [trade(): lax.ppermute(first, ('px', 'py'), ring)]
    ppermute x2, starting transfers between devices: 3.67 us -> 4.09 us  [per_device(): fetched.append((lax.ppermute(pairs, ('px', 'py'), routes), even, odd))]
    ppermute x1, waiting for transfers between devices: 0.36 us -> 0.01 us  [trade_pairs(): lax.ppermute(first, ('px', 'py'), far)]
  transfers between devices with their start and end apart: 13 -> 13, of which waited for: 8 -> 4; matrix products, arithmetic and copies ran while one was open for 0% -> 0% of each run, Pallas kernels for 13% -> 14%
where the time goes in v11:
time: 24.6 us; the launch traced here: 24.3 us
  starting transfers between devices  13.3 us (54%)
  Pallas kernels  5.18 us (21%)
  waiting for transfers between devices  5.05 us (21%)
  local copies, waits for them, and re-layouts  0.58 us (2%)
    pallas_call x10, Pallas kernels, call(): pl.pallas_call(body, out_shape=out_shape, in_specs=[whole] * len(operands...  5.18 us
    ppermute x2, starting transfers between devices, per_device(): fetched.append((lax.ppermute(pairs, ('px', 'py'), routes), even, odd))  4.09 us
    ppermute x1, starting transfers between devices, trade_pairs(): lax.ppermute(second, 'px', near)  4.03 us
    ppermute x7, waiting for transfers between devices, swap(): return lax.ppermute(value, 'py', [(i, i ^ bits) for i in range(m)])  3.11 us
    ppermute x7, starting transfers between devices, swap(): return lax.ppermute(value, 'py', [(i, i ^ bits) for i in range(m)])  2.61 us
    ppermute x1, waiting for transfers between devices, trade_pairs(): lax.ppermute(second, 'px', near)  1.9 us
    ppermute x1, starting transfers between devices, trade(): lax.ppermute(second, ('px', 'py'), back)  1.54 us
    unnamed x16, local copies, waits for them, and re-layouts  0.58 us
  transfers between devices with their start and end apart: 13, of which 4 were waited for; matrix products, arithmetic and copies ran while one was open for 0% of the time, Pallas kernels for 14%

profile of v11, /device:TPU:0, one launch (start us, length us, event | category | flops | bytes accessed | tf_op | source)
XLA Modules:
  0.0 24.3 jit_solution(14890073823587729557)
XLA Ops:
  0.0 0.4 %shard_map.82.shrink_ref = bf16[4,128,128]{2,1,0:T(8,128)(2,1)S(1)} custom-call(), custom_call_target="tpu_custom_call" | custom-call | flops 4000000000 | bytes 12000000 | tf_op jit(solution)/shard_map/pallas_call | solution.py:236
  0.4 0.5 %copy-done.4 = f32[32,16,128]{2,1,0:T(8,128)S(1)} copy-done((f32[32,16,128]{2,1,0:T(8,128)S(1)}, f32[32,16,128]{2,1,0:T(8,128)}, u32[]{:S(2)}) %copy-start.4) | copy-done | bytes 262168
  1.0 0.4 %shard_map.83 = (f32[6,32,128]{2,1,0:T(8,128)S(1)}, f32[4,32,128]{2,1,0:T(8,128)S(1)}, f32[3,32,128]{2,1,0:T(8,128)S(1)}, f32[3,32,128]{2,1,0:T(8,128)S(1)}, f32[16,32,128]{2,1,0:T(8,128)S(1)}) custom-call(f32[512,128]{1,0:T(8,128)S(1)} %bitcast.3, bf16[4,128,128]{2,1,0:T(8,128)(2,1)S(1)} %shard_map.82.shrink_ref), custom_call_target="tpu_custom_call" | custom-call | flops 1000000000 | bytes 3000000 | tf_op jit(solution)/shard_map/pallas_call | solution.py:236
  1.3 0.5 %collective-permute-start = (f32[3,32,128]{2,1,0:T(8,128)S(1)}, f32[3,32,128]{2,1,0:T(8,128)S(1)}, u32[]{:S(2)}, u32[]{:S(2)}) collective-permute-start(f32[3,32,128]{2,1,0:T(8,128)S(1)} %get-tuple-element.35), channel_id=1, source_target_pairs={{0,1},{1,0},{2,3},{3,2},{4,8},{5,9},{6,10},{7,11},{8,4},{9,5},{10,... | collective-permute-start | bytes 147464 | tf_op jit(solution)/shard_map/ppermute | solution.py:747
  1.8 4.0 %collective-permute-start.1 = (f32[3,32,128]{2,1,0:T(8,128)S(1)}, f32[3,32,128]{2,1,0:T(8,128)S(1)}, u32[]{:S(2)}, u32[]{:S(2)}) collective-permute-start(f32[3,32,128]{2,1,0:T(8,128)S(1)} %get-tuple-element.36), channel_id=1, source_target_pairs={{0,4},{4,0},{8,12},{12,8},{16,20},{20,16},{24,28},{28,24},{1,5},{5... | collective-permute-start | bytes 147464 | tf_op jit(solution)/shard_map/ppermute | solution.py:747
  5.8 0.1 shard_map.84.refs_3_.refs_0_
  6.0 0.0 collective-permute-done.first_ref
  6.0 1.9 %collective-permute-done.1.second_ref = f32[3,32,128]{2,1,0:T(8,128)S(1)} collective-permute-done((f32[3,32,128]{2,1,0:T(8,128)S(1)}, f32[3,32,128]{2,1,0:T(8,128)S(1)}, u32[]{:S(2)}, u32[]{:S(2)}) %collective-permute-start.1) | collective-permute-done | bytes 49184 | tf_op jit(solution)/shard_map/ppermute | solution.py:747
  7.9 0.2 shard_map.85.refs_0_.refs_7_.refs_4_
  8.1 1.6 %collective-permute-start.5 = (f32[136,128]{1,0:T(8,128)S(1)}, f32[136,128]{1,0:T(8,128)S(1)}, u32[]{:S(2)}, u32[]{:S(2)}) collective-permute-start(f32[136,128]{1,0:T(8,128)S(1)} %shard_map.85.refs_0_.refs_7_.refs_4_), channel_id=1, source_target_pairs={{0,2},{1,3},{2,0},{3,1},{4,6},{5,7},{6,4},{7,5},{8,10},{9,11},{10,... | collective-permute-start | bytes 208904 | tf_op jit(solution)/shard_map/ppermute | solution.py:750
  9.6 0.5 %collective-permute-start.3 = (f32[4,32,128]{2,1,0:T(8,128)S(1)}, f32[4,32,128]{2,1,0:T(8,128)S(1)}, u32[]{:S(2)}, u32[]{:S(2)}) collective-permute-start(f32[4,32,128]{2,1,0:T(8,128)S(1)} %shard_map.84.refs_3_.refs_0_), channel_id=1, source_target_pairs={{0,2},{1,3},{2,0},{3,1},{4,6},{5,7},{6,4},{7,5},{8,10},{9,11},{10,... | collective-permute-start | bytes 196616 | tf_op jit(solution)/shard_map/ppermute | solution.py:750
  10.2 0.0 copy-done.2
  10.2 0.6 %shard_map.86 = (f32[16,32,128]{2,1,0:T(8,128)S(1)}, bf16[8,16,256]{2,1,0:T(8,128)(2,1)S(1)}) custom-call(f32[16,32,128]{2,1,0:T(8,128)S(1)} %get-tuple-element.34.rows_ref, f32[3,32,128]{2,1,0:T(8,128)S(1)} %collective-permute-done.first_ref, f32[3,32,128]{2,1,0:T(8,128)S(1)} %collective-permute-done.1.second_ref, bf16[8,1,520,256]{3,2,1,0:T(8,128)(2,1)S(1)} %copy-done.2), custom_call_target="tpu_custom_call" | custom-call | flops 700000000 | bytes 2100000 | tf_op jit(solution)/shard_map/pallas_call | solution.py:236
  10.8 0.0 copy-start.1
  10.8 0.0 copy-start.3
  10.8 0.0 copy-start.6
  10.8 1.6 %collective-permute-done.5.refs_2_.refs_9_.refs_6_ = f32[136,128]{1,0:T(8,128)S(1)} collective-permute-done((f32[136,128]{1,0:T(8,128)S(1)}, f32[136,128]{1,0:T(8,128)S(1)}, u32[]{:S(2)}, u32[]{:S(2)}) %collective-permute-start.5) | collective-permute-done | bytes 69664 | tf_op jit(solution)/shard_map/ppermute | solution.py:750
  12.4 0.0 collective-permute-start.6
  12.4 0.5 %collective-permute-start.7 = (f32[136,128]{1,0:T(8,128)S(1)}, f32[136,128]{1,0:T(8,128)S(1)}, u32[]{:S(2)}, u32[]{:S(2)}) collective-permute-start(f32[136,128]{1,0:T(8,128)S(1)} %collective-permute-done.5.refs_2_.refs_9_.refs_6_), channel_id=1, source_target_pairs={{0,1},{1,0},{2,3},{3,2},{4,5},{5,4},{6,7},{7,6},{8,9},{9,8},{10,11... | collective-permute-start | bytes 208904 | tf_op jit(solution)/shard_map/ppermute | solution.py:750
  13.0 0.0 collective-permute-start.2
  13.0 0.9 %collective-permute-done.3.refs_5_.refs_2_ = f32[4,32,128]{2,1,0:T(8,128)S(1)} collective-permute-done((f32[4,32,128]{2,1,0:T(8,128)S(1)}, f32[4,32,128]{2,1,0:T(8,128)S(1)}, u32[]{:S(2)}, u32[]{:S(2)}) %collective-permute-start.3) | collective-permute-done | bytes 65568 | tf_op jit(solution)/shard_map/ppermute | solution.py:750
  13.9 0.0 collective-permute-start.4
  13.9 0.0 collective-permute-done.6.refs_1_.refs_8_.refs_5_
  13.9 0.0 collective-permute-done.7.refs_3_.refs_10_.refs_7_
  13.9 0.0 copy-done
  13.9 0.2 shard_map.87.refs_0_
  14.1 4.1 %collective-permute-start.8 = (f32[32,128]{1,0:T(8,128)S(1)}, f32[32,128]{1,0:T(8,128)S(1)}, u32[]{:S(2)}, u32[]{:S(2)}) collective-permute-start(f32[32,128]{1,0:T(8,128)S(1)} %shard_map.87.refs_0_), channel_id=1, source_target_pairs={{0,24},{1,17},{2,26},{3,19},{4,28},{5,21},{6,30},{7,23},{8,16},{9,... | collective-permute-start | bytes 49160 | tf_op jit(solution)/shard_map/ppermute | solution.py:815
  18.2 0.0 collective-permute-start.10
  18.2 0.0 collective-permute-done.2.refs_4_.refs_1_
  18.2 0.0 collective-permute-done.4.refs_6_.refs_3_
  18.2 0.0 copy-done.1
  18.3 0.0 copy-done.3
  18.3 0.0 copy-done.6
  18.3 0.9 %shard_map.88 = (f32[2,2,32,256]{3,2,1,0:T(8,128)S(1)}, f32[1,2,32,256]{3,2,1,0:T(8,128)S(1)}, f32[1,1,32,128]{3,2,1,0:T(8,128)S(1)}, f32[6,32,256]{2,1,0:T(8,12...) custom-call(bf16[102,128,128]{2,1,0:T(8,128)(2,1)S(1)} %copy-done, bf16[4,2,520,256]{3,2,1,0:T(8,128)(2,1)S(1)} %copy-done.1, ...), custom_call_target="tpu_custom_call" | custom-call | flops 2500000000 | bytes 7500000 | tf_op jit(solution)/shard_map/pallas_call | solution.py:236
  19.2 0.5 %collective-permute-start.11 = (f32[1,32,128]{2,1,0:T(8,128)S(1)}, f32[1,32,128]{2,1,0:T(8,128)S(1)}, u32[]{:S(2)}, u32[]{:S(2)}) collective-permute-start(f32[1,32,128]{2,1,0:T(8,128)S(1)} %get-tuple-element.59), channel_id=1, source_target_pairs={{0,1},{1,5},{2,3},{3,7},{4,0},{5,9},{6,2},{7,11},{8,4},{9,13},{10,... | collective-permute-start | bytes 49160 | tf_op jit(solution)/shard_map/ppermute | solution.py:737
  19.8 1.5 %collective-permute-start.12 = (f32[1,32,128]{2,1,0:T(8,128)S(1)}, f32[1,32,128]{2,1,0:T(8,128)S(1)}, u32[]{:S(2)}, u32[]{:S(2)}) collective-permute-start(f32[1,32,128]{2,1,0:T(8,128)S(1)} %get-tuple-element.60), channel_id=1, source_target_pairs={{1,0},{5,1},{3,2},{7,3},{0,4},{9,5},{2,6},{11,7},{4,8},{13,9},{6,1... | collective-permute-start | bytes 49160 | tf_op jit(solution)/shard_map/ppermute | solution.py:737
  21.3 0.0 collective-permute-done.8.refs_1_
  21.3 0.0 collective-permute-start.9
  21.3 0.0 copy-start.7
  21.3 0.6 %shard_map.89 = (f32[8,32,128]{2,1,0:T(8,128)S(1)}, f32[4,32,128]{2,1,0:T(8,128)S(1)}, f32[2,32,128]{2,1,0:T(8,128)S(1)}, f32[16,32,128]{2,1,0:T(8,128)S(1)}) custom-call(bf16[102,128,128]{2,1,0:T(8,128)(2,1)S(1)} %copy-done, bf16[4,2,520,256]{3,2,1,0:T(8,128)(2,1)S(1)} %copy-done.1, f32[6,32,256]{2,1,0:T(8,128)S(1)} %get-tuple-element.49.rows_ref, ...), custom_call_target="tpu_custom_call" | custom-call | flops 1200000000 | bytes 3600000 | tf_op jit(solution)/shard_map/pallas_call | solution.py:236
  22.0 0.0 collective-permute-done.10.refs_3_
  22.0 0.5 %collective-permute-done.9.refs_2_ = f32[32,128]{1,0:T(8,128)S(1)} collective-permute-done((f32[32,128]{1,0:T(8,128)S(1)}, f32[32,128]{1,0:T(8,128)S(1)}, u32[]{:S(2)}, u32[]{:S(2)}) %collective-permute-start.9) | collective-permute-done | bytes 16416 | tf_op jit(solution)/shard_map/ppermute | solution.py:750
  22.5 0.0 copy-done.5
  22.5 0.0 copy-done.7
  22.5 0.8 %shard_map.90.four_ref = f32[3,32,128]{2,1,0:T(8,128)S(1)} custom-call(bf16[102,128,128]{2,1,0:T(8,128)(2,1)S(1)} %copy-done, bf16[4,1,64,136]{3,2,1,0:T(8,128)(2,1)S(1)} %bitcast.4, bf16[64,64]{1,0:T(8,128)(2,1)S(1)} %copy-done.7, f32[32,128]{1,0:T(8,128)S(1)} %shard_map.87.refs_0_, f32[32,128]{1,0:T(8,128)S(1)} %collective-permute-done.8.refs_1_, ...), custom_call_target="tpu_custom_call" | custom-call | flops 1000000000 | bytes 3000000 | tf_op jit(solution)/shard_map/pallas_call | solution.py:236
  23.3 0.0 collective-permute-done.11.first_ref
  23.3 0.0 collective-permute-done.12.second_ref
  23.3 0.9 %shard_map.91 = f32[512,128]{1,0:T(8,128)} custom-call(bf16[102,128,128]{2,1,0:T(8,128)(2,1)S(1)} %copy-done, f32[16,32,128]{2,1,0:T(8,128)S(1)} %get-tuple-element.55.fine_ref, f32[8,32,128]{2,1,0:T(8,128)S(1)} %get-tuple-element.56.one_ref, f32[4,32,128]{2,1,0:T(8,128)S(1)} %get-tuple-element.57.two_ref, f32[2,32,128]{2,1,0:T(8,128)S(1)} %get-tuple-element.58.three_ref, ...), custom_call_target="tpu_custom_call" | custom-call | flops 1000000000 | bytes 3000000 | tf_op jit(solution)/shard_map/pallas_call | solution.py:236
  (4 shorter events, 0.0 us)
Async XLA Ops:
  0.0 0.9 %copy-start.4 = (f32[32,16,128]{2,1,0:T(8,128)S(1)}, f32[32,16,128]{2,1,0:T(8,128)}, u32[]{:S(2)}) copy-start(f32[32,16,128]{2,1,0:T(8,128)} %param.8) | copy-start | bytes 786436
  1.3 4.7 %collective-permute-start = (f32[3,32,128]{2,1,0:T(8,128)S(1)}, f32[3,32,128]{2,1,0:T(8,128)S(1)}, u32[]{:S(2)}, u32[]{:S(2)}) collective-permute-start(f32[3,32,128]{2,1,0:T(8,128)S(1)} %get-tuple-element.35), channel_id=1, source_target_pairs={{0,1},{1,0},{2,3},{3,2},{4,8},{5,9},{6,10},{7,11},{8,4},{9,5},{10,... | collective-permute-start | bytes 147464 | tf_op jit(solution)/shard_map/ppermute | solution.py:747
  1.8 6.1 %collective-permute-start.1 = (f32[3,32,128]{2,1,0:T(8,128)S(1)}, f32[3,32,128]{2,1,0:T(8,128)S(1)}, u32[]{:S(2)}, u32[]{:S(2)}) collective-permute-start(f32[3,32,128]{2,1,0:T(8,128)S(1)} %get-tuple-element.36), channel_id=1, source_target_pairs={{0,4},{4,0},{8,12},{12,8},{16,20},{20,16},{24,28},{28,24},{1,5},{5... | collective-permute-start | bytes 147464 | tf_op jit(solution)/shard_map/ppermute | solution.py:747
  5.8 4.3 %copy-start.2 = (bf16[8,1,520,256]{3,2,1,0:T(8,128)(2,1)S(1)}, bf16[8,1,520,256]{3,2,1,0:T(8,128)(2,1)}, u32[]{:S(2)}) copy-start(bf16[8,1,520,256]{3,2,1,0:T(8,128)(2,1)} %factor_ref.2) | copy-start | bytes 6389764
  7.9 6.0 %copy-start = (bf16[102,128,128]{2,1,0:T(8,128)(2,1)S(1)}, bf16[102,128,128]{2,1,0:T(8,128)(2,1)}, u32[]{:S(2)}) copy-start(bf16[102,128,128]{2,1,0:T(8,128)(2,1)} %constant.2.clone.block_ref) | copy-start | bytes 10027012
  8.1 4.4 %collective-permute-start.5 = (f32[136,128]{1,0:T(8,128)S(1)}, f32[136,128]{1,0:T(8,128)S(1)}, u32[]{:S(2)}, u32[]{:S(2)}) collective-permute-start(f32[136,128]{1,0:T(8,128)S(1)} %shard_map.85.refs_0_.refs_7_.refs_4_), channel_id=1, source_target_pairs={{0,2},{1,3},{2,0},{3,1},{4,6},{5,7},{6,4},{7,5},{8,10},{9,11},{10,... | collective-permute-start | bytes 208904 | tf_op jit(solution)/shard_map/ppermute | solution.py:750
  9.6 4.3 %collective-permute-start.3 = (f32[4,32,128]{2,1,0:T(8,128)S(1)}, f32[4,32,128]{2,1,0:T(8,128)S(1)}, u32[]{:S(2)}, u32[]{:S(2)}) collective-permute-start(f32[4,32,128]{2,1,0:T(8,128)S(1)} %shard_map.84.refs_3_.refs_0_), channel_id=1, source_target_pairs={{0,2},{1,3},{2,0},{3,1},{4,6},{5,7},{6,4},{7,5},{8,10},{9,11},{10,... | collective-permute-start | bytes 196616 | tf_op jit(solution)/shard_map/ppermute | solution.py:750
  10.8 7.5 %copy-start.1 = (bf16[4,2,520,256]{3,2,1,0:T(8,128)(2,1)S(1)}, bf16[4,2,520,256]{3,2,1,0:T(8,128)(2,1)}, u32[]{:S(2)}) copy-start(bf16[4,2,520,256]{3,2,1,0:T(8,128)(2,1)} %factor_ref.3) | copy-start | bytes 6389764
  10.8 7.5 %copy-start.3 = (bf16[2,1,520,256]{3,2,1,0:T(8,128)(2,1)S(1)}, bf16[2,1,520,256]{3,2,1,0:T(8,128)(2,1)}, u32[]{:S(2)}) copy-start(bf16[2,1,520,256]{3,2,1,0:T(8,128)(2,1)} %refs_1_.1) | copy-start | bytes 1597444
  10.8 7.5 %copy-start.6 = (bf16[1,1,264,128]{3,2,1,0:T(8,128)(2,1)S(1)}, bf16[1,1,264,128]{3,2,1,0:T(8,128)(2,1)}, u32[]{:S(2)}) copy-start(bf16[1,1,264,128]{3,2,1,0:T(8,128)(2,1)} %refs_2_.1) | copy-start | bytes 202756
  12.4 1.5 %collective-permute-start.6 = (f32[136,128]{1,0:T(8,128)S(1)}, f32[136,128]{1,0:T(8,128)S(1)}, u32[]{:S(2)}, u32[]{:S(2)}) collective-permute-start(f32[136,128]{1,0:T(8,128)S(1)} %shard_map.85.refs_0_.refs_7_.refs_4_), channel_id=1, source_target_pairs={{0,1},{1,0},{2,3},{3,2},{4,5},{5,4},{6,7},{7,6},{8,9},{9,8},{10,11... | collective-permute-start | bytes 208904 | tf_op jit(solution)/shard_map/ppermute | solution.py:750
  12.4 1.5 %collective-permute-start.7 = (f32[136,128]{1,0:T(8,128)S(1)}, f32[136,128]{1,0:T(8,128)S(1)}, u32[]{:S(2)}, u32[]{:S(2)}) collective-permute-start(f32[136,128]{1,0:T(8,128)S(1)} %collective-permute-done.5.refs_2_.refs_9_.refs_6_), channel_id=1, source_target_pairs={{0,1},{1,0},{2,3},{3,2},{4,5},{5,4},{6,7},{7,6},{8,9},{9,8},{10,11... | collective-permute-start | bytes 208904 | tf_op jit(solution)/shard_map/ppermute | solution.py:750
  13.0 5.3 %collective-permute-start.2 = (f32[4,32,128]{2,1,0:T(8,128)S(1)}, f32[4,32,128]{2,1,0:T(8,128)S(1)}, u32[]{:S(2)}, u32[]{:S(2)}) collective-permute-start(f32[4,32,128]{2,1,0:T(8,128)S(1)} %shard_map.84.refs_3_.refs_0_), channel_id=1, source_target_pairs={{0,1},{1,0},{2,3},{3,2},{4,5},{5,4},{6,7},{7,6},{8,9},{9,8},{10,11... | collective-permute-start | bytes 196616 | tf_op jit(solution)/shard_map/ppermute | solution.py:750
  13.9 4.4 %collective-permute-start.4 = (f32[4,32,128]{2,1,0:T(8,128)S(1)}, f32[4,32,128]{2,1,0:T(8,128)S(1)}, u32[]{:S(2)}, u32[]{:S(2)}) collective-permute-start(f32[4,32,128]{2,1,0:T(8,128)S(1)} %collective-permute-done.3.refs_5_.refs_2_), channel_id=1, source_target_pairs={{0,1},{1,0},{2,3},{3,2},{4,5},{5,4},{6,7},{7,6},{8,9},{9,8},{10,11... | collective-permute-start | bytes 196616 | tf_op jit(solution)/shard_map/ppermute | solution.py:750
  14.1 7.2 %collective-permute-start.8 = (f32[32,128]{1,0:T(8,128)S(1)}, f32[32,128]{1,0:T(8,128)S(1)}, u32[]{:S(2)}, u32[]{:S(2)}) collective-permute-start(f32[32,128]{1,0:T(8,128)S(1)} %shard_map.87.refs_0_), channel_id=1, source_target_pairs={{0,24},{1,17},{2,26},{3,19},{4,28},{5,21},{6,30},{7,23},{8,16},{9,... | collective-permute-start | bytes 49160 | tf_op jit(solution)/shard_map/ppermute | solution.py:815
  18.2 3.7 %collective-permute-start.10 = (f32[32,128]{1,0:T(8,128)S(1)}, f32[32,128]{1,0:T(8,128)S(1)}, u32[]{:S(2)}, u32[]{:S(2)}) collective-permute-start(f32[32,128]{1,0:T(8,128)S(1)} %shard_map.87.refs_0_), channel_id=1, source_target_pairs={{0,8},{1,9},{2,10},{3,11},{4,12},{5,13},{6,14},{7,15},{8,0},{9,1},... | collective-permute-start | bytes 49160 | tf_op jit(solution)/shard_map/ppermute | solution.py:815
  19.2 4.1 %collective-permute-start.11 = (f32[1,32,128]{2,1,0:T(8,128)S(1)}, f32[1,32,128]{2,1,0:T(8,128)S(1)}, u32[]{:S(2)}, u32[]{:S(2)}) collective-permute-start(f32[1,32,128]{2,1,0:T(8,128)S(1)} %get-tuple-element.59), channel_id=1, source_target_pairs={{0,1},{1,5},{2,3},{3,7},{4,0},{5,9},{6,2},{7,11},{8,4},{9,13},{10,... | collective-permute-start | bytes 49160 | tf_op jit(solution)/shard_map/ppermute | solution.py:737
  19.8 3.5 %collective-permute-start.12 = (f32[1,32,128]{2,1,0:T(8,128)S(1)}, f32[1,32,128]{2,1,0:T(8,128)S(1)}, u32[]{:S(2)}, u32[]{:S(2)}) collective-permute-start(f32[1,32,128]{2,1,0:T(8,128)S(1)} %get-tuple-element.60), channel_id=1, source_target_pairs={{1,0},{5,1},{3,2},{7,3},{0,4},{9,5},{2,6},{11,7},{4,8},{13,9},{6,1... | collective-permute-start | bytes 49160 | tf_op jit(solution)/shard_map/ppermute | solution.py:737
  21.3 1.2 %collective-permute-start.9 = (f32[32,128]{1,0:T(8,128)S(1)}, f32[32,128]{1,0:T(8,128)S(1)}, u32[]{:S(2)}, u32[]{:S(2)}) collective-permute-start(f32[32,128]{1,0:T(8,128)S(1)} %collective-permute-done.8.refs_1_), channel_id=1, source_target_pairs={{0,1},{1,0},{2,3},{3,2},{4,5},{5,4},{6,7},{7,6},{8,9},{9,8},{10,11... | collective-permute-start | bytes 49160 | tf_op jit(solution)/shard_map/ppermute | solution.py:750
  21.3 1.2 %copy-start.5 = (bf16[4,1,136,64]{2,3,1,0:T(8,128)(2,1)S(1)}, bf16[4,1,136,64]{2,3,1,0:T(8,128)(2,1)}, u32[]{:S(2)}) copy-start(bf16[4,1,136,64]{2,3,1,0:T(8,128)(2,1)} %param.13) | copy-start | bytes 208900
  21.3 1.2 %copy-start.7 = (bf16[64,64]{1,0:T(8,128)(2,1)S(1)}, bf16[64,64]{1,0:T(8,128)(2,1)}, u32[]{:S(2)}) copy-start(bf16[64,64]{1,0:T(8,128)(2,1)} %inverse_ref.1) | copy-start | bytes 24580

commit v12 on v11

--- a/solution.py
+++ b/solution.py
@@ -167,6 +167,11 @@
 def product(value, matrix):
     high, low = split(value)
     count = value.shape[0]
+    if matrix.shape[0] == LANES:
+        return jnp.dot(
+            jnp.concatenate([high, low], axis=1), jnp.concatenate([matrix, matrix], axis=0),
+            preferred_element_type=F32,
+        )
     both = jnp.dot(
         jnp.concatenate([high, low], axis=0), matrix, preferred_element_type=F32
     )

time: 24.6 us -> 24.6 us (level)
  no operation moved by 1% of the time
where the time goes in v12:
time: 24.6 us; the launch traced here: 24.3 us
  starting transfers between devices  13.3 us (54%)
  Pallas kernels  5.18 us (21%)
  waiting for transfers between devices  5.04 us (20%)
  local copies, waits for them, and re-layouts  0.58 us (2%)
    pallas_call x10, Pallas kernels, call(): pl.pallas_call(body, out_shape=out_shape, in_specs=[whole] * len(operands...  5.18 us
    ppermute x2, starting transfers between devices, per_device(): fetched.append((lax.ppermute(pairs, ('px', 'py'), routes), even, odd))  4.08 us
    ppermute x1, starting transfers between devices, trade_pairs(): lax.ppermute(second, 'px', near)  4.03 us
    ppermute x7, waiting for transfers between devices, swap(): return lax.ppermute(value, 'py', [(i, i ^ bits) for i in range(m)])  3.11 us
    ppermute x7, starting transfers between devices, swap(): return lax.ppermute(value, 'py', [(i, i ^ bits) for i in range(m)])  2.61 us
    ppermute x1, waiting for transfers between devices, trade_pairs(): lax.ppermute(second, 'px', near)  1.9 us
    ppermute x1, starting transfers between devices, trade(): lax.ppermute(second, ('px', 'py'), back)  1.53 us
    unnamed x16, local copies, waits for them, and re-layouts  0.58 us
  transfers between devices with their start and end apart: 13, of which 4 were waited for; matrix products, arithmetic and copies ran while one was open for 0% of the time, Pallas kernels for 14%

profile of v12, /device:TPU:0, one launch (start us, length us, event | category | flops | bytes accessed | tf_op | source)
XLA Modules:
  0.0 24.3 jit_solution(13831496262582728250)
XLA Ops:
  0.0 0.4 %shard_map.82.shrink_ref = bf16[4,128,128]{2,1,0:T(8,128)(2,1)S(1)} custom-call(), custom_call_target="tpu_custom_call" | custom-call | flops 4000000000 | bytes 12000000 | tf_op jit(solution)/shard_map/pallas_call | solution.py:241
  0.4 0.5 %copy-done.4 = f32[32,16,128]{2,1,0:T(8,128)S(1)} copy-done((f32[32,16,128]{2,1,0:T(8,128)S(1)}, f32[32,16,128]{2,1,0:T(8,128)}, u32[]{:S(2)}) %copy-start.4) | copy-done | bytes 262168
  1.0 0.4 %shard_map.83 = (f32[6,32,128]{2,1,0:T(8,128)S(1)}, f32[4,32,128]{2,1,0:T(8,128)S(1)}, f32[3,32,128]{2,1,0:T(8,128)S(1)}, f32[3,32,128]{2,1,0:T(8,128)S(1)}, f32[16,32,128]{2,1,0:T(8,128)S(1)}) custom-call(f32[512,128]{1,0:T(8,128)S(1)} %bitcast.3, bf16[4,128,128]{2,1,0:T(8,128)(2,1)S(1)} %shard_map.82.shrink_ref), custom_call_target="tpu_custom_call" | custom-call | flops 1000000000 | bytes 3000000 | tf_op jit(solution)/shard_map/pallas_call | solution.py:241
  1.3 0.5 %collective-permute-start = (f32[3,32,128]{2,1,0:T(8,128)S(1)}, f32[3,32,128]{2,1,0:T(8,128)S(1)}, u32[]{:S(2)}, u32[]{:S(2)}) collective-permute-start(f32[3,32,128]{2,1,0:T(8,128)S(1)} %get-tuple-element.35), channel_id=1, source_target_pairs={{0,1},{1,0},{2,3},{3,2},{4,8},{5,9},{6,10},{7,11},{8,4},{9,5},{10,... | collective-permute-start | bytes 147464 | tf_op jit(solution)/shard_map/ppermute | solution.py:752
  1.8 4.0 %collective-permute-start.1 = (f32[3,32,128]{2,1,0:T(8,128)S(1)}, f32[3,32,128]{2,1,0:T(8,128)S(1)}, u32[]{:S(2)}, u32[]{:S(2)}) collective-permute-start(f32[3,32,128]{2,1,0:T(8,128)S(1)} %get-tuple-element.36), channel_id=1, source_target_pairs={{0,4},{4,0},{8,12},{12,8},{16,20},{20,16},{24,28},{28,24},{1,5},{5... | collective-permute-start | bytes 147464 | tf_op jit(solution)/shard_map/ppermute | solution.py:752
  5.9 0.1 shard_map.84.refs_3_.refs_0_
  6.0 0.0 collective-permute-done.first_ref
  6.0 1.9 %collective-permute-done.1.second_ref = f32[3,32,128]{2,1,0:T(8,128)S(1)} collective-permute-done((f32[3,32,128]{2,1,0:T(8,128)S(1)}, f32[3,32,128]{2,1,0:T(8,128)S(1)}, u32[]{:S(2)}, u32[]{:S(2)}) %collective-permute-start.1) | collective-permute-done | bytes 49184 | tf_op jit(solution)/shard_map/ppermute | solution.py:752
  7.9 0.2 shard_map.85.refs_0_.refs_7_.refs_4_
  8.1 1.6 %collective-permute-start.5 = (f32[136,128]{1,0:T(8,128)S(1)}, f32[136,128]{1,0:T(8,128)S(1)}, u32[]{:S(2)}, u32[]{:S(2)}) collective-permute-start(f32[136,128]{1,0:T(8,128)S(1)} %shard_map.85.refs_0_.refs_7_.refs_4_), channel_id=1, source_target_pairs={{0,2},{1,3},{2,0},{3,1},{4,6},{5,7},{6,4},{7,5},{8,10},{9,11},{10,... | collective-permute-start | bytes 208904 | tf_op jit(solution)/shard_map/ppermute | solution.py:755
  9.6 0.5 %collective-permute-start.3 = (f32[4,32,128]{2,1,0:T(8,128)S(1)}, f32[4,32,128]{2,1,0:T(8,128)S(1)}, u32[]{:S(2)}, u32[]{:S(2)}) collective-permute-start(f32[4,32,128]{2,1,0:T(8,128)S(1)} %shard_map.84.refs_3_.refs_0_), channel_id=1, source_target_pairs={{0,2},{1,3},{2,0},{3,1},{4,6},{5,7},{6,4},{7,5},{8,10},{9,11},{10,... | collective-permute-start | bytes 196616 | tf_op jit(solution)/shard_map/ppermute | solution.py:755
  10.2 0.0 copy-done.2
  10.2 0.6 %shard_map.86 = (f32[16,32,128]{2,1,0:T(8,128)S(1)}, bf16[8,16,256]{2,1,0:T(8,128)(2,1)S(1)}) custom-call(f32[16,32,128]{2,1,0:T(8,128)S(1)} %get-tuple-element.34.rows_ref, f32[3,32,128]{2,1,0:T(8,128)S(1)} %collective-permute-done.first_ref, f32[3,32,128]{2,1,0:T(8,128)S(1)} %collective-permute-done.1.second_ref, bf16[8,1,520,256]{3,2,1,0:T(8,128)(2,1)S(1)} %copy-done.2), custom_call_target="tpu_custom_call" | custom-call | flops 700000000 | bytes 2100000 | tf_op jit(solution)/shard_map/pallas_call | solution.py:241
  10.8 0.0 copy-start.1
  10.8 0.0 copy-start.3
  10.8 0.0 copy-start.6
  10.8 1.6 %collective-permute-done.5.refs_2_.refs_9_.refs_6_ = f32[136,128]{1,0:T(8,128)S(1)} collective-permute-done((f32[136,128]{1,0:T(8,128)S(1)}, f32[136,128]{1,0:T(8,128)S(1)}, u32[]{:S(2)}, u32[]{:S(2)}) %collective-permute-start.5) | collective-permute-done | bytes 69664 | tf_op jit(solution)/shard_map/ppermute | solution.py:755
  12.5 0.0 collective-permute-start.6
  12.5 0.5 %collective-permute-start.7 = (f32[136,128]{1,0:T(8,128)S(1)}, f32[136,128]{1,0:T(8,128)S(1)}, u32[]{:S(2)}, u32[]{:S(2)}) collective-permute-start(f32[136,128]{1,0:T(8,128)S(1)} %collective-permute-done.5.refs_2_.refs_9_.refs_6_), channel_id=1, source_target_pairs={{0,1},{1,0},{2,3},{3,2},{4,5},{5,4},{6,7},{7,6},{8,9},{9,8},{10,11... | collective-permute-start | bytes 208904 | tf_op jit(solution)/shard_map/ppermute | solution.py:755
  13.0 0.0 collective-permute-start.2
  13.0 0.9 %collective-permute-done.3.refs_5_.refs_2_ = f32[4,32,128]{2,1,0:T(8,128)S(1)} collective-permute-done((f32[4,32,128]{2,1,0:T(8,128)S(1)}, f32[4,32,128]{2,1,0:T(8,128)S(1)}, u32[]{:S(2)}, u32[]{:S(2)}) %collective-permute-start.3) | collective-permute-done | bytes 65568 | tf_op jit(solution)/shard_map/ppermute | solution.py:755
  13.9 0.0 collective-permute-start.4
  13.9 0.0 collective-permute-done.6.refs_1_.refs_8_.refs_5_
  13.9 0.0 collective-permute-done.7.refs_3_.refs_10_.refs_7_
  13.9 0.0 copy-done
  13.9 0.2 shard_map.87.refs_0_
  14.2 4.1 %collective-permute-start.8 = (f32[32,128]{1,0:T(8,128)S(1)}, f32[32,128]{1,0:T(8,128)S(1)}, u32[]{:S(2)}, u32[]{:S(2)}) collective-permute-start(f32[32,128]{1,0:T(8,128)S(1)} %shard_map.87.refs_0_), channel_id=1, source_target_pairs={{0,24},{1,17},{2,26},{3,19},{4,28},{5,21},{6,30},{7,23},{8,16},{9,... | collective-permute-start | bytes 49160 | tf_op jit(solution)/shard_map/ppermute | solution.py:820
  18.3 0.0 collective-permute-start.10
  18.3 0.0 collective-permute-done.2.refs_4_.refs_1_
  18.3 0.0 collective-permute-done.4.refs_6_.refs_3_
  18.3 0.0 copy-done.1
  18.3 0.0 copy-done.3
  18.3 0.0 copy-done.6
  18.3 0.9 %shard_map.88 = (f32[2,2,32,256]{3,2,1,0:T(8,128)S(1)}, f32[1,2,32,256]{3,2,1,0:T(8,128)S(1)}, f32[1,1,32,128]{3,2,1,0:T(8,128)S(1)}, f32[6,32,256]{2,1,0:T(8,12...) custom-call(bf16[102,128,128]{2,1,0:T(8,128)(2,1)S(1)} %copy-done, bf16[4,2,520,256]{3,2,1,0:T(8,128)(2,1)S(1)} %copy-done.1, ...), custom_call_target="tpu_custom_call" | custom-call | flops 2500000000 | bytes 7500000 | tf_op jit(solution)/shard_map/pallas_call | solution.py:241
  19.2 0.5 %collective-permute-start.11 = (f32[1,32,128]{2,1,0:T(8,128)S(1)}, f32[1,32,128]{2,1,0:T(8,128)S(1)}, u32[]{:S(2)}, u32[]{:S(2)}) collective-permute-start(f32[1,32,128]{2,1,0:T(8,128)S(1)} %get-tuple-element.59), channel_id=1, source_target_pairs={{0,1},{1,5},{2,3},{3,7},{4,0},{5,9},{6,2},{7,11},{8,4},{9,13},{10,... | collective-permute-start | bytes 49160 | tf_op jit(solution)/shard_map/ppermute | solution.py:742
  19.8 1.5 %collective-permute-start.12 = (f32[1,32,128]{2,1,0:T(8,128)S(1)}, f32[1,32,128]{2,1,0:T(8,128)S(1)}, u32[]{:S(2)}, u32[]{:S(2)}) collective-permute-start(f32[1,32,128]{2,1,0:T(8,128)S(1)} %get-tuple-element.60), channel_id=1, source_target_pairs={{1,0},{5,1},{3,2},{7,3},{0,4},{9,5},{2,6},{11,7},{4,8},{13,9},{6,1... | collective-permute-start | bytes 49160 | tf_op jit(solution)/shard_map/ppermute | solution.py:742
  21.3 0.0 collective-permute-done.8.refs_1_
  21.3 0.0 collective-permute-start.9
  21.3 0.0 copy-start.7
  21.4 0.6 %shard_map.89 = (f32[8,32,128]{2,1,0:T(8,128)S(1)}, f32[4,32,128]{2,1,0:T(8,128)S(1)}, f32[2,32,128]{2,1,0:T(8,128)S(1)}, f32[16,32,128]{2,1,0:T(8,128)S(1)}) custom-call(bf16[102,128,128]{2,1,0:T(8,128)(2,1)S(1)} %copy-done, bf16[4,2,520,256]{3,2,1,0:T(8,128)(2,1)S(1)} %copy-done.1, f32[6,32,256]{2,1,0:T(8,128)S(1)} %get-tuple-element.49.rows_ref, ...), custom_call_target="tpu_custom_call" | custom-call | flops 1200000000 | bytes 3600000 | tf_op jit(solution)/shard_map/pallas_call | solution.py:241
  22.0 0.0 collective-permute-done.10.refs_3_
  22.0 0.5 %collective-permute-done.9.refs_2_ = f32[32,128]{1,0:T(8,128)S(1)} collective-permute-done((f32[32,128]{1,0:T(8,128)S(1)}, f32[32,128]{1,0:T(8,128)S(1)}, u32[]{:S(2)}, u32[]{:S(2)}) %collective-permute-start.9) | collective-permute-done | bytes 16416 | tf_op jit(solution)/shard_map/ppermute | solution.py:755
  22.5 0.0 copy-done.5
  22.5 0.0 copy-done.7
  22.5 0.8 %shard_map.90.four_ref = f32[3,32,128]{2,1,0:T(8,128)S(1)} custom-call(bf16[102,128,128]{2,1,0:T(8,128)(2,1)S(1)} %copy-done, bf16[4,1,64,136]{3,2,1,0:T(8,128)(2,1)S(1)} %bitcast.4, bf16[64,64]{1,0:T(8,128)(2,1)S(1)} %copy-done.7, f32[32,128]{1,0:T(8,128)S(1)} %shard_map.87.refs_0_, f32[32,128]{1,0:T(8,128)S(1)} %collective-permute-done.8.refs_1_, ...), custom_call_target="tpu_custom_call" | custom-call | flops 1000000000 | bytes 3000000 | tf_op jit(solution)/shard_map/pallas_call | solution.py:241
  23.3 0.0 collective-permute-done.11.first_ref
  23.3 0.0 collective-permute-done.12.second_ref
  23.3 0.9 %shard_map.91 = f32[512,128]{1,0:T(8,128)} custom-call(bf16[102,128,128]{2,1,0:T(8,128)(2,1)S(1)} %copy-done, f32[16,32,128]{2,1,0:T(8,128)S(1)} %get-tuple-element.55.fine_ref, f32[8,32,128]{2,1,0:T(8,128)S(1)} %get-tuple-element.56.one_ref, f32[4,32,128]{2,1,0:T(8,128)S(1)} %get-tuple-element.57.two_ref, f32[2,32,128]{2,1,0:T(8,128)S(1)} %get-tuple-element.58.three_ref, ...), custom_call_target="tpu_custom_call" | custom-call | flops 1000000000 | bytes 3000000 | tf_op jit(solution)/shard_map/pallas_call | solution.py:241
  (4 shorter events, 0.0 us)
Async XLA Ops:
  0.0 0.9 %copy-start.4 = (f32[32,16,128]{2,1,0:T(8,128)S(1)}, f32[32,16,128]{2,1,0:T(8,128)}, u32[]{:S(2)}) copy-start(f32[32,16,128]{2,1,0:T(8,128)} %param.8) | copy-start | bytes 786436
  1.3 4.7 %collective-permute-start = (f32[3,32,128]{2,1,0:T(8,128)S(1)}, f32[3,32,128]{2,1,0:T(8,128)S(1)}, u32[]{:S(2)}, u32[]{:S(2)}) collective-permute-start(f32[3,32,128]{2,1,0:T(8,128)S(1)} %get-tuple-element.35), channel_id=1, source_target_pairs={{0,1},{1,0},{2,3},{3,2},{4,8},{5,9},{6,10},{7,11},{8,4},{9,5},{10,... | collective-permute-start | bytes 147464 | tf_op jit(solution)/shard_map/ppermute | solution.py:752
  1.8 6.1 %collective-permute-start.1 = (f32[3,32,128]{2,1,0:T(8,128)S(1)}, f32[3,32,128]{2,1,0:T(8,128)S(1)}, u32[]{:S(2)}, u32[]{:S(2)}) collective-permute-start(f32[3,32,128]{2,1,0:T(8,128)S(1)} %get-tuple-element.36), channel_id=1, source_target_pairs={{0,4},{4,0},{8,12},{12,8},{16,20},{20,16},{24,28},{28,24},{1,5},{5... | collective-permute-start | bytes 147464 | tf_op jit(solution)/shard_map/ppermute | solution.py:752
  5.9 4.3 %copy-start.2 = (bf16[8,1,520,256]{3,2,1,0:T(8,128)(2,1)S(1)}, bf16[8,1,520,256]{3,2,1,0:T(8,128)(2,1)}, u32[]{:S(2)}) copy-start(bf16[8,1,520,256]{3,2,1,0:T(8,128)(2,1)} %factor_ref.2) | copy-start | bytes 6389764
  7.9 6.0 %copy-start = (bf16[102,128,128]{2,1,0:T(8,128)(2,1)S(1)}, bf16[102,128,128]{2,1,0:T(8,128)(2,1)}, u32[]{:S(2)}) copy-start(bf16[102,128,128]{2,1,0:T(8,128)(2,1)} %constant.2.clone.block_ref) | copy-start | bytes 10027012
  8.1 4.4 %collective-permute-start.5 = (f32[136,128]{1,0:T(8,128)S(1)}, f32[136,128]{1,0:T(8,128)S(1)}, u32[]{:S(2)}, u32[]{:S(2)}) collective-permute-start(f32[136,128]{1,0:T(8,128)S(1)} %shard_map.85.refs_0_.refs_7_.refs_4_), channel_id=1, source_target_pairs={{0,2},{1,3},{2,0},{3,1},{4,6},{5,7},{6,4},{7,5},{8,10},{9,11},{10,... | collective-permute-start | bytes 208904 | tf_op jit(solution)/shard_map/ppermute | solution.py:755
  9.6 4.3 %collective-permute-start.3 = (f32[4,32,128]{2,1,0:T(8,128)S(1)}, f32[4,32,128]{2,1,0:T(8,128)S(1)}, u32[]{:S(2)}, u32[]{:S(2)}) collective-permute-start(f32[4,32,128]{2,1,0:T(8,128)S(1)} %shard_map.84.refs_3_.refs_0_), channel_id=1, source_target_pairs={{0,2},{1,3},{2,0},{3,1},{4,6},{5,7},{6,4},{7,5},{8,10},{9,11},{10,... | collective-permute-start | bytes 196616 | tf_op jit(solution)/shard_map/ppermute | solution.py:755
  10.8 7.5 %copy-start.1 = (bf16[4,2,520,256]{3,2,1,0:T(8,128)(2,1)S(1)}, bf16[4,2,520,256]{3,2,1,0:T(8,128)(2,1)}, u32[]{:S(2)}) copy-start(bf16[4,2,520,256]{3,2,1,0:T(8,128)(2,1)} %factor_ref.3) | copy-start | bytes 6389764
  10.8 7.5 %copy-start.3 = (bf16[2,1,520,256]{3,2,1,0:T(8,128)(2,1)S(1)}, bf16[2,1,520,256]{3,2,1,0:T(8,128)(2,1)}, u32[]{:S(2)}) copy-start(bf16[2,1,520,256]{3,2,1,0:T(8,128)(2,1)} %refs_1_.1) | copy-start | bytes 1597444
  10.8 7.5 %copy-start.6 = (bf16[1,1,264,128]{3,2,1,0:T(8,128)(2,1)S(1)}, bf16[1,1,264,128]{3,2,1,0:T(8,128)(2,1)}, u32[]{:S(2)}) copy-start(bf16[1,1,264,128]{3,2,1,0:T(8,128)(2,1)} %refs_2_.1) | copy-start | bytes 202756
  12.5 1.5 %collective-permute-start.6 = (f32[136,128]{1,0:T(8,128)S(1)}, f32[136,128]{1,0:T(8,128)S(1)}, u32[]{:S(2)}, u32[]{:S(2)}) collective-permute-start(f32[136,128]{1,0:T(8,128)S(1)} %shard_map.85.refs_0_.refs_7_.refs_4_), channel_id=1, source_target_pairs={{0,1},{1,0},{2,3},{3,2},{4,5},{5,4},{6,7},{7,6},{8,9},{9,8},{10,11... | collective-permute-start | bytes 208904 | tf_op jit(solution)/shard_map/ppermute | solution.py:755
  12.5 1.5 %collective-permute-start.7 = (f32[136,128]{1,0:T(8,128)S(1)}, f32[136,128]{1,0:T(8,128)S(1)}, u32[]{:S(2)}, u32[]{:S(2)}) collective-permute-start(f32[136,128]{1,0:T(8,128)S(1)} %collective-permute-done.5.refs_2_.refs_9_.refs_6_), channel_id=1, source_target_pairs={{0,1},{1,0},{2,3},{3,2},{4,5},{5,4},{6,7},{7,6},{8,9},{9,8},{10,11... | collective-permute-start | bytes 208904 | tf_op jit(solution)/shard_map/ppermute | solution.py:755
  13.0 5.3 %collective-permute-start.2 = (f32[4,32,128]{2,1,0:T(8,128)S(1)}, f32[4,32,128]{2,1,0:T(8,128)S(1)}, u32[]{:S(2)}, u32[]{:S(2)}) collective-permute-start(f32[4,32,128]{2,1,0:T(8,128)S(1)} %shard_map.84.refs_3_.refs_0_), channel_id=1, source_target_pairs={{0,1},{1,0},{2,3},{3,2},{4,5},{5,4},{6,7},{7,6},{8,9},{9,8},{10,11... | collective-permute-start | bytes 196616 | tf_op jit(solution)/shard_map/ppermute | solution.py:755
  13.9 4.3 %collective-permute-start.4 = (f32[4,32,128]{2,1,0:T(8,128)S(1)}, f32[4,32,128]{2,1,0:T(8,128)S(1)}, u32[]{:S(2)}, u32[]{:S(2)}) collective-permute-start(f32[4,32,128]{2,1,0:T(8,128)S(1)} %collective-permute-done.3.refs_5_.refs_2_), channel_id=1, source_target_pairs={{0,1},{1,0},{2,3},{3,2},{4,5},{5,4},{6,7},{7,6},{8,9},{9,8},{10,11... | collective-permute-start | bytes 196616 | tf_op jit(solution)/shard_map/ppermute | solution.py:755
  14.2 7.2 %collective-permute-start.8 = (f32[32,128]{1,0:T(8,128)S(1)}, f32[32,128]{1,0:T(8,128)S(1)}, u32[]{:S(2)}, u32[]{:S(2)}) collective-permute-start(f32[32,128]{1,0:T(8,128)S(1)} %shard_map.87.refs_0_), channel_id=1, source_target_pairs={{0,24},{1,17},{2,26},{3,19},{4,28},{5,21},{6,30},{7,23},{8,16},{9,... | collective-permute-start | bytes 49160 | tf_op jit(solution)/shard_map/ppermute | solution.py:820
  18.3 3.7 %collective-permute-start.10 = (f32[32,128]{1,0:T(8,128)S(1)}, f32[32,128]{1,0:T(8,128)S(1)}, u32[]{:S(2)}, u32[]{:S(2)}) collective-permute-start(f32[32,128]{1,0:T(8,128)S(1)} %shard_map.87.refs_0_), channel_id=1, source_target_pairs={{0,8},{1,9},{2,10},{3,11},{4,12},{5,13},{6,14},{7,15},{8,0},{9,1},... | collective-permute-start | bytes 49160 | tf_op jit(solution)/shard_map/ppermute | solution.py:820
  19.2 4.1 %collective-permute-start.11 = (f32[1,32,128]{2,1,0:T(8,128)S(1)}, f32[1,32,128]{2,1,0:T(8,128)S(1)}, u32[]{:S(2)}, u32[]{:S(2)}) collective-permute-start(f32[1,32,128]{2,1,0:T(8,128)S(1)} %get-tuple-element.59), channel_id=1, source_target_pairs={{0,1},{1,5},{2,3},{3,7},{4,0},{5,9},{6,2},{7,11},{8,4},{9,13},{10,... | collective-permute-start | bytes 49160 | tf_op jit(solution)/shard_map/ppermute | solution.py:742
  19.8 3.5 %collective-permute-start.12 = (f32[1,32,128]{2,1,0:T(8,128)S(1)}, f32[1,32,128]{2,1,0:T(8,128)S(1)}, u32[]{:S(2)}, u32[]{:S(2)}) collective-permute-start(f32[1,32,128]{2,1,0:T(8,128)S(1)} %get-tuple-element.60), channel_id=1, source_target_pairs={{1,0},{5,1},{3,2},{7,3},{0,4},{9,5},{2,6},{11,7},{4,8},{13,9},{6,1... | collective-permute-start | bytes 49160 | tf_op jit(solution)/shard_map/ppermute | solution.py:742
  21.3 1.2 %collective-permute-start.9 = (f32[32,128]{1,0:T(8,128)S(1)}, f32[32,128]{1,0:T(8,128)S(1)}, u32[]{:S(2)}, u32[]{:S(2)}) collective-permute-start(f32[32,128]{1,0:T(8,128)S(1)} %collective-permute-done.8.refs_1_), channel_id=1, source_target_pairs={{0,1},{1,0},{2,3},{3,2},{4,5},{5,4},{6,7},{7,6},{8,9},{9,8},{10,11... | collective-permute-start | bytes 49160 | tf_op jit(solution)/shard_map/ppermute | solution.py:755
  21.3 1.2 %copy-start.5 = (bf16[4,1,136,64]{2,3,1,0:T(8,128)(2,1)S(1)}, bf16[4,1,136,64]{2,3,1,0:T(8,128)(2,1)}, u32[]{:S(2)}) copy-start(bf16[4,1,136,64]{2,3,1,0:T(8,128)(2,1)} %param.13) | copy-start | bytes 208900
  21.3 1.2 %copy-start.7 = (bf16[64,64]{1,0:T(8,128)(2,1)S(1)}, bf16[64,64]{1,0:T(8,128)(2,1)}, u32[]{:S(2)}) copy-start(bf16[64,64]{1,0:T(8,128)(2,1)} %inverse_ref.1) | copy-start | bytes 24580
